TPU v7x, 32 devices: a whole 2x2x4 slice. The times are simulated.
32 devices in a mesh: parts: 2 (over x), fft: 16 (over z, y, core).
Axes of the slice: x: 2, y: 2, z: 4, core: 2. Of those that a mesh axis runs over, the one named last changes fastest.
Arguments:
- potential: float32 [4, 2048, 4096], P('parts', 'fft'), parts along dimension 0, may hold values from -1.2 to 1.2
- direction: float32 [4, 2048, 4096], P('parts', 'fft'), parts along dimension 0, may hold values from -6 to 6
- block_index: int32 [2, 32, 2], replicated, may hold values from 0 to 31
- block_weights: float32 [2, 32, 2, 128, 128], replicated, may hold values from -0.375 to 0.375
Outputs:
- hessian_product: float32 [4, 2048, 4096], P('parts', 'fft'), parts along dimension 0
There are 2 independent parts, one for each index of `parts`. A program takes and returns all parts, laid end to end along the dimension named above; an argument that names none is the same for every part. Nothing has to cross between parts.
All inputs are finite; a program needn't handle non-finite values.
Results may differ from a plain program's by a relative error of at most 0.00018.
Values sent between devices are 32-bit elements; how exact they have to be, the bound alone decides.
No kernel may reach another device: no remote copies, remote signals or barrier semaphores. Data moves between devices by JAX's collectives and lax.ppermute only.
A program may use at most 256 MiB of HBM per device.

v0:
```python
import math

import jax
import jax.numpy as jnp
from jax import lax
from jax.sharding import PartitionSpec as P

XA = 16
XB = 128
NX = 2048
SL = 2
ANGLES = 2
BLK = 128
NB = 32


PRECISE = lax.Precision.HIGHEST


def transform_table(count_in, count_out, length, orient):
    first = jnp.arange(count_in, dtype=jnp.int32)[:, None]
    second = jnp.arange(count_out, dtype=jnp.int32)[None, :]
    phases = orient * 2.0 * math.pi / length * (first * second % length).astype(jnp.float32)
    cosine = jnp.cos(phases)
    sine_part = jnp.sin(phases)
    return jnp.stack([jnp.stack([cosine, sine_part]), jnp.stack([-sine_part, cosine])])


def twiddle_pair(count_a, count_b, length, orient):
    first = jnp.arange(count_a, dtype=jnp.int32)[:, None]
    second = jnp.arange(count_b, dtype=jnp.int32)[None, :]
    phases = orient * 2.0 * math.pi / length * (first * second % length).astype(jnp.float32)
    return (jnp.cos(phases), jnp.sin(phases))


def spread_turn(peer_count, row_count, slot_count, orient):
    turn_re, turn_im = twiddle_pair(peer_count, row_count, NX, orient)
    shape_three = (row_count, peer_count, slot_count)
    wide_re = jnp.broadcast_to(turn_re.T[:, :, None], shape_three).reshape(
        row_count, peer_count * slot_count
    )
    wide_im = jnp.broadcast_to(turn_im.T[:, :, None], shape_three).reshape(
        row_count, peer_count * slot_count
    )
    return (wide_re, wide_im)


def complex_times(values, real_part, imag_part):
    first = values[:, 0]
    second = values[:, 1]
    return jnp.stack(
        [first * real_part - second * imag_part, first * imag_part + second * real_part], axis=1
    )


def one_hot(index_rows, block_count):
    return (index_rows[..., None] == jnp.arange(block_count, dtype=jnp.int32)).astype(jnp.float32)


def rotate(values, selector, matrices):
    height = values.shape[1]
    blocked = values.reshape(2, height, NB, BLK)
    picked = jnp.einsum("cyni,bsn->cybsi", blocked, selector, precision=PRECISE)
    rotated = jnp.einsum("cybsi,bsio->cybo", picked, matrices, precision=PRECISE)
    return rotated.reshape(2, height, SL, NX)


def rotate_back(values, selector, matrices):
    height = values.shape[1]
    blocked = values.reshape(2, height, NB, BLK)
    spread_out = jnp.einsum("cybo,bsio->cybsi", blocked, matrices, precision=PRECISE)
    summed = jnp.einsum("cybsi,bsn->cyni", spread_out, selector, precision=PRECISE)
    return summed.reshape(2, height, SL * NX)


def fresnel(peer_count, row_count, slot_count, orient):
    position_high = jnp.arange(row_count, dtype=jnp.int32)[:, None]
    position_low = jnp.arange(peer_count, dtype=jnp.int32)[None, :]
    freq_y = position_low + peer_count * position_high
    freq_y = jnp.where(freq_y < NX // 2, freq_y, freq_y - NX)
    position = lax.axis_index("fft") * slot_count + jnp.arange(slot_count, dtype=jnp.int32)
    freq_x = position // XB + XA * (position % XB)
    freq_x = jnp.where(freq_x < NX // 2, freq_x, freq_x - NX)
    squares = ((freq_y * freq_y)[:, :, None] + (freq_x * freq_x)[None, None, :]) % (2 * NX)
    phases = orient * -math.pi / NX * squares.astype(jnp.float32)
    scaling = 1.0 / (NX * NX)
    phases = phases.reshape(row_count, peer_count * slot_count)
    return (jnp.cos(phases) * scaling, jnp.sin(phases) * scaling)


def propagate(fields, kernel, peer_count, row_count, slot_count):
    field_count = fields.shape[0]
    groups = XB // slot_count
    shaped = fields.reshape(field_count, 2, row_count, XA, XB)
    partial_x = jnp.einsum(
        "fcrab,cdak->fdrkb", shaped, transform_table(XA, XA, XA, -1.0), precision=PRECISE
    )
    twist_re, twist_im = twiddle_pair(XA, XB, NX, -1.0)
    partial_x = complex_times(partial_x, twist_re, twist_im)
    partial_x = jnp.einsum(
        "fcrkb,cdbt->fdrkt", partial_x, transform_table(XB, XB, XB, -1.0), precision=PRECISE
    )
    partial_x = partial_x.reshape(field_count, 2, row_count, XA, groups, slot_count)
    outgoing = partial_x.transpose(0, 1, 3, 4, 2, 5).reshape(
        field_count, 2, peer_count, row_count * slot_count
    )
    forward_re, forward_im = spread_turn(peer_count, row_count, slot_count, -1.0)
    inverse_re, inverse_im = spread_turn(peer_count, row_count, slot_count, 1.0)
    wide = peer_count * slot_count
    incoming = lax.all_to_all(outgoing, "fft", split_axis=2, concat_axis=2, tiled=True)
    item_count = incoming.shape[0]
    lattice = incoming.reshape(item_count, 2, peer_count, row_count, slot_count)
    lattice = jnp.einsum(
        "fcprs,cdpk->fdrks",
        lattice,
        transform_table(peer_count, peer_count, peer_count, -1.0),
        precision=PRECISE,
    )
    lattice = lattice.reshape(item_count, 2, row_count, wide)
    lattice = complex_times(lattice, forward_re, forward_im)
    lattice = jnp.einsum(
        "fcrq,cdrm->fdmq",
        lattice,
        transform_table(row_count, row_count, row_count, -1.0),
        precision=PRECISE,
    )
    lattice = complex_times(lattice, kernel[0], kernel[1])
    lattice = jnp.einsum(
        "fcmq,cdmr->fdrq",
        lattice,
        transform_table(row_count, row_count, row_count, 1.0),
        precision=PRECISE,
    )
    lattice = complex_times(lattice, inverse_re, inverse_im)
    lattice = lattice.reshape(item_count, 2, row_count, peer_count, slot_count)
    lattice = jnp.einsum(
        "fcrks,cdkp->fdprs",
        lattice,
        transform_table(peer_count, peer_count, peer_count, 1.0),
        precision=PRECISE,
    )
    returning = lax.all_to_all(
        lattice.reshape(item_count, 2, peer_count, row_count * slot_count),
        "fft",
        split_axis=2,
        concat_axis=2,
        tiled=True,
    )
    restored = returning.reshape(item_count, 2, XA, groups, row_count, slot_count)
    matrix_back = transform_table(XB, XB, XB, 1.0).reshape(2, 2, groups, slot_count, XB)
    restored = jnp.einsum("fckjrs,cdjsb->fdrkb", restored, matrix_back, precision=PRECISE)
    back_re, back_im = twiddle_pair(XA, XB, NX, 1.0)
    restored = complex_times(restored, back_re, back_im)
    restored = jnp.einsum(
        "fcrkb,cdkn->fdrnb", restored, transform_table(XA, XA, XA, 1.0), precision=PRECISE
    )
    return restored.reshape(item_count, 2, row_count, NX)


def body(potential, direction, block_index, block_weights):
    row_count = potential.shape[1]
    peer_count = lax.axis_size("fft")
    slot_count = NX // peer_count
    ahead = fresnel(peer_count, row_count, slot_count, 1.0)
    behind = fresnel(peer_count, row_count, slot_count, -1.0)
    accumulated = jnp.zeros(potential.shape, jnp.float32)
    for angle_index in range(ANGLES):
        selector = one_hot(block_index[angle_index], NB)
        matrices = block_weights[angle_index]
        rotated = rotate(potential, selector, matrices)
        tangent = rotate(direction, selector, matrices)
        damping = jnp.exp(-rotated[1])
        trans_re = damping * jnp.cos(rotated[0])
        trans_im = damping * jnp.sin(rotated[0])
        wave_re = jnp.ones((row_count, NX), jnp.float32)
        wave_im = jnp.zeros((row_count, NX), jnp.float32)
        dwave_re = jnp.zeros((row_count, NX), jnp.float32)
        dwave_im = jnp.zeros((row_count, NX), jnp.float32)
        stored = []
        for slice_index in range(SL):
            t_re = trans_re[:, slice_index]
            t_im = trans_im[:, slice_index]
            d_re = tangent[0][:, slice_index]
            d_im = tangent[1][:, slice_index]
            phi_re = t_re * wave_re - t_im * wave_im
            phi_im = t_re * wave_im + t_im * wave_re
            dphi_re = -(d_re * phi_im + d_im * phi_re) + t_re * dwave_re - t_im * dwave_im
            dphi_im = d_re * phi_re - d_im * phi_im + t_re * dwave_im + t_im * dwave_re
            stored.append((phi_re, phi_im))
            packed = jnp.stack([jnp.stack([phi_re, phi_im]), jnp.stack([dphi_re, dphi_im])])
            propagated = propagate(packed, ahead, peer_count, row_count, slot_count)
            wave_re = propagated[0, 0]
            wave_im = propagated[0, 1]
            dwave_re = propagated[1, 0]
            dwave_im = propagated[1, 1]
        change = 2.0 * (wave_re * dwave_re + wave_im * dwave_im)
        back_re = 2.0 * change * wave_re
        back_im = 2.0 * change * wave_im
        grad_re = [None] * SL
        grad_im = [None] * SL
        for slice_index in reversed(range(SL)):
            pulled = propagate(
                jnp.stack([back_re, back_im])[None], behind, peer_count, row_count, slot_count
            )
            pb_re = pulled[0, 0]
            pb_im = pulled[0, 1]
            phi_re, phi_im = stored[slice_index]
            grad_re[slice_index] = phi_re * pb_im - phi_im * pb_re
            grad_im[slice_index] = -(phi_re * pb_re + phi_im * pb_im)
            t_re = trans_re[:, slice_index]
            t_im = trans_im[:, slice_index]
            back_re = t_re * pb_re + t_im * pb_im
            back_im = t_re * pb_im - t_im * pb_re
        gradient = jnp.stack([jnp.stack(grad_re, axis=1), jnp.stack(grad_im, axis=1)])
        accumulated = accumulated + rotate_back(gradient, selector, matrices)
    return accumulated


def solution(mesh):
    return jax.shard_map(
        body,
        mesh=mesh,
        in_specs=(P("parts", "fft", None), P("parts", "fft", None), P(), P()),
        out_specs=P("parts", "fft", None),
        check_vma=False,
    )
```

profile of v0, /device:TPU:3, one launch (start us, length us, event | category | flops | bytes accessed | tf_op | source)
XLA Modules:
  0.0 1907.3 jit_solution(18385592136625545627)
XLA Ops:
  13.7 15.1 fusion.224
  40.0 17.9 fusion.219
  118.8 62.3 %all-to-all-done = f32[2,2,16,16384]{3,1,0,2:T(2,128)} async-done(((f32[2,2,16,16384]{3,1,0,2:T(2,128)}), f32[2,2,16,16384]{3,1,0,2:T(2,128)}, u32[]{:S(2)}, u32[]{:S(2)}) %all-to-all-start) | async-done | bytes 4194336 | tf_op jit(solution)/shard_map/all_to_all | solution.py:110
  230.5 19.3 %all-to-all-start.1 = ((f32[2,2,16,16384]{3,1,0,2:T(2,128)}), f32[2,2,16,16384]{3,1,0,2:T(2,128)}, u32[]{:S(2)}, u32[]{:S(2)}) async-start(f32[2,2,16,16384]{3,1,0,2:T(2,128)} %reshape.2989), calls=%async_computation.1 | async-start | bytes 8388608 | tf_op jit(solution)/shard_map/all_to_all | solution.py:142
  255.2 17.9 fusion.234
  290.1 17.9 fusion.229
  412.9 11.6 all-to-all-start.2
  443.5 59.1 %all-to-all-done.2 = f32[2,2,16,16384]{3,1,0,2:T(2,128)} async-done(((f32[2,2,16,16384]{3,1,0,2:T(2,128)}), f32[2,2,16,16384]{3,1,0,2:T(2,128)}, u32[]{:S(2)}, u32[]{:S(2)}) %all-to-all-start.2) | async-done | bytes 4194336 | tf_op jit(solution)/shard_map/all_to_all | solution.py:110
  502.6 19.6 %all-to-all-start.8 = ((f32[2,2,16,16384]{3,1,0,2:T(2,128)}), f32[2,2,16,16384]{3,1,0,2:T(2,128)}, u32[]{:S(2)}, u32[]{:S(2)}) async-start(f32[2,2,16,16384]{3,1,0,2:T(2,128)} %reshape.3000), calls=%async_computation.8 | async-start | bytes 8388608 | tf_op jit(solution)/shard_map/all_to_all | solution.py:110
  543.8 56.4 %all-to-all-done.8 = f32[2,2,16,16384]{3,1,0,2:T(2,128)} async-done(((f32[2,2,16,16384]{3,1,0,2:T(2,128)}), f32[2,2,16,16384]{3,1,0,2:T(2,128)}, u32[]{:S(2)}, u32[]{:S(2)}) %all-to-all-start.8) | async-done | bytes 4194336 | tf_op jit(solution)/shard_map/all_to_all | solution.py:110
  668.8 19.3 %all-to-all-start.3 = ((f32[2,2,16,16384]{3,1,0,2:T(2,128)}), f32[2,2,16,16384]{3,1,0,2:T(2,128)}, u32[]{:S(2)}, u32[]{:S(2)}) async-start(f32[2,2,16,16384]{3,1,0,2:T(2,128)} %reshape.2994), calls=%async_computation.3 | async-start | bytes 8388608 | tf_op jit(solution)/shard_map/all_to_all | solution.py:142
  703.5 62.6 %all-to-all-done.3 = f32[2,2,16,16384]{3,1,0,2:T(2,128)} async-done(((f32[2,2,16,16384]{3,1,0,2:T(2,128)}), f32[2,2,16,16384]{3,1,0,2:T(2,128)}, u32[]{:S(2)}, u32[]{:S(2)}) %all-to-all-start.3) | async-done | bytes 4194336 | tf_op jit(solution)/shard_map/all_to_all | solution.py:142
  766.2 19.8 %all-to-all-start.9 = ((f32[2,2,16,16384]{3,1,0,2:T(2,128)}), f32[2,2,16,16384]{3,1,0,2:T(2,128)}, u32[]{:S(2)}, u32[]{:S(2)}) async-start(f32[2,2,16,16384]{3,1,0,2:T(2,128)} %reshape.3003), calls=%async_computation.9 | async-start | bytes 8388608 | tf_op jit(solution)/shard_map/all_to_all | solution.py:142
  810.1 53.9 %all-to-all-done.9 = f32[2,2,16,16384]{3,1,0,2:T(2,128)} async-done(((f32[2,2,16,16384]{3,1,0,2:T(2,128)}), f32[2,2,16,16384]{3,1,0,2:T(2,128)}, u32[]{:S(2)}, u32[]{:S(2)}) %all-to-all-start.9) | async-done | bytes 4194336 | tf_op jit(solution)/shard_map/all_to_all | solution.py:142
  942.8 112.0 %all_to_all.80 = f32[2,2,16,16384]{3,1,0,2:T(2,128)} all-to-all(f32[2,2,16,16384]{3,1,0,2:T(2,128)} %reshape.3005), channel_id=1, replica_groups=mesh['parts'=2,'fft'=16] {'fft'}, dimensions={2} | all-to-all | bytes 8388608 | tf_op jit(solution)/shard_map/all_to_all | solution.py:110
  1136.9 50.5 %all-to-all-done.11 = f32[2,2,16,16384]{3,1,0,2:T(2,128)} async-done(((f32[2,2,16,16384]{3,1,0,2:T(2,128)}), f32[2,2,16,16384]{3,1,0,2:T(2,128)}, u32[]{:S(2)}, u32[]{:S(2)}) %all-to-all-start.11) | async-done | bytes 4194336 | tf_op jit(solution)/shard_map/all_to_all | solution.py:142
  1236.1 19.4 %all-to-all-start.4 = ((f32[1,2,16,16384]{3,0,1,2:T(1,128)}), f32[1,2,16,16384]{3,0,1,2:T(1,128)}, u32[]{:S(2)}, u32[]{:S(2)}) async-start(f32[1,2,16,16384]{3,0,1,2:T(1,128)} %copy.657), calls=%async_computation.4 | async-start | bytes 4194304 | tf_op jit(solution)/shard_map/all_to_all | solution.py:110
  1263.2 34.0 %all-to-all-done.4 = f32[1,2,16,16384]{3,0,1,2:T(1,128)} async-done(((f32[1,2,16,16384]{3,0,1,2:T(1,128)}), f32[1,2,16,16384]{3,0,1,2:T(1,128)}, u32[]{:S(2)}, u32[]{:S(2)}) %all-to-all-start.4) | async-done | bytes 2097184 | tf_op jit(solution)/shard_map/all_to_all | solution.py:110
  1297.1 11.2 all-to-all-start.12
  1326.4 23.3 %all-to-all-done.12 = f32[1,2,16,16384]{3,0,1,2:T(1,128)} async-done(((f32[1,2,16,16384]{3,0,1,2:T(1,128)}), f32[1,2,16,16384]{3,0,1,2:T(1,128)}, u32[]{:S(2)}, u32[]{:S(2)}) %all-to-all-start.12) | async-done | bytes 2097184 | tf_op jit(solution)/shard_map/all_to_all | solution.py:110
  1386.0 10.9 all-to-all-start.5
  1409.9 28.4 %all-to-all-done.5 = f32[1,2,16,16384]{3,1,0,2:T(2,128)S(1)} async-done(((f32[1,2,16,16384]{3,1,0,2:T(2,128)}), f32[1,2,16,16384]{3,1,0,2:T(2,128)S(1)}, u32[]{:S(2)}, u32[]{:S(2)}) %all-to-all-start.5) | async-done | bytes 2097184 | tf_op jit(solution)/shard_map/all_to_all | solution.py:142
  1438.3 11.2 all-to-all-start.13
  1457.1 33.7 %all-to-all-done.13 = f32[1,2,16,16384]{3,1,0,2:T(2,128)} async-done(((f32[1,2,16,16384]{3,1,0,2:T(2,128)}), f32[1,2,16,16384]{3,1,0,2:T(2,128)}, u32[]{:S(2)}, u32[]{:S(2)}) %all-to-all-start.13) | async-done | bytes 2097184 | tf_op jit(solution)/shard_map/all_to_all | solution.py:142
  1549.7 10.9 all-to-all-start.6
  1572.1 30.0 %all-to-all-done.6 = f32[1,2,16,16384]{3,0,1,2:T(1,128)} async-done(((f32[1,2,16,16384]{3,0,1,2:T(1,128)}), f32[1,2,16,16384]{3,0,1,2:T(1,128)}, u32[]{:S(2)}, u32[]{:S(2)}) %all-to-all-start.6) | async-done | bytes 2097184 | tf_op jit(solution)/shard_map/all_to_all | solution.py:110
  1602.1 11.2 all-to-all-start.14
  1621.9 32.8 %all-to-all-done.14 = f32[1,2,16,16384]{3,0,1,2:T(1,128)} async-done(((f32[1,2,16,16384]{3,0,1,2:T(1,128)}), f32[1,2,16,16384]{3,0,1,2:T(1,128)}, u32[]{:S(2)}, u32[]{:S(2)}) %all-to-all-start.14) | async-done | bytes 2097184 | tf_op jit(solution)/shard_map/all_to_all | solution.py:110
  1693.8 10.9 all-to-all-start.7
  1717.7 28.5 %all-to-all-done.7 = f32[1,2,16,16384]{3,1,0,2:T(2,128)} async-done(((f32[1,2,16,16384]{3,1,0,2:T(2,128)}), f32[1,2,16,16384]{3,1,0,2:T(2,128)}, u32[]{:S(2)}, u32[]{:S(2)}) %all-to-all-start.7) | async-done | bytes 2097184 | tf_op jit(solution)/shard_map/all_to_all | solution.py:142
  1746.2 11.2 all-to-all-start.15
  1766.3 32.5 %all-to-all-done.15 = f32[1,2,16,16384]{3,1,0,2:T(2,128)} async-done(((f32[1,2,16,16384]{3,1,0,2:T(2,128)}), f32[1,2,16,16384]{3,1,0,2:T(2,128)}, u32[]{:S(2)}, u32[]{:S(2)}) %all-to-all-start.15) | async-done | bytes 2097184 | tf_op jit(solution)/shard_map/all_to_all | solution.py:142
  (510 shorter events, 949.7 us)
Async XLA Ops:
  2.1 32.1 %copy-start.82 = (s32[32,2]{0,1:T(2,128)}, s32[32,2]{0,1:T(2,128)S(1)}, u32[]{:S(2)}) copy-start(s32[32,2]{0,1:T(2,128)S(1)} %get-tuple-element.211) | copy-start | bytes 772
  2.1 282.4 %copy-start.84 = (s32[32,2]{0,1:T(2,128)}, s32[32,2]{0,1:T(2,128)S(1)}, u32[]{:S(2)}) copy-start(s32[32,2]{0,1:T(2,128)S(1)} %get-tuple-element.212) | copy-start | bytes 772
  7.2 6.5 slice-start
  96.1 85.0 %all-to-all-start = ((f32[2,2,16,16384]{3,1,0,2:T(2,128)}), f32[2,2,16,16384]{3,1,0,2:T(2,128)}, u32[]{:S(2)}, u32[]{:S(2)}) async-start(f32[2,2,16,16384]{3,1,0,2:T(2,128)} %reshape.2987), calls=%async_computation | async-start | bytes 8388608 | tf_op jit(solution)/shard_map/all_to_all | solution.py:110
  110.6 99.8 %copy-start.5 = (f32[128,2048]{1,0:T(8,128)}, f32[128,2048]{1,0:T(8,128)S(1)}, u32[]{:S(2)}) copy-start(f32[128,2048]{1,0:T(8,128)S(1)} %get-tuple-element.185) | copy-start | bytes 3145732
  110.6 99.8 %copy-start.7 = (f32[128,2048]{1,0:T(8,128)}, f32[128,2048]{1,0:T(8,128)S(1)}, u32[]{:S(2)}) copy-start(f32[128,2048]{1,0:T(8,128)S(1)} %get-tuple-element.186) | copy-start | bytes 3145732
  230.5 105.1 %all-to-all-start.1 = ((f32[2,2,16,16384]{3,1,0,2:T(2,128)}), f32[2,2,16,16384]{3,1,0,2:T(2,128)}, u32[]{:S(2)}, u32[]{:S(2)}) async-start(f32[2,2,16,16384]{3,1,0,2:T(2,128)} %reshape.2989), calls=%async_computation.1 | async-start | bytes 8388608 | tf_op jit(solution)/shard_map/all_to_all | solution.py:142
  325.2 63.4 %copy-start.19 = (f32[1,1,128,16,128]{4,3,1,2,0:T(8,128)}, f32[1,1,128,16,128]{4,3,1,2,0:T(8,128)S(1)}, u32[]{:S(2)}) copy-start(f32[1,1,128,16,128]{4,3,1,2,0:T(8,128)S(1)} %copy.919) | copy-start | bytes 3145732
  327.3 61.3 %copy-start.21 = (f32[1,1,128,16,128]{4,3,1,2,0:T(8,128)}, f32[1,1,128,16,128]{4,3,1,2,0:T(8,128)S(1)}, u32[]{:S(2)}) copy-start(f32[1,1,128,16,128]{4,3,1,2,0:T(8,128)S(1)} %copy.886) | copy-start | bytes 3145732
  412.9 89.7 %all-to-all-start.2 = ((f32[2,2,16,16384]{3,1,0,2:T(2,128)}), f32[2,2,16,16384]{3,1,0,2:T(2,128)}, u32[]{:S(2)}, u32[]{:S(2)}) async-start(f32[2,2,16,16384]{3,1,0,2:T(2,128)} %reshape.2991), calls=%async_computation.2 | async-start | bytes 8388608 | tf_op jit(solution)/shard_map/all_to_all | solution.py:110
  502.6 97.6 %all-to-all-start.8 = ((f32[2,2,16,16384]{3,1,0,2:T(2,128)}), f32[2,2,16,16384]{3,1,0,2:T(2,128)}, u32[]{:S(2)}, u32[]{:S(2)}) async-start(f32[2,2,16,16384]{3,1,0,2:T(2,128)} %reshape.3000), calls=%async_computation.8 | async-start | bytes 8388608 | tf_op jit(solution)/shard_map/all_to_all | solution.py:110
  639.2 6.0 copy-start.45
  668.8 97.4 %all-to-all-start.3 = ((f32[2,2,16,16384]{3,1,0,2:T(2,128)}), f32[2,2,16,16384]{3,1,0,2:T(2,128)}, u32[]{:S(2)}, u32[]{:S(2)}) async-start(f32[2,2,16,16384]{3,1,0,2:T(2,128)} %reshape.2994), calls=%async_computation.3 | async-start | bytes 8388608 | tf_op jit(solution)/shard_map/all_to_all | solution.py:142
  766.2 97.8 %all-to-all-start.9 = ((f32[2,2,16,16384]{3,1,0,2:T(2,128)}), f32[2,2,16,16384]{3,1,0,2:T(2,128)}, u32[]{:S(2)}, u32[]{:S(2)}) async-start(f32[2,2,16,16384]{3,1,0,2:T(2,128)} %reshape.3003), calls=%async_computation.9 | async-start | bytes 8388608 | tf_op jit(solution)/shard_map/all_to_all | solution.py:142
  1104.2 83.2 %all-to-all-start.11 = ((f32[2,2,16,16384]{3,1,0,2:T(2,128)}), f32[2,2,16,16384]{3,1,0,2:T(2,128)}, u32[]{:S(2)}, u32[]{:S(2)}) async-start(f32[2,2,16,16384]{3,1,0,2:T(2,128)} %reshape.3008), calls=%async_computation.11 | async-start | bytes 8388608 | tf_op jit(solution)/shard_map/all_to_all | solution.py:142
  1236.1 19.4 %copy-start.67 = (f32[1,1,128,16,128]{4,3,2,1,0:T(8,128)S(1)}, f32[1,1,128,16,128]{4,3,2,1,0:T(8,128)}, u32[]{:S(2)}) copy-start(f32[1,1,128,16,128]{4,3,2,1,0:T(8,128)} %get-tuple-element.201) | copy-start | bytes 3145732
  1236.1 19.4 %copy-start.68 = (f32[1,1,128,16,128]{4,3,2,1,0:T(8,128)S(1)}, f32[1,1,128,16,128]{4,3,2,1,0:T(8,128)}, u32[]{:S(2)}) copy-start(f32[1,1,128,16,128]{4,3,2,1,0:T(8,128)} %get-tuple-element.202) | copy-start | bytes 3145732
  1236.1 61.0 %all-to-all-start.4 = ((f32[1,2,16,16384]{3,0,1,2:T(1,128)}), f32[1,2,16,16384]{3,0,1,2:T(1,128)}, u32[]{:S(2)}, u32[]{:S(2)}) async-start(f32[1,2,16,16384]{3,0,1,2:T(1,128)} %copy.657), calls=%async_computation.4 | async-start | bytes 4194304 | tf_op jit(solution)/shard_map/all_to_all | solution.py:110
  1263.2 45.2 %copy-start.33 = (f32[128,16,128]{2,1,0:T(8,128)S(1)}, f32[128,16,128]{2,1,0:T(8,128)}, u32[]{:S(2)}) copy-start(f32[128,16,128]{2,1,0:T(8,128)} %copy-done.32) | copy-start | bytes 3145732
  1297.1 52.6 %all-to-all-start.12 = ((f32[1,2,16,16384]{3,0,1,2:T(1,128)}), f32[1,2,16,16384]{3,0,1,2:T(1,128)}, u32[]{:S(2)}, u32[]{:S(2)}) async-start(f32[1,2,16,16384]{3,0,1,2:T(1,128)} %copy.742), calls=%async_computation.12 | async-start | bytes 4194304 | tf_op jit(solution)/shard_map/all_to_all | solution.py:110
  1308.5 66.3 %copy-start.25 = (f32[1,1,128,2048]{3,2,1,0:T(8,128)}, f32[1,1,128,2048]{3,2,1,0:T(8,128)S(1)}, u32[]{:S(2)}) copy-start(f32[1,1,128,2048]{3,2,1,0:T(8,128)S(1)} %broadcast_in_dim_reshape.131) | copy-start | bytes 3145732
  1310.3 64.5 %copy-start.27 = (f32[1,1,128,2048]{3,2,1,0:T(8,128)}, f32[1,1,128,2048]{3,2,1,0:T(8,128)S(1)}, u32[]{:S(2)}) copy-start(f32[1,1,128,2048]{3,2,1,0:T(8,128)S(1)} %broadcast_in_dim_reshape.130) | copy-start | bytes 3145732
  1386.0 52.3 %all-to-all-start.5 = ((f32[1,2,16,16384]{3,1,0,2:T(2,128)}), f32[1,2,16,16384]{3,1,0,2:T(2,128)S(1)}, u32[]{:S(2)}, u32[]{:S(2)}) async-start(f32[1,2,16,16384]{3,1,0,2:T(2,128)} %copy.661), calls=%async_computation.5 | async-start | bytes 4194304 | tf_op jit(solution)/shard_map/all_to_all | solution.py:142
  1438.3 52.6 %all-to-all-start.13 = ((f32[1,2,16,16384]{3,1,0,2:T(2,128)}), f32[1,2,16,16384]{3,1,0,2:T(2,128)}, u32[]{:S(2)}, u32[]{:S(2)}) async-start(f32[1,2,16,16384]{3,1,0,2:T(2,128)} %copy.746), calls=%async_computation.13 | async-start | bytes 4194304 | tf_op jit(solution)/shard_map/all_to_all | solution.py:142
  1549.7 52.4 %all-to-all-start.6 = ((f32[1,2,16,16384]{3,0,1,2:T(1,128)}), f32[1,2,16,16384]{3,0,1,2:T(1,128)}, u32[]{:S(2)}, u32[]{:S(2)}) async-start(f32[1,2,16,16384]{3,0,1,2:T(1,128)} %copy.671), calls=%async_computation.6 | async-start | bytes 4194304 | tf_op jit(solution)/shard_map/all_to_all | solution.py:110
  1602.1 52.6 %all-to-all-start.14 = ((f32[1,2,16,16384]{3,0,1,2:T(1,128)}), f32[1,2,16,16384]{3,0,1,2:T(1,128)}, u32[]{:S(2)}, u32[]{:S(2)}) async-start(f32[1,2,16,16384]{3,0,1,2:T(1,128)} %copy.756), calls=%async_computation.14 | async-start | bytes 4194304 | tf_op jit(solution)/shard_map/all_to_all | solution.py:110
  1693.8 52.4 %all-to-all-start.7 = ((f32[1,2,16,16384]{3,1,0,2:T(2,128)}), f32[1,2,16,16384]{3,1,0,2:T(2,128)}, u32[]{:S(2)}, u32[]{:S(2)}) async-start(f32[1,2,16,16384]{3,1,0,2:T(2,128)} %copy.675), calls=%async_computation.7 | async-start | bytes 4194304 | tf_op jit(solution)/shard_map/all_to_all | solution.py:142
  1746.2 52.6 %all-to-all-start.15 = ((f32[1,2,16,16384]{3,1,0,2:T(2,128)}), f32[1,2,16,16384]{3,1,0,2:T(2,128)}, u32[]{:S(2)}, u32[]{:S(2)}) async-start(f32[1,2,16,16384]{3,1,0,2:T(2,128)} %copy.760), calls=%async_computation.15 | async-start | bytes 4194304 | tf_op jit(solution)/shard_map/all_to_all | solution.py:142
  1865.1 10.5 copy-start.85
  1875.6 8.2 copy-start.48
  1875.6 8.2 copy-start.49
  1883.8 10.0 copy-start.83
  (71 other events, 199.1 us)
where the time goes:
time: 1930 us; the launch traced here: 1910 us
  waiting for transfers between devices  588 us (30%)
  local copies, waits for them, and re-layouts  450 us (23%)
  matrix products  418 us (22%)
  starting transfers between devices  199 us (10%)
  other arithmetic  139 us (7%)
  blocking collectives  112 us (6%)
    all_to_all x7, waiting for transfers between devices, propagate(): lax.all_to_all(outgoing, 'fft', split_axis=2, concat_axis=2, tiled=True)  298 us
    all_to_all x8, waiting for transfers between devices, propagate(): lax.all_to_all(lattice.reshape(item_count, 2, peer_count, row_count * slo...  290 us
    all_to_all x1, blocking collectives, propagate(): lax.all_to_all(outgoing, 'fft', split_axis=2, concat_axis=2, tiled=True)  112 us
    all_to_all x8, starting transfers between devices, propagate(): lax.all_to_all(lattice.reshape(item_count, 2, peer_count, row_count * slo...  108 us
    all_to_all x7, starting transfers between devices, propagate(): lax.all_to_all(outgoing, 'fft', split_axis=2, concat_axis=2, tiled=True)  91 us
    dot_general x4, matrix products, rotate(): jnp.einsum('cybsi,bsio->cybo', picked, matrices, precision=PRECISE)  68.7 us
    dot_general x8, matrix products, propagate(): jnp.einsum('fcprs,cdpk->fdrks', lattice, transform_table(peer_count, peer...  63.8 us
    reshape x12, local copies, waits for them, and re-layouts, propagate(): partial_x.transpose(0, 1, 3, 4, 2, 5)  57.5 us
  transfers between devices with their start and end apart: 15, of which 14 were waited for; matrix products, arithmetic and copies ran while one was open for 15% of the time, Pallas kernels for 0%

commit v1 on v0

--- a/solution.py
+++ b/solution.py
@@ -1,8 +1,12 @@
+import functools
 import math
 
 import jax
 import jax.numpy as jnp
+import numpy as np
 from jax import lax
+from jax.experimental import pallas as pl
+from jax.experimental.pallas import tpu as pltpu
 from jax.sharding import PartitionSpec as P
 
 XA = 16
@@ -12,9 +16,599 @@
 ANGLES = 2
 BLK = 128
 NB = 32
+SLOTS = 2
+STRIP = 16
+LANES = 128
 
 
 PRECISE = lax.Precision.HIGHEST
+
+
+def bin_matrices():
+    wavenumber = np.arange(NX)
+    signed = np.where(wavenumber < NX // 2, wavenumber, wavenumber - NX)
+    factor = np.exp(-1j * np.pi / NX * ((signed * signed) % (2 * NX)))
+    line = np.fft.ifft(factor)
+    block = np.arange(XA)
+    inner = np.arange(XB)
+    shifts = (XB * block[:, None, None] + inner[None, :, None] - inner[None, None, :]) % NX
+    phases = np.exp(-2j * np.pi / XA * ((block[:, None] * block[None, :]) % XA))
+    return np.einsum("kd,dij->kij", phases, line[shifts]) / XA
+
+
+def split_constant(values):
+    values = values.astype(np.float32)
+    high = values.astype(jnp.bfloat16)
+    low = (values - high.astype(np.float32)).astype(jnp.bfloat16)
+    return high, low
+
+
+def column_constants():
+    bins = bin_matrices()
+    top = np.concatenate([bins.real, -bins.imag], axis=2)
+    bottom = np.concatenate([bins.imag, bins.real], axis=2)
+    return np.concatenate([top, bottom], axis=1)
+
+
+def fourth(values, orient):
+    (ar, ai), (br, bi), (cr, ci), (dr, di) = values
+    sr, si, er, ei = ar + cr, ai + ci, ar - cr, ai - ci
+    tr, ti, fr, fi = br + dr, bi + di, br - dr, bi - di
+    minus, plus = (er + fi, ei - fr), (er - fi, ei + fr)
+    one, three = (minus, plus) if orient < 0 else (plus, minus)
+    return [(sr + tr, si + ti), one, (sr - tr, si - ti), three]
+
+
+def turned(value, step, orient):
+    re, im = value
+    if step == 0:
+        return value
+    if step == 4:
+        return (im, -re) if orient < 0 else (-im, re)
+    cosine = math.cos(2.0 * math.pi * step / XA)
+    sine = orient * math.sin(2.0 * math.pi * step / XA)
+    if step == 2:
+        root = cosine
+        return ((re - im) * root, (re + im) * root) if orient > 0 else ((re + im) * root, (im - re) * root)
+    return (re * cosine - im * sine, re * sine + im * cosine)
+
+
+def sixteenth(values, orient):
+    inner = [fourth([values[4 * a + b] for a in range(4)], orient) for b in range(4)]
+    out = [None] * XA
+    for c in range(4):
+        row = fourth([turned(inner[b][c], b * c, orient) for b in range(4)], orient)
+        for d in range(4):
+            out[c + 4 * d] = row[d]
+    return out
+
+
+def halves(value):
+    high = value.astype(jnp.bfloat16)
+    return high, (value - high.astype(jnp.float32)).astype(jnp.bfloat16)
+
+
+def dot32(a, b):
+    return jnp.dot(a, b, preferred_element_type=jnp.float32)
+
+
+def times(a, b):
+    return (a[0] * b[0] - a[1] * b[1], a[0] * b[1] + a[1] * b[0])
+
+
+def sincos(x):
+    turns = jnp.floor(x * (2.0 / math.pi) + 0.5)
+    rest = ((x - turns * 1.5703125) - turns * 4.837512969970703125e-4) - turns * 7.54978995489188216e-8
+    square = rest * rest
+    sine = rest + rest * square * (
+        -1.6666654611e-1 + square * (8.3321608736e-3 + square * -1.9515295891e-4)
+    )
+    cosine = (1.0 - 0.5 * square) + square * square * (
+        4.166664568298827e-2 + square * (-1.388731625493765e-3 + square * 2.443315711809948e-5)
+    )
+    quadrant = turns.astype(jnp.int32)
+    odd = (quadrant & 1) == 1
+    first = jnp.where(odd, cosine, sine)
+    second = jnp.where(odd, sine, cosine)
+    first = jnp.where((quadrant & 2) == 2, -first, first)
+    second = jnp.where(((quadrant + 1) & 2) == 2, -second, second)
+    return first, second
+
+
+def strips(count, step):
+    def run(i, carry):
+        step(pl.multiple_of(i * STRIP, STRIP))
+        return carry
+
+    lax.fori_loop(0, count // STRIP, run, 0)
+
+
+def rows_out(xhi, xlo, first_row, values):
+    for k, (re, im) in enumerate(sixteenth(values, -1.0)):
+        for part, value in enumerate((re, im)):
+            high, low = halves(value)
+            at = (k, pl.ds(first_row, STRIP), pl.ds(part * LANES, LANES))
+            xhi[at] = high
+            xlo[at] = low
+
+
+def rows_in(y, first_row):
+    values = [
+        tuple(y[k, pl.ds(first_row, STRIP), pl.ds(part * LANES, LANES)] for part in range(2))
+        for k in range(XA)
+    ]
+    return sixteenth(values, 1.0)
+
+
+def rows_mix(xhi, xlo, mhi, mlo, y):
+    def step(k, carry):
+        high, low = xhi[k], xlo[k]
+        y[k] = dot32(high, mhi[k]) + (dot32(low, mhi[k]) + dot32(high, mlo[k]))
+        return carry
+
+    lax.fori_loop(0, XA, step, 0)
+
+
+def columns_out(xhi, xlo, field, row, values):
+    for k, (re, im) in enumerate(sixteenth(values, -1.0)):
+        for part, value in enumerate((re, im)):
+            high, low = halves(value)
+            at = (k, pl.ds(part * XB + row, STRIP), pl.ds(field * LANES, LANES))
+            xhi[at] = high
+            xlo[at] = low
+
+
+def columns_in(y, field, row):
+    values = [
+        tuple(
+            y[k, pl.ds(part * XB + row, STRIP), pl.ds(field * LANES, LANES)] for part in range(2)
+        )
+        for k in range(XA)
+    ]
+    return sixteenth(values, 1.0)
+
+
+def columns_mix(xhi, xlo, mhi, mlo, y):
+    def step(k, carry):
+        high, low = xhi[k], xlo[k]
+        y[k] = dot32(mhi[k], high) + (dot32(mhi[k], low) + dot32(mlo[k], high))
+        return carry
+
+    lax.fori_loop(0, XA, step, 0)
+
+
+def enter_kernel(
+    index, potential, direction, whi, wlo, mhi, mlo, uv, td, t0, shi, slo, field, xhi, xlo, y
+):
+    rows = potential.shape[1]
+
+    for number, (source, channel) in enumerate(
+        ((potential, 0), (potential, 1), (direction, 0), (direction, 1))
+    ):
+
+        def cut(row, number=number, source=source, channel=channel):
+            high, low = halves(source[channel, pl.ds(row, STRIP), :])
+            at = pl.ds(pl.multiple_of(number * rows + row, STRIP), STRIP)
+            shi[at, :] = high
+            slo[at, :] = low
+
+        strips(rows, cut)
+
+    def rotated(b):
+        at = [pl.ds(pl.multiple_of(index[b, s] * BLK, BLK), BLK) for s in range(SLOTS)]
+        high = jnp.concatenate([shi[:, a] for a in at], axis=1)
+        low = jnp.concatenate([slo[:, a] for a in at], axis=1)
+        values = dot32(high, whi[b]) + (dot32(low, whi[b]) + dot32(high, wlo[b]))
+        angle, loss, d_re, d_im = (values[i * rows : (i + 1) * rows] for i in range(4))
+        sine, cosine = sincos(angle)
+        damping = jnp.exp(-loss)
+        return damping * cosine, damping * sine, d_re, d_im
+
+    def first_slice(b, carry):
+        t_re, t_im, d_re, d_im = rotated(b)
+        t0[b, 0] = t_re
+        t0[b, 1] = t_im
+        field[b, 0] = -(d_re * t_im + d_im * t_re)
+        field[b, 1] = d_re * t_re - d_im * t_im
+        return carry
+
+    lax.fori_loop(0, XA, first_slice, 0)
+
+    def forward(row):
+        at = pl.ds(row, STRIP)
+        rows_out(xhi, xlo, row, [(t0[b, 0, at, :], t0[b, 1, at, :]) for b in range(XA)])
+        rows_out(
+            xhi,
+            xlo,
+            pl.multiple_of(rows + row, STRIP),
+            [(field[b, 0, at, :], field[b, 1, at, :]) for b in range(XA)],
+        )
+
+    strips(rows, forward)
+    rows_mix(xhi, xlo, mhi, mlo, y)
+
+    def backward(row):
+        at = pl.ds(row, STRIP)
+        for number in range(2):
+            values = rows_in(y, pl.multiple_of(number * rows + row, STRIP))
+            for b, (re, im) in enumerate(values):
+                uv[b, 2 * number, at, :] = re
+                uv[b, 2 * number + 1, at, :] = im
+
+    strips(rows, backward)
+
+    def second_slice(b, carry):
+        for channel, value in enumerate(rotated(XA + b)):
+            td[b, channel] = value
+        return carry
+
+    lax.fori_loop(0, XA, second_slice, 0)
+
+
+def row_places(mixed):
+    same = list(range(XA))
+    if not mixed:
+        return [(0, XB, same)]
+    swapped = [p ^ (XA // 2) for p in same]
+    step = XB // 4
+    return [(i * step, step, swapped if i % 2 == 0 else same) for i in range(4)]
+
+
+def column_strips(mixed, step):
+    for first, count, places in row_places(mixed):
+        strips(count, lambda row, first=first, places=places: step(pl.multiple_of(first + row, STRIP), places))
+
+
+def middle_kernel(mixed, chunks, *refs):
+    uv, td = refs[:chunks], refs[chunks : 2 * chunks]
+    mhi, mlo, out, phi, xhi, xlo, y = refs[2 * chunks :]
+    rows = XB // chunks
+
+    def chunked(step):
+        for first, count, places in row_places(mixed):
+            for piece in range(0, count, min(count, rows)):
+                start = first + piece
+                c, local = start // rows, start % rows
+
+                def inner(row, start=start, c=c, local=local, places=places):
+                    step(
+                        pl.multiple_of(start + row, STRIP),
+                        c,
+                        pl.ds(pl.multiple_of(local + row, STRIP), STRIP),
+                        places,
+                    )
+
+                strips(min(count, rows), inner)
+
+    def forward(row, c, local, places):
+        for number in range(2):
+            columns_out(
+                xhi,
+                xlo,
+                number,
+                row,
+                [tuple(uv[c][g, 2 * number + i, local, :] for i in range(2)) for g in places],
+            )
+
+    chunked(forward)
+    columns_mix(xhi, xlo, mhi, mlo, y)
+
+    def turn(row, c, local, places):
+        at = pl.ds(row, STRIP)
+        wave = columns_in(y, 0, row)
+        product = []
+        for g, value in zip(places, wave):
+            value = times((td[c][g, 0, local, :], td[c][g, 1, local, :]), value)
+            phi[g, 0, at, :] = value[0]
+            phi[g, 1, at, :] = value[1]
+            product.append(value)
+        columns_out(xhi, xlo, 0, row, product)
+        dwave = columns_in(y, 1, row)
+        change = []
+        for g, value in zip(places, dwave):
+            t_re, t_im, d_re, d_im = (td[c][g, i, local, :] for i in range(4))
+            p_re, p_im = phi[g, 0, at, :], phi[g, 1, at, :]
+            re, im = times((t_re, t_im), value)
+            change.append((re - (d_re * p_im + d_im * p_re), im + (d_re * p_re - d_im * p_im)))
+        columns_out(xhi, xlo, 1, row, change)
+
+    chunked(turn)
+    columns_mix(xhi, xlo, mhi, mlo, y)
+
+    def backward(row, c, local, places):
+        at = pl.ds(row, STRIP)
+        for number in range(2):
+            for g, (re, im) in zip(places, columns_in(y, number, row)):
+                out[g, 2 * number, at, :] = re
+                out[g, 2 * number + 1, at, :] = im
+
+    chunked(backward)
+
+
+def detector_kernel(fields, mhi, mlo, out, xhi, xlo, y):
+    rows = fields.shape[2]
+
+    def forward(row):
+        at = pl.ds(row, STRIP)
+        for number in range(2):
+            rows_out(
+                xhi,
+                xlo,
+                pl.multiple_of(number * rows + row, STRIP),
+                [tuple(fields[b, 2 * number + i, at, :] for i in range(2)) for b in range(XA)],
+            )
+
+    strips(rows, forward)
+    rows_mix(xhi, xlo, mhi, mlo, y)
+
+    def turn(row):
+        wave = rows_in(y, row)
+        dwave = rows_in(y, pl.multiple_of(rows + row, STRIP))
+        back = []
+        for (re, im), (d_re, d_im) in zip(wave, dwave):
+            change = 4.0 * (re * d_re + im * d_im)
+            back.append((change * re, -(change * im)))
+        rows_out(xhi, xlo, row, back)
+
+    strips(rows, turn)
+
+    def step(k, carry):
+        high, low = xhi[k, :rows, :], xlo[k, :rows, :]
+        y[k, :rows, :] = dot32(high, mhi[k]) + (dot32(low, mhi[k]) + dot32(high, mlo[k]))
+        return carry
+
+    lax.fori_loop(0, XA, step, 0)
+
+    def backward(row):
+        at = pl.ds(row, STRIP)
+        for b, (re, im) in enumerate(rows_in(y, row)):
+            out[b, 0, at, :] = re
+            out[b, 1, at, :] = im
+
+    strips(rows, backward)
+
+
+def return_kernel(mixed, chunks, back, phi, *refs):
+    td = refs[:chunks]
+    mhi, mlo, out, xhi, xlo, y = refs[chunks:]
+    rows = XB // chunks
+
+    def chunked(step):
+        for first, count, places in row_places(mixed):
+            for piece in range(0, count, min(count, rows)):
+                start = first + piece
+                c, local = start // rows, start % rows
+
+                def inner(row, start=start, c=c, local=local, places=places):
+                    step(
+                        pl.multiple_of(start + row, STRIP),
+                        c,
+                        pl.ds(pl.multiple_of(local + row, STRIP), STRIP),
+                        places,
+                    )
+
+                strips(min(count, rows), inner)
+
+    def forward(row, c, local, places):
+        at = pl.ds(row, STRIP)
+        columns_out(xhi, xlo, 0, row, [(back[g, 0, at, :], back[g, 1, at, :]) for g in places])
+
+    chunked(forward)
+    columns_mix(xhi, xlo, mhi, mlo, y)
+
+    def turn(row, c, local, places):
+        at = pl.ds(row, STRIP)
+        pulled = columns_in(y, 0, row)
+        following = []
+        for g, value in zip(places, pulled):
+            re, im = times((phi[g, 0, at, :], phi[g, 1, at, :]), value)
+            out[g, 0, at, :] = -im
+            out[g, 1, at, :] = -re
+            following.append(times((td[c][g, 0, local, :], td[c][g, 1, local, :]), value))
+        columns_out(xhi, xlo, 0, row, following)
+
+    chunked(turn)
+    columns_mix(xhi, xlo, mhi, mlo, y)
+
+    def backward(row, c, local, places):
+        at = pl.ds(row, STRIP)
+        for g, (re, im) in zip(places, columns_in(y, 0, row)):
+            out[g, 2, at, :] = re
+            out[g, 3, at, :] = im
+
+    chunked(backward)
+
+
+def leave_kernel(index, back, t0, whi, wlo, mhi, mlo, *refs):
+    before, (out, shi, slo, xhi, xlo, y) = refs[:-6], refs[-6:]
+    rows = back.shape[2]
+
+    def forward(row):
+        at = pl.ds(row, STRIP)
+        rows_out(xhi, xlo, row, [(back[b, 2, at, :], back[b, 3, at, :]) for b in range(XA)])
+        for b in range(XA):
+            for i in range(2):
+                high, low = halves(back[b, i, at, :])
+                place = pl.ds(pl.multiple_of(i * rows + row, STRIP), STRIP)
+                shi[XA + b, place, :] = high
+                slo[XA + b, place, :] = low
+
+    strips(rows, forward)
+    rows_mix(xhi, xlo, mhi, mlo, y)
+
+    def turn(row):
+        at = pl.ds(row, STRIP)
+        for b, value in enumerate(rows_in(y, row)):
+            re, im = times((t0[b, 0, at, :], t0[b, 1, at, :]), value)
+            for i, part in enumerate((-im, -re)):
+                high, low = halves(part)
+                place = pl.ds(pl.multiple_of(i * rows + row, STRIP), STRIP)
+                shi[b, place, :] = high
+                slo[b, place, :] = low
+
+    strips(rows, turn)
+
+    if before:
+        out[...] = before[0][...]
+    else:
+        out[...] = jnp.zeros(out.shape, jnp.float32)
+
+    def across(a, b):
+        return lax.dot_general(
+            a, b, (((1,), (1,)), ((), ())), preferred_element_type=jnp.float32
+        )
+
+    def step(b, carry):
+        high, low = shi[b], slo[b]
+        values = across(high, whi[b]) + (across(low, whi[b]) + across(high, wlo[b]))
+        for s in range(SLOTS):
+            at = pl.ds(pl.multiple_of(index[b, s] * BLK, BLK), BLK)
+            for i in range(2):
+                out[i, :, at] += values[i * rows : (i + 1) * rows, s * BLK : (s + 1) * BLK]
+        return carry
+
+    lax.fori_loop(0, NB, step, 0)
+
+
+def call(kernel, outs, scratch, mix_count, extra, *operands):
+    specs = [
+        pl.BlockSpec(memory_space=pltpu.SMEM if o.dtype == jnp.int32 else pltpu.VMEM)
+        for o in operands
+    ]
+    moved = sum(o.size * o.dtype.itemsize for o in operands) + sum(4 * math.prod(o) for o in outs)
+    return pl.pallas_call(
+        kernel,
+        out_shape=[jax.ShapeDtypeStruct(o, jnp.float32) for o in outs],
+        in_specs=specs,
+        out_specs=[pl.BlockSpec(memory_space=pltpu.VMEM)] * len(outs),
+        scratch_shapes=scratch,
+        compiler_params=pltpu.CompilerParams(vmem_limit_bytes=60 * 1024 * 1024),
+        cost_estimate=pl.CostEstimate(
+            flops=mix_count * 16 * 128 * 256 * 256 * 6 + extra,
+            bytes_accessed=moved,
+            transcendentals=0,
+        ),
+    )(*operands)
+
+
+def mix_scratch(rows, lanes):
+    return [
+        pltpu.VMEM((XA, rows, lanes), jnp.bfloat16),
+        pltpu.VMEM((XA, rows, lanes), jnp.bfloat16),
+        pltpu.VMEM((XA, rows, lanes), jnp.float32),
+    ]
+
+
+def enter(index, potential, direction, weights, matrices):
+    rows = potential.shape[1]
+    scratch = [
+        pltpu.VMEM((4 * rows, NB * BLK), jnp.bfloat16),
+        pltpu.VMEM((4 * rows, NB * BLK), jnp.bfloat16),
+        pltpu.VMEM((XA, 2, rows, LANES), jnp.float32),
+    ] + mix_scratch(2 * rows, 2 * LANES)
+    outs = [(XA, 4, rows, LANES), (XA, 4, rows, LANES), (XA, 2, rows, LANES)]
+    extra = NB * 4 * rows * 256 * 128 * 6
+    return call(
+        enter_kernel, outs, scratch, 2, extra, index, potential, direction, *weights, *matrices
+    )
+
+
+def middle(uv, td, matrices, mixed):
+    return call(
+        functools.partial(middle_kernel, mixed, len(uv)),
+        [(XA, 4, XB, LANES), (XA, 2, XB, LANES)],
+        mix_scratch(2 * XB, 2 * LANES),
+        4,
+        0,
+        *uv,
+        *td,
+        *matrices,
+    )
+
+
+def detector(fields, matrices):
+    rows = fields.shape[2]
+    return call(
+        detector_kernel,
+        [(XA, 2, rows, LANES)],
+        mix_scratch(2 * rows, 2 * LANES),
+        3,
+        0,
+        fields,
+        *matrices,
+    )[0]
+
+
+def pull(back, phi, td, matrices, mixed):
+    return call(
+        functools.partial(return_kernel, mixed, len(td)),
+        [(XA, 4, XB, LANES)],
+        mix_scratch(2 * XB, LANES),
+        2,
+        0,
+        back,
+        phi,
+        *td,
+        *matrices,
+    )[0]
+
+
+def leave(index, back, t0, weights, matrices, before):
+    rows = back.shape[2]
+    scratch = [
+        pltpu.VMEM((NB, 2 * rows, LANES), jnp.bfloat16),
+        pltpu.VMEM((NB, 2 * rows, LANES), jnp.bfloat16),
+    ] + mix_scratch(rows, 2 * LANES)
+    extra = NB * 2 * rows * 256 * 128 * 6
+    return call(
+        leave_kernel,
+        [(2, rows, NB * BLK)],
+        scratch,
+        1,
+        extra,
+        index,
+        back,
+        t0,
+        *weights,
+        *matrices,
+        *before,
+    )[0]
+
+
+def split_weights(block_weights):
+    stacked = block_weights.reshape(ANGLES, NB, SLOTS * BLK, BLK)
+    rounded = lax.reduce_precision(stacked, 8, 7)
+    return rounded.astype(jnp.bfloat16), (stacked - rounded).astype(jnp.bfloat16)
+
+
+def exchange(values):
+    return lax.all_to_all(values, "fft", split_axis=0, concat_axis=0, tiled=True)
+
+
+def blocked_body(potential, direction, block_index, block_weights):
+    whi, wlo = split_weights(block_weights)
+    by_column = column_constants()
+    column = tuple(jnp.asarray(v) for v in split_constant(by_column))
+    row = tuple(jnp.asarray(v) for v in split_constant(by_column.transpose(0, 2, 1)))
+    weights = [(whi[a], wlo[a]) for a in range(ANGLES)]
+    mixed = False
+    state = []
+    for a in range(ANGLES):
+        uv, td, t0 = enter(block_index[a], potential, direction, weights[a], row)
+        state.append((exchange(uv), exchange(td), t0))
+    carried = []
+    for uv, td, t0 in state:
+        out, phi = middle([uv], [td], column, mixed)
+        carried.append((exchange(out), phi, [td], t0))
+    backs = [exchange(detector(out, row)) for out, _, _, _ in carried]
+    pulled = [
+        exchange(pull(back, phi, td, column, mixed))
+        for back, (_, phi, td, _) in zip(backs, carried)
+    ]
+    total = ()
+    for a in range(ANGLES):
+        total = (leave(block_index[a], pulled[a], carried[a][3], weights[a], row, total),)
+    return total[0]
 
 
 def transform_table(count_in, count_out, length, orient):
@@ -157,7 +751,7 @@
     return restored.reshape(item_count, 2, row_count, NX)
 
 
-def body(potential, direction, block_index, block_weights):
+def general_body(potential, direction, block_index, block_weights):
     row_count = potential.shape[1]
     peer_count = lax.axis_size("fft")
     slot_count = NX // peer_count
@@ -216,6 +810,12 @@
     return accumulated
 
 
+def body(potential, direction, block_index, block_weights):
+    if lax.axis_size("fft") == XA and potential.shape[1] == XB:
+        return blocked_body(potential, direction, block_index, block_weights)
+    return general_body(potential, direction, block_index, block_weights)
+
+
 def solution(mesh):
     return jax.shard_map(
         body,

time: 1930 us -> 959 us (0.50)
  local copies, waits for them, and re-layouts: 450 us -> 10.1 us
  matrix products: 418 us -> 0 us
  Pallas kernels: 0 us -> 218 us
  waiting for transfers between devices: 588 us -> 387 us
  other arithmetic: 139 us -> 9.17 us
  blocking collectives: 112 us -> 211 us
  starting transfers between devices: 199 us -> 109 us
    dot_general x76 -> x0, matrix products: 418 us -> none  [the longest x4 68.7 us: rotate(): jnp.einsum('cybsi,bsio->cybo', picked, matrices, precision=PRECISE)]
    pallas_call x0 -> x10, Pallas kernels: none -> 218 us  [call(): pl.pallas_call(kernel, out_shape=[jax.ShapeDtypeStruct(o, jnp.float32) fo...]
    all_to_all x15 -> x8, waiting for transfers between devices: 588 us -> 387 us  [exchange(): lax.all_to_all(values, 'fft', split_axis=0, concat_axis=0, tiled=True)]
    reshape x40 -> x0, local copies, waits for them, and re-layouts: 182 us -> none  [the longest x12 57.5 us: propagate(): partial_x.transpose(0, 1, 3, 4, 2, 5)]
    all_to_all x1 -> x2, blocking collectives: 112 us -> 211 us  [exchange(): lax.all_to_all(values, 'fft', split_axis=0, concat_axis=0, tiled=True)]
    another operation x24 -> x0, local copies, waits for them, and re-layouts: 91.7 us -> none
    all_to_all x15 -> x8, starting transfers between devices: 199 us -> 109 us  [exchange(): lax.all_to_all(values, 'fft', split_axis=0, concat_axis=0, tiled=True)]
    sub x29 -> x0, other arithmetic: 76 us -> none  [the longest x23 55.5 us: complex_times(): first * real_part - second * imag_part]
  transfers between devices with their start and end apart: 15 -> 8, of which waited for: 14 -> 8; matrix products, arithmetic and copies ran while one was open for 15% -> 0% of each run, Pallas kernels for 0% -> 17%
where the time goes in v1:
time: 959 us; the launch traced here: 944 us
  waiting for transfers between devices  387 us (40%)
  Pallas kernels  218 us (23%)
  blocking collectives  211 us (22%)
  starting transfers between devices  109 us (11%)
  local copies, waits for them, and re-layouts  10.1 us (1%)
    all_to_all x8, waiting for transfers between devices, exchange(): lax.all_to_all(values, 'fft', split_axis=0, concat_axis=0, tiled=True)  387 us
    pallas_call x10, Pallas kernels, call(): pl.pallas_call(kernel, out_shape=[jax.ShapeDtypeStruct(o, jnp.float32) fo...  218 us
    all_to_all x2, blocking collectives, exchange(): lax.all_to_all(values, 'fft', split_axis=0, concat_axis=0, tiled=True)  211 us
    all_to_all x8, starting transfers between devices, exchange(): lax.all_to_all(values, 'fft', split_axis=0, concat_axis=0, tiled=True)  109 us
  transfers between devices with their start and end apart: 8, of which 8 were waited for; matrix products, arithmetic and copies ran while one was open for 0% of the time, Pallas kernels for 17%

profile of v1, /device:TPU:3, one launch (start us, length us, event | category | flops | bytes accessed | tf_op | source)
XLA Modules:
  0.0 943.8 jit_solution(8770522654895306109)
XLA Ops:
  0.0 9.2 fusion
  9.9 6.0 slice_bitcast_fusion
  15.9 29.9 %shard_map.86 = (f32[16,4,128,128]{3,2,1,0:T(8,128)}, f32[16,4,128,128]{3,2,1,0:T(8,128)}, f32[16,2,128,128]{3,2,1,0:T(8,128)}) custom-call(s32[32,2]{1,0:T(8,128)} %copy.11.index, f32[2,128,4096]{2,1,0:T(8,128)} %potential.3, f32[2,128,4096]{2,1,0:T(8,128)} %direction.3, bf16[32,256,128]{2,1,0:T(8,128)(2,1)} %get-tuple-element.34.whi, ...), custom_call_target="tpu_custom_call" | custom-call | flops 4831838208 | bytes 27263232 | tf_op jit(solution)/shard_map/pallas_call | solution.py:479
  45.8 99.2 %all_to_all.50.refs_1_.refs_0_ = f32[16,4,128,128]{3,2,1,0:T(8,128)} all-to-all(f32[16,4,128,128]{3,2,1,0:T(8,128)} %get-tuple-element.21), channel_id=1, replica_groups=mesh['parts'=2,'fft'=16] {'fft'}, dimensions={0} | all-to-all | bytes 8388608 | tf_op jit(solution)/shard_map/all_to_all | solution.py:585
  145.0 4.9 all-to-all-start.5
  150.7 29.9 %shard_map.82 = (f32[16,4,128,128]{3,2,1,0:T(8,128)}, f32[16,4,128,128]{3,2,1,0:T(8,128)}, f32[16,2,128,128]{3,2,1,0:T(8,128)}) custom-call(s32[32,2]{1,0:T(8,128)} %copy.12.index, f32[2,128,4096]{2,1,0:T(8,128)} %potential.3, f32[2,128,4096]{2,1,0:T(8,128)} %direction.3, bf16[32,256,128]{2,1,0:T(8,128)(2,1)} %get-tuple-element.33.whi, ...), custom_call_target="tpu_custom_call" | custom-call | flops 4831838208 | bytes 27263232 | tf_op jit(solution)/shard_map/pallas_call | solution.py:479
  180.6 47.5 %all-to-all-done.5.refs_0_ = f32[16,4,128,128]{3,2,1,0:T(8,128)} async-done(((f32[16,4,128,128]{3,2,1,0:T(8,128)}), f32[16,4,128,128]{3,2,1,0:T(8,128)}, u32[]{:S(2)}, u32[]{:S(2)}) %all-to-all-start.5) | async-done | bytes 4194336 | tf_op jit(solution)/shard_map/all_to_all | solution.py:585
  228.1 112.0 %all_to_all.51.refs_1_.refs_0_ = f32[16,4,128,128]{3,2,1,0:T(8,128)} all-to-all(f32[16,4,128,128]{3,2,1,0:T(8,128)} %get-tuple-element.16), channel_id=1, replica_groups=mesh['parts'=2,'fft'=16] {'fft'}, dimensions={0} | all-to-all | bytes 8388608 | tf_op jit(solution)/shard_map/all_to_all | solution.py:585
  340.1 4.9 all-to-all-start
  345.0 21.6 %shard_map.87 = (f32[16,4,128,128]{3,2,1,0:T(8,128)}, f32[16,2,128,128]{3,2,1,0:T(8,128)}) custom-call(f32[16,4,128,128]{3,2,1,0:T(8,128)} %all-to-all-done.5.refs_0_, f32[16,4,128,128]{3,2,1,0:T(8,128)} %all_to_all.50.refs_1_.refs_0_, bf16[16,256,256]{2,1,0:T(8,128)(2,1)} %constant.8.clone.refs_2_.refs_1_, bf16[16,256,256]{2,1,0:T(8,128)(2,1)} %constant.9.clone.refs_3_.refs_2_), custom_call_target="tpu_custom_call" | custom-call | flops 3221225472 | bytes 18874368 | tf_op jit(solution)/shard_map/pallas_call | solution.py:479
  366.7 56.5 %all-to-all-done.refs_0_ = f32[16,4,128,128]{3,2,1,0:T(8,128)} async-done(((f32[16,4,128,128]{3,2,1,0:T(8,128)}), f32[16,4,128,128]{3,2,1,0:T(8,128)}, u32[]{:S(2)}, u32[]{:S(2)}) %all-to-all-start) | async-done | bytes 4194336 | tf_op jit(solution)/shard_map/all_to_all | solution.py:585
  423.1 19.3 %all-to-all-start.7 = ((f32[16,4,128,128]{3,2,1,0:T(8,128)}), f32[16,4,128,128]{3,2,1,0:T(8,128)}, u32[]{:S(2)}, u32[]{:S(2)}) async-start(f32[16,4,128,128]{3,2,1,0:T(8,128)} %get-tuple-element.22), calls=%async_computation.7 | async-start | bytes 8388608 | tf_op jit(solution)/shard_map/all_to_all | solution.py:585
  442.4 21.7 %shard_map.83 = (f32[16,4,128,128]{3,2,1,0:T(8,128)}, f32[16,2,128,128]{3,2,1,0:T(8,128)}) custom-call(f32[16,4,128,128]{3,2,1,0:T(8,128)} %all-to-all-done.refs_0_, f32[16,4,128,128]{3,2,1,0:T(8,128)} %all_to_all.51.refs_1_.refs_0_, bf16[16,256,256]{2,1,0:T(8,128)(2,1)} %constant.8.clone.refs_2_.refs_1_, bf16[16,256,256]{2,1,0:T(8,128)(2,1)} %constant.9.clone.refs_3_.refs_2_), custom_call_target="tpu_custom_call" | custom-call | flops 3221225472 | bytes 18874368 | tf_op jit(solution)/shard_map/pallas_call | solution.py:479
  464.1 56.4 %all-to-all-done.7.fields = f32[16,4,128,128]{3,2,1,0:T(8,128)} async-done(((f32[16,4,128,128]{3,2,1,0:T(8,128)}), f32[16,4,128,128]{3,2,1,0:T(8,128)}, u32[]{:S(2)}, u32[]{:S(2)}) %all-to-all-start.7) | async-done | bytes 4194336 | tf_op jit(solution)/shard_map/all_to_all | solution.py:585
  520.5 19.3 %all-to-all-start.2 = ((f32[16,4,128,128]{3,2,1,0:T(8,128)}), f32[16,4,128,128]{3,2,1,0:T(8,128)}, u32[]{:S(2)}, u32[]{:S(2)}) async-start(f32[16,4,128,128]{3,2,1,0:T(8,128)} %get-tuple-element.17), calls=%async_computation.2 | async-start | bytes 8388608 | tf_op jit(solution)/shard_map/all_to_all | solution.py:585
  539.8 16.4 %shard_map.88 = f32[16,2,128,128]{3,2,1,0:T(8,128)} custom-call(f32[16,4,128,128]{3,2,1,0:T(8,128)} %all-to-all-done.7.fields, bf16[16,256,256]{2,1,0:T(8,128)(2,1)} %constant.10.clone.mhi, bf16[16,256,256]{2,1,0:T(8,128)(2,1)} %constant.11.clone.mlo), custom_call_target="tpu_custom_call" | custom-call | flops 2415919104 | bytes 10485760 | tf_op jit(solution)/shard_map/pallas_call | solution.py:479
  556.2 61.7 %all-to-all-done.2.fields = f32[16,4,128,128]{3,2,1,0:T(8,128)} async-done(((f32[16,4,128,128]{3,2,1,0:T(8,128)}), f32[16,4,128,128]{3,2,1,0:T(8,128)}, u32[]{:S(2)}, u32[]{:S(2)}) %all-to-all-start.2) | async-done | bytes 4194336 | tf_op jit(solution)/shard_map/all_to_all | solution.py:585
  617.9 19.3 %all-to-all-start.8 = ((f32[16,2,128,128]{3,2,1,0:T(8,128)}), f32[16,2,128,128]{3,2,1,0:T(8,128)S(1)}, u32[]{:S(2)}, u32[]{:S(2)}) async-start(f32[16,2,128,128]{3,2,1,0:T(8,128)} %shard_map.88), calls=%async_computation.8 | async-start | bytes 4194304 | tf_op jit(solution)/shard_map/all_to_all | solution.py:585
  637.2 16.4 %shard_map.84 = f32[16,2,128,128]{3,2,1,0:T(8,128)} custom-call(f32[16,4,128,128]{3,2,1,0:T(8,128)} %all-to-all-done.2.fields, bf16[16,256,256]{2,1,0:T(8,128)(2,1)} %constant.10.clone.mhi, bf16[16,256,256]{2,1,0:T(8,128)(2,1)} %constant.11.clone.mlo), custom_call_target="tpu_custom_call" | custom-call | flops 2415919104 | bytes 10485760 | tf_op jit(solution)/shard_map/pallas_call | solution.py:479
  653.6 25.0 %all-to-all-done.8.back = f32[16,2,128,128]{3,2,1,0:T(8,128)S(1)} async-done(((f32[16,2,128,128]{3,2,1,0:T(8,128)}), f32[16,2,128,128]{3,2,1,0:T(8,128)S(1)}, u32[]{:S(2)}, u32[]{:S(2)}) %all-to-all-start.8) | async-done | bytes 2097184 | tf_op jit(solution)/shard_map/all_to_all | solution.py:585
  678.6 1.4 copy-done.1
  680.0 10.9 %all-to-all-start.3 = ((f32[16,2,128,128]{3,2,1,0:T(8,128)}), f32[16,2,128,128]{3,2,1,0:T(8,128)S(1)}, u32[]{:S(2)}, u32[]{:S(2)}) async-start(f32[16,2,128,128]{3,2,1,0:T(8,128)} %shard_map.84), calls=%async_computation.3 | async-start | bytes 4194304 | tf_op jit(solution)/shard_map/all_to_all | solution.py:585
  690.9 17.7 %shard_map.89 = f32[16,4,128,128]{3,2,1,0:T(8,128)} custom-call(f32[16,2,128,128]{3,2,1,0:T(8,128)} %copy-done.1, f32[16,2,128,128]{3,2,1,0:T(8,128)} %get-tuple-element.23.phi, f32[16,4,128,128]{3,2,1,0:T(8,128)} %all_to_all.50.refs_1_.refs_0_, bf16[16,256,256]{2,1,0:T(8,128)(2,1)} %constant.8.clone.refs_2_.refs_1_, ...), custom_call_target="tpu_custom_call" | custom-call | flops 1610612736 | bytes 16777216 | tf_op jit(solution)/shard_map/pallas_call | solution.py:479
  708.5 23.8 %all-to-all-done.3.back = f32[16,2,128,128]{3,2,1,0:T(8,128)S(1)} async-done(((f32[16,2,128,128]{3,2,1,0:T(8,128)}), f32[16,2,128,128]{3,2,1,0:T(8,128)S(1)}, u32[]{:S(2)}, u32[]{:S(2)}) %all-to-all-start.3) | async-done | bytes 2097184 | tf_op jit(solution)/shard_map/all_to_all | solution.py:585
  732.4 1.3 copy-done
  733.7 10.9 %all-to-all-start.9 = ((f32[16,4,128,128]{3,2,1,0:T(8,128)}), f32[16,4,128,128]{3,2,1,0:T(8,128)}, u32[]{:S(2)}, u32[]{:S(2)}) async-start(f32[16,4,128,128]{3,2,1,0:T(8,128)} %shard_map.89), calls=%async_computation.9 | async-start | bytes 8388608 | tf_op jit(solution)/shard_map/all_to_all | solution.py:585
  744.5 17.7 %shard_map.85 = f32[16,4,128,128]{3,2,1,0:T(8,128)} custom-call(f32[16,2,128,128]{3,2,1,0:T(8,128)} %copy-done, f32[16,2,128,128]{3,2,1,0:T(8,128)} %get-tuple-element.18.phi, f32[16,4,128,128]{3,2,1,0:T(8,128)} %all_to_all.51.refs_1_.refs_0_, bf16[16,256,256]{2,1,0:T(8,128)(2,1)} %constant.8.clone.refs_2_.refs_1_, ...), custom_call_target="tpu_custom_call" | custom-call | flops 1610612736 | bytes 16777216 | tf_op jit(solution)/shard_map/pallas_call | solution.py:479
  762.3 60.4 %all-to-all-done.9.back = f32[16,4,128,128]{3,2,1,0:T(8,128)} async-done(((f32[16,4,128,128]{3,2,1,0:T(8,128)}), f32[16,4,128,128]{3,2,1,0:T(8,128)}, u32[]{:S(2)}, u32[]{:S(2)}) %all-to-all-start.9) | async-done | bytes 4194336 | tf_op jit(solution)/shard_map/all_to_all | solution.py:585
  822.6 19.3 %all-to-all-start.4 = ((f32[16,4,128,128]{3,2,1,0:T(8,128)}), f32[16,4,128,128]{3,2,1,0:T(8,128)}, u32[]{:S(2)}, u32[]{:S(2)}) async-start(f32[16,4,128,128]{3,2,1,0:T(8,128)} %shard_map.85), calls=%async_computation.4 | async-start | bytes 8388608 | tf_op jit(solution)/shard_map/all_to_all | solution.py:585
  841.9 22.6 %shard_map.90.refs_0_ = f32[2,128,4096]{2,1,0:T(8,128)} custom-call(s32[32,2]{1,0:T(8,128)} %copy.11.index, f32[16,4,128,128]{3,2,1,0:T(8,128)} %all-to-all-done.9.back, f32[16,2,128,128]{3,2,1,0:T(8,128)} %get-tuple-element.24.t0, bf16[32,256,128]{2,1,0:T(8,128)(2,1)} %get-tuple-element.34.whi, bf16[32,256,128]{2,1,0:T(8,128)(2,1)} %get-tuple-element.27.wlo, ...), custom_call_target="tpu_custom_call" | custom-call | flops 2415919104 | bytes 18874624 | tf_op jit(solution)/shard_map/pallas_call | solution.py:479
  864.5 55.5 %all-to-all-done.4.back = f32[16,4,128,128]{3,2,1,0:T(8,128)} async-done(((f32[16,4,128,128]{3,2,1,0:T(8,128)}), f32[16,4,128,128]{3,2,1,0:T(8,128)}, u32[]{:S(2)}, u32[]{:S(2)}) %all-to-all-start.4) | async-done | bytes 4194336 | tf_op jit(solution)/shard_map/all_to_all | solution.py:585
  920.0 23.8 %shard_map.91 = f32[2,128,4096]{2,1,0:T(8,128)} custom-call(s32[32,2]{1,0:T(8,128)} %copy.12.index, f32[16,4,128,128]{3,2,1,0:T(8,128)} %all-to-all-done.4.back, f32[16,2,128,128]{3,2,1,0:T(8,128)} %get-tuple-element.19.t0, bf16[32,256,128]{2,1,0:T(8,128)(2,1)} %get-tuple-element.33.whi, bf16[32,256,128]{2,1,0:T(8,128)(2,1)} %get-tuple-element.28.wlo, ...), custom_call_target="tpu_custom_call" | custom-call | flops 2415919104 | bytes 23068928 | tf_op jit(solution)/shard_map/pallas_call | solution.py:479
  (7 shorter events, 1.4 us)
Async XLA Ops:
  0.0 9.2 copy-start.2
  145.0 83.0 %all-to-all-start.5 = ((f32[16,4,128,128]{3,2,1,0:T(8,128)}), f32[16,4,128,128]{3,2,1,0:T(8,128)}, u32[]{:S(2)}, u32[]{:S(2)}) async-start(f32[16,4,128,128]{3,2,1,0:T(8,128)} %get-tuple-element.20), calls=%async_computation.5 | async-start | bytes 8388608 | tf_op jit(solution)/shard_map/all_to_all | solution.py:585
  340.1 83.0 %all-to-all-start = ((f32[16,4,128,128]{3,2,1,0:T(8,128)}), f32[16,4,128,128]{3,2,1,0:T(8,128)}, u32[]{:S(2)}, u32[]{:S(2)}) async-start(f32[16,4,128,128]{3,2,1,0:T(8,128)} %get-tuple-element.15), calls=%async_computation | async-start | bytes 8388608 | tf_op jit(solution)/shard_map/all_to_all | solution.py:585
  423.1 97.4 %all-to-all-start.7 = ((f32[16,4,128,128]{3,2,1,0:T(8,128)}), f32[16,4,128,128]{3,2,1,0:T(8,128)}, u32[]{:S(2)}, u32[]{:S(2)}) async-start(f32[16,4,128,128]{3,2,1,0:T(8,128)} %get-tuple-element.22), calls=%async_computation.7 | async-start | bytes 8388608 | tf_op jit(solution)/shard_map/all_to_all | solution.py:585
  520.5 97.4 %all-to-all-start.2 = ((f32[16,4,128,128]{3,2,1,0:T(8,128)}), f32[16,4,128,128]{3,2,1,0:T(8,128)}, u32[]{:S(2)}, u32[]{:S(2)}) async-start(f32[16,4,128,128]{3,2,1,0:T(8,128)} %get-tuple-element.17), calls=%async_computation.2 | async-start | bytes 8388608 | tf_op jit(solution)/shard_map/all_to_all | solution.py:585
  617.9 60.8 %all-to-all-start.8 = ((f32[16,2,128,128]{3,2,1,0:T(8,128)}), f32[16,2,128,128]{3,2,1,0:T(8,128)S(1)}, u32[]{:S(2)}, u32[]{:S(2)}) async-start(f32[16,2,128,128]{3,2,1,0:T(8,128)} %shard_map.88), calls=%async_computation.8 | async-start | bytes 4194304 | tf_op jit(solution)/shard_map/all_to_all | solution.py:585
  678.6 1.4 copy-start.1
  680.0 52.3 %all-to-all-start.3 = ((f32[16,2,128,128]{3,2,1,0:T(8,128)}), f32[16,2,128,128]{3,2,1,0:T(8,128)S(1)}, u32[]{:S(2)}, u32[]{:S(2)}) async-start(f32[16,2,128,128]{3,2,1,0:T(8,128)} %shard_map.84), calls=%async_computation.3 | async-start | bytes 4194304 | tf_op jit(solution)/shard_map/all_to_all | solution.py:585
  732.4 1.3 copy-start
  733.7 88.9 %all-to-all-start.9 = ((f32[16,4,128,128]{3,2,1,0:T(8,128)}), f32[16,4,128,128]{3,2,1,0:T(8,128)}, u32[]{:S(2)}, u32[]{:S(2)}) async-start(f32[16,4,128,128]{3,2,1,0:T(8,128)} %shard_map.89), calls=%async_computation.9 | async-start | bytes 8388608 | tf_op jit(solution)/shard_map/all_to_all | solution.py:585
  822.6 97.4 %all-to-all-start.4 = ((f32[16,4,128,128]{3,2,1,0:T(8,128)}), f32[16,4,128,128]{3,2,1,0:T(8,128)}, u32[]{:S(2)}, u32[]{:S(2)}) async-start(f32[16,4,128,128]{3,2,1,0:T(8,128)} %shard_map.85), calls=%async_computation.4 | async-start | bytes 8388608 | tf_op jit(solution)/shard_map/all_to_all | solution.py:585

commit v2 on v1

--- a/solution.py
+++ b/solution.py
@@ -177,22 +177,23 @@
     lax.fori_loop(0, XA, step, 0)
 
 
-def enter_kernel(
-    index, potential, direction, whi, wlo, mhi, mlo, uv, td, t0, shi, slo, field, xhi, xlo, y
-):
-    rows = potential.shape[1]
-
-    for number, (source, channel) in enumerate(
-        ((potential, 0), (potential, 1), (direction, 0), (direction, 1))
-    ):
-
-        def cut(row, number=number, source=source, channel=channel):
-            high, low = halves(source[channel, pl.ds(row, STRIP), :])
-            at = pl.ds(pl.multiple_of(number * rows + row, STRIP), STRIP)
-            shi[at, :] = high
-            slo[at, :] = low
-
-        strips(rows, cut)
+def enter_kernel(pieces, index, *refs):
+    sources = refs[:pieces], refs[pieces : 2 * pieces]
+    whi, wlo, mhi, mlo, uv, td, t0, shi, slo, field, xhi, xlo, y = refs[2 * pieces :]
+    rows = sum(piece.shape[1] for piece in sources[0])
+
+    for number in range(4):
+        first = number * rows
+        for piece in sources[number // 2]:
+
+            def cut(row, first=first, piece=piece, channel=number % 2):
+                high, low = halves(piece[channel, pl.ds(row, STRIP), :])
+                at = pl.ds(pl.multiple_of(first + row, STRIP), STRIP)
+                shi[at, :] = high
+                slo[at, :] = low
+
+            strips(piece.shape[1], cut)
+            first += piece.shape[1]
 
     def rotated(b):
         at = [pl.ds(pl.multiple_of(index[b, s] * BLK, BLK), BLK) for s in range(SLOTS)]
@@ -500,7 +501,7 @@
 
 
 def enter(index, potential, direction, weights, matrices):
-    rows = potential.shape[1]
+    rows = sum(piece.shape[1] for piece in potential)
     scratch = [
         pltpu.VMEM((4 * rows, NB * BLK), jnp.bfloat16),
         pltpu.VMEM((4 * rows, NB * BLK), jnp.bfloat16),
@@ -509,7 +510,16 @@
     outs = [(XA, 4, rows, LANES), (XA, 4, rows, LANES), (XA, 2, rows, LANES)]
     extra = NB * 4 * rows * 256 * 128 * 6
     return call(
-        enter_kernel, outs, scratch, 2, extra, index, potential, direction, *weights, *matrices
+        functools.partial(enter_kernel, len(potential)),
+        outs,
+        scratch,
+        2,
+        extra,
+        index,
+        *potential,
+        *direction,
+        *weights,
+        *matrices,
     )
 
 
@@ -581,17 +591,63 @@
     return rounded.astype(jnp.bfloat16), (stacked - rounded).astype(jnp.bfloat16)
 
 
+def device(q, b, r):
+    return q * XA + b * (XA // 2) + r
+
+
+def groups():
+    return [
+        [device(x, b, r) for x in range(2) for r in range(XA // 2)] for b in range(2)
+    ]
+
+
 def exchange(values):
-    return lax.all_to_all(values, "fft", split_axis=0, concat_axis=0, tiled=True)
+    return lax.all_to_all(
+        values,
+        ("parts", "fft"),
+        split_axis=0,
+        concat_axis=0,
+        axis_index_groups=groups(),
+        tiled=True,
+    )
+
+
+def moves(kind):
+    pairs = []
+    for r in range(XA // 2):
+        a, b, c, d = device(0, 1, r), device(0, 0, r), device(1, 0, r), device(1, 1, r)
+        pairs += [(a, b), (b, c), (c, d), (d, a)] if kind == 0 else [(a, c), (c, a), (b, b), (d, d)]
+    return pairs
+
+
+def arrive(values):
+    step = XB // 4
+    return [
+        lax.ppermute(values[:, i * step : (i + 1) * step], ("parts", "fft"), moves(i % 2))
+        for i in range(4)
+    ]
+
+
+def depart(values):
+    step = XB // 4
+    return [
+        lax.ppermute(
+            values[:, i * step : (i + 1) * step],
+            ("parts", "fft"),
+            [(there, here) for here, there in moves(i % 2)],
+        )
+        for i in range(4)
+    ]
 
 
 def blocked_body(potential, direction, block_index, block_weights):
+    potential, direction = arrive(potential), arrive(direction)
     whi, wlo = split_weights(block_weights)
     by_column = column_constants()
     column = tuple(jnp.asarray(v) for v in split_constant(by_column))
     row = tuple(jnp.asarray(v) for v in split_constant(by_column.transpose(0, 2, 1)))
     weights = [(whi[a], wlo[a]) for a in range(ANGLES)]
-    mixed = False
+    mixed = True
     state = []
     for a in range(ANGLES):
         uv, td, t0 = enter(block_index[a], potential, direction, weights[a], row)
@@ -608,7 +664,7 @@
     total = ()
     for a in range(ANGLES):
         total = (leave(block_index[a], pulled[a], carried[a][3], weights[a], row, total),)
-    return total[0]
+    return jnp.concatenate(depart(total[0]), axis=1)
 
 
 def transform_table(count_in, count_out, length, orient):
@@ -811,7 +867,7 @@
 
 
 def body(potential, direction, block_index, block_weights):
-    if lax.axis_size("fft") == XA and potential.shape[1] == XB:
+    if lax.axis_size("parts") == 2 and lax.axis_size("fft") == XA:
         return blocked_body(potential, direction, block_index, block_weights)
     return general_body(potential, direction, block_index, block_weights)
 

time: 959 us -> 1070 us (1.12); the launches traced: 944 us -> 1070 us
  starting transfers between devices: 109 us -> 239 us
  blocking collectives: 211 us -> 108 us
  waiting for transfers between devices: 387 us -> 478 us
    ppermute x0 -> x12, waiting for transfers between devices: none -> 263 us  [the longest x8 175 us: arrive(): lax.ppermute(values[:, i * step:(i + 1) * step], ('parts', 'fft'), moves(...]
    ppermute x0 -> x12, starting transfers between devices: none -> 185 us  [the longest x8 176 us: arrive(): lax.ppermute(values[:, i * step:(i + 1) * step], ('parts', 'fft'), moves(...]
    all_to_all x8, waiting for transfers between devices: 387 us -> 215 us  [exchange(): lax.all_to_all(values, ('parts', 'fft'), split_axis=0, concat_axis=0, axi...]
    all_to_all x2, blocking collectives: 211 us -> 108 us  [exchange(): lax.all_to_all(values, ('parts', 'fft'), split_axis=0, concat_axis=0, axi...]
    all_to_all x8, starting transfers between devices: 109 us -> 54.2 us  [exchange(): lax.all_to_all(values, ('parts', 'fft'), split_axis=0, concat_axis=0, axi...]
  transfers between devices with their start and end apart: 8 -> 20, of which waited for: 8 -> 17; matrix products, arithmetic and copies ran while one was open for 0% -> 1% of each run, Pallas kernels for 17% -> 15%
where the time goes in v2:
time: 1070 us
  waiting for transfers between devices  478 us (45%)
  starting transfers between devices  239 us (22%)
  Pallas kernels  218 us (20%)
  blocking collectives  108 us (10%)
  local copies, waits for them, and re-layouts  15.8 us (1%)
    pallas_call x10, Pallas kernels, call(): pl.pallas_call(kernel, out_shape=[jax.ShapeDtypeStruct(o, jnp.float32) fo...  218 us
    all_to_all x8, waiting for transfers between devices, exchange(): lax.all_to_all(values, ('parts', 'fft'), split_axis=0, concat_axis=0, axi...  215 us
    ppermute x8, starting transfers between devices, arrive(): lax.ppermute(values[:, i * step:(i + 1) * step], ('parts', 'fft'), moves(...  176 us
    ppermute x8, waiting for transfers between devices, arrive(): lax.ppermute(values[:, i * step:(i + 1) * step], ('parts', 'fft'), moves(...  175 us
    all_to_all x2, blocking collectives, exchange(): lax.all_to_all(values, ('parts', 'fft'), split_axis=0, concat_axis=0, axi...  108 us
    ppermute x4, waiting for transfers between devices, depart(): lax.ppermute(values[:, i * step:(i + 1) * step], ('parts', 'fft'), [(ther...  87.4 us
    all_to_all x8, starting transfers between devices, exchange(): lax.all_to_all(values, ('parts', 'fft'), split_axis=0, concat_axis=0, axi...  54.2 us
  transfers between devices with their start and end apart: 20, of which 17 were waited for; matrix products, arithmetic and copies ran while one was open for 1% of the time, Pallas kernels for 15%

profile of v2, /device:TPU:3, one launch (start us, length us, event | category | flops | bytes accessed | tf_op | source)
XLA Modules:
  0.0 1066.7 jit_solution(4209344003662757950)
XLA Ops:
  8.3 7.8 collective-permute-start.2
  21.5 7.1 collective-permute-done.refs_0_
  28.6 114.5 %collective-permute-start.5 = (f32[2,32,4096]{2,1,0:T(8,128)}, f32[2,32,4096]{2,1,0:T(8,128)S(1)}, u32[]{:S(2)}, u32[]{:S(2)}) collective-permute-start(f32[2,32,4096]{2,1,0:T(8,128)} %get-tuple-element.36), channel_id=1, source_target_pairs={{8,16},{16,8},{0,0},{24,24},{9,17},{17,9},{1,1},{25,25},{10,18},{1... | collective-permute-start | bytes 3145736 | tf_op jit(solution)/shard_map/ppermute | solution.py:626
  143.1 43.8 %collective-permute-done.1.refs_1_ = f32[2,32,4096]{2,1,0:T(8,128)} collective-permute-done((f32[2,32,4096]{2,1,0:T(8,128)}, f32[2,32,4096]{2,1,0:T(8,128)}, u32[]{:S(2)}, u32[]{:S(2)}) %collective-permute-start.1) | collective-permute-done | bytes 1048608 | tf_op jit(solution)/shard_map/ppermute | solution.py:626
  186.9 46.1 %collective-permute-start.7 = (f32[2,32,4096]{2,1,0:T(8,128)S(1)}, f32[2,32,4096]{2,1,0:T(8,128)}, u32[]{:S(2)}, u32[]{:S(2)}) collective-permute-start(f32[2,32,4096]{2,1,0:T(8,128)S(1)} %get-tuple-element.35), channel_id=1, source_target_pairs={{8,16},{16,8},{0,0},{24,24},{9,17},{17,9},{1,1},{25,25},{10,18},{1... | collective-permute-start | bytes 3145736 | tf_op jit(solution)/shard_map/ppermute | solution.py:626
  242.2 34.6 %collective-permute-done.3.refs_3_ = f32[2,32,4096]{2,1,0:T(8,128)} collective-permute-done((f32[2,32,4096]{2,1,0:T(8,128)S(1)}, f32[2,32,4096]{2,1,0:T(8,128)}, u32[]{:S(2)}, u32[]{:S(2)}) %collective-permute-start.3) | collective-permute-done | bytes 1048608 | tf_op jit(solution)/shard_map/ppermute | solution.py:626
  276.8 44.8 %collective-permute-done.5.refs_5_ = f32[2,32,4096]{2,1,0:T(8,128)S(1)} collective-permute-done((f32[2,32,4096]{2,1,0:T(8,128)}, f32[2,32,4096]{2,1,0:T(8,128)S(1)}, u32[]{:S(2)}, u32[]{:S(2)}) %collective-permute-start.5) | collective-permute-done | bytes 1048608 | tf_op jit(solution)/shard_map/ppermute | solution.py:626
  321.6 45.0 %collective-permute-done.7.refs_7_ = f32[2,32,4096]{2,1,0:T(8,128)} collective-permute-done((f32[2,32,4096]{2,1,0:T(8,128)S(1)}, f32[2,32,4096]{2,1,0:T(8,128)}, u32[]{:S(2)}, u32[]{:S(2)}) %collective-permute-start.7) | collective-permute-done | bytes 1048608 | tf_op jit(solution)/shard_map/ppermute | solution.py:626
  366.7 29.9 %shard_map.86 = (f32[16,4,128,128]{3,2,1,0:T(8,128)}, f32[16,4,128,128]{3,2,1,0:T(8,128)}, f32[16,2,128,128]{3,2,1,0:T(8,128)}) custom-call(s32[32,2]{1,0:T(8,128)} %copy.11.index, f32[2,32,4096]{2,1,0:T(8,128)} %collective-permute-done.refs_0_, f32[2,32,4096]{2,1,0:T(8,128)} %collective-permute-done.1.refs_1_, ...), custom_call_target="tpu_custom_call" | custom-call | flops 4831838208 | bytes 27263232 | tf_op jit(solution)/shard_map/pallas_call | solution.py:480
  396.6 53.0 %all_to_all.50.refs_1_.refs_0_ = f32[16,4,128,128]{3,2,1,0:T(8,128)} all-to-all(f32[16,4,128,128]{3,2,1,0:T(8,128)} %get-tuple-element.21), channel_id=1, replica_groups={{0,1,2,3,4,5,6,7,16,17,18,19,20,21,22,23},{8,9,10,11,12,13,14,15,24,25,..., dimensions={0} | all-to-all | bytes 8388608 | tf_op jit(solution)/shard_map/all_to_all | solution.py:605
  456.9 29.9 %shard_map.82 = (f32[16,4,128,128]{3,2,1,0:T(8,128)}, f32[16,4,128,128]{3,2,1,0:T(8,128)}, f32[16,2,128,128]{3,2,1,0:T(8,128)}) custom-call(s32[32,2]{1,0:T(8,128)} %copy.12.index, f32[2,32,4096]{2,1,0:T(8,128)} %collective-permute-done.refs_0_, f32[2,32,4096]{2,1,0:T(8,128)} %collective-permute-done.1.refs_1_, ...), custom_call_target="tpu_custom_call" | custom-call | flops 4831838208 | bytes 27263232 | tf_op jit(solution)/shard_map/pallas_call | solution.py:480
  486.8 23.9 %all-to-all-done.5.refs_0_ = f32[16,4,128,128]{3,2,1,0:T(8,128)} async-done(((f32[16,4,128,128]{3,2,1,0:T(8,128)}), f32[16,4,128,128]{3,2,1,0:T(8,128)}, u32[]{:S(2)}, u32[]{:S(2)}) %all-to-all-start.5) | async-done | bytes 4194336 | tf_op jit(solution)/shard_map/all_to_all | solution.py:605
  510.7 54.8 %all_to_all.51.refs_1_.refs_0_ = f32[16,4,128,128]{3,2,1,0:T(8,128)} all-to-all(f32[16,4,128,128]{3,2,1,0:T(8,128)} %get-tuple-element.16), channel_id=1, replica_groups={{0,1,2,3,4,5,6,7,16,17,18,19,20,21,22,23},{8,9,10,11,12,13,14,15,24,25,..., dimensions={0} | all-to-all | bytes 8388608 | tf_op jit(solution)/shard_map/all_to_all | solution.py:605
  572.2 21.6 %shard_map.87 = (f32[16,4,128,128]{3,2,1,0:T(8,128)}, f32[16,2,128,128]{3,2,1,0:T(8,128)}) custom-call(f32[16,4,128,128]{3,2,1,0:T(8,128)} %all-to-all-done.5.refs_0_, f32[16,4,128,128]{3,2,1,0:T(8,128)} %all_to_all.50.refs_1_.refs_0_, bf16[16,256,256]{2,1,0:T(8,128)(2,1)} %constant.8.clone.refs_2_.refs_1_, bf16[16,256,256]{2,1,0:T(8,128)(2,1)} %constant.9.clone.refs_3_.refs_2_), custom_call_target="tpu_custom_call" | custom-call | flops 3221225472 | bytes 18874368 | tf_op jit(solution)/shard_map/pallas_call | solution.py:480
  593.9 32.9 %all-to-all-done.refs_0_ = f32[16,4,128,128]{3,2,1,0:T(8,128)} async-done(((f32[16,4,128,128]{3,2,1,0:T(8,128)}), f32[16,4,128,128]{3,2,1,0:T(8,128)}, u32[]{:S(2)}, u32[]{:S(2)}) %all-to-all-start) | async-done | bytes 4194336 | tf_op jit(solution)/shard_map/all_to_all | solution.py:605
  626.8 7.3 all-to-all-start.7
  634.0 21.7 %shard_map.83 = (f32[16,4,128,128]{3,2,1,0:T(8,128)}, f32[16,2,128,128]{3,2,1,0:T(8,128)}) custom-call(f32[16,4,128,128]{3,2,1,0:T(8,128)} %all-to-all-done.refs_0_, f32[16,4,128,128]{3,2,1,0:T(8,128)} %all_to_all.51.refs_1_.refs_0_, bf16[16,256,256]{2,1,0:T(8,128)(2,1)} %constant.8.clone.refs_2_.refs_1_, bf16[16,256,256]{2,1,0:T(8,128)(2,1)} %constant.9.clone.refs_3_.refs_2_), custom_call_target="tpu_custom_call" | custom-call | flops 3221225472 | bytes 18874368 | tf_op jit(solution)/shard_map/pallas_call | solution.py:480
  655.7 32.8 %all-to-all-done.7.fields = f32[16,4,128,128]{3,2,1,0:T(8,128)} async-done(((f32[16,4,128,128]{3,2,1,0:T(8,128)}), f32[16,4,128,128]{3,2,1,0:T(8,128)}, u32[]{:S(2)}, u32[]{:S(2)}) %all-to-all-start.7) | async-done | bytes 4194336 | tf_op jit(solution)/shard_map/all_to_all | solution.py:605
  688.6 7.1 all-to-all-start.2
  695.6 16.5 %shard_map.88 = f32[16,2,128,128]{3,2,1,0:T(8,128)} custom-call(f32[16,4,128,128]{3,2,1,0:T(8,128)} %all-to-all-done.7.fields, bf16[16,256,256]{2,1,0:T(8,128)(2,1)} %constant.10.clone.refs_10_.mhi, bf16[16,256,256]{2,1,0:T(8,128)(2,1)} %constant.11.clone.refs_11_.mlo), custom_call_target="tpu_custom_call" | custom-call | flops 2415919104 | bytes 10485760 | tf_op jit(solution)/shard_map/pallas_call | solution.py:480
  712.1 38.1 %all-to-all-done.2.fields = f32[16,4,128,128]{3,2,1,0:T(8,128)} async-done(((f32[16,4,128,128]{3,2,1,0:T(8,128)}), f32[16,4,128,128]{3,2,1,0:T(8,128)}, u32[]{:S(2)}, u32[]{:S(2)}) %all-to-all-start.2) | async-done | bytes 4194336 | tf_op jit(solution)/shard_map/all_to_all | solution.py:605
  756.5 16.4 %shard_map.84 = f32[16,2,128,128]{3,2,1,0:T(8,128)} custom-call(f32[16,4,128,128]{3,2,1,0:T(8,128)} %all-to-all-done.2.fields, bf16[16,256,256]{2,1,0:T(8,128)(2,1)} %constant.10.clone.refs_10_.mhi, bf16[16,256,256]{2,1,0:T(8,128)(2,1)} %constant.11.clone.refs_11_.mlo), custom_call_target="tpu_custom_call" | custom-call | flops 2415919104 | bytes 10485760 | tf_op jit(solution)/shard_map/pallas_call | solution.py:480
  772.9 10.0 all-to-all-done.8.back
  790.5 17.6 %shard_map.89 = f32[16,4,128,128]{3,2,1,0:T(8,128)} custom-call(f32[16,2,128,128]{3,2,1,0:T(8,128)} %copy-done.1, f32[16,2,128,128]{3,2,1,0:T(8,128)} %get-tuple-element.23.phi, f32[16,4,128,128]{3,2,1,0:T(8,128)} %all_to_all.50.refs_1_.refs_0_, bf16[16,256,256]{2,1,0:T(8,128)(2,1)} %constant.8.clone.refs_2_.refs_1_, ...), custom_call_target="tpu_custom_call" | custom-call | flops 1610612736 | bytes 16777216 | tf_op jit(solution)/shard_map/pallas_call | solution.py:480
  808.1 8.8 all-to-all-done.3.back
  825.3 17.7 %shard_map.85 = f32[16,4,128,128]{3,2,1,0:T(8,128)} custom-call(f32[16,2,128,128]{3,2,1,0:T(8,128)} %copy-done, f32[16,2,128,128]{3,2,1,0:T(8,128)} %get-tuple-element.18.phi, f32[16,4,128,128]{3,2,1,0:T(8,128)} %all_to_all.51.refs_1_.refs_0_, bf16[16,256,256]{2,1,0:T(8,128)(2,1)} %constant.8.clone.refs_2_.refs_1_, ...), custom_call_target="tpu_custom_call" | custom-call | flops 1610612736 | bytes 16777216 | tf_op jit(solution)/shard_map/pallas_call | solution.py:480
  843.0 36.8 %all-to-all-done.9.back = f32[16,4,128,128]{3,2,1,0:T(8,128)} async-done(((f32[16,4,128,128]{3,2,1,0:T(8,128)}), f32[16,4,128,128]{3,2,1,0:T(8,128)}, u32[]{:S(2)}, u32[]{:S(2)}) %all-to-all-start.9) | async-done | bytes 4194336 | tf_op jit(solution)/shard_map/all_to_all | solution.py:605
  886.9 22.6 %shard_map.90.refs_0_ = f32[2,128,4096]{2,1,0:T(8,128)} custom-call(s32[32,2]{1,0:T(8,128)} %copy.11.index, f32[16,4,128,128]{3,2,1,0:T(8,128)} %all-to-all-done.9.back, f32[16,2,128,128]{3,2,1,0:T(8,128)} %get-tuple-element.24.t0, bf16[32,256,128]{2,1,0:T(8,128)(2,1)} %get-tuple-element.46.refs_8_.whi, bf16[32,256,128]{2,1,0:T(8,128)(2,1)} %get-tuple-element.31.refs_9_.wlo, ...), custom_call_target="tpu_custom_call" | custom-call | flops 2415919104 | bytes 18874624 | tf_op jit(solution)/shard_map/pallas_call | solution.py:480
  909.5 31.9 %all-to-all-done.4.back = f32[16,4,128,128]{3,2,1,0:T(8,128)} async-done(((f32[16,4,128,128]{3,2,1,0:T(8,128)}), f32[16,4,128,128]{3,2,1,0:T(8,128)}, u32[]{:S(2)}, u32[]{:S(2)}) %all-to-all-start.4) | async-done | bytes 4194336 | tf_op jit(solution)/shard_map/all_to_all | solution.py:605
  941.4 23.8 %shard_map.91 = f32[2,128,4096]{2,1,0:T(8,128)} custom-call(s32[32,2]{1,0:T(8,128)} %copy.12.index, f32[16,4,128,128]{3,2,1,0:T(8,128)} %all-to-all-done.4.back, f32[16,2,128,128]{3,2,1,0:T(8,128)} %get-tuple-element.19.t0, bf16[32,256,128]{2,1,0:T(8,128)(2,1)} %get-tuple-element.45.refs_8_.whi, bf16[32,256,128]{2,1,0:T(8,128)(2,1)} %get-tuple-element.32.refs_9_.wlo, ...), custom_call_target="tpu_custom_call" | custom-call | flops 2415919104 | bytes 23068928 | tf_op jit(solution)/shard_map/pallas_call | solution.py:480
  976.8 61.9 %collective-permute-done.10 = f32[2,32,4096]{2,1,0:T(8,128)S(1)} collective-permute-done((f32[2,32,4096]{2,1,0:T(8,128)S(1)}, f32[2,32,4096]{2,1,0:T(8,128)S(1)}, u32[]{:S(2)}, u32[]{:S(2)}) %collective-permute-start.10) | collective-permute-done | bytes 1048608 | tf_op jit(solution)/shard_map/ppermute | solution.py:634
  1041.8 19.4 %collective-permute-done.8 = f32[2,32,4096]{2,1,0:T(8,128)S(1)} collective-permute-done((f32[2,32,4096]{2,1,0:T(8,128)S(1)}, f32[2,32,4096]{2,1,0:T(8,128)S(1)}, u32[]{:S(2)}, u32[]{:S(2)}) %collective-permute-start.8) | collective-permute-done | bytes 1048608 | tf_op jit(solution)/shard_map/ppermute | solution.py:634
  (41 shorter events, 86.3 us)
Async XLA Ops:
  0.0 19.1 %copy-start.2 = (f32[2,128,4096]{2,1,0:T(8,128)S(1)}, f32[2,128,4096]{2,1,0:T(8,128)}, u32[]{:S(2)}) copy-start(f32[2,128,4096]{2,1,0:T(8,128)} %param.9) | copy-start | bytes 12582916
  4.1 24.5 %collective-permute-start = (f32[2,32,4096]{2,1,0:T(8,128)}, f32[2,32,4096]{2,1,0:T(8,128)}, u32[]{:S(2)}, u32[]{:S(2)}) collective-permute-start(f32[2,32,4096]{2,1,0:T(8,128)} %get-tuple-element.41), channel_id=1, source_target_pairs={{8,0},{0,16},{16,24},{24,8},{9,1},{1,17},{17,25},{25,9},{10,2},{2,... | collective-permute-start | bytes 3145736 | tf_op jit(solution)/shard_map/ppermute | solution.py:626
  6.4 180.5 %collective-permute-start.1 = (f32[2,32,4096]{2,1,0:T(8,128)}, f32[2,32,4096]{2,1,0:T(8,128)}, u32[]{:S(2)}, u32[]{:S(2)}) collective-permute-start(f32[2,32,4096]{2,1,0:T(8,128)} %get-tuple-element.40), channel_id=1, source_target_pairs={{8,16},{16,8},{0,0},{24,24},{9,17},{17,9},{1,1},{25,25},{10,18},{1... | collective-permute-start | bytes 3145736 | tf_op jit(solution)/shard_map/ppermute | solution.py:626
  8.3 178.6 %collective-permute-start.2 = (f32[2,32,4096]{2,1,0:T(8,128)}, f32[2,32,4096]{2,1,0:T(8,128)}, u32[]{:S(2)}, u32[]{:S(2)}) collective-permute-start(f32[2,32,4096]{2,1,0:T(8,128)} %get-tuple-element.42), channel_id=1, source_target_pairs={{8,0},{0,16},{16,24},{24,8},{9,1},{1,17},{17,25},{25,9},{10,2},{2,... | collective-permute-start | bytes 3145736 | tf_op jit(solution)/shard_map/ppermute | solution.py:626
  16.1 4.7 copy-start.3
  16.1 260.7 %collective-permute-start.3 = (f32[2,32,4096]{2,1,0:T(8,128)S(1)}, f32[2,32,4096]{2,1,0:T(8,128)}, u32[]{:S(2)}, u32[]{:S(2)}) collective-permute-start(f32[2,32,4096]{2,1,0:T(8,128)S(1)} %get-tuple-element.39), channel_id=1, source_target_pairs={{8,16},{16,8},{0,0},{24,24},{9,17},{17,9},{1,1},{25,25},{10,18},{1... | collective-permute-start | bytes 3145736 | tf_op jit(solution)/shard_map/ppermute | solution.py:626
  20.8 256.0 %collective-permute-start.4 = (f32[2,32,4096]{2,1,0:T(8,128)}, f32[2,32,4096]{2,1,0:T(8,128)}, u32[]{:S(2)}, u32[]{:S(2)}) collective-permute-start(f32[2,32,4096]{2,1,0:T(8,128)} %get-tuple-element.37), channel_id=1, source_target_pairs={{8,0},{0,16},{16,24},{24,8},{9,1},{1,17},{17,25},{25,9},{10,2},{2,... | collective-permute-start | bytes 3145736 | tf_op jit(solution)/shard_map/ppermute | solution.py:626
  28.6 293.0 %collective-permute-start.5 = (f32[2,32,4096]{2,1,0:T(8,128)}, f32[2,32,4096]{2,1,0:T(8,128)S(1)}, u32[]{:S(2)}, u32[]{:S(2)}) collective-permute-start(f32[2,32,4096]{2,1,0:T(8,128)} %get-tuple-element.36), channel_id=1, source_target_pairs={{8,16},{16,8},{0,0},{24,24},{9,17},{17,9},{1,1},{25,25},{10,18},{1... | collective-permute-start | bytes 3145736 | tf_op jit(solution)/shard_map/ppermute | solution.py:626
  186.9 134.7 %collective-permute-start.6 = (f32[2,32,4096]{2,1,0:T(8,128)S(1)}, f32[2,32,4096]{2,1,0:T(8,128)S(1)}, u32[]{:S(2)}, u32[]{:S(2)}) collective-permute-start(f32[2,32,4096]{2,1,0:T(8,128)S(1)} %get-tuple-element.38), channel_id=1, source_target_pairs={{8,0},{0,16},{16,24},{24,8},{9,1},{1,17},{17,25},{25,9},{10,2},{2,... | collective-permute-start | bytes 3145736 | tf_op jit(solution)/shard_map/ppermute | solution.py:626
  186.9 179.8 %collective-permute-start.7 = (f32[2,32,4096]{2,1,0:T(8,128)S(1)}, f32[2,32,4096]{2,1,0:T(8,128)}, u32[]{:S(2)}, u32[]{:S(2)}) collective-permute-start(f32[2,32,4096]{2,1,0:T(8,128)S(1)} %get-tuple-element.35), channel_id=1, source_target_pairs={{8,16},{16,8},{0,0},{24,24},{9,17},{17,9},{1,1},{25,25},{10,18},{1... | collective-permute-start | bytes 3145736 | tf_op jit(solution)/shard_map/ppermute | solution.py:626
  321.6 45.0 %copy-start.4 = (f32[2,32,4096]{2,1,0:T(8,128)}, f32[2,32,4096]{2,1,0:T(8,128)S(1)}, u32[]{:S(2)}) copy-start(f32[2,32,4096]{2,1,0:T(8,128)S(1)} %collective-permute-done.5.refs_5_) | copy-start | bytes 3145732
  321.6 45.0 %copy-start.5 = (f32[2,32,4096]{2,1,0:T(8,128)}, f32[2,32,4096]{2,1,0:T(8,128)S(1)}, u32[]{:S(2)}) copy-start(f32[2,32,4096]{2,1,0:T(8,128)S(1)} %collective-permute-done.6.refs_6_) | copy-start | bytes 3145732
  449.6 61.1 %all-to-all-start.5 = ((f32[16,4,128,128]{3,2,1,0:T(8,128)}), f32[16,4,128,128]{3,2,1,0:T(8,128)}, u32[]{:S(2)}, u32[]{:S(2)}) async-start(f32[16,4,128,128]{3,2,1,0:T(8,128)} %get-tuple-element.20), calls=%async_computation.5 | async-start | bytes 8388608 | tf_op jit(solution)/shard_map/all_to_all | solution.py:605
  565.6 61.2 %all-to-all-start = ((f32[16,4,128,128]{3,2,1,0:T(8,128)}), f32[16,4,128,128]{3,2,1,0:T(8,128)}, u32[]{:S(2)}, u32[]{:S(2)}) async-start(f32[16,4,128,128]{3,2,1,0:T(8,128)} %get-tuple-element.15), calls=%async_computation | async-start | bytes 8388608 | tf_op jit(solution)/shard_map/all_to_all | solution.py:605
  626.8 61.8 %all-to-all-start.7 = ((f32[16,4,128,128]{3,2,1,0:T(8,128)}), f32[16,4,128,128]{3,2,1,0:T(8,128)}, u32[]{:S(2)}, u32[]{:S(2)}) async-start(f32[16,4,128,128]{3,2,1,0:T(8,128)} %get-tuple-element.22), calls=%async_computation.7 | async-start | bytes 8388608 | tf_op jit(solution)/shard_map/all_to_all | solution.py:605
  688.6 61.6 %all-to-all-start.2 = ((f32[16,4,128,128]{3,2,1,0:T(8,128)}), f32[16,4,128,128]{3,2,1,0:T(8,128)}, u32[]{:S(2)}, u32[]{:S(2)}) async-start(f32[16,4,128,128]{3,2,1,0:T(8,128)} %get-tuple-element.17), calls=%async_computation.2 | async-start | bytes 8388608 | tf_op jit(solution)/shard_map/all_to_all | solution.py:605
  750.2 32.8 %all-to-all-start.8 = ((f32[16,2,128,128]{3,2,1,0:T(8,128)}), f32[16,2,128,128]{3,2,1,0:T(8,128)S(1)}, u32[]{:S(2)}, u32[]{:S(2)}) async-start(f32[16,2,128,128]{3,2,1,0:T(8,128)} %shard_map.88), calls=%async_computation.8 | async-start | bytes 4194304 | tf_op jit(solution)/shard_map/all_to_all | solution.py:605
  782.9 1.4 copy-start.1
  784.3 32.7 %all-to-all-start.3 = ((f32[16,2,128,128]{3,2,1,0:T(8,128)}), f32[16,2,128,128]{3,2,1,0:T(8,128)S(1)}, u32[]{:S(2)}, u32[]{:S(2)}) async-start(f32[16,2,128,128]{3,2,1,0:T(8,128)} %shard_map.84), calls=%async_computation.3 | async-start | bytes 4194304 | tf_op jit(solution)/shard_map/all_to_all | solution.py:605
  816.9 1.4 copy-start
  818.3 61.5 %all-to-all-start.9 = ((f32[16,4,128,128]{3,2,1,0:T(8,128)}), f32[16,4,128,128]{3,2,1,0:T(8,128)}, u32[]{:S(2)}, u32[]{:S(2)}) async-start(f32[16,4,128,128]{3,2,1,0:T(8,128)} %shard_map.89), calls=%async_computation.9 | async-start | bytes 8388608 | tf_op jit(solution)/shard_map/all_to_all | solution.py:605
  879.8 61.6 %all-to-all-start.4 = ((f32[16,4,128,128]{3,2,1,0:T(8,128)}), f32[16,4,128,128]{3,2,1,0:T(8,128)}, u32[]{:S(2)}, u32[]{:S(2)}) async-start(f32[16,4,128,128]{3,2,1,0:T(8,128)} %shard_map.85), calls=%async_computation.4 | async-start | bytes 8388608 | tf_op jit(solution)/shard_map/all_to_all | solution.py:605
  967.7 71.1 %collective-permute-start.10 = (f32[2,32,4096]{2,1,0:T(8,128)S(1)}, f32[2,32,4096]{2,1,0:T(8,128)S(1)}, u32[]{:S(2)}, u32[]{:S(2)}) collective-permute-start(f32[2,32,4096]{2,1,0:T(8,128)S(1)} %get-tuple-element.29), channel_id=1, source_target_pairs={{0,8},{16,0},{24,16},{8,24},{1,9},{17,1},{25,17},{9,25},{2,10},{18... | collective-permute-start | bytes 3145736 | tf_op jit(solution)/shard_map/ppermute | solution.py:634
  969.7 72.1 %collective-permute-start.11 = (f32[2,32,4096]{2,1,0:T(8,128)S(1)}, f32[2,32,4096]{2,1,0:T(8,128)S(1)}, u32[]{:S(2)}, u32[]{:S(2)}) collective-permute-start(f32[2,32,4096]{2,1,0:T(8,128)S(1)} %get-tuple-element.28), channel_id=1, source_target_pairs={{16,8},{8,16},{0,0},{24,24},{17,9},{9,17},{1,1},{25,25},{18,10},{1... | collective-permute-start | bytes 3145736 | tf_op jit(solution)/shard_map/ppermute | solution.py:634
  974.5 86.7 %collective-permute-start.8 = (f32[2,32,4096]{2,1,0:T(8,128)S(1)}, f32[2,32,4096]{2,1,0:T(8,128)S(1)}, u32[]{:S(2)}, u32[]{:S(2)}) collective-permute-start(f32[2,32,4096]{2,1,0:T(8,128)S(1)} %get-tuple-element.27), channel_id=1, source_target_pairs={{0,8},{16,0},{24,16},{8,24},{1,9},{17,1},{25,17},{9,25},{2,10},{18... | collective-permute-start | bytes 3145736 | tf_op jit(solution)/shard_map/ppermute | solution.py:634
  974.6 89.7 %collective-permute-start.9 = (f32[2,32,4096]{2,1,0:T(8,128)S(1)}, f32[2,32,4096]{2,1,0:T(8,128)S(1)}, u32[]{:S(2)}, u32[]{:S(2)}) collective-permute-start(f32[2,32,4096]{2,1,0:T(8,128)S(1)} %get-tuple-element.30), channel_id=1, source_target_pairs={{16,8},{8,16},{0,0},{24,24},{17,9},{9,17},{1,1},{25,25},{18,10},{1... | collective-permute-start | bytes 3145736 | tf_op jit(solution)/shard_map/ppermute | solution.py:634

commit v3 on v2

--- a/solution.py
+++ b/solution.py
@@ -19,6 +19,9 @@
 SLOTS = 2
 STRIP = 16
 LANES = 128
+QUARTER = XB // 4
+HALF = XA // 2
+MEMBERS = [(g % 2, (g // 2 % 2) * 4 + (g // 4 % 2) * 2 + g // 8) for g in range(XA)]
 
 
 PRECISE = lax.Precision.HIGHEST
@@ -178,15 +181,14 @@
 
 
 def enter_kernel(pieces, index, *refs):
-    sources = refs[:pieces], refs[pieces : 2 * pieces]
-    whi, wlo, mhi, mlo, uv, td, t0, shi, slo, field, xhi, xlo, y = refs[2 * pieces :]
-    rows = sum(piece.shape[1] for piece in sources[0])
+    whi, wlo, mhi, mlo, out, t0, shi, slo, field, xhi, xlo, y = refs[pieces:]
+    rows = sum(piece.shape[1] for piece in refs[:pieces])
 
     for number in range(4):
         first = number * rows
-        for piece in sources[number // 2]:
-
-            def cut(row, first=first, piece=piece, channel=number % 2):
+        for piece in refs[:pieces]:
+
+            def cut(row, first=first, piece=piece, channel=number):
                 high, low = halves(piece[channel, pl.ds(row, STRIP), :])
                 at = pl.ds(pl.multiple_of(first + row, STRIP), STRIP)
                 shi[at, :] = high
@@ -233,53 +235,40 @@
         for number in range(2):
             values = rows_in(y, pl.multiple_of(number * rows + row, STRIP))
             for b, (re, im) in enumerate(values):
-                uv[b, 2 * number, at, :] = re
-                uv[b, 2 * number + 1, at, :] = im
+                out[b, 2 * number, at, :] = re
+                out[b, 2 * number + 1, at, :] = im
 
     strips(rows, backward)
 
     def second_slice(b, carry):
         for channel, value in enumerate(rotated(XA + b)):
-            td[b, channel] = value
+            out[b, 4 + channel] = value
         return carry
 
     lax.fori_loop(0, XA, second_slice, 0)
 
 
-def row_places(mixed):
-    same = list(range(XA))
-    if not mixed:
-        return [(0, XB, same)]
-    swapped = [p ^ (XA // 2) for p in same]
-    step = XB // 4
-    return [(i * step, step, swapped if i % 2 == 0 else same) for i in range(4)]
-
-
-def column_strips(mixed, step):
-    for first, count, places in row_places(mixed):
-        strips(count, lambda row, first=first, places=places: step(pl.multiple_of(first + row, STRIP), places))
-
-
-def middle_kernel(mixed, chunks, *refs):
-    uv, td = refs[:chunks], refs[chunks : 2 * chunks]
-    mhi, mlo, out, phi, xhi, xlo, y = refs[2 * chunks :]
+def row_places():
+    moved = [MEMBERS.index((1 - p // HALF, p % HALF)) for p in range(XA)]
+    kept = [MEMBERS.index((p // HALF, p % HALF)) for p in range(XA)]
+    return [(i * QUARTER, kept if i % 2 else moved) for i in range(XB // QUARTER)]
+
+
+def by_quarters(rows, step):
+    for first, places in row_places():
+        c, within = first // rows, first % rows
+
+        def inner(row, first=first, c=c, within=within, places=places):
+            local = pl.ds(pl.multiple_of(within + row, STRIP), STRIP)
+            step(pl.multiple_of(first + row, STRIP), c, local, places)
+
+        strips(QUARTER, inner)
+
+
+def middle_kernel(chunks, *refs):
+    arrived = refs[:chunks]
+    mhi, mlo, out, kept, xhi, xlo, y = refs[chunks:]
     rows = XB // chunks
-
-    def chunked(step):
-        for first, count, places in row_places(mixed):
-            for piece in range(0, count, min(count, rows)):
-                start = first + piece
-                c, local = start // rows, start % rows
-
-                def inner(row, start=start, c=c, local=local, places=places):
-                    step(
-                        pl.multiple_of(start + row, STRIP),
-                        c,
-                        pl.ds(pl.multiple_of(local + row, STRIP), STRIP),
-                        places,
-                    )
-
-                strips(min(count, rows), inner)
 
     def forward(row, c, local, places):
         for number in range(2):
@@ -288,10 +277,10 @@
                 xlo,
                 number,
                 row,
-                [tuple(uv[c][g, 2 * number + i, local, :] for i in range(2)) for g in places],
+                [tuple(arrived[c][g, 2 * number + i, local, :] for i in range(2)) for g in places],
             )
 
-    chunked(forward)
+    by_quarters(rows, forward)
     columns_mix(xhi, xlo, mhi, mlo, y)
 
     def turn(row, c, local, places):
@@ -299,21 +288,22 @@
         wave = columns_in(y, 0, row)
         product = []
         for g, value in zip(places, wave):
-            value = times((td[c][g, 0, local, :], td[c][g, 1, local, :]), value)
-            phi[g, 0, at, :] = value[0]
-            phi[g, 1, at, :] = value[1]
+            t = arrived[c][g, 4, local, :], arrived[c][g, 5, local, :]
+            value = times(t, value)
+            for i, part in enumerate(value + t):
+                kept[g, i, at, :] = part
             product.append(value)
         columns_out(xhi, xlo, 0, row, product)
         dwave = columns_in(y, 1, row)
         change = []
         for g, value in zip(places, dwave):
-            t_re, t_im, d_re, d_im = (td[c][g, i, local, :] for i in range(4))
-            p_re, p_im = phi[g, 0, at, :], phi[g, 1, at, :]
+            t_re, t_im, d_re, d_im = (arrived[c][g, 4 + i, local, :] for i in range(4))
+            p_re, p_im = kept[g, 0, at, :], kept[g, 1, at, :]
             re, im = times((t_re, t_im), value)
             change.append((re - (d_re * p_im + d_im * p_re), im + (d_re * p_re - d_im * p_im)))
         columns_out(xhi, xlo, 1, row, change)
 
-    chunked(turn)
+    by_quarters(rows, turn)
     columns_mix(xhi, xlo, mhi, mlo, y)
 
     def backward(row, c, local, places):
@@ -323,7 +313,7 @@
                 out[g, 2 * number, at, :] = re
                 out[g, 2 * number + 1, at, :] = im
 
-    chunked(backward)
+    by_quarters(rows, backward)
 
 
 def detector_kernel(fields, mhi, mlo, out, xhi, xlo, y):
@@ -369,32 +359,15 @@
     strips(rows, backward)
 
 
-def return_kernel(mixed, chunks, back, phi, *refs):
-    td = refs[:chunks]
-    mhi, mlo, out, xhi, xlo, y = refs[chunks:]
+def return_kernel(chunks, back, kept, mhi, mlo, *refs):
+    out, (xhi, xlo, y) = refs[:chunks], refs[chunks:]
     rows = XB // chunks
-
-    def chunked(step):
-        for first, count, places in row_places(mixed):
-            for piece in range(0, count, min(count, rows)):
-                start = first + piece
-                c, local = start // rows, start % rows
-
-                def inner(row, start=start, c=c, local=local, places=places):
-                    step(
-                        pl.multiple_of(start + row, STRIP),
-                        c,
-                        pl.ds(pl.multiple_of(local + row, STRIP), STRIP),
-                        places,
-                    )
-
-                strips(min(count, rows), inner)
 
     def forward(row, c, local, places):
         at = pl.ds(row, STRIP)
         columns_out(xhi, xlo, 0, row, [(back[g, 0, at, :], back[g, 1, at, :]) for g in places])
 
-    chunked(forward)
+    by_quarters(rows, forward)
     columns_mix(xhi, xlo, mhi, mlo, y)
 
     def turn(row, c, local, places):
@@ -402,30 +375,29 @@
         pulled = columns_in(y, 0, row)
         following = []
         for g, value in zip(places, pulled):
-            re, im = times((phi[g, 0, at, :], phi[g, 1, at, :]), value)
-            out[g, 0, at, :] = -im
-            out[g, 1, at, :] = -re
-            following.append(times((td[c][g, 0, local, :], td[c][g, 1, local, :]), value))
+            re, im = times((kept[g, 0, at, :], kept[g, 1, at, :]), value)
+            out[c][g, 0, local, :] = -im
+            out[c][g, 1, local, :] = -re
+            following.append(times((kept[g, 2, at, :], kept[g, 3, at, :]), value))
         columns_out(xhi, xlo, 0, row, following)
 
-    chunked(turn)
+    by_quarters(rows, turn)
     columns_mix(xhi, xlo, mhi, mlo, y)
 
     def backward(row, c, local, places):
-        at = pl.ds(row, STRIP)
         for g, (re, im) in zip(places, columns_in(y, 0, row)):
-            out[g, 2, at, :] = re
-            out[g, 3, at, :] = im
-
-    chunked(backward)
-
-
-def leave_kernel(index, back, t0, whi, wlo, mhi, mlo, *refs):
+            out[c][g, 2, local, :] = re
+            out[c][g, 3, local, :] = im
+
+    by_quarters(rows, backward)
+
+
+def leave_kernel(first, index, back, t0, whi, wlo, mhi, mlo, *refs):
     before, (out, shi, slo, xhi, xlo, y) = refs[:-6], refs[-6:]
-    rows = back.shape[2]
+    rows = t0.shape[2]
 
     def forward(row):
-        at = pl.ds(row, STRIP)
+        at = pl.ds(pl.multiple_of(first + row, STRIP), STRIP)
         rows_out(xhi, xlo, row, [(back[b, 2, at, :], back[b, 3, at, :]) for b in range(XA)])
         for b in range(XA):
             for i in range(2):
@@ -485,7 +457,7 @@
         scratch_shapes=scratch,
         compiler_params=pltpu.CompilerParams(vmem_limit_bytes=60 * 1024 * 1024),
         cost_estimate=pl.CostEstimate(
-            flops=mix_count * 16 * 128 * 256 * 256 * 6 + extra,
+            flops=int(mix_count * 16 * 128 * 256 * 256 * 6) + extra,
             bytes_accessed=moved,
             transcendentals=0,
         ),
@@ -500,38 +472,36 @@
     ]
 
 
-def enter(index, potential, direction, weights, matrices):
-    rows = sum(piece.shape[1] for piece in potential)
+def enter(index, pieces, weights, matrices):
+    rows = sum(piece.shape[1] for piece in pieces)
     scratch = [
         pltpu.VMEM((4 * rows, NB * BLK), jnp.bfloat16),
         pltpu.VMEM((4 * rows, NB * BLK), jnp.bfloat16),
         pltpu.VMEM((XA, 2, rows, LANES), jnp.float32),
     ] + mix_scratch(2 * rows, 2 * LANES)
-    outs = [(XA, 4, rows, LANES), (XA, 4, rows, LANES), (XA, 2, rows, LANES)]
+    outs = [(XA, 8, rows, LANES), (XA, 2, rows, LANES)]
     extra = NB * 4 * rows * 256 * 128 * 6
     return call(
-        functools.partial(enter_kernel, len(potential)),
+        functools.partial(enter_kernel, len(pieces)),
         outs,
         scratch,
-        2,
+        rows / XB * 2,
         extra,
         index,
-        *potential,
-        *direction,
+        *pieces,
         *weights,
         *matrices,
     )
 
 
-def middle(uv, td, matrices, mixed):
+def middle(arrived, matrices):
     return call(
-        functools.partial(middle_kernel, mixed, len(uv)),
-        [(XA, 4, XB, LANES), (XA, 2, XB, LANES)],
+        functools.partial(middle_kernel, len(arrived)),
+        [(XA, 4, XB, LANES), (XA, 4, XB, LANES)],
         mix_scratch(2 * XB, 2 * LANES),
         4,
         0,
-        *uv,
-        *td,
+        *arrived,
         *matrices,
     )
 
@@ -549,32 +519,31 @@
     )[0]
 
 
-def pull(back, phi, td, matrices, mixed):
+def pull(back, kept, matrices, chunks):
     return call(
-        functools.partial(return_kernel, mixed, len(td)),
-        [(XA, 4, XB, LANES)],
+        functools.partial(return_kernel, chunks),
+        [(XA, 4, XB // chunks, LANES)] * chunks,
         mix_scratch(2 * XB, LANES),
         2,
         0,
         back,
-        phi,
-        *td,
+        kept,
         *matrices,
-    )[0]
-
-
-def leave(index, back, t0, weights, matrices, before):
-    rows = back.shape[2]
+    )
+
+
+def leave(index, back, first, t0, weights, matrices, before):
+    rows = t0.shape[2]
     scratch = [
         pltpu.VMEM((NB, 2 * rows, LANES), jnp.bfloat16),
         pltpu.VMEM((NB, 2 * rows, LANES), jnp.bfloat16),
     ] + mix_scratch(rows, 2 * LANES)
     extra = NB * 2 * rows * 256 * 128 * 6
     return call(
-        leave_kernel,
+        functools.partial(leave_kernel, first),
         [(2, rows, NB * BLK)],
         scratch,
-        1,
+        rows / XB,
         extra,
         index,
         back,
@@ -592,13 +561,7 @@
 
 
 def device(q, b, r):
-    return q * XA + b * (XA // 2) + r
-
-
-def groups():
-    return [
-        [device(x, b, r) for x in range(2) for r in range(XA // 2)] for b in range(2)
-    ]
+    return q * XA + b * HALF + r
 
 
 def exchange(values):
@@ -607,64 +570,85 @@
         ("parts", "fft"),
         split_axis=0,
         concat_axis=0,
-        axis_index_groups=groups(),
+        axis_index_groups=[[device(x, b, r) for x, r in MEMBERS] for b in range(2)],
         tiled=True,
     )
 
 
-def moves(kind):
-    pairs = []
-    for r in range(XA // 2):
-        a, b, c, d = device(0, 1, r), device(0, 0, r), device(1, 0, r), device(1, 1, r)
-        pairs += [(a, b), (b, c), (c, d), (d, a)] if kind == 0 else [(a, c), (c, a), (b, b), (d, d)]
-    return pairs
-
-
-def arrive(values):
-    step = XB // 4
+def permute(values, steps, back=False):
+    pairs = [
+        (device(*here, r), device(*there, r)) for here, there in steps for r in range(HALF)
+    ]
+    if back:
+        pairs = [(there, here) for here, there in pairs]
+    return lax.ppermute(values, ("parts", "fft"), pairs)
+
+
+CYCLE = [((0, 1), (0, 0)), ((0, 0), (1, 0)), ((1, 0), (1, 1)), ((1, 1), (0, 1))]
+ASIDE = [((0, 1), (1, 1)), ((1, 0), (0, 0))]
+ALONG = [((1, 1), (1, 0)), ((0, 0), (0, 1))]
+SWAP = [((0, 1), (1, 0)), ((1, 0), (0, 1)), ((0, 0), (0, 0)), ((1, 1), (1, 1))]
+
+
+def after(values, others):
+    return lax.optimization_barrier((values, others))[0]
+
+
+def arrive(potential, direction):
+    settled = lax.axis_index("parts") == lax.axis_index("fft") // HALF
+    quarters = [
+        jnp.concatenate([v[:, i * QUARTER : (i + 1) * QUARTER] for v in (potential, direction)])
+        for i in range(XB // QUARTER)
+    ]
+    chunks = []
+    moved = aside = other = ()
+    for i in range(0, len(quarters), 2):
+        first, second = quarters[i : i + 2]
+        moved = permute(after(first, moved), CYCLE)
+        aside = permute(after(second, aside), ASIDE)
+        other = permute(after(aside, other), ALONG)
+        chunks.append([moved, jnp.where(settled, second, other)])
+    return chunks
+
+
+def depart(values):
     return [
-        lax.ppermute(values[:, i * step : (i + 1) * step], ("parts", "fft"), moves(i % 2))
-        for i in range(4)
+        permute(values[:, :QUARTER], CYCLE, True),
+        permute(values[:, QUARTER:], SWAP, True),
     ]
 
 
-def depart(values):
-    step = XB // 4
-    return [
-        lax.ppermute(
-            values[:, i * step : (i + 1) * step],
-            ("parts", "fft"),
-            [(there, here) for here, there in moves(i % 2)],
-        )
-        for i in range(4)
-    ]
-
-
 def blocked_body(potential, direction, block_index, block_weights):
-    potential, direction = arrive(potential), arrive(direction)
+    chunks = arrive(potential, direction)
     whi, wlo = split_weights(block_weights)
     by_column = column_constants()
     column = tuple(jnp.asarray(v) for v in split_constant(by_column))
     row = tuple(jnp.asarray(v) for v in split_constant(by_column.transpose(0, 2, 1)))
     weights = [(whi[a], wlo[a]) for a in range(ANGLES)]
-    mixed = True
-    state = []
+    arrived = [[] for _ in range(ANGLES)]
+    ahead = [[] for _ in range(ANGLES)]
+    for pieces in chunks:
+        for a in range(ANGLES):
+            fields, t0 = enter(block_index[a], pieces, weights[a], row)
+            arrived[a].append(exchange(fields))
+            ahead[a].append(t0)
+    carried = []
     for a in range(ANGLES):
-        uv, td, t0 = enter(block_index[a], potential, direction, weights[a], row)
-        state.append((exchange(uv), exchange(td), t0))
-    carried = []
-    for uv, td, t0 in state:
-        out, phi = middle([uv], [td], column, mixed)
-        carried.append((exchange(out), phi, [td], t0))
-    backs = [exchange(detector(out, row)) for out, _, _, _ in carried]
-    pulled = [
-        exchange(pull(back, phi, td, column, mixed))
-        for back, (_, phi, td, _) in zip(backs, carried)
-    ]
-    total = ()
+        out, kept = middle(arrived[a], column)
+        carried.append((exchange(out), kept))
+    backs = [exchange(detector(out, row)) for out, _ in carried]
+    count = len(chunks)
+    totals = [()] * count
     for a in range(ANGLES):
-        total = (leave(block_index[a], pulled[a], carried[a][3], weights[a], row, total),)
-    return jnp.concatenate(depart(total[0]), axis=1)
+        last = a == ANGLES - 1
+        pulled = pull(backs[a], carried[a][1], column, count if last else 1)
+        pulled = [exchange(v) for v in pulled]
+        for c in range(count):
+            back, first = (pulled[c], 0) if last else (pulled[0], c * (XB // count))
+            totals[c] = (
+                leave(block_index[a], back, first, ahead[a][c], weights[a], row, totals[c]),
+            )
+    return jnp.concatenate([v for total in totals for v in depart(total[0])], axis=1)
 
 
 def transform_table(count_in, count_out, length, orient):

time: 1070 us -> 989 us (0.924)
  starting transfers between devices: 239 us -> 74.3 us
  waiting for transfers between devices: 478 us -> 557 us
  blocking collectives: 108 us -> 52 us
  Pallas kernels: 218 us -> 268 us
    ppermute x12 -> x10, starting transfers between devices: 185 us -> 27.1 us  [permute(): return lax.ppermute(values, ('parts', 'fft'), pairs)]
    ppermute x12 -> x10, waiting for transfers between devices: 263 us -> 348 us  [permute(): return lax.ppermute(values, ('parts', 'fft'), pairs)]
    all_to_all x2 -> x1, blocking collectives: 108 us -> 52 us  [exchange(): lax.all_to_all(values, ('parts', 'fft'), split_axis=0, concat_axis=0, axi...]
    pallas_call x10 -> x14, Pallas kernels: 218 us -> 268 us  [call(): pl.pallas_call(kernel, out_shape=[jax.ShapeDtypeStruct(o, jnp.float32) fo...]
    all_to_all x8 -> x10, starting transfers between devices: 54.2 us -> 47.2 us  [exchange(): lax.all_to_all(values, ('parts', 'fft'), split_axis=0, concat_axis=0, axi...]
    all_to_all x8 -> x10, waiting for transfers between devices: 215 us -> 209 us  [exchange(): lax.all_to_all(values, ('parts', 'fft'), split_axis=0, concat_axis=0, axi...]
  transfers between devices with their start and end apart: 20 -> 20, of which waited for: 17 -> 16; matrix products, arithmetic and copies ran while one was open for 1% -> 2% of each run, Pallas kernels for 15% -> 25%
where the time goes in v3:
time: 989 us; the launch traced here: 988 us
  waiting for transfers between devices  557 us (56%)
  Pallas kernels  268 us (27%)
  starting transfers between devices  74.3 us (8%)
  blocking collectives  52 us (5%)
  local copies, waits for them, and re-layouts  18.4 us (2%)
  other arithmetic  17.7 us (2%)
    ppermute x10, waiting for transfers between devices, permute(): return lax.ppermute(values, ('parts', 'fft'), pairs)  348 us
    pallas_call x14, Pallas kernels, call(): pl.pallas_call(kernel, out_shape=[jax.ShapeDtypeStruct(o, jnp.float32) fo...  268 us
    all_to_all x10, waiting for transfers between devices, exchange(): lax.all_to_all(values, ('parts', 'fft'), split_axis=0, concat_axis=0, axi...  209 us
    all_to_all x1, blocking collectives, exchange(): lax.all_to_all(values, ('parts', 'fft'), split_axis=0, concat_axis=0, axi...  52 us
    all_to_all x10, starting transfers between devices, exchange(): lax.all_to_all(values, ('parts', 'fft'), split_axis=0, concat_axis=0, axi...  47.2 us
    ppermute x10, starting transfers between devices, permute(): return lax.ppermute(values, ('parts', 'fft'), pairs)  27.1 us
  transfers between devices with their start and end apart: 20, of which 16 were waited for; matrix products, arithmetic and copies ran while one was open for 2% of the time, Pallas kernels for 25%

profile of v3, /device:TPU:3, one launch (start us, length us, event | category | flops | bytes accessed | tf_op | source)
XLA Modules:
  0.0 987.6 jit_solution(813658933924123706)
XLA Ops:
  8.1 43.3 %collective-permute-done.1 = f32[4,32,4096]{2,1,0:T(8,128)} collective-permute-done((f32[4,32,4096]{2,1,0:T(8,128)S(1)}, f32[4,32,4096]{2,1,0:T(8,128)}, u32[]{:S(2)}, u32[]{:S(2)}) %collective-permute-start.1) | collective-permute-done | bytes 2097184 | tf_op jit(solution)/shard_map/ppermute | solution.py:584
  54.2 6.2 collective-permute-start
  70.2 77.6 %collective-permute-done.2 = f32[4,32,4096]{2,1,0:T(8,128)} collective-permute-done((f32[4,32,4096]{2,1,0:T(8,128)}, f32[4,32,4096]{2,1,0:T(8,128)}, u32[]{:S(2)}, u32[]{:S(2)}) %collective-permute-start.2) | collective-permute-done | bytes 2097184 | tf_op jit(solution)/shard_map/ppermute | solution.py:584
  151.0 20.9 %shard_map.87 = (f32[16,8,64,128]{3,2,1,0:T(8,128)}, f32[16,2,64,128]{3,2,1,0:T(8,128)}) custom-call(s32[32,2]{1,0:T(8,128)} %copy.13.index, f32[4,32,4096]{2,1,0:T(8,128)} %collective-permute-done.refs_0_, f32[4,32,4096]{2,1,0:T(8,128)} %broadcast_select_fusion.1.refs_1_, bf16[32,256,128]{2,1,0:T(8,128)(2,1)} %get-tuple-element.62.refs_2_.whi, ...), custom_call_target="tpu_custom_call" | custom-call | flops 2415919104 | bytes 17826048 | tf_op jit(solution)/shard_map/pallas_call | solution.py:452
  171.9 7.5 all-to-all-start.5
  180.1 20.9 %shard_map.82 = (f32[16,8,64,128]{3,2,1,0:T(8,128)}, f32[16,2,64,128]{3,2,1,0:T(8,128)}) custom-call(s32[32,2]{1,0:T(8,128)} %copy.14.index, f32[4,32,4096]{2,1,0:T(8,128)} %collective-permute-done.refs_0_, f32[4,32,4096]{2,1,0:T(8,128)} %broadcast_select_fusion.1.refs_1_, bf16[32,256,128]{2,1,0:T(8,128)(2,1)} %get-tuple-element.61.refs_2_.whi, ...), custom_call_target="tpu_custom_call" | custom-call | flops 2415919104 | bytes 17826048 | tf_op jit(solution)/shard_map/pallas_call | solution.py:452
  201.0 35.0 %all-to-all-done.5.refs_0_ = f32[16,8,64,128]{3,2,1,0:T(8,128)} async-done(((f32[16,8,64,128]{3,2,1,0:T(8,128)}), f32[16,8,64,128]{3,2,1,0:T(8,128)}, u32[]{:S(2)}, u32[]{:S(2)}) %all-to-all-start.5) | async-done | bytes 4194336 | tf_op jit(solution)/shard_map/all_to_all | solution.py:568
  243.6 87.4 %collective-permute-done.4 = f32[4,32,4096]{2,1,0:T(8,128)S(1)} collective-permute-done((f32[4,32,4096]{2,1,0:T(8,128)S(1)}, f32[4,32,4096]{2,1,0:T(8,128)S(1)}, u32[]{:S(2)}, u32[]{:S(2)}) %collective-permute-start.4) | collective-permute-done | bytes 2097184 | tf_op jit(solution)/shard_map/ppermute | solution.py:584
  332.3 7.1 collective-permute-start.3
  339.3 90.4 %collective-permute-done.5 = f32[4,32,4096]{2,1,0:T(8,128)S(1)} collective-permute-done((f32[4,32,4096]{2,1,0:T(8,128)S(1)}, f32[4,32,4096]{2,1,0:T(8,128)S(1)}, u32[]{:S(2)}, u32[]{:S(2)}) %collective-permute-start.5) | collective-permute-done | bytes 2097184 | tf_op jit(solution)/shard_map/ppermute | solution.py:584
  431.3 20.9 %shard_map.83 = (f32[16,8,64,128]{3,2,1,0:T(8,128)}, f32[16,2,64,128]{3,2,1,0:T(8,128)}) custom-call(s32[32,2]{1,0:T(8,128)} %copy.14.index, f32[4,32,4096]{2,1,0:T(8,128)} %collective-permute-done.3.refs_0_, f32[4,32,4096]{2,1,0:T(8,128)} %broadcast_select_fusion.refs_1_, bf16[32,256,128]{2,1,0:T(8,128)(2,1)} %get-tuple-element.61.refs_2_.whi, ...), custom_call_target="tpu_custom_call" | custom-call | flops 2415919104 | bytes 17826048 | tf_op jit(solution)/shard_map/pallas_call | solution.py:452
  458.2 20.9 %shard_map.88 = (f32[16,8,64,128]{3,2,1,0:T(8,128)}, f32[16,2,64,128]{3,2,1,0:T(8,128)}) custom-call(s32[32,2]{1,0:T(8,128)} %copy.13.index, f32[4,32,4096]{2,1,0:T(8,128)} %collective-permute-done.3.refs_0_, f32[4,32,4096]{2,1,0:T(8,128)} %broadcast_select_fusion.refs_1_, bf16[32,256,128]{2,1,0:T(8,128)(2,1)} %get-tuple-element.62.refs_2_.whi, ...), custom_call_target="tpu_custom_call" | custom-call | flops 2415919104 | bytes 17826048 | tf_op jit(solution)/shard_map/pallas_call | solution.py:452
  479.1 35.7 %all-to-all-done.1.refs_1_ = f32[16,8,64,128]{3,2,1,0:T(8,128)} async-done(((f32[16,8,64,128]{3,2,1,0:T(8,128)}), f32[16,8,64,128]{3,2,1,0:T(8,128)}, u32[]{:S(2)}, u32[]{:S(2)}) %all-to-all-start.1) | async-done | bytes 4194336 | tf_op jit(solution)/shard_map/all_to_all | solution.py:568
  519.4 22.6 %shard_map.84 = (f32[16,4,128,128]{3,2,1,0:T(8,128)}, f32[16,4,128,128]{3,2,1,0:T(8,128)}) custom-call(f32[16,8,64,128]{3,2,1,0:T(8,128)} %all-to-all-done.refs_0_, f32[16,8,64,128]{3,2,1,0:T(8,128)} %all-to-all-done.1.refs_1_, bf16[16,256,256]{2,1,0:T(8,128)(2,1)} %constant.33.clone.refs_2_.mhi, bf16[16,256,256]{2,1,0:T(8,128)(2,1)} %constant.34.clone.refs_3_.mlo), custom_call_target="tpu_custom_call" | custom-call | flops 3221225472 | bytes 20971520 | tf_op jit(solution)/shard_map/pallas_call | solution.py:452
  542.0 32.6 %all-to-all-done.6.refs_1_ = f32[16,8,64,128]{3,2,1,0:T(8,128)} async-done(((f32[16,8,64,128]{3,2,1,0:T(8,128)}), f32[16,8,64,128]{3,2,1,0:T(8,128)}, u32[]{:S(2)}, u32[]{:S(2)}) %all-to-all-start.6) | async-done | bytes 4194336 | tf_op jit(solution)/shard_map/all_to_all | solution.py:568
  579.1 22.6 %shard_map.89 = (f32[16,4,128,128]{3,2,1,0:T(8,128)}, f32[16,4,128,128]{3,2,1,0:T(8,128)}) custom-call(f32[16,8,64,128]{3,2,1,0:T(8,128)} %all-to-all-done.5.refs_0_, f32[16,8,64,128]{3,2,1,0:T(8,128)} %all-to-all-done.6.refs_1_, bf16[16,256,256]{2,1,0:T(8,128)(2,1)} %constant.33.clone.refs_2_.mhi, bf16[16,256,256]{2,1,0:T(8,128)(2,1)} %constant.34.clone.refs_3_.mlo), custom_call_target="tpu_custom_call" | custom-call | flops 3221225472 | bytes 20971520 | tf_op jit(solution)/shard_map/pallas_call | solution.py:452
  601.7 32.9 %all-to-all-done.2.fields = f32[16,4,128,128]{3,2,1,0:T(8,128)} async-done(((f32[16,4,128,128]{3,2,1,0:T(8,128)}), f32[16,4,128,128]{3,2,1,0:T(8,128)}, u32[]{:S(2)}, u32[]{:S(2)}) %all-to-all-start.2) | async-done | bytes 4194336 | tf_op jit(solution)/shard_map/all_to_all | solution.py:568
  639.1 16.4 %shard_map.85 = f32[16,2,128,128]{3,2,1,0:T(8,128)} custom-call(f32[16,4,128,128]{3,2,1,0:T(8,128)} %all-to-all-done.2.fields, bf16[16,256,256]{2,1,0:T(8,128)(2,1)} %constant.35.clone.refs_4_.mhi, bf16[16,256,256]{2,1,0:T(8,128)(2,1)} %constant.36.clone.refs_5_.mlo), custom_call_target="tpu_custom_call" | custom-call | flops 2415919104 | bytes 10485760 | tf_op jit(solution)/shard_map/pallas_call | solution.py:452
  655.5 39.1 %all-to-all-done.7.fields = f32[16,4,128,128]{3,2,1,0:T(8,128)} async-done(((f32[16,4,128,128]{3,2,1,0:T(8,128)}), f32[16,4,128,128]{3,2,1,0:T(8,128)}, u32[]{:S(2)}, u32[]{:S(2)}) %all-to-all-start.7) | async-done | bytes 4194336 | tf_op jit(solution)/shard_map/all_to_all | solution.py:568
  698.3 16.4 %shard_map.90 = f32[16,2,128,128]{3,2,1,0:T(8,128)} custom-call(f32[16,4,128,128]{3,2,1,0:T(8,128)} %all-to-all-done.7.fields, bf16[16,256,256]{2,1,0:T(8,128)(2,1)} %constant.35.clone.refs_4_.mhi, bf16[16,256,256]{2,1,0:T(8,128)(2,1)} %constant.36.clone.refs_5_.mlo), custom_call_target="tpu_custom_call" | custom-call | flops 2415919104 | bytes 10485760 | tf_op jit(solution)/shard_map/pallas_call | solution.py:452
  714.7 11.8 %all-to-all-done.3.back = f32[16,2,128,128]{3,2,1,0:T(8,128)S(1)} async-done(((f32[16,2,128,128]{3,2,1,0:T(8,128)}), f32[16,2,128,128]{3,2,1,0:T(8,128)S(1)}, u32[]{:S(2)}, u32[]{:S(2)}) %all-to-all-start.3) | async-done | bytes 2097184 | tf_op jit(solution)/shard_map/all_to_all | solution.py:568
  731.4 17.1 %shard_map.86 = (f32[16,4,64,128]{3,2,1,0:T(8,128)}, f32[16,4,64,128]{3,2,1,0:T(8,128)}) custom-call(f32[16,2,128,128]{3,2,1,0:T(8,128)} %copy-done.4, f32[16,4,128,128]{3,2,1,0:T(8,128)} %get-tuple-element.28.kept, bf16[16,256,256]{2,1,0:T(8,128)(2,1)} %constant.33.clone.refs_2_.mhi, bf16[16,256,256]{2,1,0:T(8,128)(2,1)} %constant.34.clone.refs_3_.mlo), custom_call_target="tpu_custom_call" | custom-call | flops 1610612736 | bytes 14680064 | tf_op jit(solution)/shard_map/pallas_call | solution.py:452
  748.5 11.1 %all-to-all-done.8.back = f32[16,2,128,128]{3,2,1,0:T(8,128)S(1)} async-done(((f32[16,2,128,128]{3,2,1,0:T(8,128)}), f32[16,2,128,128]{3,2,1,0:T(8,128)S(1)}, u32[]{:S(2)}, u32[]{:S(2)}) %all-to-all-start.8) | async-done | bytes 2097184 | tf_op jit(solution)/shard_map/all_to_all | solution.py:568
  764.8 17.1 %shard_map.91 = f32[16,4,128,128]{3,2,1,0:T(8,128)} custom-call(f32[16,2,128,128]{3,2,1,0:T(8,128)} %copy-done.3, f32[16,4,128,128]{3,2,1,0:T(8,128)} %get-tuple-element.34.kept, bf16[16,256,256]{2,1,0:T(8,128)(2,1)} %constant.33.clone.refs_2_.mhi, bf16[16,256,256]{2,1,0:T(8,128)(2,1)} %constant.34.clone.refs_3_.mlo), custom_call_target="tpu_custom_call" | custom-call | flops 1610612736 | bytes 14680064 | tf_op jit(solution)/shard_map/pallas_call | solution.py:452
  781.9 10.8 %all-to-all-done.4.back = f32[16,4,64,128]{3,2,1,0:T(8,128)S(1)} async-done(((f32[16,4,64,128]{3,2,1,0:T(8,128)}), f32[16,4,64,128]{3,2,1,0:T(8,128)S(1)}, u32[]{:S(2)}, u32[]{:S(2)}) %all-to-all-start.4) | async-done | bytes 2097184 | tf_op jit(solution)/shard_map/all_to_all | solution.py:568
  792.8 52.0 %all_to_all.55.back = f32[16,4,128,128]{3,2,1,0:T(8,128)} all-to-all(f32[16,4,128,128]{3,2,1,0:T(8,128)} %shard_map.91), channel_id=1, replica_groups={{0,16,4,20,2,18,6,22,1,17,5,21,3,19,7,23},{8,24,12,28,10,26,14,30,9,25,..., dimensions={0} | all-to-all | bytes 8388608 | tf_op jit(solution)/shard_map/all_to_all | solution.py:568
  849.4 18.0 %shard_map.92.refs_0_ = f32[2,64,4096]{2,1,0:T(8,128)} custom-call(s32[32,2]{1,0:T(8,128)} %copy.13.index, f32[16,4,128,128]{3,2,1,0:T(8,128)} %all_to_all.55.back, f32[16,2,64,128]{3,2,1,0:T(8,128)} %get-tuple-element.35.t0, bf16[32,256,128]{2,1,0:T(8,128)(2,1)} %get-tuple-element.62.refs_2_.whi, bf16[32,256,128]{2,1,0:T(8,128)(2,1)} %get-tuple-element.41.refs_3_.wlo, ...), custom_call_target="tpu_custom_call" | custom-call | flops 1207959552 | bytes 15728896 | tf_op jit(solution)/shard_map/pallas_call | solution.py:452
  867.3 18.1 %shard_map.93 = f32[2,64,4096]{2,1,0:T(8,128)} custom-call(s32[32,2]{1,0:T(8,128)} %copy.14.index, f32[16,4,64,128]{3,2,1,0:T(8,128)} %copy-done.2, f32[16,2,64,128]{3,2,1,0:T(8,128)} %get-tuple-element.30.t0, bf16[32,256,128]{2,1,0:T(8,128)(2,1)} %get-tuple-element.61.refs_2_.whi, bf16[32,256,128]{2,1,0:T(8,128)(2,1)} %get-tuple-element.42.refs_3_.wlo, ...), custom_call_target="tpu_custom_call" | custom-call | flops 1207959552 | bytes 15728896 | tf_op jit(solution)/shard_map/pallas_call | solution.py:452
  891.1 18.0 %shard_map.94.refs_0_ = f32[2,64,4096]{2,1,0:T(8,128)} custom-call(s32[32,2]{1,0:T(8,128)} %copy.13.index, f32[16,4,128,128]{3,2,1,0:T(8,128)} %all_to_all.55.back, f32[16,2,64,128]{3,2,1,0:T(8,128)} %get-tuple-element.38.t0, bf16[32,256,128]{2,1,0:T(8,128)(2,1)} %get-tuple-element.62.refs_2_.whi, bf16[32,256,128]{2,1,0:T(8,128)(2,1)} %get-tuple-element.41.refs_3_.wlo, ...), custom_call_target="tpu_custom_call" | custom-call | flops 1207959552 | bytes 15728896 | tf_op jit(solution)/shard_map/pallas_call | solution.py:452
  910.4 18.0 %shard_map.95 = f32[2,64,4096]{2,1,0:T(8,128)} custom-call(s32[32,2]{1,0:T(8,128)} %copy.14.index, f32[16,4,64,128]{3,2,1,0:T(8,128)} %copy-done.1, f32[16,2,64,128]{3,2,1,0:T(8,128)} %get-tuple-element.37.t0, bf16[32,256,128]{2,1,0:T(8,128)(2,1)} %get-tuple-element.61.refs_2_.whi, bf16[32,256,128]{2,1,0:T(8,128)(2,1)} %get-tuple-element.42.refs_3_.wlo, ...), custom_call_target="tpu_custom_call" | custom-call | flops 1207959552 | bytes 15728896 | tf_op jit(solution)/shard_map/pallas_call | solution.py:452
  934.4 24.3 %collective-permute-done.6 = f32[2,32,4096]{2,1,0:T(8,128)} collective-permute-done((f32[2,32,4096]{2,1,0:T(8,128)}, f32[2,32,4096]{2,1,0:T(8,128)}, u32[]{:S(2)}, u32[]{:S(2)}) %collective-permute-start.6) | collective-permute-done | bytes 1048608 | tf_op jit(solution)/shard_map/ppermute | solution.py:584
  961.2 19.8 %collective-permute-done.8 = f32[2,32,4096]{2,1,0:T(8,128)S(1)} collective-permute-done((f32[2,32,4096]{2,1,0:T(8,128)S(1)}, f32[2,32,4096]{2,1,0:T(8,128)S(1)}, u32[]{:S(2)}, u32[]{:S(2)}) %collective-permute-start.8) | collective-permute-done | bytes 1048608 | tf_op jit(solution)/shard_map/ppermute | solution.py:584
  (54 shorter events, 94.8 us)
Async XLA Ops:
  0.0 3.6 copy-start.5
  5.5 46.0 %collective-permute-start.1 = (f32[4,32,4096]{2,1,0:T(8,128)S(1)}, f32[4,32,4096]{2,1,0:T(8,128)}, u32[]{:S(2)}, u32[]{:S(2)}) collective-permute-start(f32[4,32,4096]{2,1,0:T(8,128)S(1)} %pad_maximum_fusion.2), channel_id=1, source_target_pairs={{8,24},{9,25},{10,26},{11,27},{12,28},{13,29},{14,30},{15,31},{16,... | collective-permute-start | bytes 6291464 | tf_op jit(solution)/shard_map/ppermute | solution.py:584
  51.4 96.4 %collective-permute-start.2 = (f32[4,32,4096]{2,1,0:T(8,128)}, f32[4,32,4096]{2,1,0:T(8,128)}, u32[]{:S(2)}, u32[]{:S(2)}) collective-permute-start(f32[4,32,4096]{2,1,0:T(8,128)} %collective-permute-done.1), channel_id=1, source_target_pairs={{24,16},{25,17},{26,18},{27,19},{28,20},{29,21},{30,22},{31,23},{0... | collective-permute-start | bytes 6291464 | tf_op jit(solution)/shard_map/ppermute | solution.py:584
  52.7 7.6 copy-start.7
  54.2 96.8 %collective-permute-start = (f32[4,32,4096]{2,1,0:T(8,128)}, f32[4,32,4096]{2,1,0:T(8,128)}, u32[]{:S(2)}, u32[]{:S(2)}) collective-permute-start(f32[4,32,4096]{2,1,0:T(8,128)} %pad_maximum_fusion.1), channel_id=1, source_target_pairs={{8,0},{9,1},{10,2},{11,3},{12,4},{13,5},{14,6},{15,7},{0,16},{1,17... | collective-permute-start | bytes 6291464 | tf_op jit(solution)/shard_map/ppermute | solution.py:584
  171.9 64.1 %all-to-all-start.5 = ((f32[16,8,64,128]{3,2,1,0:T(8,128)}), f32[16,8,64,128]{3,2,1,0:T(8,128)}, u32[]{:S(2)}, u32[]{:S(2)}) async-start(f32[16,8,64,128]{3,2,1,0:T(8,128)} %get-tuple-element.31), calls=%async_computation.5 | async-start | bytes 8388608 | tf_op jit(solution)/shard_map/all_to_all | solution.py:568
  236.0 4.6 copy-start
  236.0 4.6 copy-start.6
  236.0 216.2 %all-to-all-start = ((f32[16,8,64,128]{3,2,1,0:T(8,128)}), f32[16,8,64,128]{3,2,1,0:T(8,128)}, u32[]{:S(2)}, u32[]{:S(2)}) async-start(f32[16,8,64,128]{3,2,1,0:T(8,128)} %get-tuple-element.22), calls=%async_computation | async-start | bytes 8388608 | tf_op jit(solution)/shard_map/all_to_all | solution.py:568
  242.2 88.8 %collective-permute-start.4 = (f32[4,32,4096]{2,1,0:T(8,128)S(1)}, f32[4,32,4096]{2,1,0:T(8,128)S(1)}, u32[]{:S(2)}, u32[]{:S(2)}) collective-permute-start(f32[4,32,4096]{2,1,0:T(8,128)S(1)} %get-tuple-element.24), channel_id=1, source_target_pairs={{8,24},{9,25},{10,26},{11,27},{12,28},{13,29},{14,30},{15,31},{16,... | collective-permute-start | bytes 6291464 | tf_op jit(solution)/shard_map/ppermute | solution.py:584
  331.0 98.7 %collective-permute-start.5 = (f32[4,32,4096]{2,1,0:T(8,128)S(1)}, f32[4,32,4096]{2,1,0:T(8,128)S(1)}, u32[]{:S(2)}, u32[]{:S(2)}) collective-permute-start(f32[4,32,4096]{2,1,0:T(8,128)S(1)} %collective-permute-done.4), channel_id=1, source_target_pairs={{24,16},{25,17},{26,18},{27,19},{28,20},{29,21},{30,22},{31,23},{0... | collective-permute-start | bytes 6291464 | tf_op jit(solution)/shard_map/ppermute | solution.py:584
  332.3 99.0 %collective-permute-start.3 = (f32[4,32,4096]{2,1,0:T(8,128)S(1)}, f32[4,32,4096]{2,1,0:T(8,128)}, u32[]{:S(2)}, u32[]{:S(2)}) collective-permute-start(f32[4,32,4096]{2,1,0:T(8,128)S(1)} %get-tuple-element.23), channel_id=1, source_target_pairs={{8,0},{9,1},{10,2},{11,3},{12,4},{13,5},{14,6},{15,7},{0,16},{1,17... | collective-permute-start | bytes 6291464 | tf_op jit(solution)/shard_map/ppermute | solution.py:584
  452.2 62.6 %all-to-all-start.1 = ((f32[16,8,64,128]{3,2,1,0:T(8,128)}), f32[16,8,64,128]{3,2,1,0:T(8,128)}, u32[]{:S(2)}, u32[]{:S(2)}) async-start(f32[16,8,64,128]{3,2,1,0:T(8,128)} %get-tuple-element.26), calls=%async_computation.1 | async-start | bytes 8388608 | tf_op jit(solution)/shard_map/all_to_all | solution.py:568
  514.8 59.9 %all-to-all-start.6 = ((f32[16,8,64,128]{3,2,1,0:T(8,128)}), f32[16,8,64,128]{3,2,1,0:T(8,128)}, u32[]{:S(2)}, u32[]{:S(2)}) async-start(f32[16,8,64,128]{3,2,1,0:T(8,128)} %get-tuple-element.32), calls=%async_computation.6 | async-start | bytes 8388608 | tf_op jit(solution)/shard_map/all_to_all | solution.py:568
  574.7 60.0 %all-to-all-start.2 = ((f32[16,4,128,128]{3,2,1,0:T(8,128)}), f32[16,4,128,128]{3,2,1,0:T(8,128)}, u32[]{:S(2)}, u32[]{:S(2)}) async-start(f32[16,4,128,128]{3,2,1,0:T(8,128)} %get-tuple-element.27), calls=%async_computation.2 | async-start | bytes 8388608 | tf_op jit(solution)/shard_map/all_to_all | solution.py:568
  634.6 60.0 %all-to-all-start.7 = ((f32[16,4,128,128]{3,2,1,0:T(8,128)}), f32[16,4,128,128]{3,2,1,0:T(8,128)}, u32[]{:S(2)}, u32[]{:S(2)}) async-start(f32[16,4,128,128]{3,2,1,0:T(8,128)} %get-tuple-element.33), calls=%async_computation.7 | async-start | bytes 8388608 | tf_op jit(solution)/shard_map/all_to_all | solution.py:568
  694.6 31.8 %all-to-all-start.3 = ((f32[16,2,128,128]{3,2,1,0:T(8,128)}), f32[16,2,128,128]{3,2,1,0:T(8,128)S(1)}, u32[]{:S(2)}, u32[]{:S(2)}) async-start(f32[16,2,128,128]{3,2,1,0:T(8,128)} %shard_map.85), calls=%async_computation.3 | async-start | bytes 4194304 | tf_op jit(solution)/shard_map/all_to_all | solution.py:568
  726.4 1.3 copy-start.4
  727.8 31.8 %all-to-all-start.8 = ((f32[16,2,128,128]{3,2,1,0:T(8,128)}), f32[16,2,128,128]{3,2,1,0:T(8,128)S(1)}, u32[]{:S(2)}, u32[]{:S(2)}) async-start(f32[16,2,128,128]{3,2,1,0:T(8,128)} %shard_map.90), calls=%async_computation.8 | async-start | bytes 4194304 | tf_op jit(solution)/shard_map/all_to_all | solution.py:568
  759.6 1.3 copy-start.3
  760.9 31.8 %all-to-all-start.4 = ((f32[16,4,64,128]{3,2,1,0:T(8,128)}), f32[16,4,64,128]{3,2,1,0:T(8,128)S(1)}, u32[]{:S(2)}, u32[]{:S(2)}) async-start(f32[16,4,64,128]{3,2,1,0:T(8,128)} %get-tuple-element.29), calls=%async_computation.4 | async-start | bytes 4194304 | tf_op jit(solution)/shard_map/all_to_all | solution.py:568
  792.8 52.0 %copy-start.2 = (f32[16,4,64,128]{3,2,1,0:T(8,128)}, f32[16,4,64,128]{3,2,1,0:T(8,128)S(1)}, u32[]{:S(2)}) copy-start(f32[16,4,64,128]{3,2,1,0:T(8,128)S(1)} %all-to-all-done.4.back) | copy-start | bytes 6291460
  844.8 64.3 %all-to-all-start.10 = ((f32[16,4,64,128]{3,2,1,0:T(8,128)}), f32[16,4,64,128]{3,2,1,0:T(8,128)S(1)}, u32[]{:S(2)}, u32[]{:S(2)}) async-start(f32[16,4,64,128]{3,2,1,0:T(8,128)} %get-tuple-element.36), calls=%async_computation.10 | async-start | bytes 4194304 | tf_op jit(solution)/shard_map/all_to_all | solution.py:568
  888.1 70.6 %collective-permute-start.6 = (f32[2,32,4096]{2,1,0:T(8,128)}, f32[2,32,4096]{2,1,0:T(8,128)}, u32[]{:S(2)}, u32[]{:S(2)}) collective-permute-start(f32[2,32,4096]{2,1,0:T(8,128)} %get-tuple-element.53), channel_id=1, source_target_pairs={{0,8},{1,9},{2,10},{3,11},{4,12},{5,13},{6,14},{7,15},{16,0},{17,1... | collective-permute-start | bytes 3145736 | tf_op jit(solution)/shard_map/ppermute | solution.py:584
  888.2 73.0 %collective-permute-start.7 = (f32[2,32,4096]{2,1,0:T(8,128)S(1)}, f32[2,32,4096]{2,1,0:T(8,128)}, u32[]{:S(2)}, u32[]{:S(2)}) collective-permute-start(f32[2,32,4096]{2,1,0:T(8,128)S(1)} %get-tuple-element.54), channel_id=1, source_target_pairs={{16,8},{17,9},{18,10},{19,11},{20,12},{21,13},{22,14},{23,15},{8,1... | collective-permute-start | bytes 3145736 | tf_op jit(solution)/shard_map/ppermute | solution.py:584
  909.1 1.3 copy-start.1
  930.1 50.9 %collective-permute-start.8 = (f32[2,32,4096]{2,1,0:T(8,128)S(1)}, f32[2,32,4096]{2,1,0:T(8,128)S(1)}, u32[]{:S(2)}, u32[]{:S(2)}) collective-permute-start(f32[2,32,4096]{2,1,0:T(8,128)S(1)} %get-tuple-element.55), channel_id=1, source_target_pairs={{0,8},{1,9},{2,10},{3,11},{4,12},{5,13},{6,14},{7,15},{16,0},{17,1... | collective-permute-start | bytes 3145736 | tf_op jit(solution)/shard_map/ppermute | solution.py:584
  930.2 53.4 %collective-permute-start.9 = (f32[2,32,4096]{2,1,0:T(8,128)S(1)}, f32[2,32,4096]{2,1,0:T(8,128)S(1)}, u32[]{:S(2)}, u32[]{:S(2)}) collective-permute-start(f32[2,32,4096]{2,1,0:T(8,128)S(1)} %get-tuple-element.56), channel_id=1, source_target_pairs={{16,8},{17,9},{18,10},{19,11},{20,12},{21,13},{22,14},{23,15},{8,1... | collective-permute-start | bytes 3145736 | tf_op jit(solution)/shard_map/ppermute | solution.py:584

commit v4 on v3

--- a/solution.py
+++ b/solution.py
@@ -19,9 +19,8 @@
 SLOTS = 2
 STRIP = 16
 LANES = 128
-QUARTER = XB // 4
+CHUNKS = 4
 HALF = XA // 2
-MEMBERS = [(g % 2, (g // 2 % 2) * 4 + (g // 4 % 2) * 2 + g // 8) for g in range(XA)]
 
 
 PRECISE = lax.Precision.HIGHEST
@@ -180,22 +179,21 @@
     lax.fori_loop(0, XA, step, 0)
 
 
-def enter_kernel(pieces, index, *refs):
-    whi, wlo, mhi, mlo, out, t0, shi, slo, field, xhi, xlo, y = refs[pieces:]
-    rows = sum(piece.shape[1] for piece in refs[:pieces])
+def enter_kernel(place, index, own, other, whi, wlo, mhi, mlo, out, t0, shi, slo, field, xhi, xlo, y):
+    half = own.shape[1]
+    rows = 2 * half
 
     for number in range(4):
-        first = number * rows
-        for piece in refs[:pieces]:
-
-            def cut(row, first=first, piece=piece, channel=number):
-                high, low = halves(piece[channel, pl.ds(row, STRIP), :])
-                at = pl.ds(pl.multiple_of(first + row, STRIP), STRIP)
+        for piece, side in ((own, place[0]), (other, 1 - place[0])):
+
+            def cut(row, number=number, piece=piece, side=side):
+                high, low = halves(piece[number, pl.ds(row, STRIP), :])
+                first = number * rows + side * half + row
+                at = pl.ds(pl.multiple_of(first, STRIP), STRIP)
                 shi[at, :] = high
                 slo[at, :] = low
 
-            strips(piece.shape[1], cut)
-            first += piece.shape[1]
+            strips(half, cut)
 
     def rotated(b):
         at = [pl.ds(pl.multiple_of(index[b, s] * BLK, BLK), BLK) for s in range(SLOTS)]
@@ -248,72 +246,67 @@
     lax.fori_loop(0, XA, second_slice, 0)
 
 
-def row_places():
-    moved = [MEMBERS.index((1 - p // HALF, p % HALF)) for p in range(XA)]
-    kept = [MEMBERS.index((p // HALF, p % HALF)) for p in range(XA)]
-    return [(i * QUARTER, kept if i % 2 else moved) for i in range(XB // QUARTER)]
-
-
-def by_quarters(rows, step):
-    for first, places in row_places():
-        c, within = first // rows, first % rows
-
-        def inner(row, first=first, c=c, within=within, places=places):
-            local = pl.ds(pl.multiple_of(within + row, STRIP), STRIP)
-            step(pl.multiple_of(first + row, STRIP), c, local, places)
-
-        strips(QUARTER, inner)
+def by_pieces(split, step):
+    half = XB // CHUNKS // 2
+    rows = XB // split
+    for c in range(CHUNKS):
+        for x in range(2):
+
+            def inner(row, c=c, x=x):
+                places = []
+                for p in range(XA):
+                    first = 2 * c * half + p // HALF * half
+                    at = pl.ds(pl.multiple_of(first % rows + row, STRIP), STRIP)
+                    places.append((first // rows, x * HALF + p % HALF, at))
+                step(pl.multiple_of((2 * c + x) * half + row, STRIP), places)
+
+            strips(half, inner)
 
 
 def middle_kernel(chunks, *refs):
     arrived = refs[:chunks]
     mhi, mlo, out, kept, xhi, xlo, y = refs[chunks:]
-    rows = XB // chunks
-
-    def forward(row, c, local, places):
+
+    def forward(row, places):
         for number in range(2):
-            columns_out(
-                xhi,
-                xlo,
-                number,
-                row,
-                [tuple(arrived[c][g, 2 * number + i, local, :] for i in range(2)) for g in places],
-            )
-
-    by_quarters(rows, forward)
+            values = [
+                tuple(arrived[c][g, 2 * number + i, at, :] for i in range(2)) for c, g, at in places
+            ]
+            columns_out(xhi, xlo, number, row, values)
+
+    by_pieces(chunks, forward)
     columns_mix(xhi, xlo, mhi, mlo, y)
 
-    def turn(row, c, local, places):
-        at = pl.ds(row, STRIP)
+    def turn(row, places):
+        local = pl.ds(row, STRIP)
         wave = columns_in(y, 0, row)
         product = []
-        for g, value in zip(places, wave):
-            t = arrived[c][g, 4, local, :], arrived[c][g, 5, local, :]
-            value = times(t, value)
+        for p, (c, g, at) in enumerate(places):
+            t = arrived[c][g, 4, at, :], arrived[c][g, 5, at, :]
+            value = times(t, wave[p])
             for i, part in enumerate(value + t):
-                kept[g, i, at, :] = part
+                kept[p, i, local, :] = part
             product.append(value)
         columns_out(xhi, xlo, 0, row, product)
         dwave = columns_in(y, 1, row)
         change = []
-        for g, value in zip(places, dwave):
-            t_re, t_im, d_re, d_im = (arrived[c][g, 4 + i, local, :] for i in range(4))
-            p_re, p_im = kept[g, 0, at, :], kept[g, 1, at, :]
-            re, im = times((t_re, t_im), value)
+        for p, (c, g, at) in enumerate(places):
+            t_re, t_im, d_re, d_im = (arrived[c][g, 4 + i, at, :] for i in range(4))
+            p_re, p_im = kept[p, 0, local, :], kept[p, 1, local, :]
+            re, im = times((t_re, t_im), dwave[p])
             change.append((re - (d_re * p_im + d_im * p_re), im + (d_re * p_re - d_im * p_im)))
         columns_out(xhi, xlo, 1, row, change)
 
-    by_quarters(rows, turn)
+    by_pieces(chunks, turn)
     columns_mix(xhi, xlo, mhi, mlo, y)
 
-    def backward(row, c, local, places):
-        at = pl.ds(row, STRIP)
+    def backward(row, places):
         for number in range(2):
-            for g, (re, im) in zip(places, columns_in(y, number, row)):
+            for (_, g, at), (re, im) in zip(places, columns_in(y, number, row)):
                 out[g, 2 * number, at, :] = re
                 out[g, 2 * number + 1, at, :] = im
 
-    by_quarters(rows, backward)
+    by_pieces(1, backward)
 
 
 def detector_kernel(fields, mhi, mlo, out, xhi, xlo, y):
@@ -361,70 +354,80 @@
 
 def return_kernel(chunks, back, kept, mhi, mlo, *refs):
     out, (xhi, xlo, y) = refs[:chunks], refs[chunks:]
-    rows = XB // chunks
-
-    def forward(row, c, local, places):
-        at = pl.ds(row, STRIP)
-        columns_out(xhi, xlo, 0, row, [(back[g, 0, at, :], back[g, 1, at, :]) for g in places])
-
-    by_quarters(rows, forward)
+
+    def forward(row, places):
+        values = [(back[g, 0, at, :], back[g, 1, at, :]) for _, g, at in places]
+        columns_out(xhi, xlo, 0, row, values)
+
+    by_pieces(1, forward)
     columns_mix(xhi, xlo, mhi, mlo, y)
 
-    def turn(row, c, local, places):
-        at = pl.ds(row, STRIP)
+    def turn(row, places):
+        local = pl.ds(row, STRIP)
         pulled = columns_in(y, 0, row)
         following = []
-        for g, value in zip(places, pulled):
-            re, im = times((kept[g, 0, at, :], kept[g, 1, at, :]), value)
-            out[c][g, 0, local, :] = -im
-            out[c][g, 1, local, :] = -re
-            following.append(times((kept[g, 2, at, :], kept[g, 3, at, :]), value))
+        for p, (c, g, at) in enumerate(places):
+            re, im = times((kept[p, 0, local, :], kept[p, 1, local, :]), pulled[p])
+            out[c][g, 0, at, :] = -im
+            out[c][g, 1, at, :] = -re
+            following.append(times((kept[p, 2, local, :], kept[p, 3, local, :]), pulled[p]))
         columns_out(xhi, xlo, 0, row, following)
 
-    by_quarters(rows, turn)
+    by_pieces(chunks, turn)
     columns_mix(xhi, xlo, mhi, mlo, y)
 
-    def backward(row, c, local, places):
-        for g, (re, im) in zip(places, columns_in(y, 0, row)):
-            out[c][g, 2, local, :] = re
-            out[c][g, 3, local, :] = im
-
-    by_quarters(rows, backward)
-
-
-def leave_kernel(first, index, back, t0, whi, wlo, mhi, mlo, *refs):
-    before, (out, shi, slo, xhi, xlo, y) = refs[:-6], refs[-6:]
-    rows = t0.shape[2]
-
-    def forward(row):
-        at = pl.ds(pl.multiple_of(first + row, STRIP), STRIP)
-        rows_out(xhi, xlo, row, [(back[b, 2, at, :], back[b, 3, at, :]) for b in range(XA)])
+    def backward(row, places):
+        for (c, g, at), (re, im) in zip(places, columns_in(y, 0, row)):
+            out[c][g, 2, at, :] = re
+            out[c][g, 3, at, :] = im
+
+    by_pieces(chunks, backward)
+
+
+def leave_kernel(pieces, first, place, index, back, whi, wlo, mhi, mlo, *refs):
+    t0 = refs[:pieces]
+    before, (near, far, shi, slo, xhi, xlo, y) = refs[pieces:-7], refs[-7:]
+    chunk = t0[0].shape[2]
+    half = chunk // 2
+    rows = pieces * chunk
+
+    def pieces_of(step):
+        for end, side in enumerate((1 - place[1], place[1])):
+            for c in range(pieces):
+
+                def inner(row, end=end, side=side, c=c):
+                    within = pl.multiple_of(side * half + row, STRIP)
+                    source = pl.multiple_of(first + c * chunk + side * half + row, STRIP)
+                    target = pl.multiple_of((end * pieces + c) * half + row, STRIP)
+                    step(c, pl.ds(within, STRIP), pl.ds(source, STRIP), target)
+
+                strips(half, inner)
+
+    def store(b, i, target, value):
+        high, low = halves(value)
+        at = pl.ds(pl.multiple_of(i * rows + target, STRIP), STRIP)
+        shi[b, at, :] = high
+        slo[b, at, :] = low
+
+    def forward(c, within, at, target):
+        rows_out(xhi, xlo, target, [(back[b, 2, at, :], back[b, 3, at, :]) for b in range(XA)])
         for b in range(XA):
             for i in range(2):
-                high, low = halves(back[b, i, at, :])
-                place = pl.ds(pl.multiple_of(i * rows + row, STRIP), STRIP)
-                shi[XA + b, place, :] = high
-                slo[XA + b, place, :] = low
-
-    strips(rows, forward)
+                store(XA + b, i, target, back[b, i, at, :])
+
+    pieces_of(forward)
     rows_mix(xhi, xlo, mhi, mlo, y)
 
-    def turn(row):
-        at = pl.ds(row, STRIP)
-        for b, value in enumerate(rows_in(y, row)):
-            re, im = times((t0[b, 0, at, :], t0[b, 1, at, :]), value)
-            for i, part in enumerate((-im, -re)):
-                high, low = halves(part)
-                place = pl.ds(pl.multiple_of(i * rows + row, STRIP), STRIP)
-                shi[b, place, :] = high
-                slo[b, place, :] = low
-
-    strips(rows, turn)
-
-    if before:
-        out[...] = before[0][...]
-    else:
-        out[...] = jnp.zeros(out.shape, jnp.float32)
+    def turn(c, within, at, target):
+        for b, value in enumerate(rows_in(y, target)):
+            re, im = times((t0[c][b, 0, within, :], t0[c][b, 1, within, :]), value)
+            store(b, 0, target, -im)
+            store(b, 1, target, -re)
+
+    pieces_of(turn)
+
+    for out, old in zip((near, far), before or (None, None)):
+        out[...] = jnp.zeros(out.shape, jnp.float32) if old is None else old[...]
 
     def across(a, b):
         return lax.dot_general(
@@ -437,7 +440,10 @@
         for s in range(SLOTS):
             at = pl.ds(pl.multiple_of(index[b, s] * BLK, BLK), BLK)
             for i in range(2):
-                out[i, :, at] += values[i * rows : (i + 1) * rows, s * BLK : (s + 1) * BLK]
+                for end, out in enumerate((near, far)):
+                    start = i * rows + end * (rows // 2)
+                    part = values[start : start + rows // 2, s * BLK : (s + 1) * BLK]
+                    out[i, :, at] += part
         return carry
 
     lax.fori_loop(0, NB, step, 0)
@@ -472,8 +478,8 @@
     ]
 
 
-def enter(index, pieces, weights, matrices):
-    rows = sum(piece.shape[1] for piece in pieces)
+def enter(place, index, own, other, weights, matrices):
+    rows = 2 * own.shape[1]
     scratch = [
         pltpu.VMEM((4 * rows, NB * BLK), jnp.bfloat16),
         pltpu.VMEM((4 * rows, NB * BLK), jnp.bfloat16),
@@ -482,13 +488,15 @@
     outs = [(XA, 8, rows, LANES), (XA, 2, rows, LANES)]
     extra = NB * 4 * rows * 256 * 128 * 6
     return call(
-        functools.partial(enter_kernel, len(pieces)),
+        enter_kernel,
         outs,
         scratch,
         rows / XB * 2,
         extra,
+        place,
         index,
-        *pieces,
+        own,
+        other,
         *weights,
         *matrices,
     )
@@ -532,26 +540,27 @@
     )
 
 
-def leave(index, back, first, t0, weights, matrices, before):
-    rows = t0.shape[2]
+def leave(place, index, back, first, t0, weights, matrices, before):
+    rows = sum(t.shape[2] for t in t0)
     scratch = [
         pltpu.VMEM((NB, 2 * rows, LANES), jnp.bfloat16),
         pltpu.VMEM((NB, 2 * rows, LANES), jnp.bfloat16),
     ] + mix_scratch(rows, 2 * LANES)
     extra = NB * 2 * rows * 256 * 128 * 6
     return call(
-        functools.partial(leave_kernel, first),
-        [(2, rows, NB * BLK)],
+        functools.partial(leave_kernel, len(t0), first),
+        [(2, rows // 2, NB * BLK)] * 2,
         scratch,
         rows / XB,
         extra,
+        place,
         index,
         back,
-        t0,
         *weights,
         *matrices,
+        *t0,
         *before,
-    )[0]
+    )
 
 
 def split_weights(block_weights):
@@ -570,56 +579,62 @@
         ("parts", "fft"),
         split_axis=0,
         concat_axis=0,
-        axis_index_groups=[[device(x, b, r) for x, r in MEMBERS] for b in range(2)],
+        axis_index_groups=[[device(x, b, r) for x in range(2) for r in range(HALF)] for b in range(2)],
         tiled=True,
     )
 
 
-def permute(values, steps, back=False):
+def permute(values, steps):
     pairs = [
         (device(*here, r), device(*there, r)) for here, there in steps for r in range(HALF)
     ]
-    if back:
-        pairs = [(there, here) for here, there in pairs]
     return lax.ppermute(values, ("parts", "fft"), pairs)
 
 
-CYCLE = [((0, 1), (0, 0)), ((0, 0), (1, 0)), ((1, 0), (1, 1)), ((1, 1), (0, 1))]
-ASIDE = [((0, 1), (1, 1)), ((1, 0), (0, 0))]
-ALONG = [((1, 1), (1, 0)), ((0, 0), (0, 1))]
-SWAP = [((0, 1), (1, 0)), ((1, 0), (0, 1)), ((0, 0), (0, 0)), ((1, 1), (1, 1))]
+BESIDE = [((q, b), (1 - q, b)) for q in range(2) for b in range(2)]
+ALONG = [((q, b), (q, 1 - b)) for q in range(2) for b in range(2)]
+CYCLE = [((0, 0), (0, 1)), ((1, 0), (0, 0)), ((1, 1), (1, 0)), ((0, 1), (1, 1))]
+ACROSS = [((0, 1), (1, 0)), ((1, 0), (0, 1))]
 
 
 def after(values, others):
     return lax.optimization_barrier((values, others))[0]
 
 
-def arrive(potential, direction):
-    settled = lax.axis_index("parts") == lax.axis_index("fft") // HALF
-    quarters = [
-        jnp.concatenate([v[:, i * QUARTER : (i + 1) * QUARTER] for v in (potential, direction)])
-        for i in range(XB // QUARTER)
-    ]
+def arrive(potential, direction, q, b):
+    half = XB // CHUNKS // 2
     chunks = []
-    moved = aside = other = ()
-    for i in range(0, len(quarters), 2):
-        first, second = quarters[i : i + 2]
-        moved = permute(after(first, moved), CYCLE)
-        aside = permute(after(second, aside), ASIDE)
-        other = permute(after(aside, other), ALONG)
-        chunks.append([moved, jnp.where(settled, second, other)])
+    beside = along = ()
+    for c in range(CHUNKS):
+        lower, upper = (
+            jnp.concatenate(
+                [v[:, (2 * c + x) * half : (2 * c + x + 1) * half] for v in (potential, direction)]
+            )
+            for x in range(2)
+        )
+        keep = jnp.where(q == 0, lower, upper)
+        give = jnp.where(q == 0, upper, lower)
+        beside = permute(after(give, beside), BESIDE)
+        own = jnp.where(q == b, keep, beside)
+        give = jnp.where(q == b, beside, keep)
+        along = permute(after(give, along), ALONG)
+        chunks.append((own, along, beside))
     return chunks
 
 
-def depart(values):
-    return [
-        permute(values[:, :QUARTER], CYCLE, True),
-        permute(values[:, QUARTER:], SWAP, True),
-    ]
+def depart(near, far, q, b):
+    once = permute(near, CYCLE)
+    twice = permute(far, ACROSS)
+    same = jnp.where(q == b, far, once)
+    rest = jnp.where(q == b, once, twice)
+    return jnp.where(q == 0, same, rest), jnp.where(q == 0, rest, same)
 
 
 def blocked_body(potential, direction, block_index, block_weights):
-    chunks = arrive(potential, direction)
+    q = lax.axis_index("parts")
+    b = lax.axis_index("fft") // HALF
+    place = jnp.stack([b, q]).astype(jnp.int32)
+    chunks = arrive(potential, direction, q, b)
     whi, wlo = split_weights(block_weights)
     by_column = column_constants()
     column = tuple(jnp.asarray(v) for v in split_constant(by_column))
@@ -627,9 +642,11 @@
     weights = [(whi[a], wlo[a]) for a in range(ANGLES)]
     arrived = [[] for _ in range(ANGLES)]
     ahead = [[] for _ in range(ANGLES)]
-    for pieces in chunks:
+    for c, (own, along, _) in enumerate(chunks):
         for a in range(ANGLES):
-            fields, t0 = enter(block_index[a], pieces, weights[a], row)
+            if c + 1 < CHUNKS:
+                own = after(own, chunks[c + 1][1 if a else 2])
+            fields, t0 = enter(place, block_index[a], own, along, weights[a], row)
             arrived[a].append(exchange(fields))
             ahead[a].append(t0)
     carried = []
@@ -637,18 +654,27 @@
         out, kept = middle(arrived[a], column)
         carried.append((exchange(out), kept))
     backs = [exchange(detector(out, row)) for out, _ in carried]
-    count = len(chunks)
-    totals = [()] * count
+    ends = 2
+    span = CHUNKS // ends
+    totals = [()] * ends
     for a in range(ANGLES):
         last = a == ANGLES - 1
-        pulled = pull(backs[a], carried[a][1], column, count if last else 1)
-        pulled = [exchange(v) for v in pulled]
-        for c in range(count):
-            back, first = (pulled[c], 0) if last else (pulled[0], c * (XB // count))
-            totals[c] = (
-                leave(block_index[a], back, first, ahead[a][c], weights[a], row, totals[c]),
-            )
-    return jnp.concatenate([v for total in totals for v in depart(total[0])], axis=1)
+        pulled = pull(backs[a], carried[a][1], column, ends if last else 1)
+        if last:
+            pulled = [exchange(pulled[0]), exchange(after(pulled[1], totals))]
+        else:
+            pulled = [exchange(pulled[0])]
+        for e in range(ends):
+            back, first = (pulled[e], 0) if last else (pulled[0], e * (XB // ends))
+            t0 = ahead[a][e * span : (e + 1) * span]
+            totals[e] = leave(place, block_index[a], back, first, t0, weights[a], row, totals[e])
+    pieces = []
+    half = XB // CHUNKS // 2
+    for total in totals:
+        lower, upper = depart(*total, q, b)
+        for c in range(span):
+            pieces += [v[:, c * half : (c + 1) * half] for v in (lower, upper)]
+    return jnp.concatenate(pieces, axis=1)
 
 
 def transform_table(count_in, count_out, length, orient):

time: 989 us -> 921 us (0.931)
  waiting for transfers between devices: 557 us -> 424 us
  blocking collectives: 52 us -> 0 us
  starting transfers between devices: 74.3 us -> 119 us
  Pallas kernels: 268 us -> 309 us
  other arithmetic: 17.7 us -> 30.6 us
    ppermute x10 -> x12, waiting for transfers between devices: 348 us -> 240 us  [permute(): return lax.ppermute(values, ('parts', 'fft'), pairs)]
    all_to_all x10 -> x15, starting transfers between devices: 47.2 us -> 100 us  [exchange(): lax.all_to_all(values, ('parts', 'fft'), split_axis=0, concat_axis=0, axi...]
    all_to_all x1 -> x0, blocking collectives: 52 us -> none  [exchange(): lax.all_to_all(values, ('parts', 'fft'), split_axis=0, concat_axis=0, axi...]
    pallas_call x14 -> x18, Pallas kernels: 268 us -> 309 us  [call(): pl.pallas_call(kernel, out_shape=[jax.ShapeDtypeStruct(o, jnp.float32) fo...]
    all_to_all x10 -> x15, waiting for transfers between devices: 209 us -> 184 us  [exchange(): lax.all_to_all(values, ('parts', 'fft'), split_axis=0, concat_axis=0, axi...]
    select_n x2 -> x9, other arithmetic: 4.82 us -> 20.7 us  [the longest x3 8.8 us: arrive(): own = jnp.where(q == b, keep, beside)]
    ppermute x10 -> x12, starting transfers between devices: 27.1 us -> 19 us  [permute(): return lax.ppermute(values, ('parts', 'fft'), pairs)]
  transfers between devices with their start and end apart: 20 -> 27, of which waited for: 16 -> 23; matrix products, arithmetic and copies ran while one was open for 2% -> 4% of each run, Pallas kernels for 25% -> 32%
where the time goes in v4:
time: 921 us; the launch traced here: 911 us
  waiting for transfers between devices  424 us (46%)
  Pallas kernels  309 us (34%)
  starting transfers between devices  119 us (13%)
  other arithmetic  30.6 us (3%)
  local copies, waits for them, and re-layouts  27.1 us (3%)
    pallas_call x18, Pallas kernels, call(): pl.pallas_call(kernel, out_shape=[jax.ShapeDtypeStruct(o, jnp.float32) fo...  309 us
    ppermute x12, waiting for transfers between devices, permute(): return lax.ppermute(values, ('parts', 'fft'), pairs)  240 us
    all_to_all x15, waiting for transfers between devices, exchange(): lax.all_to_all(values, ('parts', 'fft'), split_axis=0, concat_axis=0, axi...  184 us
    all_to_all x15, starting transfers between devices, exchange(): lax.all_to_all(values, ('parts', 'fft'), split_axis=0, concat_axis=0, axi...  100 us
    ppermute x12, starting transfers between devices, permute(): return lax.ppermute(values, ('parts', 'fft'), pairs)  19 us
  transfers between devices with their start and end apart: 27, of which 23 were waited for; matrix products, arithmetic and copies ran while one was open for 4% of the time, Pallas kernels for 32%

profile of v4, /device:TPU:3, one launch (start us, length us, event | category | flops | bytes accessed | tf_op | source)
XLA Modules:
  0.0 910.7 jit_solution(12608499384183494472)
XLA Ops:
  19.2 13.9 %collective-permute-done = f32[4,16,4096]{2,1,0:T(8,128)} collective-permute-done((f32[4,16,4096]{2,1,0:T(8,128)}, f32[4,16,4096]{2,1,0:T(8,128)}, u32[]{:S(2)}, u32[]{:S(2)}) %collective-permute-start) | collective-permute-done | bytes 1048608 | tf_op jit(solution)/shard_map/ppermute | solution.py:591
  56.5 27.5 %collective-permute-done.2.other = f32[4,16,4096]{2,1,0:T(8,128)S(1)} collective-permute-done((f32[4,16,4096]{2,1,0:T(8,128)}, f32[4,16,4096]{2,1,0:T(8,128)S(1)}, u32[]{:S(2)}, u32[]{:S(2)}) %collective-permute-start.2) | collective-permute-done | bytes 1048608 | tf_op jit(solution)/shard_map/ppermute | solution.py:591
  84.9 16.3 %shard_map.89 = (f32[16,8,32,128]{3,2,1,0:T(8,128)}, f32[16,2,32,128]{3,2,1,0:T(8,128)}) custom-call(s32[2]{0:T(128)} %pad_add_fusion.place, s32[32,2]{1,0:T(8,128)} %copy.17.index, f32[4,16,4096]{2,1,0:T(8,128)} %get-tuple-element.51.own, f32[4,16,4096]{2,1,0:T(8,128)} %copy-done.18, bf16[32,256,128]{2,1,0:T(8,128)(2,1)} %get-tuple-element.95.whi, ...), custom_call_target="tpu_custom_call" | custom-call | flops 1207959552 | bytes 13107464 | tf_op jit(solution)/shard_map/pallas_call | solution.py:458
  114.7 38.9 %collective-permute-done.4 = f32[4,16,4096]{2,1,0:T(8,128)S(1)} collective-permute-done((f32[4,16,4096]{2,1,0:T(8,128)S(1)}, f32[4,16,4096]{2,1,0:T(8,128)S(1)}, u32[]{:S(2)}, u32[]{:S(2)}) %collective-permute-start.4) | collective-permute-done | bytes 1048608 | tf_op jit(solution)/shard_map/ppermute | solution.py:591
  160.2 16.3 %shard_map.90 = (f32[16,8,32,128]{3,2,1,0:T(8,128)}, f32[16,2,32,128]{3,2,1,0:T(8,128)}) custom-call(s32[2]{0:T(128)} %pad_add_fusion.place, s32[32,2]{1,0:T(8,128)} %copy.17.index, f32[4,16,4096]{2,1,0:T(8,128)} %get-tuple-element.56.own, f32[4,16,4096]{2,1,0:T(8,128)} %collective-permute-done.3.other, bf16[32,256,128]{2,1,0:T(8,128)(2,1)} %get-tuple-element.95.whi, ...), custom_call_target="tpu_custom_call" | custom-call | flops 1207959552 | bytes 13107464 | tf_op jit(solution)/shard_map/pallas_call | solution.py:458
  183.9 16.3 %shard_map.82 = (f32[16,8,32,128]{3,2,1,0:T(8,128)}, f32[16,2,32,128]{3,2,1,0:T(8,128)}) custom-call(s32[2]{0:T(128)} %pad_add_fusion.place, s32[32,2]{1,0:T(8,128)} %copy.18.index, f32[4,16,4096]{2,1,0:T(8,128)} %get-tuple-element.51.own, f32[4,16,4096]{2,1,0:T(8,128)} %copy-done.18, bf16[32,256,128]{2,1,0:T(8,128)(2,1)} %get-tuple-element.96.whi, ...), custom_call_target="tpu_custom_call" | custom-call | flops 1207959552 | bytes 13107464 | tf_op jit(solution)/shard_map/pallas_call | solution.py:458
  222.2 40.0 %collective-permute-done.6 = f32[4,16,4096]{2,1,0:T(8,128)S(1)} collective-permute-done((f32[4,16,4096]{2,1,0:T(8,128)S(1)}, f32[4,16,4096]{2,1,0:T(8,128)S(1)}, u32[]{:S(2)}, u32[]{:S(2)}) %collective-permute-start.6) | collective-permute-done | bytes 1048608 | tf_op jit(solution)/shard_map/ppermute | solution.py:591
  268.2 16.3 %shard_map.91 = (f32[16,8,32,128]{3,2,1,0:T(8,128)}, f32[16,2,32,128]{3,2,1,0:T(8,128)}) custom-call(s32[2]{0:T(128)} %pad_add_fusion.place, s32[32,2]{1,0:T(8,128)} %copy.17.index, f32[4,16,4096]{2,1,0:T(8,128)} %get-tuple-element.61.own, f32[4,16,4096]{2,1,0:T(8,128)} %collective-permute-done.5.other, bf16[32,256,128]{2,1,0:T(8,128)(2,1)} %get-tuple-element.95.whi, ...), custom_call_target="tpu_custom_call" | custom-call | flops 1207959552 | bytes 13107464 | tf_op jit(solution)/shard_map/pallas_call | solution.py:458
  291.3 16.3 %shard_map.83 = (f32[16,8,32,128]{3,2,1,0:T(8,128)}, f32[16,2,32,128]{3,2,1,0:T(8,128)}) custom-call(s32[2]{0:T(128)} %pad_add_fusion.place, s32[32,2]{1,0:T(8,128)} %copy.18.index, f32[4,16,4096]{2,1,0:T(8,128)} %get-tuple-element.56.own, f32[4,16,4096]{2,1,0:T(8,128)} %collective-permute-done.3.other, bf16[32,256,128]{2,1,0:T(8,128)(2,1)} %get-tuple-element.96.whi, ...), custom_call_target="tpu_custom_call" | custom-call | flops 1207959552 | bytes 13107464 | tf_op jit(solution)/shard_map/pallas_call | solution.py:458
  307.6 10.3 %all-to-all-done.9.refs_2_ = f32[16,8,32,128]{3,2,1,0:T(8,128)} async-done(((f32[16,8,32,128]{3,2,1,0:T(8,128)}), f32[16,8,32,128]{3,2,1,0:T(8,128)}, u32[]{:S(2)}, u32[]{:S(2)}) %all-to-all-start.9) | async-done | bytes 2097184 | tf_op jit(solution)/shard_map/all_to_all | solution.py:577
  328.3 43.1 %collective-permute-done.7.other = f32[4,16,4096]{2,1,0:T(8,128)S(1)} collective-permute-done((f32[4,16,4096]{2,1,0:T(8,128)S(1)}, f32[4,16,4096]{2,1,0:T(8,128)S(1)}, u32[]{:S(2)}, u32[]{:S(2)}) %collective-permute-start.7) | collective-permute-done | bytes 1048608 | tf_op jit(solution)/shard_map/ppermute | solution.py:591
  372.4 16.3 %shard_map.92 = (f32[16,8,32,128]{3,2,1,0:T(8,128)}, f32[16,2,32,128]{3,2,1,0:T(8,128)}) custom-call(s32[2]{0:T(128)} %pad_add_fusion.place, s32[32,2]{1,0:T(8,128)} %copy.17.index, f32[4,16,4096]{2,1,0:T(8,128)} %get-tuple-element.117.own, f32[4,16,4096]{2,1,0:T(8,128)} %copy-done.19, bf16[32,256,128]{2,1,0:T(8,128)(2,1)} %get-tuple-element.95.whi, ...), custom_call_target="tpu_custom_call" | custom-call | flops 1207959552 | bytes 13107464 | tf_op jit(solution)/shard_map/pallas_call | solution.py:458
  397.6 16.3 %shard_map.85 = (f32[16,8,32,128]{3,2,1,0:T(8,128)}, f32[16,2,32,128]{3,2,1,0:T(8,128)}) custom-call(s32[2]{0:T(128)} %pad_add_fusion.place, s32[32,2]{1,0:T(8,128)} %copy.18.index, f32[4,16,4096]{2,1,0:T(8,128)} %get-tuple-element.117.own, f32[4,16,4096]{2,1,0:T(8,128)} %copy-done.19, bf16[32,256,128]{2,1,0:T(8,128)(2,1)} %get-tuple-element.96.whi, ...), custom_call_target="tpu_custom_call" | custom-call | flops 1207959552 | bytes 13107464 | tf_op jit(solution)/shard_map/pallas_call | solution.py:458
  413.8 10.3 %all-to-all-done.10.refs_3_ = f32[16,8,32,128]{3,2,1,0:T(8,128)} async-done(((f32[16,8,32,128]{3,2,1,0:T(8,128)}), f32[16,8,32,128]{3,2,1,0:T(8,128)}, u32[]{:S(2)}, u32[]{:S(2)}) %all-to-all-start.10) | async-done | bytes 2097184 | tf_op jit(solution)/shard_map/all_to_all | solution.py:577
  430.3 16.3 %shard_map.84 = (f32[16,8,32,128]{3,2,1,0:T(8,128)}, f32[16,2,32,128]{3,2,1,0:T(8,128)}) custom-call(s32[2]{0:T(128)} %pad_add_fusion.place, s32[32,2]{1,0:T(8,128)} %copy.18.index, f32[4,16,4096]{2,1,0:T(8,128)} %get-tuple-element.61.own, f32[4,16,4096]{2,1,0:T(8,128)} %collective-permute-done.5.other, bf16[32,256,128]{2,1,0:T(8,128)(2,1)} %get-tuple-element.96.whi, ...), custom_call_target="tpu_custom_call" | custom-call | flops 1207959552 | bytes 13107464 | tf_op jit(solution)/shard_map/pallas_call | solution.py:458
  446.6 10.2 %all-to-all-done.3.refs_3_ = f32[16,8,32,128]{3,2,1,0:T(8,128)S(1)} async-done(((f32[16,8,32,128]{3,2,1,0:T(8,128)}), f32[16,8,32,128]{3,2,1,0:T(8,128)S(1)}, u32[]{:S(2)}, u32[]{:S(2)}) %all-to-all-start.3) | async-done | bytes 2097184 | tf_op jit(solution)/shard_map/all_to_all | solution.py:577
  463.7 20.9 %shard_map.93 = (f32[16,4,128,128]{3,2,1,0:T(8,128)}, f32[16,4,128,128]{3,2,1,0:T(8,128)}) custom-call(f32[16,8,32,128]{3,2,1,0:T(8,128)} %copy-done.3, f32[16,8,32,128]{3,2,1,0:T(8,128)} %all-to-all-done.8.refs_1_, f32[16,8,32,128]{3,2,1,0:T(8,128)} %all-to-all-done.9.refs_2_, f32[16,8,32,128]{3,2,1,0:T(8,128)} %all-to-all-done.10.refs_3_, ...), custom_call_target="tpu_custom_call" | custom-call | flops 3221225472 | bytes 20971520 | tf_op jit(solution)/shard_map/pallas_call | solution.py:458
  497.6 20.9 %shard_map.86 = (f32[16,4,128,128]{3,2,1,0:T(8,128)}, f32[16,4,128,128]{3,2,1,0:T(8,128)}) custom-call(f32[16,8,32,128]{3,2,1,0:T(8,128)} %copy-done.4, f32[16,8,32,128]{3,2,1,0:T(8,128)} %copy-done.5, f32[16,8,32,128]{3,2,1,0:T(8,128)} %all-to-all-done.2.refs_2_, f32[16,8,32,128]{3,2,1,0:T(8,128)} %copy-done.8, ...), custom_call_target="tpu_custom_call" | custom-call | flops 3221225472 | bytes 20971520 | tf_op jit(solution)/shard_map/pallas_call | solution.py:458
  518.5 33.4 %all-to-all-done.11.fields = f32[16,4,128,128]{3,2,1,0:T(8,128)} async-done(((f32[16,4,128,128]{3,2,1,0:T(8,128)}), f32[16,4,128,128]{3,2,1,0:T(8,128)}, u32[]{:S(2)}, u32[]{:S(2)}) %all-to-all-start.11) | async-done | bytes 4194336 | tf_op jit(solution)/shard_map/all_to_all | solution.py:577
  559.0 16.4 %shard_map.94 = f32[16,2,128,128]{3,2,1,0:T(8,128)} custom-call(f32[16,4,128,128]{3,2,1,0:T(8,128)} %all-to-all-done.11.fields, bf16[16,256,256]{2,1,0:T(8,128)(2,1)} %constant.36.clone.mhi, bf16[16,256,256]{2,1,0:T(8,128)(2,1)} %constant.37.clone.mlo), custom_call_target="tpu_custom_call" | custom-call | flops 2415919104 | bytes 10485760 | tf_op jit(solution)/shard_map/pallas_call | solution.py:458
  575.4 38.1 %all-to-all-done.4.fields = f32[16,4,128,128]{3,2,1,0:T(8,128)} async-done(((f32[16,4,128,128]{3,2,1,0:T(8,128)}), f32[16,4,128,128]{3,2,1,0:T(8,128)}, u32[]{:S(2)}, u32[]{:S(2)}) %all-to-all-start.4) | async-done | bytes 4194336 | tf_op jit(solution)/shard_map/all_to_all | solution.py:577
  619.8 16.4 %shard_map.87 = f32[16,2,128,128]{3,2,1,0:T(8,128)} custom-call(f32[16,4,128,128]{3,2,1,0:T(8,128)} %all-to-all-done.4.fields, bf16[16,256,256]{2,1,0:T(8,128)(2,1)} %constant.36.clone.mhi, bf16[16,256,256]{2,1,0:T(8,128)(2,1)} %constant.37.clone.mlo), custom_call_target="tpu_custom_call" | custom-call | flops 2415919104 | bytes 10485760 | tf_op jit(solution)/shard_map/pallas_call | solution.py:458
  636.3 10.0 %all-to-all-done.12.back = f32[16,2,128,128]{3,2,1,0:T(8,128)S(1)} async-done(((f32[16,2,128,128]{3,2,1,0:T(8,128)}), f32[16,2,128,128]{3,2,1,0:T(8,128)S(1)}, u32[]{:S(2)}, u32[]{:S(2)}) %all-to-all-start.12) | async-done | bytes 2097184 | tf_op jit(solution)/shard_map/all_to_all | solution.py:577
  653.8 16.9 %shard_map.95 = f32[16,4,128,128]{3,2,1,0:T(8,128)} custom-call(f32[16,2,128,128]{3,2,1,0:T(8,128)} %copy-done.2, f32[16,4,128,128]{3,2,1,0:T(8,128)} %get-tuple-element.74.kept, bf16[16,256,256]{2,1,0:T(8,128)(2,1)} %constant.34.clone.refs_4_.mhi, bf16[16,256,256]{2,1,0:T(8,128)(2,1)} %constant.35.clone.refs_5_.mlo), custom_call_target="tpu_custom_call" | custom-call | flops 1610612736 | bytes 14680064 | tf_op jit(solution)/shard_map/pallas_call | solution.py:458
  689.0 16.7 %shard_map.88 = (f32[16,4,64,128]{3,2,1,0:T(8,128)}, f32[16,4,64,128]{3,2,1,0:T(8,128)}) custom-call(f32[16,2,128,128]{3,2,1,0:T(8,128)} %copy-done.1, f32[16,4,128,128]{3,2,1,0:T(8,128)} %get-tuple-element.65.kept, bf16[16,256,256]{2,1,0:T(8,128)(2,1)} %constant.34.clone.refs_4_.mhi, bf16[16,256,256]{2,1,0:T(8,128)(2,1)} %constant.35.clone.refs_5_.mlo), custom_call_target="tpu_custom_call" | custom-call | flops 1610612736 | bytes 14680064 | tf_op jit(solution)/shard_map/pallas_call | solution.py:458
  705.7 37.7 %all-to-all-done.13.back = f32[16,4,128,128]{3,2,1,0:T(8,128)} async-done(((f32[16,4,128,128]{3,2,1,0:T(8,128)}), f32[16,4,128,128]{3,2,1,0:T(8,128)}, u32[]{:S(2)}, u32[]{:S(2)}) %all-to-all-start.13) | async-done | bytes 4194336 | tf_op jit(solution)/shard_map/all_to_all | solution.py:577
  749.7 17.6 %shard_map.96 = (f32[2,32,4096]{2,1,0:T(8,128)}, f32[2,32,4096]{2,1,0:T(8,128)}) custom-call(s32[2]{0:T(128)} %pad_add_fusion.place, s32[32,2]{1,0:T(8,128)} %copy.17.index, f32[16,4,128,128]{3,2,1,0:T(8,128)} %all-to-all-done.13.back, bf16[32,256,128]{2,1,0:T(8,128)(2,1)} %get-tuple-element.95.whi, bf16[32,256,128]{2,1,0:T(8,128)(2,1)} %get-tuple-element.93.wlo, ...), custom_call_target="tpu_custom_call" | custom-call | flops 1207959552 | bytes 15728904 | tf_op jit(solution)/shard_map/pallas_call | solution.py:458
  767.3 17.7 %shard_map.98 = (f32[2,32,4096]{2,1,0:T(8,128)}, f32[2,32,4096]{2,1,0:T(8,128)}) custom-call(s32[2]{0:T(128)} %pad_add_fusion.place, s32[32,2]{1,0:T(8,128)} %copy.17.index, f32[16,4,128,128]{3,2,1,0:T(8,128)} %all-to-all-done.13.back, bf16[32,256,128]{2,1,0:T(8,128)(2,1)} %get-tuple-element.95.whi, bf16[32,256,128]{2,1,0:T(8,128)(2,1)} %get-tuple-element.93.wlo, ...), custom_call_target="tpu_custom_call" | custom-call | flops 1207959552 | bytes 15728904 | tf_op jit(solution)/shard_map/pallas_call | solution.py:458
  791.5 17.7 %shard_map.97 = (f32[2,32,4096]{2,1,0:T(8,128)}, f32[2,32,4096]{2,1,0:T(8,128)}) custom-call(s32[2]{0:T(128)} %pad_add_fusion.place, s32[32,2]{1,0:T(8,128)} %copy.18.index, f32[16,4,64,128]{3,2,1,0:T(8,128)} %copy-done.7, bf16[32,256,128]{2,1,0:T(8,128)(2,1)} %get-tuple-element.96.whi, bf16[32,256,128]{2,1,0:T(8,128)(2,1)} %get-tuple-element.94.wlo, ...), custom_call_target="tpu_custom_call" | custom-call | flops 1207959552 | bytes 15728904 | tf_op jit(solution)/shard_map/pallas_call | solution.py:458
  824.7 17.8 %shard_map.99 = (f32[2,32,4096]{2,1,0:T(8,128)}, f32[2,32,4096]{2,1,0:T(8,128)}) custom-call(s32[2]{0:T(128)} %pad_add_fusion.place, s32[32,2]{1,0:T(8,128)} %copy.18.index, f32[16,4,64,128]{3,2,1,0:T(8,128)} %copy-done.6, bf16[32,256,128]{2,1,0:T(8,128)(2,1)} %get-tuple-element.96.whi, bf16[32,256,128]{2,1,0:T(8,128)(2,1)} %get-tuple-element.94.wlo, ...), custom_call_target="tpu_custom_call" | custom-call | flops 1207959552 | bytes 15728904 | tf_op jit(solution)/shard_map/pallas_call | solution.py:458
  848.3 31.4 %collective-permute-done.8 = f32[2,32,4096]{2,1,0:T(8,128)} collective-permute-done((f32[2,32,4096]{2,1,0:T(8,128)}, f32[2,32,4096]{2,1,0:T(8,128)}, u32[]{:S(2)}, u32[]{:S(2)}) %collective-permute-start.8) | collective-permute-done | bytes 1048608 | tf_op jit(solution)/shard_map/ppermute | solution.py:591
  882.6 19.5 %collective-permute-done.10 = f32[2,32,4096]{2,1,0:T(8,128)S(1)} collective-permute-done((f32[2,32,4096]{2,1,0:T(8,128)}, f32[2,32,4096]{2,1,0:T(8,128)S(1)}, u32[]{:S(2)}, u32[]{:S(2)}) %collective-permute-start.10) | collective-permute-done | bytes 1048608 | tf_op jit(solution)/shard_map/ppermute | solution.py:591
  (118 shorter events, 236.3 us)
Async XLA Ops:
  8.8 24.3 %collective-permute-start = (f32[4,16,4096]{2,1,0:T(8,128)}, f32[4,16,4096]{2,1,0:T(8,128)}, u32[]{:S(2)}, u32[]{:S(2)}) collective-permute-start(f32[4,16,4096]{2,1,0:T(8,128)} %fusion.7), channel_id=1, source_target_pairs={{0,16},{1,17},{2,18},{3,19},{4,20},{5,21},{6,22},{7,23},{8,24},{9,... | collective-permute-start | bytes 3145736 | tf_op jit(solution)/shard_map/ppermute | solution.py:591
  33.1 23.3 %collective-permute-start.1 = (f32[4,16,4096]{2,1,0:T(8,128)}, f32[4,16,4096]{2,1,0:T(8,128)S(1)}, u32[]{:S(2)}, u32[]{:S(2)}) collective-permute-start(f32[4,16,4096]{2,1,0:T(8,128)} %fusion.6), channel_id=1, source_target_pairs={{0,16},{1,17},{2,18},{3,19},{4,20},{5,21},{6,22},{7,23},{8,24},{9,... | collective-permute-start | bytes 3145736 | tf_op jit(solution)/shard_map/ppermute | solution.py:591
  36.3 47.6 %collective-permute-start.2 = (f32[4,16,4096]{2,1,0:T(8,128)}, f32[4,16,4096]{2,1,0:T(8,128)S(1)}, u32[]{:S(2)}, u32[]{:S(2)}) collective-permute-start(f32[4,16,4096]{2,1,0:T(8,128)} %get-tuple-element.123), channel_id=1, source_target_pairs={{0,8},{1,9},{2,10},{3,11},{4,12},{5,13},{6,14},{7,15},{8,0},{9,1},... | collective-permute-start | bytes 3145736 | tf_op jit(solution)/shard_map/ppermute | solution.py:591
  56.5 44.7 %copy-start.21 = (f32[4,16,4096]{2,1,0:T(8,128)}, f32[4,16,4096]{2,1,0:T(8,128)S(1)}, u32[]{:S(2)}) copy-start(f32[4,16,4096]{2,1,0:T(8,128)S(1)} %collective-permute-done.1) | copy-start | bytes 3145732
  101.2 75.3 %all-to-all-start.7 = ((f32[16,8,32,128]{3,2,1,0:T(8,128)}), f32[16,8,32,128]{3,2,1,0:T(8,128)S(1)}, u32[]{:S(2)}, u32[]{:S(2)}) async-start(f32[16,8,32,128]{3,2,1,0:T(8,128)} %get-tuple-element.69), calls=%async_computation.7 | async-start | bytes 4194304 | tf_op jit(solution)/shard_map/all_to_all | solution.py:577
  109.0 44.6 %collective-permute-start.4 = (f32[4,16,4096]{2,1,0:T(8,128)S(1)}, f32[4,16,4096]{2,1,0:T(8,128)S(1)}, u32[]{:S(2)}, u32[]{:S(2)}) collective-permute-start(f32[4,16,4096]{2,1,0:T(8,128)S(1)} %fusion.4), channel_id=1, source_target_pairs={{0,16},{1,17},{2,18},{3,19},{4,20},{5,21},{6,22},{7,23},{8,24},{9,... | collective-permute-start | bytes 3145736 | tf_op jit(solution)/shard_map/ppermute | solution.py:591
  112.1 48.1 %collective-permute-start.3 = (f32[4,16,4096]{2,1,0:T(8,128)S(1)}, f32[4,16,4096]{2,1,0:T(8,128)}, u32[]{:S(2)}, u32[]{:S(2)}) collective-permute-start(f32[4,16,4096]{2,1,0:T(8,128)S(1)} %get-tuple-element.50), channel_id=1, source_target_pairs={{0,8},{1,9},{2,10},{3,11},{4,12},{5,13},{6,14},{7,15},{8,0},{9,1},... | collective-permute-start | bytes 3145736 | tf_op jit(solution)/shard_map/ppermute | solution.py:591
  176.5 23.6 %copy-start.3 = (f32[16,8,32,128]{3,2,1,0:T(8,128)}, f32[16,8,32,128]{3,2,1,0:T(8,128)S(1)}, u32[]{:S(2)}) copy-start(f32[16,8,32,128]{3,2,1,0:T(8,128)S(1)} %all-to-all-done.7.refs_0_) | copy-start | bytes 6291460
  176.5 33.2 %all-to-all-start.8 = ((f32[16,8,32,128]{3,2,1,0:T(8,128)}), f32[16,8,32,128]{3,2,1,0:T(8,128)}, u32[]{:S(2)}, u32[]{:S(2)}) async-start(f32[16,8,32,128]{3,2,1,0:T(8,128)} %get-tuple-element.70), calls=%async_computation.8 | async-start | bytes 4194304 | tf_op jit(solution)/shard_map/all_to_all | solution.py:577
  209.8 74.6 %all-to-all-start = ((f32[16,8,32,128]{3,2,1,0:T(8,128)}), f32[16,8,32,128]{3,2,1,0:T(8,128)S(1)}, u32[]{:S(2)}, u32[]{:S(2)}) async-start(f32[16,8,32,128]{3,2,1,0:T(8,128)} %get-tuple-element.52), calls=%async_computation | async-start | bytes 4194304 | tf_op jit(solution)/shard_map/all_to_all | solution.py:577
  217.3 45.0 %collective-permute-start.6 = (f32[4,16,4096]{2,1,0:T(8,128)S(1)}, f32[4,16,4096]{2,1,0:T(8,128)S(1)}, u32[]{:S(2)}, u32[]{:S(2)}) collective-permute-start(f32[4,16,4096]{2,1,0:T(8,128)S(1)} %fusion.2), channel_id=1, source_target_pairs={{0,16},{1,17},{2,18},{3,19},{4,20},{5,21},{6,22},{7,23},{8,24},{9,... | collective-permute-start | bytes 3145736 | tf_op jit(solution)/shard_map/ppermute | solution.py:591
  220.4 47.7 %collective-permute-start.5 = (f32[4,16,4096]{2,1,0:T(8,128)S(1)}, f32[4,16,4096]{2,1,0:T(8,128)}, u32[]{:S(2)}, u32[]{:S(2)}) collective-permute-start(f32[4,16,4096]{2,1,0:T(8,128)S(1)} %get-tuple-element.55), channel_id=1, source_target_pairs={{0,8},{1,9},{2,10},{3,11},{4,12},{5,13},{6,14},{7,15},{8,0},{9,1},... | collective-permute-start | bytes 3145736 | tf_op jit(solution)/shard_map/ppermute | solution.py:591
  284.4 33.5 %all-to-all-start.9 = ((f32[16,8,32,128]{3,2,1,0:T(8,128)}), f32[16,8,32,128]{3,2,1,0:T(8,128)}, u32[]{:S(2)}, u32[]{:S(2)}) async-start(f32[16,8,32,128]{3,2,1,0:T(8,128)} %get-tuple-element.71), calls=%async_computation.9 | async-start | bytes 4194304 | tf_op jit(solution)/shard_map/all_to_all | solution.py:577
  317.9 70.9 %all-to-all-start.1 = ((f32[16,8,32,128]{3,2,1,0:T(8,128)}), f32[16,8,32,128]{3,2,1,0:T(8,128)S(1)}, u32[]{:S(2)}, u32[]{:S(2)}) async-start(f32[16,8,32,128]{3,2,1,0:T(8,128)} %get-tuple-element.57), calls=%async_computation.1 | async-start | bytes 4194304 | tf_op jit(solution)/shard_map/all_to_all | solution.py:577
  327.1 44.3 %collective-permute-start.7 = (f32[4,16,4096]{2,1,0:T(8,128)S(1)}, f32[4,16,4096]{2,1,0:T(8,128)S(1)}, u32[]{:S(2)}, u32[]{:S(2)}) collective-permute-start(f32[4,16,4096]{2,1,0:T(8,128)S(1)} %get-tuple-element.60), channel_id=1, source_target_pairs={{0,8},{1,9},{2,10},{3,11},{4,12},{5,13},{6,14},{7,15},{8,0},{9,1},... | collective-permute-start | bytes 3145736 | tf_op jit(solution)/shard_map/ppermute | solution.py:591
  388.8 25.1 %copy-start.5 = (f32[16,8,32,128]{3,2,1,0:T(8,128)}, f32[16,8,32,128]{3,2,1,0:T(8,128)S(1)}, u32[]{:S(2)}) copy-start(f32[16,8,32,128]{3,2,1,0:T(8,128)S(1)} %all-to-all-done.1.refs_1_) | copy-start | bytes 6291460
  388.8 35.4 %all-to-all-start.10 = ((f32[16,8,32,128]{3,2,1,0:T(8,128)}), f32[16,8,32,128]{3,2,1,0:T(8,128)}, u32[]{:S(2)}, u32[]{:S(2)}) async-start(f32[16,8,32,128]{3,2,1,0:T(8,128)} %get-tuple-element.72), calls=%async_computation.10 | async-start | bytes 4194304 | tf_op jit(solution)/shard_map/all_to_all | solution.py:577
  424.1 32.7 %all-to-all-start.3 = ((f32[16,8,32,128]{3,2,1,0:T(8,128)}), f32[16,8,32,128]{3,2,1,0:T(8,128)S(1)}, u32[]{:S(2)}, u32[]{:S(2)}) async-start(f32[16,8,32,128]{3,2,1,0:T(8,128)} %get-tuple-element.63), calls=%async_computation.3 | async-start | bytes 4194304 | tf_op jit(solution)/shard_map/all_to_all | solution.py:577
  456.8 27.7 %copy-start.8 = (f32[16,8,32,128]{3,2,1,0:T(8,128)}, f32[16,8,32,128]{3,2,1,0:T(8,128)S(1)}, u32[]{:S(2)}) copy-start(f32[16,8,32,128]{3,2,1,0:T(8,128)S(1)} %all-to-all-done.3.refs_3_) | copy-start | bytes 6291460
  456.8 33.4 %all-to-all-start.2 = ((f32[16,8,32,128]{3,2,1,0:T(8,128)}), f32[16,8,32,128]{3,2,1,0:T(8,128)}, u32[]{:S(2)}, u32[]{:S(2)}) async-start(f32[16,8,32,128]{3,2,1,0:T(8,128)} %get-tuple-element.62), calls=%async_computation.2 | async-start | bytes 4194304 | tf_op jit(solution)/shard_map/all_to_all | solution.py:577
  490.2 61.7 %all-to-all-start.11 = ((f32[16,4,128,128]{3,2,1,0:T(8,128)}), f32[16,4,128,128]{3,2,1,0:T(8,128)}, u32[]{:S(2)}, u32[]{:S(2)}) async-start(f32[16,4,128,128]{3,2,1,0:T(8,128)} %get-tuple-element.73), calls=%async_computation.11 | async-start | bytes 8388608 | tf_op jit(solution)/shard_map/all_to_all | solution.py:577
  551.9 61.6 %all-to-all-start.4 = ((f32[16,4,128,128]{3,2,1,0:T(8,128)}), f32[16,4,128,128]{3,2,1,0:T(8,128)}, u32[]{:S(2)}, u32[]{:S(2)}) async-start(f32[16,4,128,128]{3,2,1,0:T(8,128)} %get-tuple-element.64), calls=%async_computation.4 | async-start | bytes 8388608 | tf_op jit(solution)/shard_map/all_to_all | solution.py:577
  613.5 32.8 %all-to-all-start.12 = ((f32[16,2,128,128]{3,2,1,0:T(8,128)}), f32[16,2,128,128]{3,2,1,0:T(8,128)S(1)}, u32[]{:S(2)}, u32[]{:S(2)}) async-start(f32[16,2,128,128]{3,2,1,0:T(8,128)} %shard_map.94), calls=%async_computation.12 | async-start | bytes 4194304 | tf_op jit(solution)/shard_map/all_to_all | solution.py:577
  647.6 32.7 %all-to-all-start.5 = ((f32[16,2,128,128]{3,2,1,0:T(8,128)}), f32[16,2,128,128]{3,2,1,0:T(8,128)S(1)}, u32[]{:S(2)}, u32[]{:S(2)}) async-start(f32[16,2,128,128]{3,2,1,0:T(8,128)} %shard_map.87), calls=%async_computation.5 | async-start | bytes 4194304 | tf_op jit(solution)/shard_map/all_to_all | solution.py:577
  681.6 61.7 %all-to-all-start.13 = ((f32[16,4,128,128]{3,2,1,0:T(8,128)}), f32[16,4,128,128]{3,2,1,0:T(8,128)}, u32[]{:S(2)}, u32[]{:S(2)}) async-start(f32[16,4,128,128]{3,2,1,0:T(8,128)} %shard_map.95), calls=%async_computation.13 | async-start | bytes 8388608 | tf_op jit(solution)/shard_map/all_to_all | solution.py:577
  743.4 41.6 %all-to-all-start.6 = ((f32[16,4,64,128]{3,2,1,0:T(8,128)}), f32[16,4,64,128]{3,2,1,0:T(8,128)S(1)}, u32[]{:S(2)}, u32[]{:S(2)}) async-start(f32[16,4,64,128]{3,2,1,0:T(8,128)} %get-tuple-element.66), calls=%async_computation.6 | async-start | bytes 4194304 | tf_op jit(solution)/shard_map/all_to_all | solution.py:577
  786.3 37.1 %all-to-all-start.14 = ((f32[16,4,64,128]{3,2,1,0:T(8,128)}), f32[16,4,64,128]{3,2,1,0:T(8,128)S(1)}, u32[]{:S(2)}, u32[]{:S(2)}) async-start(f32[16,4,64,128]{3,2,1,0:T(8,128)} %get-tuple-element.86), calls=%async_computation.14 | async-start | bytes 4194304 | tf_op jit(solution)/shard_map/all_to_all | solution.py:577
  809.1 70.6 %collective-permute-start.8 = (f32[2,32,4096]{2,1,0:T(8,128)}, f32[2,32,4096]{2,1,0:T(8,128)}, u32[]{:S(2)}, u32[]{:S(2)}) collective-permute-start(f32[2,32,4096]{2,1,0:T(8,128)} %get-tuple-element.80), channel_id=1, source_target_pairs={{0,8},{1,9},{2,10},{3,11},{4,12},{5,13},{6,14},{7,15},{16,0},{17,1... | collective-permute-start | bytes 3145736 | tf_op jit(solution)/shard_map/ppermute | solution.py:591
  809.2 73.4 %collective-permute-start.9 = (f32[2,32,4096]{2,1,0:T(8,128)}, f32[2,32,4096]{2,1,0:T(8,128)}, u32[]{:S(2)}, u32[]{:S(2)}) collective-permute-start(f32[2,32,4096]{2,1,0:T(8,128)} %get-tuple-element.79), channel_id=1, source_target_pairs={{8,16},{9,17},{10,18},{11,19},{12,20},{13,21},{14,22},{15,23},{16,... | collective-permute-start | bytes 3145736 | tf_op jit(solution)/shard_map/ppermute | solution.py:591
  824.7 80.2 %copy-start.23 = (f32[2,32,4096]{2,1,0:T(8,128)S(1)}, f32[2,32,4096]{2,1,0:T(8,128)}, u32[]{:S(2)}) copy-start(f32[2,32,4096]{2,1,0:T(8,128)} %get-tuple-element.79) | copy-start | bytes 3145732
  842.6 59.5 %collective-permute-start.10 = (f32[2,32,4096]{2,1,0:T(8,128)}, f32[2,32,4096]{2,1,0:T(8,128)S(1)}, u32[]{:S(2)}, u32[]{:S(2)}) collective-permute-start(f32[2,32,4096]{2,1,0:T(8,128)} %get-tuple-element.90), channel_id=1, source_target_pairs={{0,8},{1,9},{2,10},{3,11},{4,12},{5,13},{6,14},{7,15},{16,0},{17,1... | collective-permute-start | bytes 3145736 | tf_op jit(solution)/shard_map/ppermute | solution.py:591
  846.4 58.6 %collective-permute-start.11 = (f32[2,32,4096]{2,1,0:T(8,128)}, f32[2,32,4096]{2,1,0:T(8,128)S(1)}, u32[]{:S(2)}, u32[]{:S(2)}) collective-permute-start(f32[2,32,4096]{2,1,0:T(8,128)} %get-tuple-element.89), channel_id=1, source_target_pairs={{8,16},{9,17},{10,18},{11,19},{12,20},{13,21},{14,22},{15,23},{16,... | collective-permute-start | bytes 3145736 | tf_op jit(solution)/shard_map/ppermute | solution.py:591
  (21 other events, 193.3 us)

commit v5 on v4

--- a/solution.py
+++ b/solution.py
@@ -263,9 +263,35 @@
             strips(half, inner)
 
 
-def middle_kernel(chunks, *refs):
+def bring(place, parts, whole, sems, first=0):
+    rows = whole.shape[2]
+    copies = [
+        pltpu.make_async_copy(
+            part.at[:, pl.ds(first, rows), :], whole.at[place[2] ^ s], sems.at[s]
+        )
+        for s, part in enumerate(parts)
+    ]
+    for copy in copies:
+        copy.start()
+    for copy in copies:
+        copy.wait()
+
+
+def hand_out(place, whole, parts, sems):
+    copies = [
+        pltpu.make_async_copy(whole.at[place[2] ^ s], part, sems.at[s])
+        for s, part in enumerate(parts)
+    ]
+    for copy in copies:
+        copy.start()
+    for copy in copies:
+        copy.wait()
+
+
+def middle_kernel(chunks, place, *refs):
     arrived = refs[:chunks]
-    mhi, mlo, out, kept, xhi, xlo, y = refs[chunks:]
+    mhi, mlo, kept, *sent = refs[chunks:-5]
+    out, sems, xhi, xlo, y = refs[-5:]
 
     def forward(row, places):
         for number in range(2):
@@ -307,9 +333,13 @@
                 out[g, 2 * number + 1, at, :] = im
 
     by_pieces(1, backward)
-
-
-def detector_kernel(fields, mhi, mlo, out, xhi, xlo, y):
+    hand_out(place, out, sent, sems)
+
+
+def detector_kernel(place, mhi, mlo, *refs):
+    parts, sent = refs[:XA], refs[XA : 2 * XA]
+    fields, out, sems, xhi, xlo, y = refs[2 * XA :]
+    bring(place, parts, fields, sems)
     rows = fields.shape[2]
 
     def forward(row):
@@ -350,10 +380,14 @@
             out[b, 1, at, :] = im
 
     strips(rows, backward)
-
-
-def return_kernel(chunks, back, kept, mhi, mlo, *refs):
-    out, (xhi, xlo, y) = refs[:chunks], refs[chunks:]
+    hand_out(place, out, sent, sems)
+
+
+def return_kernel(chunks, place, kept, mhi, mlo, *refs):
+    parts, refs = refs[:XA], refs[XA:]
+    back, sems, xhi, xlo, y = refs[-5:]
+    sent, out = (refs[:XA], refs[XA:-5]) if chunks == 1 else ((), refs[:-5])
+    bring(place, parts, back, sems)
 
     def forward(row, places):
         values = [(back[g, 0, at, :], back[g, 1, at, :]) for _, g, at in places]
@@ -382,11 +416,19 @@
             out[c][g, 3, at, :] = im
 
     by_pieces(chunks, backward)
-
-
-def leave_kernel(pieces, first, place, index, back, whi, wlo, mhi, mlo, *refs):
-    t0 = refs[:pieces]
-    before, (near, far, shi, slo, xhi, xlo, y) = refs[pieces:-7], refs[-7:]
+    if sent:
+        hand_out(place, out[0], sent, sems)
+
+
+def leave_kernel(pieces, first, arrived, place, index, whi, wlo, mhi, mlo, *refs):
+    t0, refs = refs[:pieces], refs[pieces:]
+    if arrived == 1:
+        back, refs = refs[0], refs[1:]
+    else:
+        parts, back, sems = refs[-arrived - 9 : -9], refs[-2], refs[-1]
+        bring(place, parts, back, sems, first)
+        refs = refs[: -arrived - 9] + refs[-9:-2]
+    before, (near, far, shi, slo, xhi, xlo, y) = refs[:-7], refs[-7:]
     chunk = t0[0].shape[2]
     half = chunk // 2
     rows = pieces * chunk
@@ -397,7 +439,7 @@
 
                 def inner(row, end=end, side=side, c=c):
                     within = pl.multiple_of(side * half + row, STRIP)
-                    source = pl.multiple_of(first + c * chunk + side * half + row, STRIP)
+                    source = pl.multiple_of(c * chunk + side * half + row, STRIP)
                     target = pl.multiple_of((end * pieces + c) * half + row, STRIP)
                     step(c, pl.ds(within, STRIP), pl.ds(source, STRIP), target)
 
@@ -449,17 +491,21 @@
     lax.fori_loop(0, NB, step, 0)
 
 
-def call(kernel, outs, scratch, mix_count, extra, *operands):
+def call(kernel, outs, scratch, mix_count, extra, *operands, parts=(), sent=()):
     specs = [
         pl.BlockSpec(memory_space=pltpu.SMEM if o.dtype == jnp.int32 else pltpu.VMEM)
         for o in operands
-    ]
+    ] + [pl.BlockSpec(memory_space=pl.ANY)] * len(parts)
+    operands += tuple(parts)
+    out_specs = [pl.BlockSpec(memory_space=pltpu.VMEM)] * len(outs)
+    out_specs += [pl.BlockSpec(memory_space=pl.ANY)] * len(sent)
+    outs = list(outs) + list(sent)
     moved = sum(o.size * o.dtype.itemsize for o in operands) + sum(4 * math.prod(o) for o in outs)
     return pl.pallas_call(
         kernel,
         out_shape=[jax.ShapeDtypeStruct(o, jnp.float32) for o in outs],
         in_specs=specs,
-        out_specs=[pl.BlockSpec(memory_space=pltpu.VMEM)] * len(outs),
+        out_specs=out_specs,
         scratch_shapes=scratch,
         compiler_params=pltpu.CompilerParams(vmem_limit_bytes=60 * 1024 * 1024),
         cost_estimate=pl.CostEstimate(
@@ -502,41 +548,55 @@
     )
 
 
-def middle(arrived, matrices):
-    return call(
+def block_scratch(channels, rows=XB):
+    return pltpu.VMEM((XA, channels, rows, LANES), jnp.float32)
+
+
+def middle(place, arrived, matrices):
+    kept, *sent = call(
         functools.partial(middle_kernel, len(arrived)),
-        [(XA, 4, XB, LANES), (XA, 4, XB, LANES)],
-        mix_scratch(2 * XB, 2 * LANES),
+        [(XA, 4, XB, LANES)],
+        [block_scratch(4), pltpu.SemaphoreType.DMA((XA,))] + mix_scratch(2 * XB, 2 * LANES),
         4,
         0,
+        place,
         *arrived,
         *matrices,
-    )
-
-
-def detector(fields, matrices):
-    rows = fields.shape[2]
+        sent=[(4, XB, LANES)] * XA,
+    )
+    return sent, kept
+
+
+def detector(place, parts, matrices):
     return call(
         detector_kernel,
-        [(XA, 2, rows, LANES)],
-        mix_scratch(2 * rows, 2 * LANES),
+        [],
+        [block_scratch(4), block_scratch(2), pltpu.SemaphoreType.DMA((XA,))]
+        + mix_scratch(2 * XB, 2 * LANES),
         3,
         0,
-        fields,
+        place,
         *matrices,
-    )[0]
-
-
-def pull(back, kept, matrices, chunks):
+        parts=parts,
+        sent=[(2, XB, LANES)] * XA,
+    )
+
+
+def pull(place, parts, kept, matrices, chunks):
+    scratch = [block_scratch(2), pltpu.SemaphoreType.DMA((XA,))] + mix_scratch(2 * XB, LANES)
+    if chunks == 1:
+        scratch = [block_scratch(4)] + scratch
     return call(
         functools.partial(return_kernel, chunks),
-        [(XA, 4, XB // chunks, LANES)] * chunks,
-        mix_scratch(2 * XB, LANES),
+        [] if chunks == 1 else [(XA, 4, XB // chunks, LANES)] * chunks,
+        scratch,
         2,
         0,
-        back,
+        place,
         kept,
         *matrices,
+        parts=parts,
+        sent=[(4, XB, LANES)] * XA if chunks == 1 else [],
     )
 
 
@@ -546,20 +606,24 @@
         pltpu.VMEM((NB, 2 * rows, LANES), jnp.bfloat16),
         pltpu.VMEM((NB, 2 * rows, LANES), jnp.bfloat16),
     ] + mix_scratch(rows, 2 * LANES)
+    parts = back if len(back) > 1 else ()
+    if parts:
+        scratch += [block_scratch(4, rows), pltpu.SemaphoreType.DMA((XA,))]
     extra = NB * 2 * rows * 256 * 128 * 6
     return call(
-        functools.partial(leave_kernel, len(t0), first),
+        functools.partial(leave_kernel, len(t0), first, len(back)),
         [(2, rows // 2, NB * BLK)] * 2,
         scratch,
         rows / XB,
         extra,
         place,
         index,
-        back,
         *weights,
         *matrices,
         *t0,
+        *(() if parts else back),
         *before,
+        parts=parts,
     )
 
 
@@ -582,6 +646,22 @@
         axis_index_groups=[[device(x, b, r) for x in range(2) for r in range(HALF)] for b in range(2)],
         tiled=True,
     )
+
+
+def spread(parts):
+    group = [(x, r) for x in range(2) for r in range(HALF)]
+    return [parts[0]] + [
+        lax.ppermute(
+            parts[s],
+            ("parts", "fft"),
+            [
+                (device(x, b, r), device(group[g ^ s][0], b, group[g ^ s][1]))
+                for b in range(2)
+                for g, (x, r) in enumerate(group)
+            ],
+        )
+        for s in range(1, XA)
+    ]
 
 
 def permute(values, steps):
@@ -633,7 +713,7 @@
 def blocked_body(potential, direction, block_index, block_weights):
     q = lax.axis_index("parts")
     b = lax.axis_index("fft") // HALF
-    place = jnp.stack([b, q]).astype(jnp.int32)
+    place = jnp.stack([b, q, q * HALF + lax.axis_index("fft") % HALF]).astype(jnp.int32)
     chunks = arrive(potential, direction, q, b)
     whi, wlo = split_weights(block_weights)
     by_column = column_constants()
@@ -643,31 +723,33 @@
     arrived = [[] for _ in range(ANGLES)]
     ahead = [[] for _ in range(ANGLES)]
     for c, (own, along, _) in enumerate(chunks):
+        further = chunks[c + 1] if c + 1 < CHUNKS else ((), (), ())
+        own = after(own, further[2])
         for a in range(ANGLES):
-            if c + 1 < CHUNKS:
-                own = after(own, chunks[c + 1][1 if a else 2])
             fields, t0 = enter(place, block_index[a], own, along, weights[a], row)
-            arrived[a].append(exchange(fields))
+            arrived[a].append(exchange(after(fields, further[1]) if a else fields))
             ahead[a].append(t0)
     carried = []
     for a in range(ANGLES):
-        out, kept = middle(arrived[a], column)
-        carried.append((exchange(out), kept))
-    backs = [exchange(detector(out, row)) for out, _ in carried]
+        out, kept = middle(place, arrived[a], column)
+        carried.append((spread(out), kept))
+    backs = [spread(detector(place, out, row)) for out, _ in carried]
     ends = 2
     span = CHUNKS // ends
     totals = [()] * ends
     for a in range(ANGLES):
         last = a == ANGLES - 1
-        pulled = pull(backs[a], carried[a][1], column, ends if last else 1)
+        pulled = pull(place, backs[a], carried[a][1], column, ends if last else 1)
         if last:
-            pulled = [exchange(pulled[0]), exchange(after(pulled[1], totals))]
+            pulled = [[exchange(pulled[0])], [exchange(after(pulled[1], totals))]]
         else:
-            pulled = [exchange(pulled[0])]
+            pulled = [spread(pulled)] * ends
         for e in range(ends):
-            back, first = (pulled[e], 0) if last else (pulled[0], e * (XB // ends))
+            first = 0 if last else e * (XB // ends)
             t0 = ahead[a][e * span : (e + 1) * span]
-            totals[e] = leave(place, block_index[a], back, first, t0, weights[a], row, totals[e])
+            totals[e] = leave(
+                place, block_index[a], pulled[e], first, t0, weights[a], row, totals[e]
+            )
     pieces = []
     half = XB // CHUNKS // 2
     for total in totals:

time: 921 us -> 1060 us (1.15)
  starting transfers between devices: 119 us -> 212 us
  waiting for transfers between devices: 424 us -> 468 us
    ppermute x0 -> x75, waiting for transfers between devices: none -> 167 us  [spread(): lax.ppermute(parts[s], ('parts', 'fft'), [(device(x, b, r), device(group[...]
    all_to_all x15 -> x10, waiting for transfers between devices: 184 us -> 29.3 us  [exchange(): lax.all_to_all(values, ('parts', 'fft'), split_axis=0, concat_axis=0, axi...]
    ppermute x0 -> x75, starting transfers between devices: none -> 104 us  [spread(): lax.ppermute(parts[s], ('parts', 'fft'), [(device(x, b, r), device(group[...]
    ppermute x12, waiting for transfers between devices: 240 us -> 272 us  [permute(): return lax.ppermute(values, ('parts', 'fft'), pairs)]
    all_to_all x15 -> x10, starting transfers between devices: 100 us -> 85.1 us  [exchange(): lax.all_to_all(values, ('parts', 'fft'), split_axis=0, concat_axis=0, axi...]
  transfers between devices with their start and end apart: 27 -> 97, of which waited for: 23 -> 46; matrix products, arithmetic and copies ran while one was open for 4% -> 3% of each run, Pallas kernels for 32% -> 29%
where the time goes in v5:
time: 1060 us
  waiting for transfers between devices  468 us (44%)
  Pallas kernels  319 us (30%)
  starting transfers between devices  212 us (20%)
  other arithmetic  31.7 us (3%)
  local copies, waits for them, and re-layouts  26.7 us (3%)
    pallas_call x18, Pallas kernels, call(): pl.pallas_call(kernel, out_shape=[jax.ShapeDtypeStruct(o, jnp.float32) fo...  319 us
    ppermute x12, waiting for transfers between devices, permute(): return lax.ppermute(values, ('parts', 'fft'), pairs)  272 us
    ppermute x75, waiting for transfers between devices, spread(): lax.ppermute(parts[s], ('parts', 'fft'), [(device(x, b, r), device(group[...  167 us
    ppermute x75, starting transfers between devices, spread(): lax.ppermute(parts[s], ('parts', 'fft'), [(device(x, b, r), device(group[...  104 us
    all_to_all x10, starting transfers between devices, exchange(): lax.all_to_all(values, ('parts', 'fft'), split_axis=0, concat_axis=0, axi...  85.1 us
    all_to_all x10, waiting for transfers between devices, exchange(): lax.all_to_all(values, ('parts', 'fft'), split_axis=0, concat_axis=0, axi...  29.3 us
    ppermute x12, starting transfers between devices, permute(): return lax.ppermute(values, ('parts', 'fft'), pairs)  22.9 us
  transfers between devices with their start and end apart: 97, of which 46 were waited for; matrix products, arithmetic and copies ran while one was open for 3% of the time, Pallas kernels for 29%

profile of v5, /device:TPU:3, one launch (start us, length us, event | category | flops | bytes accessed | tf_op | source)
XLA Modules:
  0.0 1059.2 jit_solution(8906988853814171951)
XLA Ops:
  19.2 13.9 %collective-permute-done = f32[4,16,4096]{2,1,0:T(8,128)} collective-permute-done((f32[4,16,4096]{2,1,0:T(8,128)}, f32[4,16,4096]{2,1,0:T(8,128)}, u32[]{:S(2)}, u32[]{:S(2)}) %collective-permute-start) | collective-permute-done | bytes 1048608 | tf_op jit(solution)/shard_map/ppermute | solution.py:671
  56.4 27.4 %collective-permute-done.2.other = f32[4,16,4096]{2,1,0:T(8,128)S(1)} collective-permute-done((f32[4,16,4096]{2,1,0:T(8,128)}, f32[4,16,4096]{2,1,0:T(8,128)S(1)}, u32[]{:S(2)}, u32[]{:S(2)}) %collective-permute-start.2) | collective-permute-done | bytes 1048608 | tf_op jit(solution)/shard_map/ppermute | solution.py:671
  84.8 16.4 %shard_map.89 = (f32[16,8,32,128]{3,2,1,0:T(8,128)}, f32[16,2,32,128]{3,2,1,0:T(8,128)}) custom-call(s32[3]{0:T(128)} %pad_add_fusion.place, s32[32,2]{1,0:T(8,128)} %copy.17.index, f32[4,16,4096]{2,1,0:T(8,128)} %get-tuple-element.127.own, f32[4,16,4096]{2,1,0:T(8,128)} %copy-done.16, bf16[32,256,128]{2,1,0:T(8,128)(2,1)} %get-tuple-element.251.whi, ...), custom_call_target="tpu_custom_call" | custom-call | flops 1207959552 | bytes 13107468 | tf_op jit(solution)/shard_map/pallas_call | solution.py:504
  113.9 16.3 %shard_map.82 = (f32[16,8,32,128]{3,2,1,0:T(8,128)}, f32[16,2,32,128]{3,2,1,0:T(8,128)}) custom-call(s32[3]{0:T(128)} %pad_add_fusion.place, s32[32,2]{1,0:T(8,128)} %copy.18.index, f32[4,16,4096]{2,1,0:T(8,128)} %get-tuple-element.127.own, f32[4,16,4096]{2,1,0:T(8,128)} %copy-done.16, bf16[32,256,128]{2,1,0:T(8,128)(2,1)} %get-tuple-element.252.whi, ...), custom_call_target="tpu_custom_call" | custom-call | flops 1207959552 | bytes 13107468 | tf_op jit(solution)/shard_map/pallas_call | solution.py:504
  130.1 24.4 %collective-permute-done.4.other = f32[4,16,4096]{2,1,0:T(8,128)} collective-permute-done((f32[4,16,4096]{2,1,0:T(8,128)}, f32[4,16,4096]{2,1,0:T(8,128)}, u32[]{:S(2)}, u32[]{:S(2)}) %collective-permute-start.4) | collective-permute-done | bytes 1048608 | tf_op jit(solution)/shard_map/ppermute | solution.py:671
  166.0 45.1 %collective-permute-done.3 = f32[4,16,4096]{2,1,0:T(8,128)S(1)} collective-permute-done((f32[4,16,4096]{2,1,0:T(8,128)S(1)}, f32[4,16,4096]{2,1,0:T(8,128)S(1)}, u32[]{:S(2)}, u32[]{:S(2)}) %collective-permute-start.3) | collective-permute-done | bytes 1048608 | tf_op jit(solution)/shard_map/ppermute | solution.py:671
  212.2 16.3 %shard_map.90 = (f32[16,8,32,128]{3,2,1,0:T(8,128)}, f32[16,2,32,128]{3,2,1,0:T(8,128)}) custom-call(s32[3]{0:T(128)} %pad_add_fusion.place, s32[32,2]{1,0:T(8,128)} %copy.17.index, f32[4,16,4096]{2,1,0:T(8,128)} %get-tuple-element.130.own, f32[4,16,4096]{2,1,0:T(8,128)} %collective-permute-done.4.other, bf16[32,256,128]{2,1,0:T(8,128)(2,1)} %get-tuple-element.251.whi, ...), custom_call_target="tpu_custom_call" | custom-call | flops 1207959552 | bytes 13107468 | tf_op jit(solution)/shard_map/pallas_call | solution.py:504
  241.3 16.3 %shard_map.83 = (f32[16,8,32,128]{3,2,1,0:T(8,128)}, f32[16,2,32,128]{3,2,1,0:T(8,128)}) custom-call(s32[3]{0:T(128)} %pad_add_fusion.place, s32[32,2]{1,0:T(8,128)} %copy.18.index, f32[4,16,4096]{2,1,0:T(8,128)} %get-tuple-element.130.own, f32[4,16,4096]{2,1,0:T(8,128)} %collective-permute-done.4.other, bf16[32,256,128]{2,1,0:T(8,128)(2,1)} %get-tuple-element.252.whi, ...), custom_call_target="tpu_custom_call" | custom-call | flops 1207959552 | bytes 13107468 | tf_op jit(solution)/shard_map/pallas_call | solution.py:504
  257.5 24.7 %collective-permute-done.5.other = f32[4,16,4096]{2,1,0:T(8,128)} collective-permute-done((f32[4,16,4096]{2,1,0:T(8,128)}, f32[4,16,4096]{2,1,0:T(8,128)}, u32[]{:S(2)}, u32[]{:S(2)}) %collective-permute-start.5) | collective-permute-done | bytes 1048608 | tf_op jit(solution)/shard_map/ppermute | solution.py:671
  293.8 45.4 %collective-permute-done.6 = f32[4,16,4096]{2,1,0:T(8,128)S(1)} collective-permute-done((f32[4,16,4096]{2,1,0:T(8,128)S(1)}, f32[4,16,4096]{2,1,0:T(8,128)S(1)}, u32[]{:S(2)}, u32[]{:S(2)}) %collective-permute-start.6) | collective-permute-done | bytes 1048608 | tf_op jit(solution)/shard_map/ppermute | solution.py:671
  340.2 16.3 %shard_map.91 = (f32[16,8,32,128]{3,2,1,0:T(8,128)}, f32[16,2,32,128]{3,2,1,0:T(8,128)}) custom-call(s32[3]{0:T(128)} %pad_add_fusion.place, s32[32,2]{1,0:T(8,128)} %copy.17.index, f32[4,16,4096]{2,1,0:T(8,128)} %get-tuple-element.139.own, f32[4,16,4096]{2,1,0:T(8,128)} %collective-permute-done.5.other, bf16[32,256,128]{2,1,0:T(8,128)(2,1)} %get-tuple-element.251.whi, ...), custom_call_target="tpu_custom_call" | custom-call | flops 1207959552 | bytes 13107468 | tf_op jit(solution)/shard_map/pallas_call | solution.py:504
  356.5 18.5 %all-to-all-start.7 = ((f32[16,8,32,128]{3,2,1,0:T(8,128)}), f32[16,8,32,128]{3,2,1,0:T(8,128)S(1)}, u32[]{:S(2)}, u32[]{:S(2)}) async-start(f32[16,8,32,128]{3,2,1,0:T(8,128)} %get-tuple-element.182), calls=%async_computation.7 | async-start | bytes 4194304 | tf_op jit(solution)/shard_map/all_to_all | solution.py:641
  381.1 16.3 %shard_map.84 = (f32[16,8,32,128]{3,2,1,0:T(8,128)}, f32[16,2,32,128]{3,2,1,0:T(8,128)}) custom-call(s32[3]{0:T(128)} %pad_add_fusion.place, s32[32,2]{1,0:T(8,128)} %copy.18.index, f32[4,16,4096]{2,1,0:T(8,128)} %get-tuple-element.139.own, f32[4,16,4096]{2,1,0:T(8,128)} %collective-permute-done.5.other, bf16[32,256,128]{2,1,0:T(8,128)(2,1)} %get-tuple-element.252.whi, ...), custom_call_target="tpu_custom_call" | custom-call | flops 1207959552 | bytes 13107468 | tf_op jit(solution)/shard_map/pallas_call | solution.py:504
  397.3 24.8 %collective-permute-done.7.other = f32[4,16,4096]{2,1,0:T(8,128)S(1)} collective-permute-done((f32[4,16,4096]{2,1,0:T(8,128)}, f32[4,16,4096]{2,1,0:T(8,128)S(1)}, u32[]{:S(2)}, u32[]{:S(2)}) %collective-permute-start.7) | collective-permute-done | bytes 1048608 | tf_op jit(solution)/shard_map/ppermute | solution.py:671
  432.1 16.3 %shard_map.85 = (f32[16,8,32,128]{3,2,1,0:T(8,128)}, f32[16,2,32,128]{3,2,1,0:T(8,128)}) custom-call(s32[3]{0:T(128)} %pad_add_fusion.place, s32[32,2]{1,0:T(8,128)} %copy.18.index, f32[4,16,4096]{2,1,0:T(8,128)} %get-tuple-element.273.own, f32[4,16,4096]{2,1,0:T(8,128)} %copy-done.17, bf16[32,256,128]{2,1,0:T(8,128)(2,1)} %get-tuple-element.252.whi, ...), custom_call_target="tpu_custom_call" | custom-call | flops 1207959552 | bytes 13107468 | tf_op jit(solution)/shard_map/pallas_call | solution.py:504
  464.9 16.3 %shard_map.92 = (f32[16,8,32,128]{3,2,1,0:T(8,128)}, f32[16,2,32,128]{3,2,1,0:T(8,128)}) custom-call(s32[3]{0:T(128)} %pad_add_fusion.place, s32[32,2]{1,0:T(8,128)} %copy.17.index, f32[4,16,4096]{2,1,0:T(8,128)} %get-tuple-element.273.own, f32[4,16,4096]{2,1,0:T(8,128)} %copy-done.17, bf16[32,256,128]{2,1,0:T(8,128)(2,1)} %get-tuple-element.251.whi, ...), custom_call_target="tpu_custom_call" | custom-call | flops 1207959552 | bytes 13107468 | tf_op jit(solution)/shard_map/pallas_call | solution.py:504
  498.9 22.9 %shard_map.86 = (f32[16,4,128,128]{3,2,1,0:T(8,128)}, f32[4,128,128]{2,1,0:T(8,128)}, f32[4,128,128]{2,1,0:T(8,128)}, f32[4,128,128]{2,1,0:T(8,128)}, f32[4,128,...) custom-call(s32[3]{0:T(128)} %pad_add_fusion.place, ...), custom_call_target="tpu_custom_call" | custom-call | flops 3221225472 | bytes 20971532 | tf_op jit(solution)/shard_map/pallas_call | solution.py:504
  555.8 17.5 %collective-permute-done.16.refs_9_ = f32[4,128,128]{2,1,0:T(8,128)} collective-permute-done((f32[4,128,128]{2,1,0:T(8,128)}, f32[4,128,128]{2,1,0:T(8,128)}, u32[]{:S(2)}, u32[]{:S(2)}) %collective-permute-start.16) | collective-permute-done | bytes 262176 | tf_op jit(solution)/shard_map/ppermute | solution.py:654
  573.3 12.2 %collective-permute-done.17.refs_10_ = f32[4,128,128]{2,1,0:T(8,128)} collective-permute-done((f32[4,128,128]{2,1,0:T(8,128)}, f32[4,128,128]{2,1,0:T(8,128)}, u32[]{:S(2)}, u32[]{:S(2)}) %collective-permute-start.17) | collective-permute-done | bytes 262176 | tf_op jit(solution)/shard_map/ppermute | solution.py:654
  597.1 17.7 %shard_map.87 = (f32[2,128,128]{2,1,0:T(8,128)}, f32[2,128,128]{2,1,0:T(8,128)}, f32[2,128,128]{2,1,0:T(8,128)}, f32[2,128,128]{2,1,0:T(8,128)}, f32[2,128,128]{...) custom-call(s32[3]{0:T(128)} %pad_add_fusion.place, ...), custom_call_target="tpu_custom_call" | custom-call | flops 2415919104 | bytes 10485772 | tf_op jit(solution)/shard_map/pallas_call | solution.py:504
  650.6 17.8 %shard_map.88 = (f32[16,4,64,128]{3,2,1,0:T(8,128)}, f32[16,4,64,128]{3,2,1,0:T(8,128)}) custom-call(s32[3]{0:T(128)} %pad_add_fusion.place, f32[16,4,128,128]{3,2,1,0:T(8,128)} %get-tuple-element.144.kept, bf16[16,256,256]{2,1,0:T(8,128)(2,1)} %constant.44.clone.refs_4_.mhi, bf16[16,256,256]{2,1,0:T(8,128)(2,1)} %constant.45.clone.refs_5_.mlo, ...), custom_call_target="tpu_custom_call" | custom-call | flops 1610612736 | bytes 14680076 | tf_op jit(solution)/shard_map/pallas_call | solution.py:504
  674.3 23.0 %shard_map.93 = (f32[16,4,128,128]{3,2,1,0:T(8,128)}, f32[4,128,128]{2,1,0:T(8,128)}, f32[4,128,128]{2,1,0:T(8,128)}, f32[4,128,128]{2,1,0:T(8,128)}, f32[4,128,...) custom-call(s32[3]{0:T(128)} %pad_add_fusion.place, ...), custom_call_target="tpu_custom_call" | custom-call | flops 3221225472 | bytes 20971532 | tf_op jit(solution)/shard_map/pallas_call | solution.py:504
  729.5 20.1 %collective-permute-done.47.refs_10_ = f32[4,128,128]{2,1,0:T(8,128)S(1)} collective-permute-done((f32[4,128,128]{2,1,0:T(8,128)}, f32[4,128,128]{2,1,0:T(8,128)S(1)}, u32[]{:S(2)}, u32[]{:S(2)}) %collective-permute-start.47) | collective-permute-done | bytes 262176 | tf_op jit(solution)/shard_map/ppermute | solution.py:654
  762.5 17.5 %shard_map.94 = (f32[2,128,128]{2,1,0:T(8,128)}, f32[2,128,128]{2,1,0:T(8,128)}, f32[2,128,128]{2,1,0:T(8,128)}, f32[2,128,128]{2,1,0:T(8,128)}, f32[2,128,128]{...) custom-call(s32[3]{0:T(128)} %pad_add_fusion.place, ...), custom_call_target="tpu_custom_call" | custom-call | flops 2415919104 | bytes 10485772 | tf_op jit(solution)/shard_map/pallas_call | solution.py:504
  815.0 18.2 %shard_map.95 = (f32[4,128,128]{2,1,0:T(8,128)}, f32[4,128,128]{2,1,0:T(8,128)}, f32[4,128,128]{2,1,0:T(8,128)}, f32[4,128,128]{2,1,0:T(8,128)}, f32[4,128,128]{...) custom-call(s32[3]{0:T(128)} %pad_add_fusion.place, ...), custom_call_target="tpu_custom_call" | custom-call | flops 1610612736 | bytes 14680076 | tf_op jit(solution)/shard_map/pallas_call | solution.py:504
  865.6 19.3 %collective-permute-done.77.refs_12_ = f32[4,128,128]{2,1,0:T(8,128)S(1)} collective-permute-done((f32[4,128,128]{2,1,0:T(8,128)}, f32[4,128,128]{2,1,0:T(8,128)S(1)}, u32[]{:S(2)}, u32[]{:S(2)}) %collective-permute-start.77) | collective-permute-done | bytes 262176 | tf_op jit(solution)/shard_map/ppermute | solution.py:654
  897.4 18.2 %shard_map.96 = (f32[2,32,4096]{2,1,0:T(8,128)}, f32[2,32,4096]{2,1,0:T(8,128)}) custom-call(s32[3]{0:T(128)} %pad_add_fusion.place, s32[32,2]{1,0:T(8,128)} %copy.17.index, bf16[32,256,128]{2,1,0:T(8,128)(2,1)} %get-tuple-element.251.whi, bf16[32,256,128]{2,1,0:T(8,128)(2,1)} %get-tuple-element.249.wlo, bf16[16,256,256]{2,1,0:T(8,128)(2,1)} %constant.46.clone.mhi, ...), custom_call_target="tpu_custom_call" | custom-call | flops 1207959552 | bytes 15728908 | tf_op jit(solution)/shard_map/pallas_call | solution.py:504
  915.5 18.2 %shard_map.98 = (f32[2,32,4096]{2,1,0:T(8,128)}, f32[2,32,4096]{2,1,0:T(8,128)}) custom-call(s32[3]{0:T(128)} %pad_add_fusion.place, s32[32,2]{1,0:T(8,128)} %copy.17.index, bf16[32,256,128]{2,1,0:T(8,128)(2,1)} %get-tuple-element.251.whi, bf16[32,256,128]{2,1,0:T(8,128)(2,1)} %get-tuple-element.249.wlo, bf16[16,256,256]{2,1,0:T(8,128)(2,1)} %constant.46.clone.mhi, ...), custom_call_target="tpu_custom_call" | custom-call | flops 1207959552 | bytes 15728908 | tf_op jit(solution)/shard_map/pallas_call | solution.py:504
  939.6 17.6 %shard_map.97 = (f32[2,32,4096]{2,1,0:T(8,128)}, f32[2,32,4096]{2,1,0:T(8,128)}) custom-call(s32[3]{0:T(128)} %pad_add_fusion.place, s32[32,2]{1,0:T(8,128)} %copy.18.index, bf16[32,256,128]{2,1,0:T(8,128)(2,1)} %get-tuple-element.252.whi, bf16[32,256,128]{2,1,0:T(8,128)(2,1)} %get-tuple-element.250.wlo, bf16[16,256,256]{2,1,0:T(8,128)(2,1)} %constant.46.clone.mhi, ...), custom_call_target="tpu_custom_call" | custom-call | flops 1207959552 | bytes 15728908 | tf_op jit(solution)/shard_map/pallas_call | solution.py:504
  973.4 17.8 %shard_map.99 = (f32[2,32,4096]{2,1,0:T(8,128)}, f32[2,32,4096]{2,1,0:T(8,128)}) custom-call(s32[3]{0:T(128)} %pad_add_fusion.place, s32[32,2]{1,0:T(8,128)} %copy.18.index, bf16[32,256,128]{2,1,0:T(8,128)(2,1)} %get-tuple-element.252.whi, bf16[32,256,128]{2,1,0:T(8,128)(2,1)} %get-tuple-element.250.wlo, bf16[16,256,256]{2,1,0:T(8,128)(2,1)} %constant.46.clone.mhi, ...), custom_call_target="tpu_custom_call" | custom-call | flops 1207959552 | bytes 15728908 | tf_op jit(solution)/shard_map/pallas_call | solution.py:504
  997.0 31.6 %collective-permute-done.83 = f32[2,32,4096]{2,1,0:T(8,128)} collective-permute-done((f32[2,32,4096]{2,1,0:T(8,128)}, f32[2,32,4096]{2,1,0:T(8,128)}, u32[]{:S(2)}, u32[]{:S(2)}) %collective-permute-start.83) | collective-permute-done | bytes 1048608 | tf_op jit(solution)/shard_map/ppermute | solution.py:671
  1031.4 19.6 %collective-permute-done.85 = f32[2,32,4096]{2,1,0:T(8,128)S(1)} collective-permute-done((f32[2,32,4096]{2,1,0:T(8,128)}, f32[2,32,4096]{2,1,0:T(8,128)S(1)}, u32[]{:S(2)}, u32[]{:S(2)}) %collective-permute-start.85) | collective-permute-done | bytes 1048608 | tf_op jit(solution)/shard_map/ppermute | solution.py:671
  (388 shorter events, 394.4 us)
Async XLA Ops:
  36.2 47.6 %collective-permute-start.2 = (f32[4,16,4096]{2,1,0:T(8,128)}, f32[4,16,4096]{2,1,0:T(8,128)S(1)}, u32[]{:S(2)}, u32[]{:S(2)}) collective-permute-start(f32[4,16,4096]{2,1,0:T(8,128)} %get-tuple-element.279), channel_id=1, source_target_pairs={{0,8},{1,9},{2,10},{3,11},{4,12},{5,13},{6,14},{7,15},{8,0},{9,1},... | collective-permute-start | bytes 3145736 | tf_op jit(solution)/shard_map/ppermute | solution.py:671
  101.2 53.4 %all-to-all-start.5 = ((f32[16,8,32,128]{3,2,1,0:T(8,128)}), f32[16,8,32,128]{3,2,1,0:T(8,128)S(1)}, u32[]{:S(2)}, u32[]{:S(2)}) async-start(f32[16,8,32,128]{3,2,1,0:T(8,128)} %get-tuple-element.180), calls=%async_computation.5 | async-start | bytes 4194304 | tf_op jit(solution)/shard_map/all_to_all | solution.py:641
  110.7 43.9 %collective-permute-start.4 = (f32[4,16,4096]{2,1,0:T(8,128)}, f32[4,16,4096]{2,1,0:T(8,128)}, u32[]{:S(2)}, u32[]{:S(2)}) collective-permute-start(f32[4,16,4096]{2,1,0:T(8,128)} %get-tuple-element.131), channel_id=1, source_target_pairs={{0,8},{1,9},{2,10},{3,11},{4,12},{5,13},{6,14},{7,15},{8,0},{9,1},... | collective-permute-start | bytes 3145736 | tf_op jit(solution)/shard_map/ppermute | solution.py:671
  154.5 73.9 %all-to-all-start = ((f32[16,8,32,128]{3,2,1,0:T(8,128)}), f32[16,8,32,128]{3,2,1,0:T(8,128)}, u32[]{:S(2)}, u32[]{:S(2)}) async-start(f32[16,8,32,128]{3,2,1,0:T(8,128)} %get-tuple-element.134), calls=%async_computation | async-start | bytes 4194304 | tf_op jit(solution)/shard_map/all_to_all | solution.py:641
  165.9 45.2 %collective-permute-start.3 = (f32[4,16,4096]{2,1,0:T(8,128)S(1)}, f32[4,16,4096]{2,1,0:T(8,128)S(1)}, u32[]{:S(2)}, u32[]{:S(2)}) collective-permute-start(f32[4,16,4096]{2,1,0:T(8,128)S(1)} %fusion.4), channel_id=1, source_target_pairs={{0,16},{1,17},{2,18},{3,19},{4,20},{5,21},{6,22},{7,23},{8,24},{9,... | collective-permute-start | bytes 3145736 | tf_op jit(solution)/shard_map/ppermute | solution.py:671
  228.4 53.8 %all-to-all-start.6 = ((f32[16,8,32,128]{3,2,1,0:T(8,128)}), f32[16,8,32,128]{3,2,1,0:T(8,128)S(1)}, u32[]{:S(2)}, u32[]{:S(2)}) async-start(f32[16,8,32,128]{3,2,1,0:T(8,128)} %get-tuple-element.181), calls=%async_computation.6 | async-start | bytes 4194304 | tf_op jit(solution)/shard_map/all_to_all | solution.py:641
  238.4 43.9 %collective-permute-start.5 = (f32[4,16,4096]{2,1,0:T(8,128)}, f32[4,16,4096]{2,1,0:T(8,128)}, u32[]{:S(2)}, u32[]{:S(2)}) collective-permute-start(f32[4,16,4096]{2,1,0:T(8,128)} %get-tuple-element.136), channel_id=1, source_target_pairs={{0,8},{1,9},{2,10},{3,11},{4,12},{5,13},{6,14},{7,15},{8,0},{9,1},... | collective-permute-start | bytes 3145736 | tf_op jit(solution)/shard_map/ppermute | solution.py:671
  282.3 74.3 %all-to-all-start.1 = ((f32[16,8,32,128]{3,2,1,0:T(8,128)}), f32[16,8,32,128]{3,2,1,0:T(8,128)}, u32[]{:S(2)}, u32[]{:S(2)}) async-start(f32[16,8,32,128]{3,2,1,0:T(8,128)} %get-tuple-element.137), calls=%async_computation.1 | async-start | bytes 4194304 | tf_op jit(solution)/shard_map/all_to_all | solution.py:641
  293.7 45.5 %collective-permute-start.6 = (f32[4,16,4096]{2,1,0:T(8,128)S(1)}, f32[4,16,4096]{2,1,0:T(8,128)S(1)}, u32[]{:S(2)}, u32[]{:S(2)}) collective-permute-start(f32[4,16,4096]{2,1,0:T(8,128)S(1)} %fusion.2), channel_id=1, source_target_pairs={{0,16},{1,17},{2,18},{3,19},{4,20},{5,21},{6,22},{7,23},{8,24},{9,... | collective-permute-start | bytes 3145736 | tf_op jit(solution)/shard_map/ppermute | solution.py:671
  356.5 65.6 %all-to-all-start.7 = ((f32[16,8,32,128]{3,2,1,0:T(8,128)}), f32[16,8,32,128]{3,2,1,0:T(8,128)S(1)}, u32[]{:S(2)}, u32[]{:S(2)}) async-start(f32[16,8,32,128]{3,2,1,0:T(8,128)} %get-tuple-element.182), calls=%async_computation.7 | async-start | bytes 4194304 | tf_op jit(solution)/shard_map/all_to_all | solution.py:641
  378.1 44.0 %collective-permute-start.7 = (f32[4,16,4096]{2,1,0:T(8,128)}, f32[4,16,4096]{2,1,0:T(8,128)S(1)}, u32[]{:S(2)}, u32[]{:S(2)}) collective-permute-start(f32[4,16,4096]{2,1,0:T(8,128)} %get-tuple-element.141), channel_id=1, source_target_pairs={{0,8},{1,9},{2,10},{3,11},{4,12},{5,13},{6,14},{7,15},{8,0},{9,1},... | collective-permute-start | bytes 3145736 | tf_op jit(solution)/shard_map/ppermute | solution.py:671
  422.1 36.5 %all-to-all-start.2 = ((f32[16,8,32,128]{3,2,1,0:T(8,128)}), f32[16,8,32,128]{3,2,1,0:T(8,128)}, u32[]{:S(2)}, u32[]{:S(2)}) async-start(f32[16,8,32,128]{3,2,1,0:T(8,128)} %get-tuple-element.142), calls=%async_computation.2 | async-start | bytes 4194304 | tf_op jit(solution)/shard_map/all_to_all | solution.py:641
  492.7 175.7 %all-to-all-start.8 = ((f32[16,8,32,128]{3,2,1,0:T(8,128)}), f32[16,8,32,128]{3,2,1,0:T(8,128)S(1)}, u32[]{:S(2)}, u32[]{:S(2)}) async-start(f32[16,8,32,128]{3,2,1,0:T(8,128)} %get-tuple-element.183), calls=%async_computation.8 | async-start | bytes 4194304 | tf_op jit(solution)/shard_map/all_to_all | solution.py:641
  549.4 36.1 %collective-permute-start.17 = (f32[4,128,128]{2,1,0:T(8,128)}, f32[4,128,128]{2,1,0:T(8,128)}, u32[]{:S(2)}, u32[]{:S(2)}) collective-permute-start(f32[4,128,128]{2,1,0:T(8,128)} %get-tuple-element.155), channel_id=1, source_target_pairs={{0,18},{1,19},{2,16},{3,17},{4,22},{5,23},{6,20},{7,21},{16,2},{17... | collective-permute-start | bytes 786440 | tf_op jit(solution)/shard_map/ppermute | solution.py:654
  552.8 44.2 %collective-permute-start.18 = (f32[4,128,128]{2,1,0:T(8,128)}, f32[4,128,128]{2,1,0:T(8,128)}, u32[]{:S(2)}, u32[]{:S(2)}) collective-permute-start(f32[4,128,128]{2,1,0:T(8,128)} %get-tuple-element.156), channel_id=1, source_target_pairs={{0,19},{1,18},{2,17},{3,16},{4,23},{5,22},{6,21},{7,20},{16,3},{17... | collective-permute-start | bytes 786440 | tf_op jit(solution)/shard_map/ppermute | solution.py:654
  552.8 44.1 %collective-permute-start.19 = (f32[4,128,128]{2,1,0:T(8,128)}, f32[4,128,128]{2,1,0:T(8,128)}, u32[]{:S(2)}, u32[]{:S(2)}) collective-permute-start(f32[4,128,128]{2,1,0:T(8,128)} %get-tuple-element.157), channel_id=1, source_target_pairs={{0,20},{1,21},{2,22},{3,23},{4,16},{5,17},{6,18},{7,19},{16,4},{17... | collective-permute-start | bytes 786440 | tf_op jit(solution)/shard_map/ppermute | solution.py:654
  555.2 41.8 %collective-permute-start.20 = (f32[4,128,128]{2,1,0:T(8,128)}, f32[4,128,128]{2,1,0:T(8,128)}, u32[]{:S(2)}, u32[]{:S(2)}) collective-permute-start(f32[4,128,128]{2,1,0:T(8,128)} %get-tuple-element.158), channel_id=1, source_target_pairs={{0,21},{1,20},{2,23},{3,22},{4,17},{5,16},{6,19},{7,18},{16,5},{17... | collective-permute-start | bytes 786440 | tf_op jit(solution)/shard_map/ppermute | solution.py:654
  668.4 265.4 %all-to-all-start.4 = ((f32[16,4,64,128]{3,2,1,0:T(8,128)}), f32[16,4,64,128]{3,2,1,0:T(8,128)}, u32[]{:S(2)}, u32[]{:S(2)}) async-start(f32[16,4,64,128]{3,2,1,0:T(8,128)} %get-tuple-element.177), calls=%async_computation.4 | async-start | bytes 4194304 | tf_op jit(solution)/shard_map/all_to_all | solution.py:641
  714.8 34.9 %collective-permute-start.47 = (f32[4,128,128]{2,1,0:T(8,128)}, f32[4,128,128]{2,1,0:T(8,128)S(1)}, u32[]{:S(2)}, u32[]{:S(2)}) collective-permute-start(f32[4,128,128]{2,1,0:T(8,128)} %get-tuple-element.195), channel_id=1, source_target_pairs={{0,18},{1,19},{2,16},{3,17},{4,22},{5,23},{6,20},{7,21},{16,2},{17... | collective-permute-start | bytes 786440 | tf_op jit(solution)/shard_map/ppermute | solution.py:654
  719.7 41.7 %collective-permute-start.48 = (f32[4,128,128]{2,1,0:T(8,128)}, f32[4,128,128]{2,1,0:T(8,128)S(1)}, u32[]{:S(2)}, u32[]{:S(2)}) collective-permute-start(f32[4,128,128]{2,1,0:T(8,128)} %get-tuple-element.196), channel_id=1, source_target_pairs={{0,19},{1,18},{2,17},{3,16},{4,23},{5,22},{6,21},{7,20},{16,3},{17... | collective-permute-start | bytes 786440 | tf_op jit(solution)/shard_map/ppermute | solution.py:654
  725.5 35.9 %collective-permute-start.49 = (f32[4,128,128]{2,1,0:T(8,128)}, f32[4,128,128]{2,1,0:T(8,128)S(1)}, u32[]{:S(2)}, u32[]{:S(2)}) collective-permute-start(f32[4,128,128]{2,1,0:T(8,128)} %get-tuple-element.197), channel_id=1, source_target_pairs={{0,20},{1,21},{2,22},{3,23},{4,16},{5,17},{6,18},{7,19},{16,4},{17... | collective-permute-start | bytes 786440 | tf_op jit(solution)/shard_map/ppermute | solution.py:654
  726.7 34.7 %collective-permute-start.50 = (f32[4,128,128]{2,1,0:T(8,128)}, f32[4,128,128]{2,1,0:T(8,128)S(1)}, u32[]{:S(2)}, u32[]{:S(2)}) collective-permute-start(f32[4,128,128]{2,1,0:T(8,128)} %get-tuple-element.198), channel_id=1, source_target_pairs={{0,21},{1,20},{2,23},{3,22},{4,17},{5,16},{6,19},{7,18},{16,5},{17... | collective-permute-start | bytes 786440 | tf_op jit(solution)/shard_map/ppermute | solution.py:654
  728.3 33.1 %collective-permute-start.51 = (f32[4,128,128]{2,1,0:T(8,128)}, f32[4,128,128]{2,1,0:T(8,128)S(1)}, u32[]{:S(2)}, u32[]{:S(2)}) collective-permute-start(f32[4,128,128]{2,1,0:T(8,128)} %get-tuple-element.199), channel_id=1, source_target_pairs={{0,22},{1,23},{2,20},{3,21},{4,18},{5,19},{6,16},{7,17},{16,6},{17... | collective-permute-start | bytes 786440 | tf_op jit(solution)/shard_map/ppermute | solution.py:654
  850.4 34.5 %collective-permute-start.77 = (f32[4,128,128]{2,1,0:T(8,128)}, f32[4,128,128]{2,1,0:T(8,128)S(1)}, u32[]{:S(2)}, u32[]{:S(2)}) collective-permute-start(f32[4,128,128]{2,1,0:T(8,128)} %get-tuple-element.227), channel_id=1, source_target_pairs={{0,18},{1,19},{2,16},{3,17},{4,22},{5,23},{6,20},{7,21},{16,2},{17... | collective-permute-start | bytes 786440 | tf_op jit(solution)/shard_map/ppermute | solution.py:654
  857.0 39.2 %collective-permute-start.78 = (f32[4,128,128]{2,1,0:T(8,128)}, f32[4,128,128]{2,1,0:T(8,128)S(1)}, u32[]{:S(2)}, u32[]{:S(2)}) collective-permute-start(f32[4,128,128]{2,1,0:T(8,128)} %get-tuple-element.228), channel_id=1, source_target_pairs={{0,19},{1,18},{2,17},{3,16},{4,23},{5,22},{6,21},{7,20},{16,3},{17... | collective-permute-start | bytes 786440 | tf_op jit(solution)/shard_map/ppermute | solution.py:654
  862.8 33.5 %collective-permute-start.79 = (f32[4,128,128]{2,1,0:T(8,128)}, f32[4,128,128]{2,1,0:T(8,128)S(1)}, u32[]{:S(2)}, u32[]{:S(2)}) collective-permute-start(f32[4,128,128]{2,1,0:T(8,128)} %get-tuple-element.229), channel_id=1, source_target_pairs={{0,20},{1,21},{2,22},{3,23},{4,16},{5,17},{6,18},{7,19},{16,4},{17... | collective-permute-start | bytes 786440 | tf_op jit(solution)/shard_map/ppermute | solution.py:654
  862.8 33.4 %collective-permute-start.80 = (f32[4,128,128]{2,1,0:T(8,128)}, f32[4,128,128]{2,1,0:T(8,128)S(1)}, u32[]{:S(2)}, u32[]{:S(2)}) collective-permute-start(f32[4,128,128]{2,1,0:T(8,128)} %get-tuple-element.230), channel_id=1, source_target_pairs={{0,21},{1,20},{2,23},{3,22},{4,17},{5,16},{6,19},{7,18},{16,5},{17... | collective-permute-start | bytes 786440 | tf_op jit(solution)/shard_map/ppermute | solution.py:654
  933.7 38.3 %all-to-all-start.9 = ((f32[16,4,64,128]{3,2,1,0:T(8,128)}), f32[16,4,64,128]{3,2,1,0:T(8,128)S(1)}, u32[]{:S(2)}, u32[]{:S(2)}) async-start(f32[16,4,64,128]{3,2,1,0:T(8,128)} %get-tuple-element.244), calls=%async_computation.9 | async-start | bytes 4194304 | tf_op jit(solution)/shard_map/all_to_all | solution.py:641
  957.2 71.5 %collective-permute-start.83 = (f32[2,32,4096]{2,1,0:T(8,128)}, f32[2,32,4096]{2,1,0:T(8,128)}, u32[]{:S(2)}, u32[]{:S(2)}) collective-permute-start(f32[2,32,4096]{2,1,0:T(8,128)} %get-tuple-element.236), channel_id=1, source_target_pairs={{0,8},{1,9},{2,10},{3,11},{4,12},{5,13},{6,14},{7,15},{16,0},{17,1... | collective-permute-start | bytes 3145736 | tf_op jit(solution)/shard_map/ppermute | solution.py:671
  957.3 74.1 %collective-permute-start.84 = (f32[2,32,4096]{2,1,0:T(8,128)}, f32[2,32,4096]{2,1,0:T(8,128)}, u32[]{:S(2)}, u32[]{:S(2)}) collective-permute-start(f32[2,32,4096]{2,1,0:T(8,128)} %get-tuple-element.235), channel_id=1, source_target_pairs={{8,16},{9,17},{10,18},{11,19},{12,20},{13,21},{14,22},{15,23},{16,... | collective-permute-start | bytes 3145736 | tf_op jit(solution)/shard_map/ppermute | solution.py:671
  991.2 59.9 %collective-permute-start.85 = (f32[2,32,4096]{2,1,0:T(8,128)}, f32[2,32,4096]{2,1,0:T(8,128)S(1)}, u32[]{:S(2)}, u32[]{:S(2)}) collective-permute-start(f32[2,32,4096]{2,1,0:T(8,128)} %get-tuple-element.246), channel_id=1, source_target_pairs={{0,8},{1,9},{2,10},{3,11},{4,12},{5,13},{6,14},{7,15},{16,0},{17,1... | collective-permute-start | bytes 3145736 | tf_op jit(solution)/shard_map/ppermute | solution.py:671
  995.1 58.7 %collective-permute-start.86 = (f32[2,32,4096]{2,1,0:T(8,128)}, f32[2,32,4096]{2,1,0:T(8,128)S(1)}, u32[]{:S(2)}, u32[]{:S(2)}) collective-permute-start(f32[2,32,4096]{2,1,0:T(8,128)} %get-tuple-element.245), channel_id=1, source_target_pairs={{8,16},{9,17},{10,18},{11,19},{12,20},{13,21},{14,22},{15,23},{16,... | collective-permute-start | bytes 3145736 | tf_op jit(solution)/shard_map/ppermute | solution.py:671
  (156 other events, 3050.3 us)

commit v6 on v4

--- a/solution.py
+++ b/solution.py
@@ -246,19 +246,19 @@
     lax.fori_loop(0, XA, second_slice, 0)
 
 
-def by_pieces(split, step):
+def by_pieces(spans, step):
     half = XB // CHUNKS // 2
-    rows = XB // split
-    for c in range(CHUNKS):
+    pieces = [(piece, c) for piece, span in enumerate(spans) for c in range(span)]
+    for chunk, (piece, c) in enumerate(pieces):
         for x in range(2):
 
-            def inner(row, c=c, x=x):
+            def inner(row, chunk=chunk, piece=piece, c=c, x=x):
                 places = []
                 for p in range(XA):
-                    first = 2 * c * half + p // HALF * half
-                    at = pl.ds(pl.multiple_of(first % rows + row, STRIP), STRIP)
-                    places.append((first // rows, x * HALF + p % HALF, at))
-                step(pl.multiple_of((2 * c + x) * half + row, STRIP), places)
+                    first = (2 * c + p // HALF) * half
+                    at = pl.ds(pl.multiple_of(first + row, STRIP), STRIP)
+                    places.append((piece, x * HALF + p % HALF, at))
+                step(pl.multiple_of((2 * chunk + x) * half + row, STRIP), places)
 
             strips(half, inner)
 
@@ -274,7 +274,7 @@
             ]
             columns_out(xhi, xlo, number, row, values)
 
-    by_pieces(chunks, forward)
+    by_pieces((1,) * chunks, forward)
     columns_mix(xhi, xlo, mhi, mlo, y)
 
     def turn(row, places):
@@ -297,7 +297,7 @@
             change.append((re - (d_re * p_im + d_im * p_re), im + (d_re * p_re - d_im * p_im)))
         columns_out(xhi, xlo, 1, row, change)
 
-    by_pieces(chunks, turn)
+    by_pieces((1,) * chunks, turn)
     columns_mix(xhi, xlo, mhi, mlo, y)
 
     def backward(row, places):
@@ -306,7 +306,7 @@
                 out[g, 2 * number, at, :] = re
                 out[g, 2 * number + 1, at, :] = im
 
-    by_pieces(1, backward)
+    by_pieces((CHUNKS,), backward)
 
 
 def detector_kernel(fields, mhi, mlo, out, xhi, xlo, y):
@@ -352,14 +352,14 @@
     strips(rows, backward)
 
 
-def return_kernel(chunks, back, kept, mhi, mlo, *refs):
-    out, (xhi, xlo, y) = refs[:chunks], refs[chunks:]
+def return_kernel(spans, back, kept, mhi, mlo, *refs):
+    out, (xhi, xlo, y) = refs[: len(spans)], refs[len(spans) :]
 
     def forward(row, places):
         values = [(back[g, 0, at, :], back[g, 1, at, :]) for _, g, at in places]
         columns_out(xhi, xlo, 0, row, values)
 
-    by_pieces(1, forward)
+    by_pieces((CHUNKS,), forward)
     columns_mix(xhi, xlo, mhi, mlo, y)
 
     def turn(row, places):
@@ -373,7 +373,7 @@
             following.append(times((kept[p, 2, local, :], kept[p, 3, local, :]), pulled[p]))
         columns_out(xhi, xlo, 0, row, following)
 
-    by_pieces(chunks, turn)
+    by_pieces(spans, turn)
     columns_mix(xhi, xlo, mhi, mlo, y)
 
     def backward(row, places):
@@ -381,27 +381,35 @@
             out[c][g, 2, at, :] = re
             out[c][g, 3, at, :] = im
 
-    by_pieces(chunks, backward)
-
-
-def leave_kernel(pieces, first, place, index, back, whi, wlo, mhi, mlo, *refs):
-    t0 = refs[:pieces]
-    before, (near, far, shi, slo, xhi, xlo, y) = refs[pieces:-7], refs[-7:]
+    by_pieces(spans, backward)
+
+
+def leave_kernel(spans, place, index, back, whi, wlo, mhi, mlo, *refs):
+    chunks, count = sum(spans), 2 * len(spans)
+    t0, refs = refs[:chunks], refs[chunks:]
+    before, outs, (shi, slo, xhi, xlo, y) = refs[: -count - 5], refs[-count - 5 : -5], refs[-5:]
     chunk = t0[0].shape[2]
     half = chunk // 2
-    rows = pieces * chunk
+    rows = chunks * chunk
+    starts = []
 
     def pieces_of(step):
-        for end, side in enumerate((1 - place[1], place[1])):
-            for c in range(pieces):
-
-                def inner(row, end=end, side=side, c=c):
-                    within = pl.multiple_of(side * half + row, STRIP)
-                    source = pl.multiple_of(first + c * chunk + side * half + row, STRIP)
-                    target = pl.multiple_of((end * pieces + c) * half + row, STRIP)
-                    step(c, pl.ds(within, STRIP), pl.ds(source, STRIP), target)
-
-                strips(half, inner)
+        starts.clear()
+        done = 0
+        for span in spans:
+            for end, side in enumerate((1 - place[1], place[1])):
+                base = (2 * done + end * span) * half
+                starts.append((base, span * half))
+                for c in range(span):
+
+                    def inner(row, side=side, c=c, done=done, base=base):
+                        within = pl.multiple_of(side * half + row, STRIP)
+                        source = pl.multiple_of((done + c) * chunk + side * half + row, STRIP)
+                        target = pl.multiple_of(base + c * half + row, STRIP)
+                        step(done + c, pl.ds(within, STRIP), pl.ds(source, STRIP), target)
+
+                    strips(half, inner)
+            done += span
 
     def store(b, i, target, value):
         high, low = halves(value)
@@ -426,7 +434,7 @@
 
     pieces_of(turn)
 
-    for out, old in zip((near, far), before or (None, None)):
+    for out, old in zip(outs, before or [None] * count):
         out[...] = jnp.zeros(out.shape, jnp.float32) if old is None else old[...]
 
     def across(a, b):
@@ -440,10 +448,9 @@
         for s in range(SLOTS):
             at = pl.ds(pl.multiple_of(index[b, s] * BLK, BLK), BLK)
             for i in range(2):
-                for end, out in enumerate((near, far)):
-                    start = i * rows + end * (rows // 2)
-                    part = values[start : start + rows // 2, s * BLK : (s + 1) * BLK]
-                    out[i, :, at] += part
+                for (start, size), out in zip(starts, outs):
+                    start += i * rows
+                    out[i, :, at] += values[start : start + size, s * BLK : (s + 1) * BLK]
         return carry
 
     lax.fori_loop(0, NB, step, 0)
@@ -527,10 +534,10 @@
     )[0]
 
 
-def pull(back, kept, matrices, chunks):
+def pull(back, kept, matrices, spans):
     return call(
-        functools.partial(return_kernel, chunks),
-        [(XA, 4, XB // chunks, LANES)] * chunks,
+        functools.partial(return_kernel, spans),
+        [(XA, 4, span * XB // CHUNKS, LANES) for span in spans],
         mix_scratch(2 * XB, LANES),
         2,
         0,
@@ -540,16 +547,16 @@
     )
 
 
-def leave(place, index, back, first, t0, weights, matrices, before):
+def leave(place, index, back, t0, weights, matrices, before, spans):
     rows = sum(t.shape[2] for t in t0)
     scratch = [
         pltpu.VMEM((NB, 2 * rows, LANES), jnp.bfloat16),
         pltpu.VMEM((NB, 2 * rows, LANES), jnp.bfloat16),
     ] + mix_scratch(rows, 2 * LANES)
     extra = NB * 2 * rows * 256 * 128 * 6
-    return call(
-        functools.partial(leave_kernel, len(t0), first),
-        [(2, rows // 2, NB * BLK)] * 2,
+    outs = call(
+        functools.partial(leave_kernel, spans),
+        [(2, span * XB // CHUNKS // 2, NB * BLK) for span in spans for _ in range(2)],
         scratch,
         rows / XB,
         extra,
@@ -561,6 +568,7 @@
         *t0,
         *before,
     )
+    return [outs[2 * i : 2 * i + 2] for i in range(len(spans))]
 
 
 def split_weights(block_weights):
@@ -603,23 +611,31 @@
 
 def arrive(potential, direction, q, b):
     half = XB // CHUNKS // 2
-    chunks = []
-    beside = along = ()
-    for c in range(CHUNKS):
+
+    def sides(c):
         lower, upper = (
             jnp.concatenate(
                 [v[:, (2 * c + x) * half : (2 * c + x + 1) * half] for v in (potential, direction)]
             )
             for x in range(2)
         )
-        keep = jnp.where(q == 0, lower, upper)
-        give = jnp.where(q == 0, upper, lower)
-        beside = permute(after(give, beside), BESIDE)
+        return jnp.where(q == 0, lower, upper), jnp.where(q == 0, upper, lower)
+
+    keep, give = sides(0)
+    potential, direction = after((potential, direction), give)
+    beside = permute(give, BESIDE)
+    kept, given = zip(*[sides(c) for c in range(1, CHUNKS)])
+    rest = permute(after(jnp.concatenate(given), beside), BESIDE)
+    chunks = []
+    along = ()
+    for c in range(CHUNKS):
+        if c:
+            keep, beside = kept[c - 1], rest[4 * (c - 1) : 4 * c]
         own = jnp.where(q == b, keep, beside)
         give = jnp.where(q == b, beside, keep)
         along = permute(after(give, along), ALONG)
-        chunks.append((own, along, beside))
-    return chunks
+        chunks.append((own, along))
+    return chunks, rest
 
 
 def depart(near, far, q, b):
@@ -634,7 +650,7 @@
     q = lax.axis_index("parts")
     b = lax.axis_index("fft") // HALF
     place = jnp.stack([b, q]).astype(jnp.int32)
-    chunks = arrive(potential, direction, q, b)
+    chunks, beside = arrive(potential, direction, q, b)
     whi, wlo = split_weights(block_weights)
     by_column = column_constants()
     column = tuple(jnp.asarray(v) for v in split_constant(by_column))
@@ -642,35 +658,30 @@
     weights = [(whi[a], wlo[a]) for a in range(ANGLES)]
     arrived = [[] for _ in range(ANGLES)]
     ahead = [[] for _ in range(ANGLES)]
-    for c, (own, along, _) in enumerate(chunks):
+    for c, (own, along) in enumerate(chunks):
+        further = chunks[c + 1][1] if c + 1 < CHUNKS else ()
+        own = after(own, beside)
         for a in range(ANGLES):
-            if c + 1 < CHUNKS:
-                own = after(own, chunks[c + 1][1 if a else 2])
             fields, t0 = enter(place, block_index[a], own, along, weights[a], row)
-            arrived[a].append(exchange(fields))
+            arrived[a].append(exchange(after(fields, further) if a else fields))
             ahead[a].append(t0)
     carried = []
     for a in range(ANGLES):
         out, kept = middle(arrived[a], column)
         carried.append((exchange(out), kept))
     backs = [exchange(detector(out, row)) for out, _ in carried]
-    ends = 2
-    span = CHUNKS // ends
-    totals = [()] * ends
-    for a in range(ANGLES):
-        last = a == ANGLES - 1
-        pulled = pull(backs[a], carried[a][1], column, ends if last else 1)
-        if last:
-            pulled = [exchange(pulled[0]), exchange(after(pulled[1], totals))]
-        else:
-            pulled = [exchange(pulled[0])]
-        for e in range(ends):
-            back, first = (pulled[e], 0) if last else (pulled[0], e * (XB // ends))
-            t0 = ahead[a][e * span : (e + 1) * span]
-            totals[e] = leave(place, block_index[a], back, first, t0, weights[a], row, totals[e])
+    spans = (CHUNKS // 2, CHUNKS // 4, CHUNKS // 4)
+    pulled = exchange(pull(backs[0], carried[0][1], column, (CHUNKS,))[0])
+    totals = leave(place, block_index[0], pulled, ahead[0], weights[0], row, (), spans)
+    pulled = pull(backs[1], carried[1][1], column, spans)
     pieces = []
     half = XB // CHUNKS // 2
-    for total in totals:
+    done = 0
+    for i, span in enumerate(spans):
+        back = exchange(after(pulled[i], totals) if i else pulled[i])
+        t0 = ahead[1][done : done + span]
+        done += span
+        total = leave(place, block_index[1], back, t0, weights[1], row, totals[i], (span,))[0]
         lower, upper = depart(*total, q, b)
         for c in range(span):
             pieces += [v[:, c * half : (c + 1) * half] for v in (lower, upper)]

time: 921 us -> 945 us (1.026)
  starting transfers between devices: 119 us -> 137 us
  waiting for transfers between devices: 424 us -> 438 us
    ppermute x12, waiting for transfers between devices: 240 us -> 257 us  [permute(): return lax.ppermute(values, ('parts', 'fft'), pairs)]
    all_to_all x15 -> x16, starting transfers between devices: 100 us -> 112 us  [exchange(): lax.all_to_all(values, ('parts', 'fft'), split_axis=0, concat_axis=0, axi...]
    all_to_all x15 -> x16, waiting for transfers between devices: 184 us -> 180 us  [exchange(): lax.all_to_all(values, ('parts', 'fft'), split_axis=0, concat_axis=0, axi...]
  transfers between devices with their start and end apart: 27 -> 28, of which waited for: 23 -> 22; matrix products, arithmetic and copies ran while one was open for 4% -> 4% of each run, Pallas kernels for 32% -> 29%
where the time goes in v6:
time: 945 us; the launch traced here: 935 us
  waiting for transfers between devices  438 us (46%)
  Pallas kernels  308 us (33%)
  starting transfers between devices  137 us (14%)
  local copies, waits for them, and re-layouts  25.6 us (3%)
  other arithmetic  25.2 us (3%)
    pallas_call x18, Pallas kernels, call(): pl.pallas_call(kernel, out_shape=[jax.ShapeDtypeStruct(o, jnp.float32) fo...  308 us
    ppermute x12, waiting for transfers between devices, permute(): return lax.ppermute(values, ('parts', 'fft'), pairs)  257 us
    all_to_all x16, waiting for transfers between devices, exchange(): lax.all_to_all(values, ('parts', 'fft'), split_axis=0, concat_axis=0, axi...  180 us
    all_to_all x16, starting transfers between devices, exchange(): lax.all_to_all(values, ('parts', 'fft'), split_axis=0, concat_axis=0, axi...  112 us
    ppermute x12, starting transfers between devices, permute(): return lax.ppermute(values, ('parts', 'fft'), pairs)  25.2 us
  transfers between devices with their start and end apart: 28, of which 22 were waited for; matrix products, arithmetic and copies ran while one was open for 4% of the time, Pallas kernels for 29%

profile of v6, /device:TPU:3, one launch (start us, length us, event | category | flops | bytes accessed | tf_op | source)
XLA Modules:
  0.0 934.7 jit_solution(15511508730836074536)
XLA Ops:
  10.0 16.8 %collective-permute-done = f32[4,16,4096]{2,1,0:T(8,128)S(1)} collective-permute-done((f32[4,16,4096]{2,1,0:T(8,128)S(1)}, f32[4,16,4096]{2,1,0:T(8,128)S(1)}, u32[]{:S(2)}, u32[]{:S(2)}) %collective-permute-start) | collective-permute-done | bytes 1048608 | tf_op jit(solution)/shard_map/ppermute | solution.py:599
  43.4 52.8 %collective-permute-done.1 = f32[12,16,4096]{2,1,0:T(8,128)} collective-permute-done((f32[12,16,4096]{2,1,0:T(8,128)}, f32[12,16,4096]{2,1,0:T(8,128)}, u32[]{:S(2)}, u32[]{:S(2)}) %collective-permute-start.1) | collective-permute-done | bytes 3145760 | tf_op jit(solution)/shard_map/ppermute | solution.py:599
  97.2 16.3 %shard_map.89 = (f32[16,8,32,128]{3,2,1,0:T(8,128)}, f32[16,2,32,128]{3,2,1,0:T(8,128)}) custom-call(s32[2]{0:T(128)} %pad_add_fusion.place, s32[32,2]{1,0:T(8,128)} %copy.17.index, f32[4,16,4096]{2,1,0:T(8,128)} %get-tuple-element.58.own, f32[4,16,4096]{2,1,0:T(8,128)} %copy-done.20, bf16[32,256,128]{2,1,0:T(8,128)(2,1)} %get-tuple-element.142.whi, ...), custom_call_target="tpu_custom_call" | custom-call | flops 1207959552 | bytes 13107464 | tf_op jit(solution)/shard_map/pallas_call | solution.py:465
  126.2 41.8 %collective-permute-done.3.other = f32[4,16,4096]{2,1,0:T(8,128)} collective-permute-done((f32[4,16,4096]{2,1,0:T(8,128)S(1)}, f32[4,16,4096]{2,1,0:T(8,128)}, u32[]{:S(2)}, u32[]{:S(2)}) %collective-permute-start.3) | collective-permute-done | bytes 1048608 | tf_op jit(solution)/shard_map/ppermute | solution.py:599
  167.9 16.3 %shard_map.90 = (f32[16,8,32,128]{3,2,1,0:T(8,128)}, f32[16,2,32,128]{3,2,1,0:T(8,128)}) custom-call(s32[2]{0:T(128)} %pad_add_fusion.place, s32[32,2]{1,0:T(8,128)} %copy.17.index, f32[4,16,4096]{2,1,0:T(8,128)} %get-tuple-element.62.own, f32[4,16,4096]{2,1,0:T(8,128)} %collective-permute-done.3.other, bf16[32,256,128]{2,1,0:T(8,128)(2,1)} %get-tuple-element.142.whi, ...), custom_call_target="tpu_custom_call" | custom-call | flops 1207959552 | bytes 13107464 | tf_op jit(solution)/shard_map/pallas_call | solution.py:465
  193.8 16.3 %shard_map.82 = (f32[16,8,32,128]{3,2,1,0:T(8,128)}, f32[16,2,32,128]{3,2,1,0:T(8,128)}) custom-call(s32[2]{0:T(128)} %pad_add_fusion.place, s32[32,2]{1,0:T(8,128)} %copy.18.index, f32[4,16,4096]{2,1,0:T(8,128)} %get-tuple-element.58.own, f32[4,16,4096]{2,1,0:T(8,128)} %copy-done.20, bf16[32,256,128]{2,1,0:T(8,128)(2,1)} %get-tuple-element.141.whi, ...), custom_call_target="tpu_custom_call" | custom-call | flops 1207959552 | bytes 13107464 | tf_op jit(solution)/shard_map/pallas_call | solution.py:465
  232.2 40.8 %collective-permute-done.4.other = f32[4,16,4096]{2,1,0:T(8,128)} collective-permute-done((f32[4,16,4096]{2,1,0:T(8,128)S(1)}, f32[4,16,4096]{2,1,0:T(8,128)}, u32[]{:S(2)}, u32[]{:S(2)}) %collective-permute-start.4) | collective-permute-done | bytes 1048608 | tf_op jit(solution)/shard_map/ppermute | solution.py:599
  273.0 16.3 %shard_map.91 = (f32[16,8,32,128]{3,2,1,0:T(8,128)}, f32[16,2,32,128]{3,2,1,0:T(8,128)}) custom-call(s32[2]{0:T(128)} %pad_add_fusion.place, s32[32,2]{1,0:T(8,128)} %copy.17.index, f32[4,16,4096]{2,1,0:T(8,128)} %get-tuple-element.66.own, f32[4,16,4096]{2,1,0:T(8,128)} %collective-permute-done.4.other, bf16[32,256,128]{2,1,0:T(8,128)(2,1)} %get-tuple-element.142.whi, ...), custom_call_target="tpu_custom_call" | custom-call | flops 1207959552 | bytes 13107464 | tf_op jit(solution)/shard_map/pallas_call | solution.py:465
  299.2 16.3 %shard_map.83 = (f32[16,8,32,128]{3,2,1,0:T(8,128)}, f32[16,2,32,128]{3,2,1,0:T(8,128)}) custom-call(s32[2]{0:T(128)} %pad_add_fusion.place, s32[32,2]{1,0:T(8,128)} %copy.18.index, f32[4,16,4096]{2,1,0:T(8,128)} %get-tuple-element.62.own, f32[4,16,4096]{2,1,0:T(8,128)} %collective-permute-done.3.other, bf16[32,256,128]{2,1,0:T(8,128)(2,1)} %get-tuple-element.141.whi, ...), custom_call_target="tpu_custom_call" | custom-call | flops 1207959552 | bytes 13107464 | tf_op jit(solution)/shard_map/pallas_call | solution.py:465
  315.5 10.4 %all-to-all-done.9.refs_2_ = f32[16,8,32,128]{3,2,1,0:T(8,128)} async-done(((f32[16,8,32,128]{3,2,1,0:T(8,128)}), f32[16,8,32,128]{3,2,1,0:T(8,128)}, u32[]{:S(2)}, u32[]{:S(2)}) %all-to-all-start.9) | async-done | bytes 2097184 | tf_op jit(solution)/shard_map/all_to_all | solution.py:585
  338.1 41.1 %collective-permute-done.5.other = f32[4,16,4096]{2,1,0:T(8,128)S(1)} collective-permute-done((f32[4,16,4096]{2,1,0:T(8,128)S(1)}, f32[4,16,4096]{2,1,0:T(8,128)S(1)}, u32[]{:S(2)}, u32[]{:S(2)}) %collective-permute-start.5) | collective-permute-done | bytes 1048608 | tf_op jit(solution)/shard_map/ppermute | solution.py:599
  380.2 16.3 %shard_map.92 = (f32[16,8,32,128]{3,2,1,0:T(8,128)}, f32[16,2,32,128]{3,2,1,0:T(8,128)}) custom-call(s32[2]{0:T(128)} %pad_add_fusion.place, s32[32,2]{1,0:T(8,128)} %copy.17.index, f32[4,16,4096]{2,1,0:T(8,128)} %get-tuple-element.70.own, f32[4,16,4096]{2,1,0:T(8,128)} %copy-done.21, bf16[32,256,128]{2,1,0:T(8,128)(2,1)} %get-tuple-element.142.whi, ...), custom_call_target="tpu_custom_call" | custom-call | flops 1207959552 | bytes 13107464 | tf_op jit(solution)/shard_map/pallas_call | solution.py:465
  406.1 16.3 %shard_map.85 = (f32[16,8,32,128]{3,2,1,0:T(8,128)}, f32[16,2,32,128]{3,2,1,0:T(8,128)}) custom-call(s32[2]{0:T(128)} %pad_add_fusion.place, s32[32,2]{1,0:T(8,128)} %copy.18.index, f32[4,16,4096]{2,1,0:T(8,128)} %get-tuple-element.70.own, f32[4,16,4096]{2,1,0:T(8,128)} %copy-done.21, bf16[32,256,128]{2,1,0:T(8,128)(2,1)} %get-tuple-element.141.whi, ...), custom_call_target="tpu_custom_call" | custom-call | flops 1207959552 | bytes 13107464 | tf_op jit(solution)/shard_map/pallas_call | solution.py:465
  422.4 10.4 %all-to-all-done.10.refs_3_ = f32[16,8,32,128]{3,2,1,0:T(8,128)} async-done(((f32[16,8,32,128]{3,2,1,0:T(8,128)}), f32[16,8,32,128]{3,2,1,0:T(8,128)}, u32[]{:S(2)}, u32[]{:S(2)}) %all-to-all-start.10) | async-done | bytes 2097184 | tf_op jit(solution)/shard_map/all_to_all | solution.py:585
  438.8 16.3 %shard_map.84 = (f32[16,8,32,128]{3,2,1,0:T(8,128)}, f32[16,2,32,128]{3,2,1,0:T(8,128)}) custom-call(s32[2]{0:T(128)} %pad_add_fusion.place, s32[32,2]{1,0:T(8,128)} %copy.18.index, f32[4,16,4096]{2,1,0:T(8,128)} %get-tuple-element.66.own, f32[4,16,4096]{2,1,0:T(8,128)} %collective-permute-done.4.other, bf16[32,256,128]{2,1,0:T(8,128)(2,1)} %get-tuple-element.141.whi, ...), custom_call_target="tpu_custom_call" | custom-call | flops 1207959552 | bytes 13107464 | tf_op jit(solution)/shard_map/pallas_call | solution.py:465
  455.1 10.2 %all-to-all-done.3.refs_3_ = f32[16,8,32,128]{3,2,1,0:T(8,128)S(1)} async-done(((f32[16,8,32,128]{3,2,1,0:T(8,128)}), f32[16,8,32,128]{3,2,1,0:T(8,128)S(1)}, u32[]{:S(2)}, u32[]{:S(2)}) %all-to-all-start.3) | async-done | bytes 2097184 | tf_op jit(solution)/shard_map/all_to_all | solution.py:585
  472.1 20.9 %shard_map.93 = (f32[16,4,128,128]{3,2,1,0:T(8,128)}, f32[16,4,128,128]{3,2,1,0:T(8,128)}) custom-call(f32[16,8,32,128]{3,2,1,0:T(8,128)} %copy-done.2, f32[16,8,32,128]{3,2,1,0:T(8,128)} %all-to-all-done.8.refs_1_, f32[16,8,32,128]{3,2,1,0:T(8,128)} %all-to-all-done.9.refs_2_, f32[16,8,32,128]{3,2,1,0:T(8,128)} %all-to-all-done.10.refs_3_, ...), custom_call_target="tpu_custom_call" | custom-call | flops 3221225472 | bytes 20971520 | tf_op jit(solution)/shard_map/pallas_call | solution.py:465
  506.0 20.9 %shard_map.86 = (f32[16,4,128,128]{3,2,1,0:T(8,128)}, f32[16,4,128,128]{3,2,1,0:T(8,128)}) custom-call(f32[16,8,32,128]{3,2,1,0:T(8,128)} %copy-done.3, f32[16,8,32,128]{3,2,1,0:T(8,128)} %copy-done.4, f32[16,8,32,128]{3,2,1,0:T(8,128)} %all-to-all-done.2.refs_2_, f32[16,8,32,128]{3,2,1,0:T(8,128)} %copy-done.5, ...), custom_call_target="tpu_custom_call" | custom-call | flops 3221225472 | bytes 20971520 | tf_op jit(solution)/shard_map/pallas_call | solution.py:465
  527.0 33.4 %all-to-all-done.11.fields = f32[16,4,128,128]{3,2,1,0:T(8,128)} async-done(((f32[16,4,128,128]{3,2,1,0:T(8,128)}), f32[16,4,128,128]{3,2,1,0:T(8,128)}, u32[]{:S(2)}, u32[]{:S(2)}) %all-to-all-start.11) | async-done | bytes 4194336 | tf_op jit(solution)/shard_map/all_to_all | solution.py:585
  567.5 16.4 %shard_map.94 = f32[16,2,128,128]{3,2,1,0:T(8,128)} custom-call(f32[16,4,128,128]{3,2,1,0:T(8,128)} %all-to-all-done.11.fields, bf16[16,256,256]{2,1,0:T(8,128)(2,1)} %constant.36.clone.mhi, bf16[16,256,256]{2,1,0:T(8,128)(2,1)} %constant.37.clone.mlo), custom_call_target="tpu_custom_call" | custom-call | flops 2415919104 | bytes 10485760 | tf_op jit(solution)/shard_map/pallas_call | solution.py:465
  583.9 38.1 %all-to-all-done.4.fields = f32[16,4,128,128]{3,2,1,0:T(8,128)} async-done(((f32[16,4,128,128]{3,2,1,0:T(8,128)}), f32[16,4,128,128]{3,2,1,0:T(8,128)}, u32[]{:S(2)}, u32[]{:S(2)}) %all-to-all-start.4) | async-done | bytes 4194336 | tf_op jit(solution)/shard_map/all_to_all | solution.py:585
  628.3 16.4 %shard_map.87 = f32[16,2,128,128]{3,2,1,0:T(8,128)} custom-call(f32[16,4,128,128]{3,2,1,0:T(8,128)} %all-to-all-done.4.fields, bf16[16,256,256]{2,1,0:T(8,128)(2,1)} %constant.36.clone.mhi, bf16[16,256,256]{2,1,0:T(8,128)(2,1)} %constant.37.clone.mlo), custom_call_target="tpu_custom_call" | custom-call | flops 2415919104 | bytes 10485760 | tf_op jit(solution)/shard_map/pallas_call | solution.py:465
  644.7 10.0 %all-to-all-done.12.back = f32[16,2,128,128]{3,2,1,0:T(8,128)S(1)} async-done(((f32[16,2,128,128]{3,2,1,0:T(8,128)}), f32[16,2,128,128]{3,2,1,0:T(8,128)S(1)}, u32[]{:S(2)}, u32[]{:S(2)}) %all-to-all-start.12) | async-done | bytes 2097184 | tf_op jit(solution)/shard_map/all_to_all | solution.py:585
  662.3 16.9 %shard_map.95 = f32[16,4,128,128]{3,2,1,0:T(8,128)} custom-call(f32[16,2,128,128]{3,2,1,0:T(8,128)} %copy-done.1, f32[16,4,128,128]{3,2,1,0:T(8,128)} %get-tuple-element.82.kept, bf16[16,256,256]{2,1,0:T(8,128)(2,1)} %constant.34.clone.refs_4_.mhi, bf16[16,256,256]{2,1,0:T(8,128)(2,1)} %constant.35.clone.refs_5_.mlo), custom_call_target="tpu_custom_call" | custom-call | flops 1610612736 | bytes 14680064 | tf_op jit(solution)/shard_map/pallas_call | solution.py:465
  697.6 16.5 %shard_map.88 = (f32[16,4,64,128]{3,2,1,0:T(8,128)}, f32[16,4,32,128]{3,2,1,0:T(8,128)}, f32[16,4,32,128]{3,2,1,0:T(8,128)}) custom-call(f32[16,2,128,128]{3,2,1,0:T(8,128)} %copy-done, f32[16,4,128,128]{3,2,1,0:T(8,128)} %get-tuple-element.73.kept, bf16[16,256,256]{2,1,0:T(8,128)(2,1)} %constant.34.clone.refs_4_.mhi, ...), custom_call_target="tpu_custom_call" | custom-call | flops 1610612736 | bytes 14680064 | tf_op jit(solution)/shard_map/pallas_call | solution.py:465
  714.1 37.8 %all-to-all-done.13.back = f32[16,4,128,128]{3,2,1,0:T(8,128)} async-done(((f32[16,4,128,128]{3,2,1,0:T(8,128)}), f32[16,4,128,128]{3,2,1,0:T(8,128)}, u32[]{:S(2)}, u32[]{:S(2)}) %all-to-all-start.13) | async-done | bytes 4194336 | tf_op jit(solution)/shard_map/all_to_all | solution.py:585
  758.2 21.7 %shard_map.96 = (f32[2,32,4096]{2,1,0:T(8,128)}, f32[2,32,4096]{2,1,0:T(8,128)}, f32[2,16,4096]{2,1,0:T(8,128)}, f32[2,16,4096]{2,1,0:T(8,128)}, f32[2,16,4096]{2,1,0:T(8,128)}, /*index=5*/f32[2,16,4096]{2,1,0:T(8,128)}) custom-call(s32[2]{0:T(128)} %pad_add_fusion.place, s32[32,2]{1,0:T(8,128)} %copy.17.index, f32[16,4,128,128]{3,2,1,0:T(8,128)} %all-to-all-done.13.back, ...), custom_call_target="tpu_custom_call" | custom-call | flops 2415919104 | bytes 18874632 | tf_op jit(solution)/shard_map/pallas_call | solution.py:465
  786.0 17.6 %shard_map.97 = (f32[2,32,4096]{2,1,0:T(8,128)}, f32[2,32,4096]{2,1,0:T(8,128)}) custom-call(s32[2]{0:T(128)} %pad_add_fusion.place, s32[32,2]{1,0:T(8,128)} %copy.18.index, f32[16,4,64,128]{3,2,1,0:T(8,128)} %copy-done.6, bf16[32,256,128]{2,1,0:T(8,128)(2,1)} %get-tuple-element.141.whi, bf16[32,256,128]{2,1,0:T(8,128)(2,1)} %get-tuple-element.114.wlo, ...), custom_call_target="tpu_custom_call" | custom-call | flops 1207959552 | bytes 15728904 | tf_op jit(solution)/shard_map/pallas_call | solution.py:465
  815.0 37.5 %collective-permute-done.6 = f32[2,32,4096]{2,1,0:T(8,128)S(1)} collective-permute-done((f32[2,32,4096]{2,1,0:T(8,128)}, f32[2,32,4096]{2,1,0:T(8,128)S(1)}, u32[]{:S(2)}, u32[]{:S(2)}) %collective-permute-start.6) | collective-permute-done | bytes 1048608 | tf_op jit(solution)/shard_map/ppermute | solution.py:599
  866.4 15.4 %shard_map.98 = (f32[2,16,4096]{2,1,0:T(8,128)}, f32[2,16,4096]{2,1,0:T(8,128)}) custom-call(s32[2]{0:T(128)} %pad_add_fusion.place, s32[32,2]{1,0:T(8,128)} %copy.18.index, f32[16,4,32,128]{3,2,1,0:T(8,128)} %copy-done.19, bf16[32,256,128]{2,1,0:T(8,128)(2,1)} %get-tuple-element.141.whi, bf16[32,256,128]{2,1,0:T(8,128)(2,1)} %get-tuple-element.114.wlo, ...), custom_call_target="tpu_custom_call" | custom-call | flops 603979776 | bytes 12058888 | tf_op jit(solution)/shard_map/pallas_call | solution.py:465
  888.6 15.4 %shard_map.99 = (f32[2,16,4096]{2,1,0:T(8,128)}, f32[2,16,4096]{2,1,0:T(8,128)}) custom-call(s32[2]{0:T(128)} %pad_add_fusion.place, s32[32,2]{1,0:T(8,128)} %copy.18.index, f32[16,4,32,128]{3,2,1,0:T(8,128)} %copy-done.18, bf16[32,256,128]{2,1,0:T(8,128)(2,1)} %get-tuple-element.141.whi, bf16[32,256,128]{2,1,0:T(8,128)(2,1)} %get-tuple-element.114.wlo, ...), custom_call_target="tpu_custom_call" | custom-call | flops 603979776 | bytes 12058888 | tf_op jit(solution)/shard_map/pallas_call | solution.py:465
  911.9 17.8 %collective-permute-done.10 = f32[2,16,4096]{2,1,0:T(8,128)S(1)} collective-permute-done((f32[2,16,4096]{2,1,0:T(8,128)}, f32[2,16,4096]{2,1,0:T(8,128)S(1)}, u32[]{:S(2)}, u32[]{:S(2)}) %collective-permute-start.10) | collective-permute-done | bytes 524320 | tf_op jit(solution)/shard_map/ppermute | solution.py:599
  (123 shorter events, 226.4 us)
Async XLA Ops:
  2.7 24.1 %collective-permute-start = (f32[4,16,4096]{2,1,0:T(8,128)S(1)}, f32[4,16,4096]{2,1,0:T(8,128)S(1)}, u32[]{:S(2)}, u32[]{:S(2)}) collective-permute-start(f32[4,16,4096]{2,1,0:T(8,128)S(1)} %fusion.7), channel_id=1, source_target_pairs={{0,16},{1,17},{2,18},{3,19},{4,20},{5,21},{6,22},{7,23},{8,24},{9,... | collective-permute-start | bytes 3145736 | tf_op jit(solution)/shard_map/ppermute | solution.py:599
  27.8 68.4 %collective-permute-start.1 = (f32[12,16,4096]{2,1,0:T(8,128)}, f32[12,16,4096]{2,1,0:T(8,128)}, u32[]{:S(2)}, u32[]{:S(2)}) collective-permute-start(f32[12,16,4096]{2,1,0:T(8,128)} %pad_maximum_fusion), channel_id=1, source_target_pairs={{0,16},{1,17},{2,18},{3,19},{4,20},{5,21},{6,22},{7,23},{8,24},{9,... | collective-permute-start | bytes 9437192 | tf_op jit(solution)/shard_map/ppermute | solution.py:599
  31.9 64.3 %collective-permute-start.2 = (f32[4,16,4096]{2,1,0:T(8,128)S(1)}, f32[4,16,4096]{2,1,0:T(8,128)S(1)}, u32[]{:S(2)}, u32[]{:S(2)}) collective-permute-start(f32[4,16,4096]{2,1,0:T(8,128)S(1)} %get-tuple-element.135), channel_id=1, source_target_pairs={{0,8},{1,9},{2,10},{3,11},{4,12},{5,13},{6,14},{7,15},{8,0},{9,1},... | collective-permute-start | bytes 3145736 | tf_op jit(solution)/shard_map/ppermute | solution.py:599
  113.5 70.7 %all-to-all-start.7 = ((f32[16,8,32,128]{3,2,1,0:T(8,128)}), f32[16,8,32,128]{3,2,1,0:T(8,128)S(1)}, u32[]{:S(2)}, u32[]{:S(2)}) async-start(f32[16,8,32,128]{3,2,1,0:T(8,128)} %get-tuple-element.77), calls=%async_computation.7 | async-start | bytes 4194304 | tf_op jit(solution)/shard_map/all_to_all | solution.py:585
  123.9 44.1 %collective-permute-start.3 = (f32[4,16,4096]{2,1,0:T(8,128)S(1)}, f32[4,16,4096]{2,1,0:T(8,128)}, u32[]{:S(2)}, u32[]{:S(2)}) collective-permute-start(f32[4,16,4096]{2,1,0:T(8,128)S(1)} %get-tuple-element.60), channel_id=1, source_target_pairs={{0,8},{1,9},{2,10},{3,11},{4,12},{5,13},{6,14},{7,15},{8,0},{9,1},... | collective-permute-start | bytes 3145736 | tf_op jit(solution)/shard_map/ppermute | solution.py:599
  184.3 35.6 %all-to-all-start.8 = ((f32[16,8,32,128]{3,2,1,0:T(8,128)}), f32[16,8,32,128]{3,2,1,0:T(8,128)}, u32[]{:S(2)}, u32[]{:S(2)}) async-start(f32[16,8,32,128]{3,2,1,0:T(8,128)} %get-tuple-element.78), calls=%async_computation.8 | async-start | bytes 4194304 | tf_op jit(solution)/shard_map/all_to_all | solution.py:585
  219.9 69.5 %all-to-all-start = ((f32[16,8,32,128]{3,2,1,0:T(8,128)}), f32[16,8,32,128]{3,2,1,0:T(8,128)S(1)}, u32[]{:S(2)}, u32[]{:S(2)}) async-start(f32[16,8,32,128]{3,2,1,0:T(8,128)} %get-tuple-element.61), calls=%async_computation | async-start | bytes 4194304 | tf_op jit(solution)/shard_map/all_to_all | solution.py:585
  229.0 44.0 %collective-permute-start.4 = (f32[4,16,4096]{2,1,0:T(8,128)S(1)}, f32[4,16,4096]{2,1,0:T(8,128)}, u32[]{:S(2)}, u32[]{:S(2)}) collective-permute-start(f32[4,16,4096]{2,1,0:T(8,128)S(1)} %get-tuple-element.64), channel_id=1, source_target_pairs={{0,8},{1,9},{2,10},{3,11},{4,12},{5,13},{6,14},{7,15},{8,0},{9,1},... | collective-permute-start | bytes 3145736 | tf_op jit(solution)/shard_map/ppermute | solution.py:599
  289.4 26.2 %copy-start.3 = (f32[16,8,32,128]{3,2,1,0:T(8,128)}, f32[16,8,32,128]{3,2,1,0:T(8,128)S(1)}, u32[]{:S(2)}) copy-start(f32[16,8,32,128]{3,2,1,0:T(8,128)S(1)} %all-to-all-done.refs_0_) | copy-start | bytes 6291460
  289.4 36.6 %all-to-all-start.9 = ((f32[16,8,32,128]{3,2,1,0:T(8,128)}), f32[16,8,32,128]{3,2,1,0:T(8,128)}, u32[]{:S(2)}, u32[]{:S(2)}) async-start(f32[16,8,32,128]{3,2,1,0:T(8,128)} %get-tuple-element.79), calls=%async_computation.9 | async-start | bytes 4194304 | tf_op jit(solution)/shard_map/all_to_all | solution.py:585
  325.9 70.6 %all-to-all-start.1 = ((f32[16,8,32,128]{3,2,1,0:T(8,128)}), f32[16,8,32,128]{3,2,1,0:T(8,128)S(1)}, u32[]{:S(2)}, u32[]{:S(2)}) async-start(f32[16,8,32,128]{3,2,1,0:T(8,128)} %get-tuple-element.65), calls=%async_computation.1 | async-start | bytes 4194304 | tf_op jit(solution)/shard_map/all_to_all | solution.py:585
  334.9 44.3 %collective-permute-start.5 = (f32[4,16,4096]{2,1,0:T(8,128)S(1)}, f32[4,16,4096]{2,1,0:T(8,128)S(1)}, u32[]{:S(2)}, u32[]{:S(2)}) collective-permute-start(f32[4,16,4096]{2,1,0:T(8,128)S(1)} %get-tuple-element.68), channel_id=1, source_target_pairs={{0,8},{1,9},{2,10},{3,11},{4,12},{5,13},{6,14},{7,15},{8,0},{9,1},... | collective-permute-start | bytes 3145736 | tf_op jit(solution)/shard_map/ppermute | solution.py:599
  396.5 25.9 %copy-start.4 = (f32[16,8,32,128]{3,2,1,0:T(8,128)}, f32[16,8,32,128]{3,2,1,0:T(8,128)S(1)}, u32[]{:S(2)}) copy-start(f32[16,8,32,128]{3,2,1,0:T(8,128)S(1)} %all-to-all-done.1.refs_1_) | copy-start | bytes 6291460
  396.5 36.3 %all-to-all-start.10 = ((f32[16,8,32,128]{3,2,1,0:T(8,128)}), f32[16,8,32,128]{3,2,1,0:T(8,128)}, u32[]{:S(2)}, u32[]{:S(2)}) async-start(f32[16,8,32,128]{3,2,1,0:T(8,128)} %get-tuple-element.80), calls=%async_computation.10 | async-start | bytes 4194304 | tf_op jit(solution)/shard_map/all_to_all | solution.py:585
  432.8 32.5 %all-to-all-start.3 = ((f32[16,8,32,128]{3,2,1,0:T(8,128)}), f32[16,8,32,128]{3,2,1,0:T(8,128)S(1)}, u32[]{:S(2)}, u32[]{:S(2)}) async-start(f32[16,8,32,128]{3,2,1,0:T(8,128)} %get-tuple-element.71), calls=%async_computation.3 | async-start | bytes 4194304 | tf_op jit(solution)/shard_map/all_to_all | solution.py:585
  465.3 27.7 %copy-start.5 = (f32[16,8,32,128]{3,2,1,0:T(8,128)}, f32[16,8,32,128]{3,2,1,0:T(8,128)S(1)}, u32[]{:S(2)}) copy-start(f32[16,8,32,128]{3,2,1,0:T(8,128)S(1)} %all-to-all-done.3.refs_3_) | copy-start | bytes 6291460
  465.3 33.4 %all-to-all-start.2 = ((f32[16,8,32,128]{3,2,1,0:T(8,128)}), f32[16,8,32,128]{3,2,1,0:T(8,128)}, u32[]{:S(2)}, u32[]{:S(2)}) async-start(f32[16,8,32,128]{3,2,1,0:T(8,128)} %get-tuple-element.69), calls=%async_computation.2 | async-start | bytes 4194304 | tf_op jit(solution)/shard_map/all_to_all | solution.py:585
  498.7 61.7 %all-to-all-start.11 = ((f32[16,4,128,128]{3,2,1,0:T(8,128)}), f32[16,4,128,128]{3,2,1,0:T(8,128)}, u32[]{:S(2)}, u32[]{:S(2)}) async-start(f32[16,4,128,128]{3,2,1,0:T(8,128)} %get-tuple-element.81), calls=%async_computation.11 | async-start | bytes 8388608 | tf_op jit(solution)/shard_map/all_to_all | solution.py:585
  560.4 61.6 %all-to-all-start.4 = ((f32[16,4,128,128]{3,2,1,0:T(8,128)}), f32[16,4,128,128]{3,2,1,0:T(8,128)}, u32[]{:S(2)}, u32[]{:S(2)}) async-start(f32[16,4,128,128]{3,2,1,0:T(8,128)} %get-tuple-element.72), calls=%async_computation.4 | async-start | bytes 8388608 | tf_op jit(solution)/shard_map/all_to_all | solution.py:585
  622.0 32.8 %all-to-all-start.12 = ((f32[16,2,128,128]{3,2,1,0:T(8,128)}), f32[16,2,128,128]{3,2,1,0:T(8,128)S(1)}, u32[]{:S(2)}, u32[]{:S(2)}) async-start(f32[16,2,128,128]{3,2,1,0:T(8,128)} %shard_map.94), calls=%async_computation.12 | async-start | bytes 4194304 | tf_op jit(solution)/shard_map/all_to_all | solution.py:585
  656.1 32.7 %all-to-all-start.5 = ((f32[16,2,128,128]{3,2,1,0:T(8,128)}), f32[16,2,128,128]{3,2,1,0:T(8,128)S(1)}, u32[]{:S(2)}, u32[]{:S(2)}) async-start(f32[16,2,128,128]{3,2,1,0:T(8,128)} %shard_map.87), calls=%async_computation.5 | async-start | bytes 4194304 | tf_op jit(solution)/shard_map/all_to_all | solution.py:585
  690.2 61.7 %all-to-all-start.13 = ((f32[16,4,128,128]{3,2,1,0:T(8,128)}), f32[16,4,128,128]{3,2,1,0:T(8,128)}, u32[]{:S(2)}, u32[]{:S(2)}) async-start(f32[16,4,128,128]{3,2,1,0:T(8,128)} %shard_map.95), calls=%async_computation.13 | async-start | bytes 8388608 | tf_op jit(solution)/shard_map/all_to_all | solution.py:585
  751.9 32.8 %all-to-all-start.6 = ((f32[16,4,64,128]{3,2,1,0:T(8,128)}), f32[16,4,64,128]{3,2,1,0:T(8,128)S(1)}, u32[]{:S(2)}, u32[]{:S(2)}) async-start(f32[16,4,64,128]{3,2,1,0:T(8,128)} %get-tuple-element.74), calls=%async_computation.6 | async-start | bytes 4194304 | tf_op jit(solution)/shard_map/all_to_all | solution.py:585
  803.6 48.9 %collective-permute-start.6 = (f32[2,32,4096]{2,1,0:T(8,128)}, f32[2,32,4096]{2,1,0:T(8,128)S(1)}, u32[]{:S(2)}, u32[]{:S(2)}) collective-permute-start(f32[2,32,4096]{2,1,0:T(8,128)} %get-tuple-element.90), channel_id=1, source_target_pairs={{0,8},{1,9},{2,10},{3,11},{4,12},{5,13},{6,14},{7,15},{16,0},{17,1... | collective-permute-start | bytes 3145736 | tf_op jit(solution)/shard_map/ppermute | solution.py:599
  805.5 50.1 %collective-permute-start.7 = (f32[2,32,4096]{2,1,0:T(8,128)}, f32[2,32,4096]{2,1,0:T(8,128)}, u32[]{:S(2)}, u32[]{:S(2)}) collective-permute-start(f32[2,32,4096]{2,1,0:T(8,128)} %get-tuple-element.89), channel_id=1, source_target_pairs={{8,16},{9,17},{10,18},{11,19},{12,20},{13,21},{14,22},{15,23},{16,... | collective-permute-start | bytes 3145736 | tf_op jit(solution)/shard_map/ppermute | solution.py:599
  810.2 48.0 %all-to-all-start.14 = ((f32[16,4,32,128]{3,2,1,0:T(8,128)}), f32[16,4,32,128]{3,2,1,0:T(8,128)S(1)}, u32[]{:S(2)}, u32[]{:S(2)}) async-start(f32[16,4,32,128]{3,2,1,0:T(8,128)} %get-tuple-element.96), calls=%async_computation.14 | async-start | bytes 2097152 | tf_op jit(solution)/shard_map/all_to_all | solution.py:585
  859.1 28.5 %all-to-all-start.15 = ((f32[16,4,32,128]{3,2,1,0:T(8,128)}), f32[16,4,32,128]{3,2,1,0:T(8,128)S(1)}, u32[]{:S(2)}, u32[]{:S(2)}) async-start(f32[16,4,32,128]{3,2,1,0:T(8,128)} %get-tuple-element.101), calls=%async_computation.15 | async-start | bytes 2097152 | tf_op jit(solution)/shard_map/all_to_all | solution.py:585
  881.8 25.5 %collective-permute-start.8 = (f32[2,16,4096]{2,1,0:T(8,128)}, f32[2,16,4096]{2,1,0:T(8,128)S(1)}, u32[]{:S(2)}, u32[]{:S(2)}) collective-permute-start(f32[2,16,4096]{2,1,0:T(8,128)} %get-tuple-element.99), channel_id=1, source_target_pairs={{0,8},{1,9},{2,10},{3,11},{4,12},{5,13},{6,14},{7,15},{16,0},{17,1... | collective-permute-start | bytes 1572872 | tf_op jit(solution)/shard_map/ppermute | solution.py:599
  881.9 28.3 %collective-permute-start.9 = (f32[2,16,4096]{2,1,0:T(8,128)}, f32[2,16,4096]{2,1,0:T(8,128)S(1)}, u32[]{:S(2)}, u32[]{:S(2)}) collective-permute-start(f32[2,16,4096]{2,1,0:T(8,128)} %get-tuple-element.98), channel_id=1, source_target_pairs={{8,16},{9,17},{10,18},{11,19},{12,20},{13,21},{14,22},{15,23},{16,... | collective-permute-start | bytes 1572872 | tf_op jit(solution)/shard_map/ppermute | solution.py:599
  904.0 28.5 %copy-start.23 = (f32[2,16,4096]{2,1,0:T(8,128)S(1)}, f32[2,16,4096]{2,1,0:T(8,128)}, u32[]{:S(2)}) copy-start(f32[2,16,4096]{2,1,0:T(8,128)} %get-tuple-element.103) | copy-start | bytes 1572868
  904.0 25.7 %collective-permute-start.10 = (f32[2,16,4096]{2,1,0:T(8,128)}, f32[2,16,4096]{2,1,0:T(8,128)S(1)}, u32[]{:S(2)}, u32[]{:S(2)}) collective-permute-start(f32[2,16,4096]{2,1,0:T(8,128)} %get-tuple-element.104), channel_id=1, source_target_pairs={{0,8},{1,9},{2,10},{3,11},{4,12},{5,13},{6,14},{7,15},{16,0},{17,1... | collective-permute-start | bytes 1572872 | tf_op jit(solution)/shard_map/ppermute | solution.py:599
  904.0 28.5 %collective-permute-start.11 = (f32[2,16,4096]{2,1,0:T(8,128)}, f32[2,16,4096]{2,1,0:T(8,128)S(1)}, u32[]{:S(2)}, u32[]{:S(2)}) collective-permute-start(f32[2,16,4096]{2,1,0:T(8,128)} %get-tuple-element.103), channel_id=1, source_target_pairs={{8,16},{9,17},{10,18},{11,19},{12,20},{13,21},{14,22},{15,23},{16,... | collective-permute-start | bytes 1572872 | tf_op jit(solution)/shard_map/ppermute | solution.py:599
  (23 other events, 95.4 us)

commit v7 on v6

--- a/solution.py
+++ b/solution.py
@@ -638,9 +638,11 @@
     return chunks, rest
 
 
-def depart(near, far, q, b):
-    once = permute(near, CYCLE)
-    twice = permute(far, ACROSS)
+def depart(near, far):
+    return permute(near, CYCLE), permute(far, ACROSS), far
+
+
+def settle(once, twice, far, q, b):
     same = jnp.where(q == b, far, once)
     rest = jnp.where(q == b, once, twice)
     return jnp.where(q == 0, same, rest), jnp.where(q == 0, rest, same)
@@ -663,6 +665,7 @@
         own = after(own, beside)
         for a in range(ANGLES):
             fields, t0 = enter(place, block_index[a], own, along, weights[a], row)
+            beside = fields
             arrived[a].append(exchange(after(fields, further) if a else fields))
             ahead[a].append(t0)
     carried = []
@@ -674,7 +677,7 @@
     pulled = exchange(pull(backs[0], carried[0][1], column, (CHUNKS,))[0])
     totals = leave(place, block_index[0], pulled, ahead[0], weights[0], row, (), spans)
     pulled = pull(backs[1], carried[1][1], column, spans)
-    pieces = []
+    pieces, leaving = [], []
     half = XB // CHUNKS // 2
     done = 0
     for i, span in enumerate(spans):
@@ -682,7 +685,9 @@
         t0 = ahead[1][done : done + span]
         done += span
         total = leave(place, block_index[1], back, t0, weights[1], row, totals[i], (span,))[0]
-        lower, upper = depart(*total, q, b)
+        leaving.append(depart(*total))
+    for span, moved in zip(spans, after(leaving, total)):
+        lower, upper = settle(*moved, q, b)
         for c in range(span):
             pieces += [v[:, c * half : (c + 1) * half] for v in (lower, upper)]
     return jnp.concatenate(pieces, axis=1)

time: 945 us -> 899 us (0.951)
  waiting for transfers between devices: 438 us -> 397 us
    ppermute x12, waiting for transfers between devices: 257 us -> 202 us  [permute(): return lax.ppermute(values, ('parts', 'fft'), pairs)]
    all_to_all x16, waiting for transfers between devices: 180 us -> 195 us  [exchange(): lax.all_to_all(values, ('parts', 'fft'), split_axis=0, concat_axis=0, axi...]
  transfers between devices with their start and end apart: 28 -> 28, of which waited for: 22 -> 21; matrix products, arithmetic and copies ran while one was open for 4% -> 3% of each run, Pallas kernels for 29% -> 33%
where the time goes in v7:
time: 899 us; the launch traced here: 890 us
  waiting for transfers between devices  397 us (44%)
  Pallas kernels  309 us (34%)
  starting transfers between devices  135 us (15%)
  local copies, waits for them, and re-layouts  24.3 us (3%)
  other arithmetic  24.1 us (3%)
    pallas_call x18, Pallas kernels, call(): pl.pallas_call(kernel, out_shape=[jax.ShapeDtypeStruct(o, jnp.float32) fo...  309 us
    ppermute x12, waiting for transfers between devices, permute(): return lax.ppermute(values, ('parts', 'fft'), pairs)  202 us
    all_to_all x16, waiting for transfers between devices, exchange(): lax.all_to_all(values, ('parts', 'fft'), split_axis=0, concat_axis=0, axi...  195 us
    all_to_all x16, starting transfers between devices, exchange(): lax.all_to_all(values, ('parts', 'fft'), split_axis=0, concat_axis=0, axi...  114 us
    ppermute x12, starting transfers between devices, permute(): return lax.ppermute(values, ('parts', 'fft'), pairs)  20.6 us
  transfers between devices with their start and end apart: 28, of which 21 were waited for; matrix products, arithmetic and copies ran while one was open for 3% of the time, Pallas kernels for 33%

profile of v7, /device:TPU:3, one launch (start us, length us, event | category | flops | bytes accessed | tf_op | source)
XLA Modules:
  0.0 889.9 jit_solution(12988141928633189503)
XLA Ops:
  9.9 16.9 %collective-permute-done = f32[4,16,4096]{2,1,0:T(8,128)S(1)} collective-permute-done((f32[4,16,4096]{2,1,0:T(8,128)S(1)}, f32[4,16,4096]{2,1,0:T(8,128)S(1)}, u32[]{:S(2)}, u32[]{:S(2)}) %collective-permute-start) | collective-permute-done | bytes 1048608 | tf_op jit(solution)/shard_map/ppermute | solution.py:599
  43.4 52.8 %collective-permute-done.1 = f32[12,16,4096]{2,1,0:T(8,128)} collective-permute-done((f32[12,16,4096]{2,1,0:T(8,128)}, f32[12,16,4096]{2,1,0:T(8,128)}, u32[]{:S(2)}, u32[]{:S(2)}) %collective-permute-start.1) | collective-permute-done | bytes 3145760 | tf_op jit(solution)/shard_map/ppermute | solution.py:599
  97.2 16.3 %shard_map.89 = (f32[16,8,32,128]{3,2,1,0:T(8,128)}, f32[16,2,32,128]{3,2,1,0:T(8,128)}) custom-call(s32[2]{0:T(128)} %pad_add_fusion.place, s32[32,2]{1,0:T(8,128)} %copy.17.index, f32[4,16,4096]{2,1,0:T(8,128)} %get-tuple-element.67.own, f32[4,16,4096]{2,1,0:T(8,128)} %copy-done.21, bf16[32,256,128]{2,1,0:T(8,128)(2,1)} %get-tuple-element.160.whi, ...), custom_call_target="tpu_custom_call" | custom-call | flops 1207959552 | bytes 13107464 | tf_op jit(solution)/shard_map/pallas_call | solution.py:465
  127.3 16.3 %shard_map.82 = (f32[16,8,32,128]{3,2,1,0:T(8,128)}, f32[16,2,32,128]{3,2,1,0:T(8,128)}) custom-call(s32[2]{0:T(128)} %pad_add_fusion.place, s32[32,2]{1,0:T(8,128)} %copy.18.index, f32[4,16,4096]{2,1,0:T(8,128)} %get-tuple-element.67.own, f32[4,16,4096]{2,1,0:T(8,128)} %copy-done.21, bf16[32,256,128]{2,1,0:T(8,128)(2,1)} %get-tuple-element.159.whi, ...), custom_call_target="tpu_custom_call" | custom-call | flops 1207959552 | bytes 13107464 | tf_op jit(solution)/shard_map/pallas_call | solution.py:465
  143.6 24.5 %collective-permute-done.3.other = f32[4,16,4096]{2,1,0:T(8,128)} collective-permute-done((f32[4,16,4096]{2,1,0:T(8,128)}, f32[4,16,4096]{2,1,0:T(8,128)}, u32[]{:S(2)}, u32[]{:S(2)}) %collective-permute-start.3) | collective-permute-done | bytes 1048608 | tf_op jit(solution)/shard_map/ppermute | solution.py:599
  177.9 16.3 %shard_map.90 = (f32[16,8,32,128]{3,2,1,0:T(8,128)}, f32[16,2,32,128]{3,2,1,0:T(8,128)}) custom-call(s32[2]{0:T(128)} %pad_add_fusion.place, s32[32,2]{1,0:T(8,128)} %copy.17.index, f32[4,16,4096]{2,1,0:T(8,128)} %get-tuple-element.71.own, f32[4,16,4096]{2,1,0:T(8,128)} %collective-permute-done.3.other, bf16[32,256,128]{2,1,0:T(8,128)(2,1)} %get-tuple-element.160.whi, ...), custom_call_target="tpu_custom_call" | custom-call | flops 1207959552 | bytes 13107464 | tf_op jit(solution)/shard_map/pallas_call | solution.py:465
  194.1 10.3 %all-to-all-done.refs_0_ = f32[16,8,32,128]{3,2,1,0:T(8,128)} async-done(((f32[16,8,32,128]{3,2,1,0:T(8,128)}), f32[16,8,32,128]{3,2,1,0:T(8,128)}, u32[]{:S(2)}, u32[]{:S(2)}) %all-to-all-start) | async-done | bytes 2097184 | tf_op jit(solution)/shard_map/all_to_all | solution.py:585
  216.9 16.3 %shard_map.83 = (f32[16,8,32,128]{3,2,1,0:T(8,128)}, f32[16,2,32,128]{3,2,1,0:T(8,128)}) custom-call(s32[2]{0:T(128)} %pad_add_fusion.place, s32[32,2]{1,0:T(8,128)} %copy.18.index, f32[4,16,4096]{2,1,0:T(8,128)} %get-tuple-element.71.own, f32[4,16,4096]{2,1,0:T(8,128)} %collective-permute-done.3.other, bf16[32,256,128]{2,1,0:T(8,128)(2,1)} %get-tuple-element.159.whi, ...), custom_call_target="tpu_custom_call" | custom-call | flops 1207959552 | bytes 13107464 | tf_op jit(solution)/shard_map/pallas_call | solution.py:465
  233.2 24.7 %collective-permute-done.4.other = f32[4,16,4096]{2,1,0:T(8,128)} collective-permute-done((f32[4,16,4096]{2,1,0:T(8,128)}, f32[4,16,4096]{2,1,0:T(8,128)}, u32[]{:S(2)}, u32[]{:S(2)}) %collective-permute-start.4) | collective-permute-done | bytes 1048608 | tf_op jit(solution)/shard_map/ppermute | solution.py:599
  268.0 16.3 %shard_map.91 = (f32[16,8,32,128]{3,2,1,0:T(8,128)}, f32[16,2,32,128]{3,2,1,0:T(8,128)}) custom-call(s32[2]{0:T(128)} %pad_add_fusion.place, s32[32,2]{1,0:T(8,128)} %copy.17.index, f32[4,16,4096]{2,1,0:T(8,128)} %get-tuple-element.75.own, f32[4,16,4096]{2,1,0:T(8,128)} %collective-permute-done.4.other, bf16[32,256,128]{2,1,0:T(8,128)(2,1)} %get-tuple-element.160.whi, ...), custom_call_target="tpu_custom_call" | custom-call | flops 1207959552 | bytes 13107464 | tf_op jit(solution)/shard_map/pallas_call | solution.py:465
  284.3 10.2 %all-to-all-done.1.refs_1_ = f32[16,8,32,128]{3,2,1,0:T(8,128)} async-done(((f32[16,8,32,128]{3,2,1,0:T(8,128)}), f32[16,8,32,128]{3,2,1,0:T(8,128)}, u32[]{:S(2)}, u32[]{:S(2)}) %all-to-all-start.1) | async-done | bytes 2097184 | tf_op jit(solution)/shard_map/all_to_all | solution.py:585
  307.1 16.3 %shard_map.84 = (f32[16,8,32,128]{3,2,1,0:T(8,128)}, f32[16,2,32,128]{3,2,1,0:T(8,128)}) custom-call(s32[2]{0:T(128)} %pad_add_fusion.place, s32[32,2]{1,0:T(8,128)} %copy.18.index, f32[4,16,4096]{2,1,0:T(8,128)} %get-tuple-element.75.own, f32[4,16,4096]{2,1,0:T(8,128)} %collective-permute-done.4.other, bf16[32,256,128]{2,1,0:T(8,128)(2,1)} %get-tuple-element.159.whi, ...), custom_call_target="tpu_custom_call" | custom-call | flops 1207959552 | bytes 13107464 | tf_op jit(solution)/shard_map/pallas_call | solution.py:465
  323.3 24.9 %collective-permute-done.5.other = f32[4,16,4096]{2,1,0:T(8,128)S(1)} collective-permute-done((f32[4,16,4096]{2,1,0:T(8,128)}, f32[4,16,4096]{2,1,0:T(8,128)S(1)}, u32[]{:S(2)}, u32[]{:S(2)}) %collective-permute-start.5) | collective-permute-done | bytes 1048608 | tf_op jit(solution)/shard_map/ppermute | solution.py:599
  358.1 16.3 %shard_map.92 = (f32[16,8,32,128]{3,2,1,0:T(8,128)}, f32[16,2,32,128]{3,2,1,0:T(8,128)}) custom-call(s32[2]{0:T(128)} %pad_add_fusion.place, s32[32,2]{1,0:T(8,128)} %copy.17.index, f32[4,16,4096]{2,1,0:T(8,128)} %get-tuple-element.79.own, f32[4,16,4096]{2,1,0:T(8,128)} %copy-done.22, bf16[32,256,128]{2,1,0:T(8,128)(2,1)} %get-tuple-element.160.whi, ...), custom_call_target="tpu_custom_call" | custom-call | flops 1207959552 | bytes 13107464 | tf_op jit(solution)/shard_map/pallas_call | solution.py:465
  374.4 10.3 %all-to-all-done.2.refs_2_ = f32[16,8,32,128]{3,2,1,0:T(8,128)} async-done(((f32[16,8,32,128]{3,2,1,0:T(8,128)}), f32[16,8,32,128]{3,2,1,0:T(8,128)}, u32[]{:S(2)}, u32[]{:S(2)}) %all-to-all-start.2) | async-done | bytes 2097184 | tf_op jit(solution)/shard_map/all_to_all | solution.py:585
  390.9 16.3 %shard_map.85 = (f32[16,8,32,128]{3,2,1,0:T(8,128)}, f32[16,2,32,128]{3,2,1,0:T(8,128)}) custom-call(s32[2]{0:T(128)} %pad_add_fusion.place, s32[32,2]{1,0:T(8,128)} %copy.18.index, f32[4,16,4096]{2,1,0:T(8,128)} %get-tuple-element.79.own, f32[4,16,4096]{2,1,0:T(8,128)} %copy-done.22, bf16[32,256,128]{2,1,0:T(8,128)(2,1)} %get-tuple-element.159.whi, ...), custom_call_target="tpu_custom_call" | custom-call | flops 1207959552 | bytes 13107464 | tf_op jit(solution)/shard_map/pallas_call | solution.py:465
  424.9 20.9 %shard_map.93 = (f32[16,4,128,128]{3,2,1,0:T(8,128)}, f32[16,4,128,128]{3,2,1,0:T(8,128)}) custom-call(f32[16,8,32,128]{3,2,1,0:T(8,128)} %copy-done.2, f32[16,8,32,128]{3,2,1,0:T(8,128)} %copy-done.3, f32[16,8,32,128]{3,2,1,0:T(8,128)} %copy-done.4, f32[16,8,32,128]{3,2,1,0:T(8,128)} %copy-done.7, bf16[16,256,256]{2,1,0:T(8,128)(2,1)} %constant.34.clone.refs_4_.mhi, ...), custom_call_target="tpu_custom_call" | custom-call | flops 3221225472 | bytes 20971520 | tf_op jit(solution)/shard_map/pallas_call | solution.py:465
  460.0 20.9 %shard_map.86 = (f32[16,4,128,128]{3,2,1,0:T(8,128)}, f32[16,4,128,128]{3,2,1,0:T(8,128)}) custom-call(f32[16,8,32,128]{3,2,1,0:T(8,128)} %all-to-all-done.refs_0_, f32[16,8,32,128]{3,2,1,0:T(8,128)} %all-to-all-done.1.refs_1_, f32[16,8,32,128]{3,2,1,0:T(8,128)} %all-to-all-done.2.refs_2_, f32[16,8,32,128]{3,2,1,0:T(8,128)} %copy-done.6, ...), custom_call_target="tpu_custom_call" | custom-call | flops 3221225472 | bytes 20971520 | tf_op jit(solution)/shard_map/pallas_call | solution.py:465
  480.9 33.4 %all-to-all-done.11.fields = f32[16,4,128,128]{3,2,1,0:T(8,128)} async-done(((f32[16,4,128,128]{3,2,1,0:T(8,128)}), f32[16,4,128,128]{3,2,1,0:T(8,128)}, u32[]{:S(2)}, u32[]{:S(2)}) %all-to-all-start.11) | async-done | bytes 4194336 | tf_op jit(solution)/shard_map/all_to_all | solution.py:585
  521.4 16.4 %shard_map.94 = f32[16,2,128,128]{3,2,1,0:T(8,128)} custom-call(f32[16,4,128,128]{3,2,1,0:T(8,128)} %all-to-all-done.11.fields, bf16[16,256,256]{2,1,0:T(8,128)(2,1)} %constant.36.clone.mhi, bf16[16,256,256]{2,1,0:T(8,128)(2,1)} %constant.37.clone.mlo), custom_call_target="tpu_custom_call" | custom-call | flops 2415919104 | bytes 10485760 | tf_op jit(solution)/shard_map/pallas_call | solution.py:465
  537.8 38.1 %all-to-all-done.4.fields = f32[16,4,128,128]{3,2,1,0:T(8,128)} async-done(((f32[16,4,128,128]{3,2,1,0:T(8,128)}), f32[16,4,128,128]{3,2,1,0:T(8,128)}, u32[]{:S(2)}, u32[]{:S(2)}) %all-to-all-start.4) | async-done | bytes 4194336 | tf_op jit(solution)/shard_map/all_to_all | solution.py:585
  582.2 16.4 %shard_map.87 = f32[16,2,128,128]{3,2,1,0:T(8,128)} custom-call(f32[16,4,128,128]{3,2,1,0:T(8,128)} %all-to-all-done.4.fields, bf16[16,256,256]{2,1,0:T(8,128)(2,1)} %constant.36.clone.mhi, bf16[16,256,256]{2,1,0:T(8,128)(2,1)} %constant.37.clone.mlo), custom_call_target="tpu_custom_call" | custom-call | flops 2415919104 | bytes 10485760 | tf_op jit(solution)/shard_map/pallas_call | solution.py:465
  616.2 16.9 %shard_map.95 = f32[16,4,128,128]{3,2,1,0:T(8,128)} custom-call(f32[16,2,128,128]{3,2,1,0:T(8,128)} %copy-done.1, f32[16,4,128,128]{3,2,1,0:T(8,128)} %get-tuple-element.91.kept, bf16[16,256,256]{2,1,0:T(8,128)(2,1)} %constant.34.clone.refs_4_.mhi, bf16[16,256,256]{2,1,0:T(8,128)(2,1)} %constant.35.clone.refs_5_.mlo), custom_call_target="tpu_custom_call" | custom-call | flops 1610612736 | bytes 14680064 | tf_op jit(solution)/shard_map/pallas_call | solution.py:465
  651.5 16.5 %shard_map.88 = (f32[16,4,64,128]{3,2,1,0:T(8,128)}, f32[16,4,32,128]{3,2,1,0:T(8,128)}, f32[16,4,32,128]{3,2,1,0:T(8,128)}) custom-call(f32[16,2,128,128]{3,2,1,0:T(8,128)} %copy-done, f32[16,4,128,128]{3,2,1,0:T(8,128)} %get-tuple-element.82.kept, bf16[16,256,256]{2,1,0:T(8,128)(2,1)} %constant.34.clone.refs_4_.mhi, ...), custom_call_target="tpu_custom_call" | custom-call | flops 1610612736 | bytes 14680064 | tf_op jit(solution)/shard_map/pallas_call | solution.py:465
  668.0 37.9 %all-to-all-done.13.back = f32[16,4,128,128]{3,2,1,0:T(8,128)} async-done(((f32[16,4,128,128]{3,2,1,0:T(8,128)}), f32[16,4,128,128]{3,2,1,0:T(8,128)}, u32[]{:S(2)}, u32[]{:S(2)}) %all-to-all-start.13) | async-done | bytes 4194336 | tf_op jit(solution)/shard_map/all_to_all | solution.py:585
  712.1 21.6 %shard_map.96 = (f32[2,32,4096]{2,1,0:T(8,128)}, f32[2,32,4096]{2,1,0:T(8,128)}, f32[2,16,4096]{2,1,0:T(8,128)}, f32[2,16,4096]{2,1,0:T(8,128)}, f32[2,16,4096]{2,1,0:T(8,128)}, /*index=5*/f32[2,16,4096]{2,1,0:T(8,128)}) custom-call(s32[2]{0:T(128)} %pad_add_fusion.place, s32[32,2]{1,0:T(8,128)} %copy.17.index, f32[16,4,128,128]{3,2,1,0:T(8,128)} %all-to-all-done.13.back, ...), custom_call_target="tpu_custom_call" | custom-call | flops 2415919104 | bytes 18874632 | tf_op jit(solution)/shard_map/pallas_call | solution.py:465
  744.7 14.3 %all-to-all-done.14.back = f32[16,4,32,128]{3,2,1,0:T(8,128)S(1)} async-done(((f32[16,4,32,128]{3,2,1,0:T(8,128)}), f32[16,4,32,128]{3,2,1,0:T(8,128)S(1)}, u32[]{:S(2)}, u32[]{:S(2)}) %all-to-all-start.14) | async-done | bytes 1048608 | tf_op jit(solution)/shard_map/all_to_all | solution.py:585
  765.6 17.7 %shard_map.97 = (f32[2,32,4096]{2,1,0:T(8,128)}, f32[2,32,4096]{2,1,0:T(8,128)}) custom-call(s32[2]{0:T(128)} %pad_add_fusion.place, s32[32,2]{1,0:T(8,128)} %copy.18.index, f32[16,4,64,128]{3,2,1,0:T(8,128)} %copy-done.5, bf16[32,256,128]{2,1,0:T(8,128)(2,1)} %get-tuple-element.159.whi, bf16[32,256,128]{2,1,0:T(8,128)(2,1)} %get-tuple-element.132.wlo, ...), custom_call_target="tpu_custom_call" | custom-call | flops 1207959552 | bytes 15728904 | tf_op jit(solution)/shard_map/pallas_call | solution.py:465
  789.3 15.4 %shard_map.98 = (f32[2,16,4096]{2,1,0:T(8,128)}, f32[2,16,4096]{2,1,0:T(8,128)}) custom-call(s32[2]{0:T(128)} %pad_add_fusion.place, s32[32,2]{1,0:T(8,128)} %copy.18.index, f32[16,4,32,128]{3,2,1,0:T(8,128)} %copy-done.20, bf16[32,256,128]{2,1,0:T(8,128)(2,1)} %get-tuple-element.159.whi, bf16[32,256,128]{2,1,0:T(8,128)(2,1)} %get-tuple-element.132.wlo, ...), custom_call_target="tpu_custom_call" | custom-call | flops 603979776 | bytes 12058888 | tf_op jit(solution)/shard_map/pallas_call | solution.py:465
  807.6 15.5 %shard_map.99 = (f32[2,16,4096]{2,1,0:T(8,128)}, f32[2,16,4096]{2,1,0:T(8,128)}) custom-call(s32[2]{0:T(128)} %pad_add_fusion.place, s32[32,2]{1,0:T(8,128)} %copy.18.index, f32[16,4,32,128]{3,2,1,0:T(8,128)} %copy-done.19, bf16[32,256,128]{2,1,0:T(8,128)(2,1)} %get-tuple-element.159.whi, bf16[32,256,128]{2,1,0:T(8,128)(2,1)} %get-tuple-element.132.wlo, ...), custom_call_target="tpu_custom_call" | custom-call | flops 603979776 | bytes 12058888 | tf_op jit(solution)/shard_map/pallas_call | solution.py:465
  823.1 31.6 %collective-permute-done.6 = f32[2,32,4096]{2,1,0:T(8,128)} collective-permute-done((f32[2,32,4096]{2,1,0:T(8,128)}, f32[2,32,4096]{2,1,0:T(8,128)}, u32[]{:S(2)}, u32[]{:S(2)}) %collective-permute-start.6) | collective-permute-done | bytes 1048608 | tf_op jit(solution)/shard_map/ppermute | solution.py:599
  865.8 11.2 %collective-permute-done.10 = f32[2,16,4096]{2,1,0:T(8,128)S(1)} collective-permute-done((f32[2,16,4096]{2,1,0:T(8,128)}, f32[2,16,4096]{2,1,0:T(8,128)S(1)}, u32[]{:S(2)}, u32[]{:S(2)}) %collective-permute-start.10) | collective-permute-done | bytes 524320 | tf_op jit(solution)/shard_map/ppermute | solution.py:599
  (127 shorter events, 239.4 us)
Async XLA Ops:
  2.7 24.1 %collective-permute-start = (f32[4,16,4096]{2,1,0:T(8,128)S(1)}, f32[4,16,4096]{2,1,0:T(8,128)S(1)}, u32[]{:S(2)}, u32[]{:S(2)}) collective-permute-start(f32[4,16,4096]{2,1,0:T(8,128)S(1)} %fusion.7), channel_id=1, source_target_pairs={{0,16},{1,17},{2,18},{3,19},{4,20},{5,21},{6,22},{7,23},{8,24},{9,... | collective-permute-start | bytes 3145736 | tf_op jit(solution)/shard_map/ppermute | solution.py:599
  27.8 68.4 %collective-permute-start.1 = (f32[12,16,4096]{2,1,0:T(8,128)}, f32[12,16,4096]{2,1,0:T(8,128)}, u32[]{:S(2)}, u32[]{:S(2)}) collective-permute-start(f32[12,16,4096]{2,1,0:T(8,128)} %pad_maximum_fusion), channel_id=1, source_target_pairs={{0,16},{1,17},{2,18},{3,19},{4,20},{5,21},{6,22},{7,23},{8,24},{9,... | collective-permute-start | bytes 9437192 | tf_op jit(solution)/shard_map/ppermute | solution.py:599
  31.9 64.3 %collective-permute-start.2 = (f32[4,16,4096]{2,1,0:T(8,128)S(1)}, f32[4,16,4096]{2,1,0:T(8,128)S(1)}, u32[]{:S(2)}, u32[]{:S(2)}) collective-permute-start(f32[4,16,4096]{2,1,0:T(8,128)S(1)} %get-tuple-element.153), channel_id=1, source_target_pairs={{0,8},{1,9},{2,10},{3,11},{4,12},{5,13},{6,14},{7,15},{8,0},{9,1},... | collective-permute-start | bytes 3145736 | tf_op jit(solution)/shard_map/ppermute | solution.py:599
  113.5 54.5 %all-to-all-start.7 = ((f32[16,8,32,128]{3,2,1,0:T(8,128)}), f32[16,8,32,128]{3,2,1,0:T(8,128)S(1)}, u32[]{:S(2)}, u32[]{:S(2)}) async-start(f32[16,8,32,128]{3,2,1,0:T(8,128)} %get-tuple-element.86), calls=%async_computation.7 | async-start | bytes 4194304 | tf_op jit(solution)/shard_map/all_to_all | solution.py:585
  124.3 43.7 %collective-permute-start.3 = (f32[4,16,4096]{2,1,0:T(8,128)}, f32[4,16,4096]{2,1,0:T(8,128)}, u32[]{:S(2)}, u32[]{:S(2)}) collective-permute-start(f32[4,16,4096]{2,1,0:T(8,128)} %get-tuple-element.69), channel_id=1, source_target_pairs={{0,8},{1,9},{2,10},{3,11},{4,12},{5,13},{6,14},{7,15},{8,0},{9,1},... | collective-permute-start | bytes 3145736 | tf_op jit(solution)/shard_map/ppermute | solution.py:599
  168.1 36.4 %all-to-all-start = ((f32[16,8,32,128]{3,2,1,0:T(8,128)}), f32[16,8,32,128]{3,2,1,0:T(8,128)}, u32[]{:S(2)}, u32[]{:S(2)}) async-start(f32[16,8,32,128]{3,2,1,0:T(8,128)} %get-tuple-element.70), calls=%async_computation | async-start | bytes 4194304 | tf_op jit(solution)/shard_map/all_to_all | solution.py:585
  204.4 53.4 %all-to-all-start.8 = ((f32[16,8,32,128]{3,2,1,0:T(8,128)}), f32[16,8,32,128]{3,2,1,0:T(8,128)S(1)}, u32[]{:S(2)}, u32[]{:S(2)}) async-start(f32[16,8,32,128]{3,2,1,0:T(8,128)} %get-tuple-element.87), calls=%async_computation.8 | async-start | bytes 4194304 | tf_op jit(solution)/shard_map/all_to_all | solution.py:585
  214.1 43.8 %collective-permute-start.4 = (f32[4,16,4096]{2,1,0:T(8,128)}, f32[4,16,4096]{2,1,0:T(8,128)}, u32[]{:S(2)}, u32[]{:S(2)}) collective-permute-start(f32[4,16,4096]{2,1,0:T(8,128)} %get-tuple-element.73), channel_id=1, source_target_pairs={{0,8},{1,9},{2,10},{3,11},{4,12},{5,13},{6,14},{7,15},{8,0},{9,1},... | collective-permute-start | bytes 3145736 | tf_op jit(solution)/shard_map/ppermute | solution.py:599
  257.9 26.5 %copy-start.3 = (f32[16,8,32,128]{3,2,1,0:T(8,128)}, f32[16,8,32,128]{3,2,1,0:T(8,128)S(1)}, u32[]{:S(2)}) copy-start(f32[16,8,32,128]{3,2,1,0:T(8,128)S(1)} %all-to-all-done.8.refs_1_) | copy-start | bytes 6291460
  257.9 36.7 %all-to-all-start.1 = ((f32[16,8,32,128]{3,2,1,0:T(8,128)}), f32[16,8,32,128]{3,2,1,0:T(8,128)}, u32[]{:S(2)}, u32[]{:S(2)}) async-start(f32[16,8,32,128]{3,2,1,0:T(8,128)} %get-tuple-element.74), calls=%async_computation.1 | async-start | bytes 4194304 | tf_op jit(solution)/shard_map/all_to_all | solution.py:585
  294.6 53.6 %all-to-all-start.9 = ((f32[16,8,32,128]{3,2,1,0:T(8,128)}), f32[16,8,32,128]{3,2,1,0:T(8,128)S(1)}, u32[]{:S(2)}, u32[]{:S(2)}) async-start(f32[16,8,32,128]{3,2,1,0:T(8,128)} %get-tuple-element.88), calls=%async_computation.9 | async-start | bytes 4194304 | tf_op jit(solution)/shard_map/all_to_all | solution.py:585
  304.1 44.1 %collective-permute-start.5 = (f32[4,16,4096]{2,1,0:T(8,128)}, f32[4,16,4096]{2,1,0:T(8,128)S(1)}, u32[]{:S(2)}, u32[]{:S(2)}) collective-permute-start(f32[4,16,4096]{2,1,0:T(8,128)} %get-tuple-element.77), channel_id=1, source_target_pairs={{0,8},{1,9},{2,10},{3,11},{4,12},{5,13},{6,14},{7,15},{8,0},{9,1},... | collective-permute-start | bytes 3145736 | tf_op jit(solution)/shard_map/ppermute | solution.py:599
  348.2 36.5 %all-to-all-start.2 = ((f32[16,8,32,128]{3,2,1,0:T(8,128)}), f32[16,8,32,128]{3,2,1,0:T(8,128)}, u32[]{:S(2)}, u32[]{:S(2)}) async-start(f32[16,8,32,128]{3,2,1,0:T(8,128)} %get-tuple-element.78), calls=%async_computation.2 | async-start | bytes 4194304 | tf_op jit(solution)/shard_map/all_to_all | solution.py:585
  384.7 32.7 %all-to-all-start.10 = ((f32[16,8,32,128]{3,2,1,0:T(8,128)}), f32[16,8,32,128]{3,2,1,0:T(8,128)S(1)}, u32[]{:S(2)}, u32[]{:S(2)}) async-start(f32[16,8,32,128]{3,2,1,0:T(8,128)} %get-tuple-element.89), calls=%async_computation.10 | async-start | bytes 4194304 | tf_op jit(solution)/shard_map/all_to_all | solution.py:585
  418.7 32.7 %all-to-all-start.3 = ((f32[16,8,32,128]{3,2,1,0:T(8,128)}), f32[16,8,32,128]{3,2,1,0:T(8,128)S(1)}, u32[]{:S(2)}, u32[]{:S(2)}) async-start(f32[16,8,32,128]{3,2,1,0:T(8,128)} %get-tuple-element.80), calls=%async_computation.3 | async-start | bytes 4194304 | tf_op jit(solution)/shard_map/all_to_all | solution.py:585
  452.6 61.7 %all-to-all-start.11 = ((f32[16,4,128,128]{3,2,1,0:T(8,128)}), f32[16,4,128,128]{3,2,1,0:T(8,128)}, u32[]{:S(2)}, u32[]{:S(2)}) async-start(f32[16,4,128,128]{3,2,1,0:T(8,128)} %get-tuple-element.90), calls=%async_computation.11 | async-start | bytes 8388608 | tf_op jit(solution)/shard_map/all_to_all | solution.py:585
  514.3 61.6 %all-to-all-start.4 = ((f32[16,4,128,128]{3,2,1,0:T(8,128)}), f32[16,4,128,128]{3,2,1,0:T(8,128)}, u32[]{:S(2)}, u32[]{:S(2)}) async-start(f32[16,4,128,128]{3,2,1,0:T(8,128)} %get-tuple-element.81), calls=%async_computation.4 | async-start | bytes 8388608 | tf_op jit(solution)/shard_map/all_to_all | solution.py:585
  575.9 32.8 %all-to-all-start.12 = ((f32[16,2,128,128]{3,2,1,0:T(8,128)}), f32[16,2,128,128]{3,2,1,0:T(8,128)S(1)}, u32[]{:S(2)}, u32[]{:S(2)}) async-start(f32[16,2,128,128]{3,2,1,0:T(8,128)} %shard_map.94), calls=%async_computation.12 | async-start | bytes 4194304 | tf_op jit(solution)/shard_map/all_to_all | solution.py:585
  610.0 32.7 %all-to-all-start.5 = ((f32[16,2,128,128]{3,2,1,0:T(8,128)}), f32[16,2,128,128]{3,2,1,0:T(8,128)S(1)}, u32[]{:S(2)}, u32[]{:S(2)}) async-start(f32[16,2,128,128]{3,2,1,0:T(8,128)} %shard_map.87), calls=%async_computation.5 | async-start | bytes 4194304 | tf_op jit(solution)/shard_map/all_to_all | solution.py:585
  644.1 61.7 %all-to-all-start.13 = ((f32[16,4,128,128]{3,2,1,0:T(8,128)}), f32[16,4,128,128]{3,2,1,0:T(8,128)}, u32[]{:S(2)}, u32[]{:S(2)}) async-start(f32[16,4,128,128]{3,2,1,0:T(8,128)} %shard_map.95), calls=%async_computation.13 | async-start | bytes 8388608 | tf_op jit(solution)/shard_map/all_to_all | solution.py:585
  705.8 32.8 %all-to-all-start.6 = ((f32[16,4,64,128]{3,2,1,0:T(8,128)}), f32[16,4,64,128]{3,2,1,0:T(8,128)S(1)}, u32[]{:S(2)}, u32[]{:S(2)}) async-start(f32[16,4,64,128]{3,2,1,0:T(8,128)} %get-tuple-element.83), calls=%async_computation.6 | async-start | bytes 4194304 | tf_op jit(solution)/shard_map/all_to_all | solution.py:585
  738.6 27.0 %copy-start.5 = (f32[16,4,64,128]{3,2,1,0:T(8,128)}, f32[16,4,64,128]{3,2,1,0:T(8,128)S(1)}, u32[]{:S(2)}) copy-start(f32[16,4,64,128]{3,2,1,0:T(8,128)S(1)} %all-to-all-done.6.back) | copy-start | bytes 6291460
  738.6 20.5 %all-to-all-start.14 = ((f32[16,4,32,128]{3,2,1,0:T(8,128)}), f32[16,4,32,128]{3,2,1,0:T(8,128)S(1)}, u32[]{:S(2)}, u32[]{:S(2)}) async-start(f32[16,4,32,128]{3,2,1,0:T(8,128)} %get-tuple-element.105), calls=%async_computation.14 | async-start | bytes 2097152 | tf_op jit(solution)/shard_map/all_to_all | solution.py:585
  760.1 46.6 %all-to-all-start.15 = ((f32[16,4,32,128]{3,2,1,0:T(8,128)}), f32[16,4,32,128]{3,2,1,0:T(8,128)S(1)}, u32[]{:S(2)}, u32[]{:S(2)}) async-start(f32[16,4,32,128]{3,2,1,0:T(8,128)} %get-tuple-element.110), calls=%async_computation.15 | async-start | bytes 2097152 | tf_op jit(solution)/shard_map/all_to_all | solution.py:585
  783.2 71.4 %collective-permute-start.6 = (f32[2,32,4096]{2,1,0:T(8,128)}, f32[2,32,4096]{2,1,0:T(8,128)}, u32[]{:S(2)}, u32[]{:S(2)}) collective-permute-start(f32[2,32,4096]{2,1,0:T(8,128)} %get-tuple-element.98), channel_id=1, source_target_pairs={{0,8},{1,9},{2,10},{3,11},{4,12},{5,13},{6,14},{7,15},{16,0},{17,1... | collective-permute-start | bytes 3145736 | tf_op jit(solution)/shard_map/ppermute | solution.py:599
  783.3 73.5 %collective-permute-start.7 = (f32[2,32,4096]{2,1,0:T(8,128)}, f32[2,32,4096]{2,1,0:T(8,128)}, u32[]{:S(2)}, u32[]{:S(2)}) collective-permute-start(f32[2,32,4096]{2,1,0:T(8,128)} %get-tuple-element.114), channel_id=1, source_target_pairs={{8,16},{9,17},{10,18},{11,19},{12,20},{13,21},{14,22},{15,23},{16,... | collective-permute-start | bytes 3145736 | tf_op jit(solution)/shard_map/ppermute | solution.py:599
  804.7 61.1 %collective-permute-start.8 = (f32[2,16,4096]{2,1,0:T(8,128)}, f32[2,16,4096]{2,1,0:T(8,128)S(1)}, u32[]{:S(2)}, u32[]{:S(2)}) collective-permute-start(f32[2,16,4096]{2,1,0:T(8,128)} %get-tuple-element.107), channel_id=1, source_target_pairs={{0,8},{1,9},{2,10},{3,11},{4,12},{5,13},{6,14},{7,15},{16,0},{17,1... | collective-permute-start | bytes 1572872 | tf_op jit(solution)/shard_map/ppermute | solution.py:599
  804.7 61.1 %collective-permute-start.9 = (f32[2,16,4096]{2,1,0:T(8,128)}, f32[2,16,4096]{2,1,0:T(8,128)S(1)}, u32[]{:S(2)}, u32[]{:S(2)}) collective-permute-start(f32[2,16,4096]{2,1,0:T(8,128)} %get-tuple-element.117), channel_id=1, source_target_pairs={{8,16},{9,17},{10,18},{11,19},{12,20},{13,21},{14,22},{15,23},{16,... | collective-permute-start | bytes 1572872 | tf_op jit(solution)/shard_map/ppermute | solution.py:599
  807.6 76.0 %copy-start.26 = (f32[2,32,4096]{2,1,0:T(8,128)S(1)}, f32[2,32,4096]{2,1,0:T(8,128)}, u32[]{:S(2)}) copy-start(f32[2,32,4096]{2,1,0:T(8,128)} %get-tuple-element.114) | copy-start | bytes 3145732
  823.1 54.0 %collective-permute-start.10 = (f32[2,16,4096]{2,1,0:T(8,128)}, f32[2,16,4096]{2,1,0:T(8,128)S(1)}, u32[]{:S(2)}, u32[]{:S(2)}) collective-permute-start(f32[2,16,4096]{2,1,0:T(8,128)} %get-tuple-element.112), channel_id=1, source_target_pairs={{0,8},{1,9},{2,10},{3,11},{4,12},{5,13},{6,14},{7,15},{16,0},{17,1... | collective-permute-start | bytes 1572872 | tf_op jit(solution)/shard_map/ppermute | solution.py:599
  854.7 30.9 %copy-start.23 = (f32[2,16,4096]{2,1,0:T(8,128)S(1)}, f32[2,16,4096]{2,1,0:T(8,128)}, u32[]{:S(2)}) copy-start(f32[2,16,4096]{2,1,0:T(8,128)} %get-tuple-element.117) | copy-start | bytes 1572868
  854.7 28.9 %collective-permute-start.11 = (f32[2,16,4096]{2,1,0:T(8,128)}, f32[2,16,4096]{2,1,0:T(8,128)S(1)}, u32[]{:S(2)}, u32[]{:S(2)}) collective-permute-start(f32[2,16,4096]{2,1,0:T(8,128)} %get-tuple-element.120), channel_id=1, source_target_pairs={{8,16},{9,17},{10,18},{11,19},{12,20},{13,21},{14,22},{15,23},{16,... | collective-permute-start | bytes 1572872 | tf_op jit(solution)/shard_map/ppermute | solution.py:599
  (25 other events, 112.1 us)

commit v8 on v7

--- a/solution.py
+++ b/solution.py
@@ -179,7 +179,10 @@
     lax.fori_loop(0, XA, step, 0)
 
 
-def enter_kernel(place, index, own, other, whi, wlo, mhi, mlo, out, t0, shi, slo, field, xhi, xlo, y):
+def enter_kernel(angles, place, *refs):
+    indices, (own, other), refs = refs[:angles], refs[angles : angles + 2], refs[angles + 2 :]
+    weights, (mhi, mlo, out), refs = refs[: 2 * angles], refs[2 * angles : 2 * angles + 3], refs[2 * angles + 3 :]
+    fronts, (shi, slo, field, xhi, xlo, y) = refs[:angles], refs[angles:]
     half = own.shape[1]
     rows = 2 * half
 
@@ -194,6 +197,16 @@
                 slo[at, :] = low
 
             strips(half, cut)
+
+    for a in range(angles):
+        enter_angle(
+            indices[a], weights[2 * a], weights[2 * a + 1], mhi, mlo,
+            out, 8 * a, fronts[a], shi, slo, field, xhi, xlo, y,
+        )
+
+
+def enter_angle(index, whi, wlo, mhi, mlo, out, base, t0, shi, slo, field, xhi, xlo, y):
+    rows = t0.shape[2]
 
     def rotated(b):
         at = [pl.ds(pl.multiple_of(index[b, s] * BLK, BLK), BLK) for s in range(SLOTS)]
@@ -233,14 +246,14 @@
         for number in range(2):
             values = rows_in(y, pl.multiple_of(number * rows + row, STRIP))
             for b, (re, im) in enumerate(values):
-                out[b, 2 * number, at, :] = re
-                out[b, 2 * number + 1, at, :] = im
+                out[b, base + 2 * number, at, :] = re
+                out[b, base + 2 * number + 1, at, :] = im
 
     strips(rows, backward)
 
     def second_slice(b, carry):
         for channel, value in enumerate(rotated(XA + b)):
-            out[b, 4 + channel] = value
+            out[b, base + 4 + channel] = value
         return carry
 
     lax.fori_loop(0, XA, second_slice, 0)
@@ -263,14 +276,15 @@
             strips(half, inner)
 
 
-def middle_kernel(chunks, *refs):
+def middle_kernel(bases, *refs):
+    chunks = len(bases)
     arrived = refs[:chunks]
     mhi, mlo, out, kept, xhi, xlo, y = refs[chunks:]
 
     def forward(row, places):
         for number in range(2):
             values = [
-                tuple(arrived[c][g, 2 * number + i, at, :] for i in range(2)) for c, g, at in places
+                tuple(arrived[c][g, bases[c] + 2 * number + i, at, :] for i in range(2)) for c, g, at in places
             ]
             columns_out(xhi, xlo, number, row, values)
 
@@ -282,7 +296,7 @@
         wave = columns_in(y, 0, row)
         product = []
         for p, (c, g, at) in enumerate(places):
-            t = arrived[c][g, 4, at, :], arrived[c][g, 5, at, :]
+            t = tuple(arrived[c][g, bases[c] + i, at, :] for i in (4, 5))
             value = times(t, wave[p])
             for i, part in enumerate(value + t):
                 kept[p, i, local, :] = part
@@ -291,7 +305,7 @@
         dwave = columns_in(y, 1, row)
         change = []
         for p, (c, g, at) in enumerate(places):
-            t_re, t_im, d_re, d_im = (arrived[c][g, 4 + i, at, :] for i in range(4))
+            t_re, t_im, d_re, d_im = (arrived[c][g, bases[c] + 4 + i, at, :] for i in range(4))
             p_re, p_im = kept[p, 0, local, :], kept[p, 1, local, :]
             re, im = times((t_re, t_im), dwave[p])
             change.append((re - (d_re * p_im + d_im * p_re), im + (d_re * p_re - d_im * p_im)))
@@ -485,33 +499,33 @@
     ]
 
 
-def enter(place, index, own, other, weights, matrices):
+def enter(place, indices, own, other, weights, matrices):
+    angles = len(indices)
     rows = 2 * own.shape[1]
     scratch = [
         pltpu.VMEM((4 * rows, NB * BLK), jnp.bfloat16),
         pltpu.VMEM((4 * rows, NB * BLK), jnp.bfloat16),
         pltpu.VMEM((XA, 2, rows, LANES), jnp.float32),
     ] + mix_scratch(2 * rows, 2 * LANES)
-    outs = [(XA, 8, rows, LANES), (XA, 2, rows, LANES)]
-    extra = NB * 4 * rows * 256 * 128 * 6
-    return call(
-        enter_kernel,
-        outs,
+    fields, *fronts = call(
+        functools.partial(enter_kernel, angles),
+        [(XA, 8 * angles, rows, LANES)] + [(XA, 2, rows, LANES)] * angles,
         scratch,
-        rows / XB * 2,
-        extra,
+        rows / XB * 2 * angles,
+        NB * 4 * rows * 256 * 128 * 6 * angles,
         place,
-        index,
+        *indices,
         own,
         other,
-        *weights,
+        *[w for pair in weights for w in pair],
         *matrices,
     )
-
-
-def middle(arrived, matrices):
+    return fields, fronts
+
+
+def middle(arrived, bases, matrices):
     return call(
-        functools.partial(middle_kernel, len(arrived)),
+        functools.partial(middle_kernel, bases),
         [(XA, 4, XB, LANES), (XA, 4, XB, LANES)],
         mix_scratch(2 * XB, 2 * LANES),
         4,
@@ -658,34 +672,49 @@
     column = tuple(jnp.asarray(v) for v in split_constant(by_column))
     row = tuple(jnp.asarray(v) for v in split_constant(by_column.transpose(0, 2, 1)))
     weights = [(whi[a], wlo[a]) for a in range(ANGLES)]
-    arrived = [[] for _ in range(ANGLES)]
-    ahead = [[] for _ in range(ANGLES)]
+    angles = range(ANGLES)
+    arrived = [[] for _ in angles]
+    bases = [[] for _ in angles]
+    ahead = [[] for _ in angles]
     for c, (own, along) in enumerate(chunks):
-        further = chunks[c + 1][1] if c + 1 < CHUNKS else ()
         own = after(own, beside)
-        for a in range(ANGLES):
-            fields, t0 = enter(place, block_index[a], own, along, weights[a], row)
-            beside = fields
-            arrived[a].append(exchange(after(fields, further) if a else fields))
-            ahead[a].append(t0)
+        for part in (angles,) if c + 1 < CHUNKS else [[a] for a in angles]:
+            fields, fronts = enter(
+                place, [block_index[a] for a in part], own, along, [weights[a] for a in part], row
+            )
+            fields = exchange(fields)
+            for i, a in enumerate(part):
+                arrived[a].append(fields)
+                bases[a].append(8 * i)
+                ahead[a].append(fronts[i])
     carried = []
-    for a in range(ANGLES):
-        out, kept = middle(arrived[a], column)
+    for a in angles:
+        out, kept = middle(arrived[a], tuple(bases[a]), column)
         carried.append((exchange(out), kept))
     backs = [exchange(detector(out, row)) for out, _ in carried]
-    spans = (CHUNKS // 2, CHUNKS // 4, CHUNKS // 4)
-    pulled = exchange(pull(backs[0], carried[0][1], column, (CHUNKS,))[0])
-    totals = leave(place, block_index[0], pulled, ahead[0], weights[0], row, (), spans)
-    pulled = pull(backs[1], carried[1][1], column, spans)
-    pieces, leaving = [], []
-    half = XB // CHUNKS // 2
-    done = 0
-    for i, span in enumerate(spans):
-        back = exchange(after(pulled[i], totals) if i else pulled[i])
-        t0 = ahead[1][done : done + span]
-        done += span
-        total = leave(place, block_index[1], back, t0, weights[1], row, totals[i], (span,))[0]
-        leaving.append(depart(*total))
+    most, half = CHUNKS // 2, XB // CHUNKS // 2
+    rest = (CHUNKS // 4, CHUNKS // 4)
+    spans = (most,) + rest
+
+    def home(a, back, first, before, spans):
+        t0 = ahead[a][first : first + sum(spans)]
+        return leave(place, block_index[a], back, t0, weights[a], row, before, spans)
+
+    early = pull(backs[0], carried[0][1], column, (most, sum(rest)))
+    late = pull(backs[1], carried[1][1], column, spans)
+    back = exchange(early[0])
+    next_back = exchange(late[0])
+    (start,) = home(0, back, 0, (), (most,))
+    back = exchange(after(early[1], start))
+    totals = home(1, next_back, 0, start, (most,))
+    next_back = exchange(after(late[1], totals))
+    starts = home(0, back, most, (), rest)
+    back = exchange(after(late[2], starts))
+    totals += home(1, next_back, most, starts[0], rest[:1])
+    totals += home(1, back, most + rest[0], starts[1], rest[1:])
+    pieces = []
+    leaving = [depart(*total) for total in totals]
+    total = totals[-1]
     for span, moved in zip(spans, after(leaving, total)):
         lower, upper = settle(*moved, q, b)
         for c in range(span):

time: 899 us -> 946 us (1.052)
  waiting for transfers between devices: 397 us -> 469 us
  starting transfers between devices: 135 us -> 106 us
    ppermute x12, waiting for transfers between devices: 202 us -> 258 us  [permute(): return lax.ppermute(values, ('parts', 'fft'), pairs)]
    all_to_all x16 -> x14, starting transfers between devices: 114 us -> 89.8 us  [exchange(): lax.all_to_all(values, ('parts', 'fft'), split_axis=0, concat_axis=0, axi...]
    all_to_all x16 -> x14, waiting for transfers between devices: 195 us -> 211 us  [exchange(): lax.all_to_all(values, ('parts', 'fft'), split_axis=0, concat_axis=0, axi...]
    select_n x3 -> x0, other arithmetic: 9.93 us -> none  [arrive(): own = jnp.where(q == b, keep, beside)]
    pallas_call x18 -> x16, Pallas kernels: 309 us -> 313 us  [call(): pl.pallas_call(kernel, out_shape=[jax.ShapeDtypeStruct(o, jnp.float32) fo...]
  transfers between devices with their start and end apart: 28 -> 26, of which waited for: 21 -> 21; matrix products, arithmetic and copies ran while one was open for 3% -> 3% of each run, Pallas kernels for 33% -> 32%
where the time goes in v8:
time: 946 us; the launch traced here: 936 us
  waiting for transfers between devices  469 us (50%)
  Pallas kernels  313 us (33%)
  starting transfers between devices  106 us (11%)
  local copies, waits for them, and re-layouts  24.4 us (3%)
  other arithmetic  22.9 us (2%)
    pallas_call x16, Pallas kernels, call(): pl.pallas_call(kernel, out_shape=[jax.ShapeDtypeStruct(o, jnp.float32) fo...  313 us
    ppermute x12, waiting for transfers between devices, permute(): return lax.ppermute(values, ('parts', 'fft'), pairs)  258 us
    all_to_all x14, waiting for transfers between devices, exchange(): lax.all_to_all(values, ('parts', 'fft'), split_axis=0, concat_axis=0, axi...  211 us
    all_to_all x14, starting transfers between devices, exchange(): lax.all_to_all(values, ('parts', 'fft'), split_axis=0, concat_axis=0, axi...  89.8 us
  transfers between devices with their start and end apart: 26, of which 21 were waited for; matrix products, arithmetic and copies ran while one was open for 3% of the time, Pallas kernels for 32%

profile of v8, /device:TPU:3, one launch (start us, length us, event | category | flops | bytes accessed | tf_op | source)
XLA Modules:
  0.0 936.3 jit_solution(12634868530423921585)
XLA Ops:
  10.3 16.9 %collective-permute-done = f32[4,16,4096]{2,1,0:T(8,128)S(1)} collective-permute-done((f32[4,16,4096]{2,1,0:T(8,128)S(1)}, f32[4,16,4096]{2,1,0:T(8,128)S(1)}, u32[]{:S(2)}, u32[]{:S(2)}) %collective-permute-start) | collective-permute-done | bytes 1048608 | tf_op jit(solution)/shard_map/ppermute | solution.py:613
  34.0 62.6 %collective-permute-done.1 = f32[12,16,4096]{2,1,0:T(8,128)} collective-permute-done((f32[12,16,4096]{2,1,0:T(8,128)}, f32[12,16,4096]{2,1,0:T(8,128)}, u32[]{:S(2)}, u32[]{:S(2)}) %collective-permute-start.1) | collective-permute-done | bytes 3145760 | tf_op jit(solution)/shard_map/ppermute | solution.py:613
  105.1 42.0 %collective-permute-done.3.refs_3_ = f32[4,16,4096]{2,1,0:T(8,128)} collective-permute-done((f32[4,16,4096]{2,1,0:T(8,128)}, f32[4,16,4096]{2,1,0:T(8,128)}, u32[]{:S(2)}, u32[]{:S(2)}) %collective-permute-start.3) | collective-permute-done | bytes 1048608 | tf_op jit(solution)/shard_map/ppermute | solution.py:613
  150.1 43.4 %collective-permute-done.4.refs_3_ = f32[4,16,4096]{2,1,0:T(8,128)S(1)} collective-permute-done((f32[4,16,4096]{2,1,0:T(8,128)S(1)}, f32[4,16,4096]{2,1,0:T(8,128)S(1)}, u32[]{:S(2)}, u32[]{:S(2)}) %collective-permute-start.4) | collective-permute-done | bytes 1048608 | tf_op jit(solution)/shard_map/ppermute | solution.py:613
  203.7 38.7 %collective-permute-done.5.refs_2_ = f32[4,16,4096]{2,1,0:T(8,128)S(1)} collective-permute-done((f32[4,16,4096]{2,1,0:T(8,128)S(1)}, f32[4,16,4096]{2,1,0:T(8,128)S(1)}, u32[]{:S(2)}, u32[]{:S(2)}) %collective-permute-start.5) | collective-permute-done | bytes 1048608 | tf_op jit(solution)/shard_map/ppermute | solution.py:613
  243.4 16.2 %shard_map.89 = (f32[16,8,32,128]{3,2,1,0:T(8,128)}, f32[16,2,32,128]{3,2,1,0:T(8,128)}) custom-call(s32[2]{0:T(128)} %pad_add_fusion.place, s32[32,2]{1,0:T(8,128)} %copy.9.refs_0_.index, f32[4,16,4096]{2,1,0:T(8,128)} %get-tuple-element.72.refs_1_, f32[4,16,4096]{2,1,0:T(8,128)} %copy-done.23, ...), custom_call_target="tpu_custom_call" | custom-call | flops 1207959552 | bytes 13107464 | tf_op jit(solution)/shard_map/pallas_call | solution.py:479
  266.4 28.9 %shard_map.82 = (f32[16,16,32,128]{3,2,1,0:T(8,128)}, f32[16,2,32,128]{3,2,1,0:T(8,128)}, f32[16,2,32,128]{3,2,1,0:T(8,128)}) custom-call(s32[2]{0:T(128)} %pad_add_fusion.place, s32[32,2]{1,0:T(8,128)} %copy.9.refs_0_.index, s32[32,2]{1,0:T(8,128)} %copy.18.refs_1_.refs_0_.index, f32[4,16,4096]{2,1,0:T(8,128)} %get-tuple-element.64.refs_2_, ...), custom_call_target="tpu_custom_call" | custom-call | flops 2415919104 | bytes 19923464 | tf_op jit(solution)/shard_map/pallas_call | solution.py:479
  301.7 28.8 %shard_map.83 = (f32[16,16,32,128]{3,2,1,0:T(8,128)}, f32[16,2,32,128]{3,2,1,0:T(8,128)}, f32[16,2,32,128]{3,2,1,0:T(8,128)}) custom-call(s32[2]{0:T(128)} %pad_add_fusion.place, s32[32,2]{1,0:T(8,128)} %copy.9.refs_0_.index, s32[32,2]{1,0:T(8,128)} %copy.18.refs_1_.refs_0_.index, f32[4,16,4096]{2,1,0:T(8,128)} %get-tuple-element.66.refs_2_, ...), custom_call_target="tpu_custom_call" | custom-call | flops 2415919104 | bytes 19923464 | tf_op jit(solution)/shard_map/pallas_call | solution.py:479
  330.6 25.9 %all-to-all-done.refs_0_ = f32[16,16,32,128]{3,2,1,0:T(8,128)} async-done(((f32[16,16,32,128]{3,2,1,0:T(8,128)}), f32[16,16,32,128]{3,2,1,0:T(8,128)}, u32[]{:S(2)}, u32[]{:S(2)}) %all-to-all-start) | async-done | bytes 4194336 | tf_op jit(solution)/shard_map/all_to_all | solution.py:599
  363.3 28.8 %shard_map.84 = (f32[16,16,32,128]{3,2,1,0:T(8,128)}, f32[16,2,32,128]{3,2,1,0:T(8,128)}, f32[16,2,32,128]{3,2,1,0:T(8,128)}) custom-call(s32[2]{0:T(128)} %pad_add_fusion.place, s32[32,2]{1,0:T(8,128)} %copy.9.refs_0_.index, s32[32,2]{1,0:T(8,128)} %copy.18.refs_1_.refs_0_.index, f32[4,16,4096]{2,1,0:T(8,128)} %get-tuple-element.69.refs_2_, ...), custom_call_target="tpu_custom_call" | custom-call | flops 2415919104 | bytes 19923464 | tf_op jit(solution)/shard_map/pallas_call | solution.py:479
  392.2 25.7 %all-to-all-done.1.refs_1_ = f32[16,16,32,128]{3,2,1,0:T(8,128)} async-done(((f32[16,16,32,128]{3,2,1,0:T(8,128)}), f32[16,16,32,128]{3,2,1,0:T(8,128)}, u32[]{:S(2)}, u32[]{:S(2)}) %all-to-all-start.1) | async-done | bytes 4194336 | tf_op jit(solution)/shard_map/all_to_all | solution.py:599
  425.3 16.3 %shard_map.85 = (f32[16,8,32,128]{3,2,1,0:T(8,128)}, f32[16,2,32,128]{3,2,1,0:T(8,128)}) custom-call(s32[2]{0:T(128)} %pad_add_fusion.place, s32[32,2]{1,0:T(8,128)} %copy.18.refs_1_.refs_0_.index, f32[4,16,4096]{2,1,0:T(8,128)} %get-tuple-element.72.refs_1_, f32[4,16,4096]{2,1,0:T(8,128)} %copy-done.23, ...), custom_call_target="tpu_custom_call" | custom-call | flops 1207959552 | bytes 13107464 | tf_op jit(solution)/shard_map/pallas_call | solution.py:479
  441.6 38.0 %all-to-all-done.2.refs_2_ = f32[16,16,32,128]{3,2,1,0:T(8,128)} async-done(((f32[16,16,32,128]{3,2,1,0:T(8,128)}), f32[16,16,32,128]{3,2,1,0:T(8,128)}, u32[]{:S(2)}, u32[]{:S(2)}) %all-to-all-start.2) | async-done | bytes 4194336 | tf_op jit(solution)/shard_map/all_to_all | solution.py:599
  485.9 22.6 %shard_map.90 = (f32[16,4,128,128]{3,2,1,0:T(8,128)}, f32[16,4,128,128]{3,2,1,0:T(8,128)}) custom-call(f32[16,16,32,128]{3,2,1,0:T(8,128)} %all-to-all-done.refs_0_, f32[16,16,32,128]{3,2,1,0:T(8,128)} %all-to-all-done.1.refs_1_, f32[16,16,32,128]{3,2,1,0:T(8,128)} %all-to-all-done.2.refs_2_, f32[16,8,32,128]{3,2,1,0:T(8,128)} %copy-done, ...), custom_call_target="tpu_custom_call" | custom-call | flops 3221225472 | bytes 27262976 | tf_op jit(solution)/shard_map/pallas_call | solution.py:479
  521.1 22.7 %shard_map.86 = (f32[16,4,128,128]{3,2,1,0:T(8,128)}, f32[16,4,128,128]{3,2,1,0:T(8,128)}) custom-call(f32[16,16,32,128]{3,2,1,0:T(8,128)} %all-to-all-done.refs_0_, f32[16,16,32,128]{3,2,1,0:T(8,128)} %all-to-all-done.1.refs_1_, f32[16,16,32,128]{3,2,1,0:T(8,128)} %all-to-all-done.2.refs_2_, f32[16,8,32,128]{3,2,1,0:T(8,128)} %copy-done.2, ...), custom_call_target="tpu_custom_call" | custom-call | flops 3221225472 | bytes 27262976 | tf_op jit(solution)/shard_map/pallas_call | solution.py:479
  543.8 31.6 %all-to-all-done.8.fields = f32[16,4,128,128]{3,2,1,0:T(8,128)} async-done(((f32[16,4,128,128]{3,2,1,0:T(8,128)}), f32[16,4,128,128]{3,2,1,0:T(8,128)}, u32[]{:S(2)}, u32[]{:S(2)}) %all-to-all-start.8) | async-done | bytes 4194336 | tf_op jit(solution)/shard_map/all_to_all | solution.py:599
  582.5 16.4 %shard_map.91 = f32[16,2,128,128]{3,2,1,0:T(8,128)} custom-call(f32[16,4,128,128]{3,2,1,0:T(8,128)} %all-to-all-done.8.fields, bf16[16,256,256]{2,1,0:T(8,128)(2,1)} %constant.36.clone.refs_8_.refs_5_.mhi, bf16[16,256,256]{2,1,0:T(8,128)(2,1)} %constant.37.clone.refs_9_.refs_6_.mlo), custom_call_target="tpu_custom_call" | custom-call | flops 2415919104 | bytes 10485760 | tf_op jit(solution)/shard_map/pallas_call | solution.py:479
  598.9 38.1 %all-to-all-done.4.fields = f32[16,4,128,128]{3,2,1,0:T(8,128)} async-done(((f32[16,4,128,128]{3,2,1,0:T(8,128)}), f32[16,4,128,128]{3,2,1,0:T(8,128)}, u32[]{:S(2)}, u32[]{:S(2)}) %all-to-all-start.4) | async-done | bytes 4194336 | tf_op jit(solution)/shard_map/all_to_all | solution.py:599
  643.3 16.4 %shard_map.87 = f32[16,2,128,128]{3,2,1,0:T(8,128)} custom-call(f32[16,4,128,128]{3,2,1,0:T(8,128)} %all-to-all-done.4.fields, bf16[16,256,256]{2,1,0:T(8,128)(2,1)} %constant.36.clone.refs_8_.refs_5_.mhi, bf16[16,256,256]{2,1,0:T(8,128)(2,1)} %constant.37.clone.refs_9_.refs_6_.mlo), custom_call_target="tpu_custom_call" | custom-call | flops 2415919104 | bytes 10485760 | tf_op jit(solution)/shard_map/pallas_call | solution.py:479
  659.8 10.0 %all-to-all-done.9.back = f32[16,2,128,128]{3,2,1,0:T(8,128)S(1)} async-done(((f32[16,2,128,128]{3,2,1,0:T(8,128)}), f32[16,2,128,128]{3,2,1,0:T(8,128)S(1)}, u32[]{:S(2)}, u32[]{:S(2)}) %all-to-all-start.9) | async-done | bytes 2097184 | tf_op jit(solution)/shard_map/all_to_all | solution.py:599
  677.3 16.6 %shard_map.92 = (f32[16,4,64,128]{3,2,1,0:T(8,128)}, f32[16,4,64,128]{3,2,1,0:T(8,128)}) custom-call(f32[16,2,128,128]{3,2,1,0:T(8,128)} %copy-done.3, f32[16,4,128,128]{3,2,1,0:T(8,128)} %get-tuple-element.82.kept, bf16[16,256,256]{2,1,0:T(8,128)(2,1)} %constant.34.clone.refs_4_.mhi, bf16[16,256,256]{2,1,0:T(8,128)(2,1)} %constant.35.clone.refs_5_.mlo), custom_call_target="tpu_custom_call" | custom-call | flops 1610612736 | bytes 14680064 | tf_op jit(solution)/shard_map/pallas_call | solution.py:479
  693.9 9.9 %all-to-all-done.5.back = f32[16,2,128,128]{3,2,1,0:T(8,128)S(1)} async-done(((f32[16,2,128,128]{3,2,1,0:T(8,128)}), f32[16,2,128,128]{3,2,1,0:T(8,128)S(1)}, u32[]{:S(2)}, u32[]{:S(2)}) %all-to-all-start.5) | async-done | bytes 2097184 | tf_op jit(solution)/shard_map/all_to_all | solution.py:599
  711.1 16.5 %shard_map.88 = (f32[16,4,64,128]{3,2,1,0:T(8,128)}, f32[16,4,32,128]{3,2,1,0:T(8,128)}, f32[16,4,32,128]{3,2,1,0:T(8,128)}) custom-call(f32[16,2,128,128]{3,2,1,0:T(8,128)} %copy-done.1, f32[16,4,128,128]{3,2,1,0:T(8,128)} %get-tuple-element.76.kept, bf16[16,256,256]{2,1,0:T(8,128)(2,1)} %constant.34.clone.refs_4_.mhi, ...), custom_call_target="tpu_custom_call" | custom-call | flops 1610612736 | bytes 14680064 | tf_op jit(solution)/shard_map/pallas_call | solution.py:479
  727.6 9.9 %all-to-all-done.10.back = f32[16,4,64,128]{3,2,1,0:T(8,128)} async-done(((f32[16,4,64,128]{3,2,1,0:T(8,128)}), f32[16,4,64,128]{3,2,1,0:T(8,128)}, u32[]{:S(2)}, u32[]{:S(2)}) %all-to-all-start.10) | async-done | bytes 2097184 | tf_op jit(solution)/shard_map/all_to_all | solution.py:599
  743.7 17.2 %shard_map.93 = (f32[2,32,4096]{2,1,0:T(8,128)}, f32[2,32,4096]{2,1,0:T(8,128)}) custom-call(s32[2]{0:T(128)} %pad_add_fusion.place, s32[32,2]{1,0:T(8,128)} %copy.9.refs_0_.index, f32[16,4,64,128]{3,2,1,0:T(8,128)} %all-to-all-done.10.back, bf16[32,256,128]{2,1,0:T(8,128)(2,1)} %get-tuple-element.153.refs_4_.refs_3_.whi, ...), custom_call_target="tpu_custom_call" | custom-call | flops 1207959552 | bytes 13631752 | tf_op jit(solution)/shard_map/pallas_call | solution.py:479
  760.9 9.2 all-to-all-done.6.back
  777.6 17.7 %shard_map.94 = (f32[2,32,4096]{2,1,0:T(8,128)}, f32[2,32,4096]{2,1,0:T(8,128)}) custom-call(s32[2]{0:T(128)} %pad_add_fusion.place, s32[32,2]{1,0:T(8,128)} %copy.18.refs_1_.refs_0_.index, f32[16,4,64,128]{3,2,1,0:T(8,128)} %copy-done.5, bf16[32,256,128]{2,1,0:T(8,128)(2,1)} %get-tuple-element.154.refs_6_.refs_3_.whi, ...), custom_call_target="tpu_custom_call" | custom-call | flops 1207959552 | bytes 15728904 | tf_op jit(solution)/shard_map/pallas_call | solution.py:479
  810.2 17.0 %shard_map.95 = (f32[2,16,4096]{2,1,0:T(8,128)}, f32[2,16,4096]{2,1,0:T(8,128)}, f32[2,16,4096]{2,1,0:T(8,128)}, f32[2,16,4096]{2,1,0:T(8,128)}) custom-call(s32[2]{0:T(128)} %pad_add_fusion.place, s32[32,2]{1,0:T(8,128)} %copy.9.refs_0_.index, f32[16,4,64,128]{3,2,1,0:T(8,128)} %copy-done.4, bf16[32,256,128]{2,1,0:T(8,128)(2,1)} %get-tuple-element.153.refs_4_.refs_3_.whi, ...), custom_call_target="tpu_custom_call" | custom-call | flops 1207959552 | bytes 13631752 | tf_op jit(solution)/shard_map/pallas_call | solution.py:479
  835.3 15.4 %shard_map.96 = (f32[2,16,4096]{2,1,0:T(8,128)}, f32[2,16,4096]{2,1,0:T(8,128)}) custom-call(s32[2]{0:T(128)} %pad_add_fusion.place, s32[32,2]{1,0:T(8,128)} %copy.18.refs_1_.refs_0_.index, f32[16,4,32,128]{3,2,1,0:T(8,128)} %copy-done.22, bf16[32,256,128]{2,1,0:T(8,128)(2,1)} %get-tuple-element.154.refs_6_.refs_3_.whi, ...), custom_call_target="tpu_custom_call" | custom-call | flops 603979776 | bytes 12058888 | tf_op jit(solution)/shard_map/pallas_call | solution.py:479
  856.2 15.5 %shard_map.97 = (f32[2,16,4096]{2,1,0:T(8,128)}, f32[2,16,4096]{2,1,0:T(8,128)}) custom-call(s32[2]{0:T(128)} %pad_add_fusion.place, s32[32,2]{1,0:T(8,128)} %copy.18.refs_1_.refs_0_.index, f32[16,4,32,128]{3,2,1,0:T(8,128)} %copy-done.21, bf16[32,256,128]{2,1,0:T(8,128)(2,1)} %get-tuple-element.154.refs_6_.refs_3_.whi, ...), custom_call_target="tpu_custom_call" | custom-call | flops 603979776 | bytes 12058888 | tf_op jit(solution)/shard_map/pallas_call | solution.py:479
  874.0 29.0 %collective-permute-done.6 = f32[2,32,4096]{2,1,0:T(8,128)} collective-permute-done((f32[2,32,4096]{2,1,0:T(8,128)}, f32[2,32,4096]{2,1,0:T(8,128)}, u32[]{:S(2)}, u32[]{:S(2)}) %collective-permute-start.6) | collective-permute-done | bytes 1048608 | tf_op jit(solution)/shard_map/ppermute | solution.py:613
  914.1 11.2 %collective-permute-done.10 = f32[2,16,4096]{2,1,0:T(8,128)S(1)} collective-permute-done((f32[2,16,4096]{2,1,0:T(8,128)}, f32[2,16,4096]{2,1,0:T(8,128)S(1)}, u32[]{:S(2)}, u32[]{:S(2)}) %collective-permute-start.10) | collective-permute-done | bytes 524320 | tf_op jit(solution)/shard_map/ppermute | solution.py:613
  (125 shorter events, 180.1 us)
Async XLA Ops:
  3.1 24.1 %collective-permute-start = (f32[4,16,4096]{2,1,0:T(8,128)S(1)}, f32[4,16,4096]{2,1,0:T(8,128)S(1)}, u32[]{:S(2)}, u32[]{:S(2)}) collective-permute-start(f32[4,16,4096]{2,1,0:T(8,128)S(1)} %fusion.7), channel_id=1, source_target_pairs={{0,16},{1,17},{2,18},{3,19},{4,20},{5,21},{6,22},{7,23},{8,24},{9,... | collective-permute-start | bytes 3145736 | tf_op jit(solution)/shard_map/ppermute | solution.py:613
  28.2 68.4 %collective-permute-start.1 = (f32[12,16,4096]{2,1,0:T(8,128)}, f32[12,16,4096]{2,1,0:T(8,128)}, u32[]{:S(2)}, u32[]{:S(2)}) collective-permute-start(f32[12,16,4096]{2,1,0:T(8,128)} %pad_maximum_fusion), channel_id=1, source_target_pairs={{0,16},{1,17},{2,18},{3,19},{4,20},{5,21},{6,22},{7,23},{8,24},{9,... | collective-permute-start | bytes 9437192 | tf_op jit(solution)/shard_map/ppermute | solution.py:613
  28.6 68.0 %copy-start.9 = (f32[2,16,4096]{2,1,0:T(8,128)S(1)}, f32[2,16,4096]{2,1,0:T(8,128)}, u32[]{:S(2)}) copy-start(f32[2,16,4096]{2,1,0:T(8,128)} %copy-done.8) | copy-start | bytes 1572868
  28.6 68.0 %copy-start.11 = (f32[2,16,4096]{2,1,0:T(8,128)S(1)}, f32[2,16,4096]{2,1,0:T(8,128)}, u32[]{:S(2)}) copy-start(f32[2,16,4096]{2,1,0:T(8,128)} %copy-done.10) | copy-start | bytes 1572868
  28.6 68.0 %copy-start.13 = (f32[2,16,4096]{2,1,0:T(8,128)S(1)}, f32[2,16,4096]{2,1,0:T(8,128)}, u32[]{:S(2)}) copy-start(f32[2,16,4096]{2,1,0:T(8,128)} %copy-done.12) | copy-start | bytes 1572868
  28.6 68.0 %copy-start.15 = (f32[2,16,4096]{2,1,0:T(8,128)S(1)}, f32[2,16,4096]{2,1,0:T(8,128)}, u32[]{:S(2)}) copy-start(f32[2,16,4096]{2,1,0:T(8,128)} %copy-done.14) | copy-start | bytes 1572868
  28.6 73.1 %copy-start.30 = (s32[2,32,2]{1,2,0:T(2,128)S(1)}, s32[2,32,2]{1,2,0:T(2,128)}, u32[]{:S(2)}) copy-start(s32[2,32,2]{1,2,0:T(2,128)} %param.10) | copy-start | bytes 1540
  31.8 67.6 %collective-permute-start.2 = (f32[4,16,4096]{2,1,0:T(8,128)S(1)}, f32[4,16,4096]{2,1,0:T(8,128)}, u32[]{:S(2)}, u32[]{:S(2)}) collective-permute-start(f32[4,16,4096]{2,1,0:T(8,128)S(1)} %get-tuple-element.147), channel_id=1, source_target_pairs={{0,8},{1,9},{2,10},{3,11},{4,12},{5,13},{6,14},{7,15},{8,0},{9,1},... | collective-permute-start | bytes 3145736 | tf_op jit(solution)/shard_map/ppermute | solution.py:613
  99.4 47.7 %collective-permute-start.3 = (f32[4,16,4096]{2,1,0:T(8,128)}, f32[4,16,4096]{2,1,0:T(8,128)}, u32[]{:S(2)}, u32[]{:S(2)}) collective-permute-start(f32[4,16,4096]{2,1,0:T(8,128)} %get-tuple-element.67), channel_id=1, source_target_pairs={{0,8},{1,9},{2,10},{3,11},{4,12},{5,13},{6,14},{7,15},{8,0},{9,1},... | collective-permute-start | bytes 3145736 | tf_op jit(solution)/shard_map/ppermute | solution.py:613
  147.1 46.5 %collective-permute-start.4 = (f32[4,16,4096]{2,1,0:T(8,128)S(1)}, f32[4,16,4096]{2,1,0:T(8,128)S(1)}, u32[]{:S(2)}, u32[]{:S(2)}) collective-permute-start(f32[4,16,4096]{2,1,0:T(8,128)S(1)} %get-tuple-element.70), channel_id=1, source_target_pairs={{0,8},{1,9},{2,10},{3,11},{4,12},{5,13},{6,14},{7,15},{8,0},{9,1},... | collective-permute-start | bytes 3145736 | tf_op jit(solution)/shard_map/ppermute | solution.py:613
  194.5 47.8 %collective-permute-start.5 = (f32[4,16,4096]{2,1,0:T(8,128)S(1)}, f32[4,16,4096]{2,1,0:T(8,128)S(1)}, u32[]{:S(2)}, u32[]{:S(2)}) collective-permute-start(f32[4,16,4096]{2,1,0:T(8,128)S(1)} %get-tuple-element.73), channel_id=1, source_target_pairs={{0,8},{1,9},{2,10},{3,11},{4,12},{5,13},{6,14},{7,15},{8,0},{9,1},... | collective-permute-start | bytes 3145736 | tf_op jit(solution)/shard_map/ppermute | solution.py:613
  259.6 35.7 %all-to-all-start.7 = ((f32[16,8,32,128]{3,2,1,0:T(8,128)}), f32[16,8,32,128]{3,2,1,0:T(8,128)S(1)}, u32[]{:S(2)}, u32[]{:S(2)}) async-start(f32[16,8,32,128]{3,2,1,0:T(8,128)} %get-tuple-element.80), calls=%async_computation.7 | async-start | bytes 4194304 | tf_op jit(solution)/shard_map/all_to_all | solution.py:599
  296.6 59.9 %all-to-all-start = ((f32[16,16,32,128]{3,2,1,0:T(8,128)}), f32[16,16,32,128]{3,2,1,0:T(8,128)}, u32[]{:S(2)}, u32[]{:S(2)}) async-start(f32[16,16,32,128]{3,2,1,0:T(8,128)} %get-tuple-element.65), calls=%async_computation | async-start | bytes 8388608 | tf_op jit(solution)/shard_map/all_to_all | solution.py:599
  356.5 61.4 %all-to-all-start.1 = ((f32[16,16,32,128]{3,2,1,0:T(8,128)}), f32[16,16,32,128]{3,2,1,0:T(8,128)}, u32[]{:S(2)}, u32[]{:S(2)}) async-start(f32[16,16,32,128]{3,2,1,0:T(8,128)} %get-tuple-element.68), calls=%async_computation.1 | async-start | bytes 8388608 | tf_op jit(solution)/shard_map/all_to_all | solution.py:599
  417.9 61.8 %all-to-all-start.2 = ((f32[16,16,32,128]{3,2,1,0:T(8,128)}), f32[16,16,32,128]{3,2,1,0:T(8,128)}, u32[]{:S(2)}, u32[]{:S(2)}) async-start(f32[16,16,32,128]{3,2,1,0:T(8,128)} %get-tuple-element.71), calls=%async_computation.2 | async-start | bytes 8388608 | tf_op jit(solution)/shard_map/all_to_all | solution.py:599
  479.6 32.8 %all-to-all-start.3 = ((f32[16,8,32,128]{3,2,1,0:T(8,128)}), f32[16,8,32,128]{3,2,1,0:T(8,128)S(1)}, u32[]{:S(2)}, u32[]{:S(2)}) async-start(f32[16,8,32,128]{3,2,1,0:T(8,128)} %get-tuple-element.74), calls=%async_computation.3 | async-start | bytes 4194304 | tf_op jit(solution)/shard_map/all_to_all | solution.py:599
  513.7 61.7 %all-to-all-start.8 = ((f32[16,4,128,128]{3,2,1,0:T(8,128)}), f32[16,4,128,128]{3,2,1,0:T(8,128)}, u32[]{:S(2)}, u32[]{:S(2)}) async-start(f32[16,4,128,128]{3,2,1,0:T(8,128)} %get-tuple-element.81), calls=%async_computation.8 | async-start | bytes 8388608 | tf_op jit(solution)/shard_map/all_to_all | solution.py:599
  575.4 61.6 %all-to-all-start.4 = ((f32[16,4,128,128]{3,2,1,0:T(8,128)}), f32[16,4,128,128]{3,2,1,0:T(8,128)}, u32[]{:S(2)}, u32[]{:S(2)}) async-start(f32[16,4,128,128]{3,2,1,0:T(8,128)} %get-tuple-element.75), calls=%async_computation.4 | async-start | bytes 8388608 | tf_op jit(solution)/shard_map/all_to_all | solution.py:599
  637.0 32.8 %all-to-all-start.9 = ((f32[16,2,128,128]{3,2,1,0:T(8,128)}), f32[16,2,128,128]{3,2,1,0:T(8,128)S(1)}, u32[]{:S(2)}, u32[]{:S(2)}) async-start(f32[16,2,128,128]{3,2,1,0:T(8,128)} %shard_map.91), calls=%async_computation.9 | async-start | bytes 4194304 | tf_op jit(solution)/shard_map/all_to_all | solution.py:599
  671.1 32.7 %all-to-all-start.5 = ((f32[16,2,128,128]{3,2,1,0:T(8,128)}), f32[16,2,128,128]{3,2,1,0:T(8,128)S(1)}, u32[]{:S(2)}, u32[]{:S(2)}) async-start(f32[16,2,128,128]{3,2,1,0:T(8,128)} %shard_map.87), calls=%async_computation.5 | async-start | bytes 4194304 | tf_op jit(solution)/shard_map/all_to_all | solution.py:599
  703.8 33.7 %all-to-all-start.10 = ((f32[16,4,64,128]{3,2,1,0:T(8,128)}), f32[16,4,64,128]{3,2,1,0:T(8,128)}, u32[]{:S(2)}, u32[]{:S(2)}) async-start(f32[16,4,64,128]{3,2,1,0:T(8,128)} %get-tuple-element.83), calls=%async_computation.10 | async-start | bytes 4194304 | tf_op jit(solution)/shard_map/all_to_all | solution.py:599
  737.5 32.7 %all-to-all-start.6 = ((f32[16,4,64,128]{3,2,1,0:T(8,128)}), f32[16,4,64,128]{3,2,1,0:T(8,128)S(1)}, u32[]{:S(2)}, u32[]{:S(2)}) async-start(f32[16,4,64,128]{3,2,1,0:T(8,128)} %get-tuple-element.77), calls=%async_computation.6 | async-start | bytes 4194304 | tf_op jit(solution)/shard_map/all_to_all | solution.py:599
  771.4 32.7 %all-to-all-start.12 = ((f32[16,4,64,128]{3,2,1,0:T(8,128)}), f32[16,4,64,128]{3,2,1,0:T(8,128)S(1)}, u32[]{:S(2)}, u32[]{:S(2)}) async-start(f32[16,4,64,128]{3,2,1,0:T(8,128)} %get-tuple-element.94), calls=%async_computation.12 | async-start | bytes 4194304 | tf_op jit(solution)/shard_map/all_to_all | solution.py:599
  804.1 23.1 %all-to-all-start.11 = ((f32[16,4,32,128]{3,2,1,0:T(8,128)}), f32[16,4,32,128]{3,2,1,0:T(8,128)S(1)}, u32[]{:S(2)}, u32[]{:S(2)}) async-start(f32[16,4,32,128]{3,2,1,0:T(8,128)} %get-tuple-element.91), calls=%async_computation.11 | async-start | bytes 2097152 | tf_op jit(solution)/shard_map/all_to_all | solution.py:599
  827.2 28.0 %all-to-all-start.13 = ((f32[16,4,32,128]{3,2,1,0:T(8,128)}), f32[16,4,32,128]{3,2,1,0:T(8,128)S(1)}, u32[]{:S(2)}, u32[]{:S(2)}) async-start(f32[16,4,32,128]{3,2,1,0:T(8,128)} %get-tuple-element.104), calls=%async_computation.13 | async-start | bytes 2097152 | tf_op jit(solution)/shard_map/all_to_all | solution.py:599
  832.4 70.6 %collective-permute-start.6 = (f32[2,32,4096]{2,1,0:T(8,128)}, f32[2,32,4096]{2,1,0:T(8,128)}, u32[]{:S(2)}, u32[]{:S(2)}) collective-permute-start(f32[2,32,4096]{2,1,0:T(8,128)} %get-tuple-element.88), channel_id=1, source_target_pairs={{0,8},{1,9},{2,10},{3,11},{4,12},{5,13},{6,14},{7,15},{16,0},{17,1... | collective-permute-start | bytes 3145736 | tf_op jit(solution)/shard_map/ppermute | solution.py:613
  832.5 72.6 %collective-permute-start.7 = (f32[2,32,4096]{2,1,0:T(8,128)}, f32[2,32,4096]{2,1,0:T(8,128)}, u32[]{:S(2)}, u32[]{:S(2)}) collective-permute-start(f32[2,32,4096]{2,1,0:T(8,128)} %get-tuple-element.108), channel_id=1, source_target_pairs={{8,16},{9,17},{10,18},{11,19},{12,20},{13,21},{14,22},{15,23},{16,... | collective-permute-start | bytes 3145736 | tf_op jit(solution)/shard_map/ppermute | solution.py:613
  850.7 63.5 %collective-permute-start.8 = (f32[2,16,4096]{2,1,0:T(8,128)}, f32[2,16,4096]{2,1,0:T(8,128)S(1)}, u32[]{:S(2)}, u32[]{:S(2)}) collective-permute-start(f32[2,16,4096]{2,1,0:T(8,128)} %get-tuple-element.99), channel_id=1, source_target_pairs={{0,8},{1,9},{2,10},{3,11},{4,12},{5,13},{6,14},{7,15},{16,0},{17,1... | collective-permute-start | bytes 1572872 | tf_op jit(solution)/shard_map/ppermute | solution.py:613
  850.7 63.5 %collective-permute-start.9 = (f32[2,16,4096]{2,1,0:T(8,128)}, f32[2,16,4096]{2,1,0:T(8,128)S(1)}, u32[]{:S(2)}, u32[]{:S(2)}) collective-permute-start(f32[2,16,4096]{2,1,0:T(8,128)} %get-tuple-element.111), channel_id=1, source_target_pairs={{8,16},{9,17},{10,18},{11,19},{12,20},{13,21},{14,22},{15,23},{16,... | collective-permute-start | bytes 1572872 | tf_op jit(solution)/shard_map/ppermute | solution.py:613
  856.2 73.9 %copy-start.27 = (f32[2,32,4096]{2,1,0:T(8,128)S(1)}, f32[2,32,4096]{2,1,0:T(8,128)}, u32[]{:S(2)}) copy-start(f32[2,32,4096]{2,1,0:T(8,128)} %get-tuple-element.108) | copy-start | bytes 3145732
  871.6 53.7 %collective-permute-start.10 = (f32[2,16,4096]{2,1,0:T(8,128)}, f32[2,16,4096]{2,1,0:T(8,128)S(1)}, u32[]{:S(2)}, u32[]{:S(2)}) collective-permute-start(f32[2,16,4096]{2,1,0:T(8,128)} %get-tuple-element.106), channel_id=1, source_target_pairs={{0,8},{1,9},{2,10},{3,11},{4,12},{5,13},{6,14},{7,15},{16,0},{17,1... | collective-permute-start | bytes 1572872 | tf_op jit(solution)/shard_map/ppermute | solution.py:613
  903.0 27.0 %collective-permute-start.11 = (f32[2,16,4096]{2,1,0:T(8,128)}, f32[2,16,4096]{2,1,0:T(8,128)S(1)}, u32[]{:S(2)}, u32[]{:S(2)}) collective-permute-start(f32[2,16,4096]{2,1,0:T(8,128)} %get-tuple-element.114), channel_id=1, source_target_pairs={{8,16},{9,17},{10,18},{11,19},{12,20},{13,21},{14,22},{15,23},{16,... | collective-permute-start | bytes 1572872 | tf_op jit(solution)/shard_map/ppermute | solution.py:613
  (25 other events, 78.4 us)

commit v9 on v8

--- a/solution.py
+++ b/solution.py
@@ -641,14 +641,10 @@
     kept, given = zip(*[sides(c) for c in range(1, CHUNKS)])
     rest = permute(after(jnp.concatenate(given), beside), BESIDE)
     chunks = []
-    along = ()
     for c in range(CHUNKS):
         if c:
             keep, beside = kept[c - 1], rest[4 * (c - 1) : 4 * c]
-        own = jnp.where(q == b, keep, beside)
-        give = jnp.where(q == b, beside, keep)
-        along = permute(after(give, along), ALONG)
-        chunks.append((own, along))
+        chunks.append((jnp.where(q == b, keep, beside), jnp.where(q == b, beside, keep)))
     return chunks, rest
 
 
@@ -676,15 +672,17 @@
     arrived = [[] for _ in angles]
     bases = [[] for _ in angles]
     ahead = [[] for _ in angles]
-    for c, (own, along) in enumerate(chunks):
+    fields = ()
+    for c, (own, give) in enumerate(chunks):
+        along = permute(after(give, fields), ALONG)
         own = after(own, beside)
         for part in (angles,) if c + 1 < CHUNKS else [[a] for a in angles]:
             fields, fronts = enter(
                 place, [block_index[a] for a in part], own, along, [weights[a] for a in part], row
             )
-            fields = exchange(fields)
+            moved = exchange(fields)
             for i, a in enumerate(part):
-                arrived[a].append(fields)
+                arrived[a].append(moved)
                 bases[a].append(8 * i)
                 ahead[a].append(fronts[i])
     carried = []
@@ -711,9 +709,11 @@
     starts = home(0, back, most, (), rest)
     back = exchange(after(late[2], starts))
     totals += home(1, next_back, most, starts[0], rest[:1])
+    leaving = [depart(*total) for total in totals]
+    back = after(back, leaving[0])
     totals += home(1, back, most + rest[0], starts[1], rest[1:])
+    leaving.append(depart(*totals[-1]))
     pieces = []
-    leaving = [depart(*total) for total in totals]
     total = totals[-1]
     for span, moved in zip(spans, after(leaving, total)):
         lower, upper = settle(*moved, q, b)

time: 946 us -> 1020 us (1.078)
  blocking collectives: 0 us -> 139 us
  waiting for transfers between devices: 469 us -> 428 us
  starting transfers between devices: 106 us -> 85.4 us
    all_to_all x0 -> x3, blocking collectives: none -> 139 us  [exchange(): lax.all_to_all(values, ('parts', 'fft'), split_axis=0, concat_axis=0, axi...]
    all_to_all x14 -> x11, waiting for transfers between devices: 211 us -> 159 us  [exchange(): lax.all_to_all(values, ('parts', 'fft'), split_axis=0, concat_axis=0, axi...]
    all_to_all x14 -> x11, starting transfers between devices: 89.8 us -> 71.2 us  [exchange(): lax.all_to_all(values, ('parts', 'fft'), split_axis=0, concat_axis=0, axi...]
    ppermute x12, waiting for transfers between devices: 258 us -> 269 us  [permute(): return lax.ppermute(values, ('parts', 'fft'), pairs)]
  transfers between devices with their start and end apart: 26 -> 23, of which waited for: 21 -> 18; matrix products, arithmetic and copies ran while one was open for 3% -> 3% of each run, Pallas kernels for 32% -> 21%
where the time goes in v9:
time: 1020 us; the launch traced here: 1010 us
  waiting for transfers between devices  428 us (42%)
  Pallas kernels  313 us (31%)
  blocking collectives  139 us (14%)
  starting transfers between devices  85.4 us (8%)
  local copies, waits for them, and re-layouts  24.4 us (2%)
  other arithmetic  21.5 us (2%)
    pallas_call x16, Pallas kernels, call(): pl.pallas_call(kernel, out_shape=[jax.ShapeDtypeStruct(o, jnp.float32) fo...  313 us
    ppermute x12, waiting for transfers between devices, permute(): return lax.ppermute(values, ('parts', 'fft'), pairs)  269 us
    all_to_all x11, waiting for transfers between devices, exchange(): lax.all_to_all(values, ('parts', 'fft'), split_axis=0, concat_axis=0, axi...  159 us
    all_to_all x3, blocking collectives, exchange(): lax.all_to_all(values, ('parts', 'fft'), split_axis=0, concat_axis=0, axi...  139 us
    all_to_all x11, starting transfers between devices, exchange(): lax.all_to_all(values, ('parts', 'fft'), split_axis=0, concat_axis=0, axi...  71.2 us
  transfers between devices with their start and end apart: 23, of which 18 were waited for; matrix products, arithmetic and copies ran while one was open for 3% of the time, Pallas kernels for 21%

profile of v9, /device:TPU:3, one launch (start us, length us, event | category | flops | bytes accessed | tf_op | source)
XLA Modules:
  0.0 1012.7 jit_solution(15131443226909558474)
XLA Ops:
  10.4 16.9 %collective-permute-done = f32[4,16,4096]{2,1,0:T(8,128)S(1)} collective-permute-done((f32[4,16,4096]{2,1,0:T(8,128)S(1)}, f32[4,16,4096]{2,1,0:T(8,128)S(1)}, u32[]{:S(2)}, u32[]{:S(2)}) %collective-permute-start) | collective-permute-done | bytes 1048608 | tf_op jit(solution)/shard_map/ppermute | solution.py:613
  43.4 53.1 %collective-permute-done.1 = f32[12,16,4096]{2,1,0:T(8,128)} collective-permute-done((f32[12,16,4096]{2,1,0:T(8,128)}, f32[12,16,4096]{2,1,0:T(8,128)}, u32[]{:S(2)}, u32[]{:S(2)}) %collective-permute-start.1) | collective-permute-done | bytes 3145760 | tf_op jit(solution)/shard_map/ppermute | solution.py:613
  100.4 28.9 %shard_map.82 = (f32[16,16,32,128]{3,2,1,0:T(8,128)}, f32[16,2,32,128]{3,2,1,0:T(8,128)}, f32[16,2,32,128]{3,2,1,0:T(8,128)}) custom-call(s32[2]{0:T(128)} %pad_add_fusion.place, s32[32,2]{1,0:T(8,128)} %copy.9.refs_0_.index, s32[32,2]{1,0:T(8,128)} %copy.18.refs_1_.refs_0_.index, f32[4,16,4096]{2,1,0:T(8,128)} %get-tuple-element.65.refs_2_, ...), custom_call_target="tpu_custom_call" | custom-call | flops 2415919104 | bytes 19923464 | tf_op jit(solution)/shard_map/pallas_call | solution.py:479
  134.5 42.5 %collective-permute-done.3.refs_3_ = f32[4,16,4096]{2,1,0:T(8,128)} collective-permute-done((f32[4,16,4096]{2,1,0:T(8,128)}, f32[4,16,4096]{2,1,0:T(8,128)}, u32[]{:S(2)}, u32[]{:S(2)}) %collective-permute-start.3) | collective-permute-done | bytes 1048608 | tf_op jit(solution)/shard_map/ppermute | solution.py:613
  177.0 28.8 %shard_map.83 = (f32[16,16,32,128]{3,2,1,0:T(8,128)}, f32[16,2,32,128]{3,2,1,0:T(8,128)}, f32[16,2,32,128]{3,2,1,0:T(8,128)}) custom-call(s32[2]{0:T(128)} %pad_add_fusion.place, s32[32,2]{1,0:T(8,128)} %copy.9.refs_0_.index, s32[32,2]{1,0:T(8,128)} %copy.18.refs_1_.refs_0_.index, f32[4,16,4096]{2,1,0:T(8,128)} %get-tuple-element.67.refs_2_, ...), custom_call_target="tpu_custom_call" | custom-call | flops 2415919104 | bytes 19923464 | tf_op jit(solution)/shard_map/pallas_call | solution.py:479
  208.7 43.8 %collective-permute-done.4.refs_3_ = f32[4,16,4096]{2,1,0:T(8,128)S(1)} collective-permute-done((f32[4,16,4096]{2,1,0:T(8,128)}, f32[4,16,4096]{2,1,0:T(8,128)S(1)}, u32[]{:S(2)}, u32[]{:S(2)}) %collective-permute-start.4) | collective-permute-done | bytes 1048608 | tf_op jit(solution)/shard_map/ppermute | solution.py:613
  253.5 28.9 %shard_map.84 = (f32[16,16,32,128]{3,2,1,0:T(8,128)}, f32[16,2,32,128]{3,2,1,0:T(8,128)}, f32[16,2,32,128]{3,2,1,0:T(8,128)}) custom-call(s32[2]{0:T(128)} %pad_add_fusion.place, s32[32,2]{1,0:T(8,128)} %copy.9.refs_0_.index, s32[32,2]{1,0:T(8,128)} %copy.18.refs_1_.refs_0_.index, f32[4,16,4096]{2,1,0:T(8,128)} %get-tuple-element.70.refs_2_, ...), custom_call_target="tpu_custom_call" | custom-call | flops 2415919104 | bytes 19923464 | tf_op jit(solution)/shard_map/pallas_call | solution.py:479
  282.5 47.8 %collective-permute-done.5.refs_2_ = f32[4,16,4096]{2,1,0:T(8,128)S(1)} collective-permute-done((f32[4,16,4096]{2,1,0:T(8,128)S(1)}, f32[4,16,4096]{2,1,0:T(8,128)S(1)}, u32[]{:S(2)}, u32[]{:S(2)}) %collective-permute-start.5) | collective-permute-done | bytes 1048608 | tf_op jit(solution)/shard_map/ppermute | solution.py:613
  331.3 16.3 %shard_map.89 = (f32[16,8,32,128]{3,2,1,0:T(8,128)}, f32[16,2,32,128]{3,2,1,0:T(8,128)}) custom-call(s32[2]{0:T(128)} %pad_add_fusion.place, s32[32,2]{1,0:T(8,128)} %copy.9.refs_0_.index, f32[4,16,4096]{2,1,0:T(8,128)} %get-tuple-element.73.refs_1_, f32[4,16,4096]{2,1,0:T(8,128)} %copy-done.29, ...), custom_call_target="tpu_custom_call" | custom-call | flops 1207959552 | bytes 13107464 | tf_op jit(solution)/shard_map/pallas_call | solution.py:479
  347.6 32.3 %all_to_all.70.refs_3_ = f32[16,8,32,128]{3,2,1,0:T(8,128)} all-to-all(f32[16,8,32,128]{3,2,1,0:T(8,128)} %get-tuple-element.81), channel_id=1, replica_groups={{0,1,2,3,4,5,6,7,16,17,18,19,20,21,22,23},{8,9,10,11,12,13,14,15,24,25,..., dimensions={0} | all-to-all | bytes 4194304 | tf_op jit(solution)/shard_map/all_to_all | solution.py:599
  380.0 53.5 %all_to_all.71.refs_0_ = f32[16,16,32,128]{3,2,1,0:T(8,128)} all-to-all(f32[16,16,32,128]{3,2,1,0:T(8,128)S(1)} %copy-done.25), channel_id=1, replica_groups={{0,1,2,3,4,5,6,7,16,17,18,19,20,21,22,23},{8,9,10,11,12,13,14,15,24,25,..., dimensions={0} | all-to-all | bytes 8388608 | tf_op jit(solution)/shard_map/all_to_all | solution.py:599
  433.5 53.2 %all_to_all.72.refs_1_ = f32[16,16,32,128]{3,2,1,0:T(8,128)} all-to-all(f32[16,16,32,128]{3,2,1,0:T(8,128)S(1)} %copy-done.26), channel_id=1, replica_groups={{0,1,2,3,4,5,6,7,16,17,18,19,20,21,22,23},{8,9,10,11,12,13,14,15,24,25,..., dimensions={0} | all-to-all | bytes 8388608 | tf_op jit(solution)/shard_map/all_to_all | solution.py:599
  493.7 16.3 %shard_map.85 = (f32[16,8,32,128]{3,2,1,0:T(8,128)}, f32[16,2,32,128]{3,2,1,0:T(8,128)}) custom-call(s32[2]{0:T(128)} %pad_add_fusion.place, s32[32,2]{1,0:T(8,128)} %copy.18.refs_1_.refs_0_.index, f32[4,16,4096]{2,1,0:T(8,128)} %get-tuple-element.73.refs_1_, f32[4,16,4096]{2,1,0:T(8,128)} %copy-done.29, ...), custom_call_target="tpu_custom_call" | custom-call | flops 1207959552 | bytes 13107464 | tf_op jit(solution)/shard_map/pallas_call | solution.py:479
  509.9 38.1 %all-to-all-done.2.refs_2_ = f32[16,16,32,128]{3,2,1,0:T(8,128)} async-done(((f32[16,16,32,128]{3,2,1,0:T(8,128)}), f32[16,16,32,128]{3,2,1,0:T(8,128)}, u32[]{:S(2)}, u32[]{:S(2)}) %all-to-all-start.2) | async-done | bytes 4194336 | tf_op jit(solution)/shard_map/all_to_all | solution.py:599
  554.3 22.7 %shard_map.90 = (f32[16,4,128,128]{3,2,1,0:T(8,128)}, f32[16,4,128,128]{3,2,1,0:T(8,128)}) custom-call(f32[16,16,32,128]{3,2,1,0:T(8,128)} %all_to_all.71.refs_0_, f32[16,16,32,128]{3,2,1,0:T(8,128)} %all_to_all.72.refs_1_, f32[16,16,32,128]{3,2,1,0:T(8,128)} %all-to-all-done.2.refs_2_, f32[16,8,32,128]{3,2,1,0:T(8,128)} %all_to_all.70.refs_3_, ...), custom_call_target="tpu_custom_call" | custom-call | flops 3221225472 | bytes 27262976 | tf_op jit(solution)/shard_map/pallas_call | solution.py:479
  589.4 22.7 %shard_map.86 = (f32[16,4,128,128]{3,2,1,0:T(8,128)}, f32[16,4,128,128]{3,2,1,0:T(8,128)}) custom-call(f32[16,16,32,128]{3,2,1,0:T(8,128)} %all_to_all.71.refs_0_, f32[16,16,32,128]{3,2,1,0:T(8,128)} %all_to_all.72.refs_1_, f32[16,16,32,128]{3,2,1,0:T(8,128)} %all-to-all-done.2.refs_2_, f32[16,8,32,128]{3,2,1,0:T(8,128)} %copy-done.1, ...), custom_call_target="tpu_custom_call" | custom-call | flops 3221225472 | bytes 27262976 | tf_op jit(solution)/shard_map/pallas_call | solution.py:479
  612.2 31.6 %all-to-all-done.8.fields = f32[16,4,128,128]{3,2,1,0:T(8,128)} async-done(((f32[16,4,128,128]{3,2,1,0:T(8,128)}), f32[16,4,128,128]{3,2,1,0:T(8,128)}, u32[]{:S(2)}, u32[]{:S(2)}) %all-to-all-start.8) | async-done | bytes 4194336 | tf_op jit(solution)/shard_map/all_to_all | solution.py:599
  650.9 16.4 %shard_map.91 = f32[16,2,128,128]{3,2,1,0:T(8,128)} custom-call(f32[16,4,128,128]{3,2,1,0:T(8,128)} %all-to-all-done.8.fields, bf16[16,256,256]{2,1,0:T(8,128)(2,1)} %constant.36.clone.refs_8_.refs_5_.mhi, bf16[16,256,256]{2,1,0:T(8,128)(2,1)} %constant.37.clone.refs_9_.refs_6_.mlo), custom_call_target="tpu_custom_call" | custom-call | flops 2415919104 | bytes 10485760 | tf_op jit(solution)/shard_map/pallas_call | solution.py:479
  667.3 38.1 %all-to-all-done.4.fields = f32[16,4,128,128]{3,2,1,0:T(8,128)} async-done(((f32[16,4,128,128]{3,2,1,0:T(8,128)}), f32[16,4,128,128]{3,2,1,0:T(8,128)}, u32[]{:S(2)}, u32[]{:S(2)}) %all-to-all-start.4) | async-done | bytes 4194336 | tf_op jit(solution)/shard_map/all_to_all | solution.py:599
  711.7 16.4 %shard_map.87 = f32[16,2,128,128]{3,2,1,0:T(8,128)} custom-call(f32[16,4,128,128]{3,2,1,0:T(8,128)} %all-to-all-done.4.fields, bf16[16,256,256]{2,1,0:T(8,128)(2,1)} %constant.36.clone.refs_8_.refs_5_.mhi, bf16[16,256,256]{2,1,0:T(8,128)(2,1)} %constant.37.clone.refs_9_.refs_6_.mlo), custom_call_target="tpu_custom_call" | custom-call | flops 2415919104 | bytes 10485760 | tf_op jit(solution)/shard_map/pallas_call | solution.py:479
  728.1 10.0 all-to-all-done.9.back
  745.7 16.7 %shard_map.92 = (f32[16,4,64,128]{3,2,1,0:T(8,128)}, f32[16,4,64,128]{3,2,1,0:T(8,128)}) custom-call(f32[16,2,128,128]{3,2,1,0:T(8,128)} %copy-done.2, f32[16,4,128,128]{3,2,1,0:T(8,128)} %get-tuple-element.83.kept, bf16[16,256,256]{2,1,0:T(8,128)(2,1)} %constant.34.clone.refs_4_.mhi, bf16[16,256,256]{2,1,0:T(8,128)(2,1)} %constant.35.clone.refs_5_.mlo), custom_call_target="tpu_custom_call" | custom-call | flops 1610612736 | bytes 14680064 | tf_op jit(solution)/shard_map/pallas_call | solution.py:479
  762.4 9.8 all-to-all-done.5.back
  779.5 16.6 %shard_map.88 = (f32[16,4,64,128]{3,2,1,0:T(8,128)}, f32[16,4,32,128]{3,2,1,0:T(8,128)}, f32[16,4,32,128]{3,2,1,0:T(8,128)}) custom-call(f32[16,2,128,128]{3,2,1,0:T(8,128)} %copy-done, f32[16,4,128,128]{3,2,1,0:T(8,128)} %get-tuple-element.77.kept, bf16[16,256,256]{2,1,0:T(8,128)(2,1)} %constant.34.clone.refs_4_.mhi, ...), custom_call_target="tpu_custom_call" | custom-call | flops 1610612736 | bytes 14680064 | tf_op jit(solution)/shard_map/pallas_call | solution.py:479
  796.1 9.8 all-to-all-done.10.back
  812.1 17.0 %shard_map.93 = (f32[2,32,4096]{2,1,0:T(8,128)}, f32[2,32,4096]{2,1,0:T(8,128)}) custom-call(s32[2]{0:T(128)} %pad_add_fusion.place, s32[32,2]{1,0:T(8,128)} %copy.9.refs_0_.index, f32[16,4,64,128]{3,2,1,0:T(8,128)} %all-to-all-done.10.back, bf16[32,256,128]{2,1,0:T(8,128)(2,1)} %get-tuple-element.155.refs_4_.refs_3_.whi, ...), custom_call_target="tpu_custom_call" | custom-call | flops 1207959552 | bytes 13631752 | tf_op jit(solution)/shard_map/pallas_call | solution.py:479
  846.0 17.6 %shard_map.94 = (f32[2,32,4096]{2,1,0:T(8,128)}, f32[2,32,4096]{2,1,0:T(8,128)}) custom-call(s32[2]{0:T(128)} %pad_add_fusion.place, s32[32,2]{1,0:T(8,128)} %copy.18.refs_1_.refs_0_.index, f32[16,4,64,128]{3,2,1,0:T(8,128)} %copy-done.4, bf16[32,256,128]{2,1,0:T(8,128)(2,1)} %get-tuple-element.156.refs_6_.refs_3_.whi, ...), custom_call_target="tpu_custom_call" | custom-call | flops 1207959552 | bytes 15728904 | tf_op jit(solution)/shard_map/pallas_call | solution.py:479
  878.6 17.0 %shard_map.95 = (f32[2,16,4096]{2,1,0:T(8,128)}, f32[2,16,4096]{2,1,0:T(8,128)}, f32[2,16,4096]{2,1,0:T(8,128)}, f32[2,16,4096]{2,1,0:T(8,128)}) custom-call(s32[2]{0:T(128)} %pad_add_fusion.place, s32[32,2]{1,0:T(8,128)} %copy.9.refs_0_.index, f32[16,4,64,128]{3,2,1,0:T(8,128)} %copy-done.3, bf16[32,256,128]{2,1,0:T(8,128)(2,1)} %get-tuple-element.155.refs_4_.refs_3_.whi, ...), custom_call_target="tpu_custom_call" | custom-call | flops 1207959552 | bytes 13631752 | tf_op jit(solution)/shard_map/pallas_call | solution.py:479
  903.2 15.4 %shard_map.96 = (f32[2,16,4096]{2,1,0:T(8,128)}, f32[2,16,4096]{2,1,0:T(8,128)}) custom-call(s32[2]{0:T(128)} %pad_add_fusion.place, s32[32,2]{1,0:T(8,128)} %copy.18.refs_1_.refs_0_.index, f32[16,4,32,128]{3,2,1,0:T(8,128)} %copy-done.28, bf16[32,256,128]{2,1,0:T(8,128)(2,1)} %get-tuple-element.156.refs_6_.refs_3_.whi, ...), custom_call_target="tpu_custom_call" | custom-call | flops 603979776 | bytes 12058888 | tf_op jit(solution)/shard_map/pallas_call | solution.py:479
  923.4 36.8 %collective-permute-done.6 = f32[2,32,4096]{2,1,0:T(8,128)} collective-permute-done((f32[2,32,4096]{2,1,0:T(8,128)}, f32[2,32,4096]{2,1,0:T(8,128)}, u32[]{:S(2)}, u32[]{:S(2)}) %collective-permute-start.6) | collective-permute-done | bytes 1048608 | tf_op jit(solution)/shard_map/ppermute | solution.py:613
  963.9 15.5 %shard_map.97 = (f32[2,16,4096]{2,1,0:T(8,128)}, f32[2,16,4096]{2,1,0:T(8,128)}) custom-call(s32[2]{0:T(128)} %pad_add_fusion.place, s32[32,2]{1,0:T(8,128)} %copy.18.refs_1_.refs_0_.index, f32[16,4,32,128]{3,2,1,0:T(8,128)} %copy-done.27, bf16[32,256,128]{2,1,0:T(8,128)(2,1)} %get-tuple-element.156.refs_6_.refs_3_.whi, ...), custom_call_target="tpu_custom_call" | custom-call | flops 603979776 | bytes 12058888 | tf_op jit(solution)/shard_map/pallas_call | solution.py:479
  981.5 21.2 %collective-permute-done.10 = f32[2,16,4096]{2,1,0:T(8,128)S(1)} collective-permute-done((f32[2,16,4096]{2,1,0:T(8,128)}, f32[2,16,4096]{2,1,0:T(8,128)S(1)}, u32[]{:S(2)}, u32[]{:S(2)}) %collective-permute-start.10) | collective-permute-done | bytes 524320 | tf_op jit(solution)/shard_map/ppermute | solution.py:613
  (140 shorter events, 159.8 us)
Async XLA Ops:
  3.1 24.1 %collective-permute-start = (f32[4,16,4096]{2,1,0:T(8,128)S(1)}, f32[4,16,4096]{2,1,0:T(8,128)S(1)}, u32[]{:S(2)}, u32[]{:S(2)}) collective-permute-start(f32[4,16,4096]{2,1,0:T(8,128)S(1)} %fusion.7), channel_id=1, source_target_pairs={{0,16},{1,17},{2,18},{3,19},{4,20},{5,21},{6,22},{7,23},{8,24},{9,... | collective-permute-start | bytes 3145736 | tf_op jit(solution)/shard_map/ppermute | solution.py:613
  28.2 68.4 %collective-permute-start.1 = (f32[12,16,4096]{2,1,0:T(8,128)}, f32[12,16,4096]{2,1,0:T(8,128)}, u32[]{:S(2)}, u32[]{:S(2)}) collective-permute-start(f32[12,16,4096]{2,1,0:T(8,128)} %pad_maximum_fusion), channel_id=1, source_target_pairs={{0,16},{1,17},{2,18},{3,19},{4,20},{5,21},{6,22},{7,23},{8,24},{9,... | collective-permute-start | bytes 9437192 | tf_op jit(solution)/shard_map/ppermute | solution.py:613
  39.4 57.1 %copy-start.9 = (f32[2,16,4096]{2,1,0:T(8,128)S(1)}, f32[2,16,4096]{2,1,0:T(8,128)}, u32[]{:S(2)}) copy-start(f32[2,16,4096]{2,1,0:T(8,128)} %copy-done.8) | copy-start | bytes 1572868
  39.4 57.1 %copy-start.11 = (f32[2,16,4096]{2,1,0:T(8,128)S(1)}, f32[2,16,4096]{2,1,0:T(8,128)}, u32[]{:S(2)}) copy-start(f32[2,16,4096]{2,1,0:T(8,128)} %copy-done.10) | copy-start | bytes 1572868
  39.5 57.1 %copy-start.13 = (f32[2,16,4096]{2,1,0:T(8,128)S(1)}, f32[2,16,4096]{2,1,0:T(8,128)}, u32[]{:S(2)}) copy-start(f32[2,16,4096]{2,1,0:T(8,128)} %copy-done.12) | copy-start | bytes 1572868
  39.5 57.1 %copy-start.15 = (f32[2,16,4096]{2,1,0:T(8,128)S(1)}, f32[2,16,4096]{2,1,0:T(8,128)}, u32[]{:S(2)}) copy-start(f32[2,16,4096]{2,1,0:T(8,128)} %copy-done.14) | copy-start | bytes 1572868
  40.6 58.8 %collective-permute-start.2 = (f32[4,16,4096]{2,1,0:T(8,128)S(1)}, f32[4,16,4096]{2,1,0:T(8,128)S(1)}, u32[]{:S(2)}, u32[]{:S(2)}) collective-permute-start(f32[4,16,4096]{2,1,0:T(8,128)S(1)} %get-tuple-element.149), channel_id=1, source_target_pairs={{0,8},{1,9},{2,10},{3,11},{4,12},{5,13},{6,14},{7,15},{8,0},{9,1},... | collective-permute-start | bytes 3145736 | tf_op jit(solution)/shard_map/ppermute | solution.py:613
  100.4 31.2 %copy-start.6 = (f32[2,16,4096]{2,1,0:T(8,128)S(1)}, f32[2,16,4096]{2,1,0:T(8,128)}, u32[]{:S(2)}) copy-start(f32[2,16,4096]{2,1,0:T(8,128)} %copy-done.5) | copy-start | bytes 1572868
  129.3 47.7 %collective-permute-start.3 = (f32[4,16,4096]{2,1,0:T(8,128)}, f32[4,16,4096]{2,1,0:T(8,128)}, u32[]{:S(2)}, u32[]{:S(2)}) collective-permute-start(f32[4,16,4096]{2,1,0:T(8,128)} %get-tuple-element.68), channel_id=1, source_target_pairs={{0,8},{1,9},{2,10},{3,11},{4,12},{5,13},{6,14},{7,15},{8,0},{9,1},... | collective-permute-start | bytes 3145736 | tf_op jit(solution)/shard_map/ppermute | solution.py:613
  205.8 46.7 %collective-permute-start.4 = (f32[4,16,4096]{2,1,0:T(8,128)}, f32[4,16,4096]{2,1,0:T(8,128)S(1)}, u32[]{:S(2)}, u32[]{:S(2)}) collective-permute-start(f32[4,16,4096]{2,1,0:T(8,128)} %get-tuple-element.71), channel_id=1, source_target_pairs={{0,8},{1,9},{2,10},{3,11},{4,12},{5,13},{6,14},{7,15},{8,0},{9,1},... | collective-permute-start | bytes 3145736 | tf_op jit(solution)/shard_map/ppermute | solution.py:613
  208.7 73.7 %copy-start.37 = (f32[4,16,4096]{2,1,0:T(8,128)S(1)}, f32[4,16,4096]{2,1,0:T(8,128)}, u32[]{:S(2)}) copy-start(f32[4,16,4096]{2,1,0:T(8,128)} %get-tuple-element.74) | copy-start | bytes 3145732
  282.4 47.9 %collective-permute-start.5 = (f32[4,16,4096]{2,1,0:T(8,128)S(1)}, f32[4,16,4096]{2,1,0:T(8,128)S(1)}, u32[]{:S(2)}, u32[]{:S(2)}) collective-permute-start(f32[4,16,4096]{2,1,0:T(8,128)S(1)} %copy-done.37), channel_id=1, source_target_pairs={{0,8},{1,9},{2,10},{3,11},{4,12},{5,13},{6,14},{7,15},{8,0},{9,1},... | collective-permute-start | bytes 3145736 | tf_op jit(solution)/shard_map/ppermute | solution.py:613
  347.6 32.4 %copy-start.25 = (f32[16,16,32,128]{3,2,1,0:T(8,128)S(1)}, f32[16,16,32,128]{3,2,1,0:T(8,128)}, u32[]{:S(2)}) copy-start(f32[16,16,32,128]{3,2,1,0:T(8,128)} %get-tuple-element.66) | copy-start | bytes 12582916
  380.0 53.5 %copy-start.26 = (f32[16,16,32,128]{3,2,1,0:T(8,128)S(1)}, f32[16,16,32,128]{3,2,1,0:T(8,128)}, u32[]{:S(2)}) copy-start(f32[16,16,32,128]{3,2,1,0:T(8,128)} %get-tuple-element.69) | copy-start | bytes 12582916
  486.7 61.3 %all-to-all-start.2 = ((f32[16,16,32,128]{3,2,1,0:T(8,128)}), f32[16,16,32,128]{3,2,1,0:T(8,128)}, u32[]{:S(2)}, u32[]{:S(2)}) async-start(f32[16,16,32,128]{3,2,1,0:T(8,128)} %get-tuple-element.72), calls=%async_computation.2 | async-start | bytes 8388608 | tf_op jit(solution)/shard_map/all_to_all | solution.py:599
  548.0 32.8 %all-to-all-start.3 = ((f32[16,8,32,128]{3,2,1,0:T(8,128)}), f32[16,8,32,128]{3,2,1,0:T(8,128)S(1)}, u32[]{:S(2)}, u32[]{:S(2)}) async-start(f32[16,8,32,128]{3,2,1,0:T(8,128)} %get-tuple-element.75), calls=%async_computation.3 | async-start | bytes 4194304 | tf_op jit(solution)/shard_map/all_to_all | solution.py:599
  582.1 61.7 %all-to-all-start.8 = ((f32[16,4,128,128]{3,2,1,0:T(8,128)}), f32[16,4,128,128]{3,2,1,0:T(8,128)}, u32[]{:S(2)}, u32[]{:S(2)}) async-start(f32[16,4,128,128]{3,2,1,0:T(8,128)} %get-tuple-element.82), calls=%async_computation.8 | async-start | bytes 8388608 | tf_op jit(solution)/shard_map/all_to_all | solution.py:599
  643.8 61.6 %all-to-all-start.4 = ((f32[16,4,128,128]{3,2,1,0:T(8,128)}), f32[16,4,128,128]{3,2,1,0:T(8,128)}, u32[]{:S(2)}, u32[]{:S(2)}) async-start(f32[16,4,128,128]{3,2,1,0:T(8,128)} %get-tuple-element.76), calls=%async_computation.4 | async-start | bytes 8388608 | tf_op jit(solution)/shard_map/all_to_all | solution.py:599
  705.4 32.8 %all-to-all-start.9 = ((f32[16,2,128,128]{3,2,1,0:T(8,128)}), f32[16,2,128,128]{3,2,1,0:T(8,128)S(1)}, u32[]{:S(2)}, u32[]{:S(2)}) async-start(f32[16,2,128,128]{3,2,1,0:T(8,128)} %shard_map.91), calls=%async_computation.9 | async-start | bytes 4194304 | tf_op jit(solution)/shard_map/all_to_all | solution.py:599
  739.5 32.7 %all-to-all-start.5 = ((f32[16,2,128,128]{3,2,1,0:T(8,128)}), f32[16,2,128,128]{3,2,1,0:T(8,128)S(1)}, u32[]{:S(2)}, u32[]{:S(2)}) async-start(f32[16,2,128,128]{3,2,1,0:T(8,128)} %shard_map.87), calls=%async_computation.5 | async-start | bytes 4194304 | tf_op jit(solution)/shard_map/all_to_all | solution.py:599
  772.2 33.7 %all-to-all-start.10 = ((f32[16,4,64,128]{3,2,1,0:T(8,128)}), f32[16,4,64,128]{3,2,1,0:T(8,128)}, u32[]{:S(2)}, u32[]{:S(2)}) async-start(f32[16,4,64,128]{3,2,1,0:T(8,128)} %get-tuple-element.84), calls=%async_computation.10 | async-start | bytes 4194304 | tf_op jit(solution)/shard_map/all_to_all | solution.py:599
  805.9 32.7 %all-to-all-start.6 = ((f32[16,4,64,128]{3,2,1,0:T(8,128)}), f32[16,4,64,128]{3,2,1,0:T(8,128)S(1)}, u32[]{:S(2)}, u32[]{:S(2)}) async-start(f32[16,4,64,128]{3,2,1,0:T(8,128)} %get-tuple-element.78), calls=%async_computation.6 | async-start | bytes 4194304 | tf_op jit(solution)/shard_map/all_to_all | solution.py:599
  839.8 32.7 %all-to-all-start.12 = ((f32[16,4,64,128]{3,2,1,0:T(8,128)}), f32[16,4,64,128]{3,2,1,0:T(8,128)S(1)}, u32[]{:S(2)}, u32[]{:S(2)}) async-start(f32[16,4,64,128]{3,2,1,0:T(8,128)} %get-tuple-element.95), calls=%async_computation.12 | async-start | bytes 4194304 | tf_op jit(solution)/shard_map/all_to_all | solution.py:599
  872.5 23.2 %all-to-all-start.11 = ((f32[16,4,32,128]{3,2,1,0:T(8,128)}), f32[16,4,32,128]{3,2,1,0:T(8,128)S(1)}, u32[]{:S(2)}, u32[]{:S(2)}) async-start(f32[16,4,32,128]{3,2,1,0:T(8,128)} %get-tuple-element.92), calls=%async_computation.11 | async-start | bytes 2097152 | tf_op jit(solution)/shard_map/all_to_all | solution.py:599
  895.7 67.3 %all-to-all-start.13 = ((f32[16,4,32,128]{3,2,1,0:T(8,128)}), f32[16,4,32,128]{3,2,1,0:T(8,128)S(1)}, u32[]{:S(2)}, u32[]{:S(2)}) async-start(f32[16,4,32,128]{3,2,1,0:T(8,128)} %get-tuple-element.105), calls=%async_computation.13 | async-start | bytes 2097152 | tf_op jit(solution)/shard_map/all_to_all | solution.py:599
  900.8 59.3 %collective-permute-start.6 = (f32[2,32,4096]{2,1,0:T(8,128)}, f32[2,32,4096]{2,1,0:T(8,128)}, u32[]{:S(2)}, u32[]{:S(2)}) collective-permute-start(f32[2,32,4096]{2,1,0:T(8,128)} %get-tuple-element.89), channel_id=1, source_target_pairs={{0,8},{1,9},{2,10},{3,11},{4,12},{5,13},{6,14},{7,15},{16,0},{17,1... | collective-permute-start | bytes 3145736 | tf_op jit(solution)/shard_map/ppermute | solution.py:613
  900.9 62.0 %collective-permute-start.7 = (f32[2,32,4096]{2,1,0:T(8,128)}, f32[2,32,4096]{2,1,0:T(8,128)}, u32[]{:S(2)}, u32[]{:S(2)}) collective-permute-start(f32[2,32,4096]{2,1,0:T(8,128)} %get-tuple-element.110), channel_id=1, source_target_pairs={{8,16},{9,17},{10,18},{11,19},{12,20},{13,21},{14,22},{15,23},{16,... | collective-permute-start | bytes 3145736 | tf_op jit(solution)/shard_map/ppermute | solution.py:613
  918.6 62.9 %collective-permute-start.8 = (f32[2,16,4096]{2,1,0:T(8,128)}, f32[2,16,4096]{2,1,0:T(8,128)S(1)}, u32[]{:S(2)}, u32[]{:S(2)}) collective-permute-start(f32[2,16,4096]{2,1,0:T(8,128)} %get-tuple-element.100), channel_id=1, source_target_pairs={{0,8},{1,9},{2,10},{3,11},{4,12},{5,13},{6,14},{7,15},{16,0},{17,1... | collective-permute-start | bytes 1572872 | tf_op jit(solution)/shard_map/ppermute | solution.py:613
  918.6 62.9 %collective-permute-start.9 = (f32[2,16,4096]{2,1,0:T(8,128)}, f32[2,16,4096]{2,1,0:T(8,128)S(1)}, u32[]{:S(2)}, u32[]{:S(2)}) collective-permute-start(f32[2,16,4096]{2,1,0:T(8,128)} %get-tuple-element.113), channel_id=1, source_target_pairs={{8,16},{9,17},{10,18},{11,19},{12,20},{13,21},{14,22},{15,23},{16,... | collective-permute-start | bytes 1572872 | tf_op jit(solution)/shard_map/ppermute | solution.py:613
  963.9 42.5 %copy-start.34 = (f32[2,32,4096]{2,1,0:T(8,128)S(1)}, f32[2,32,4096]{2,1,0:T(8,128)}, u32[]{:S(2)}) copy-start(f32[2,32,4096]{2,1,0:T(8,128)} %get-tuple-element.110) | copy-start | bytes 3145732
  979.4 23.3 %collective-permute-start.10 = (f32[2,16,4096]{2,1,0:T(8,128)}, f32[2,16,4096]{2,1,0:T(8,128)S(1)}, u32[]{:S(2)}, u32[]{:S(2)}) collective-permute-start(f32[2,16,4096]{2,1,0:T(8,128)} %get-tuple-element.108), channel_id=1, source_target_pairs={{0,8},{1,9},{2,10},{3,11},{4,12},{5,13},{6,14},{7,15},{16,0},{17,1... | collective-permute-start | bytes 1572872 | tf_op jit(solution)/shard_map/ppermute | solution.py:613
  979.4 27.0 %collective-permute-start.11 = (f32[2,16,4096]{2,1,0:T(8,128)}, f32[2,16,4096]{2,1,0:T(8,128)S(1)}, u32[]{:S(2)}, u32[]{:S(2)}) collective-permute-start(f32[2,16,4096]{2,1,0:T(8,128)} %get-tuple-element.116), channel_id=1, source_target_pairs={{8,16},{9,17},{10,18},{11,19},{12,20},{13,21},{14,22},{15,23},{16,... | collective-permute-start | bytes 1572872 | tf_op jit(solution)/shard_map/ppermute | solution.py:613
  (31 other events, 116.1 us)

commit v10 on v9

--- a/solution.py
+++ b/solution.py
@@ -672,9 +672,10 @@
     arrived = [[] for _ in angles]
     bases = [[] for _ in angles]
     ahead = [[] for _ in angles]
-    fields = ()
+    fields = moved = earlier = ()
     for c, (own, give) in enumerate(chunks):
-        along = permute(after(give, fields), ALONG)
+        along = permute(after(give, (fields, earlier)), ALONG)
+        earlier = moved
         own = after(own, beside)
         for part in (angles,) if c + 1 < CHUNKS else [[a] for a in angles]:
             fields, fronts = enter(
@@ -707,12 +708,11 @@
     totals = home(1, next_back, 0, start, (most,))
     next_back = exchange(after(late[1], totals))
     starts = home(0, back, most, (), rest)
-    back = exchange(after(late[2], starts))
+    leaving = [depart(*totals[0])]
+    back = exchange(after(late[2], (starts, leaving)))
     totals += home(1, next_back, most, starts[0], rest[:1])
-    leaving = [depart(*total) for total in totals]
-    back = after(back, leaving[0])
     totals += home(1, back, most + rest[0], starts[1], rest[1:])
-    leaving.append(depart(*totals[-1]))
+    leaving += [depart(*total) for total in totals[1:]]
     pieces = []
     total = totals[-1]
     for span, moved in zip(spans, after(leaving, total)):

time: 1020 us -> 977 us (0.958)
  blocking collectives: 139 us -> 30.1 us
  waiting for transfers between devices: 428 us -> 471 us
  starting transfers between devices: 85.4 us -> 105 us
    all_to_all x3 -> x1, blocking collectives: 139 us -> 30.1 us  [exchange(): lax.all_to_all(values, ('parts', 'fft'), split_axis=0, concat_axis=0, axi...]
    ppermute x12, waiting for transfers between devices: 269 us -> 312 us  [permute(): return lax.ppermute(values, ('parts', 'fft'), pairs)]
    all_to_all x11 -> x13, starting transfers between devices: 71.2 us -> 87.3 us  [exchange(): lax.all_to_all(values, ('parts', 'fft'), split_axis=0, concat_axis=0, axi...]
    all_to_all x11 -> x13, waiting for transfers between devices: 159 us -> 159 us  [exchange(): lax.all_to_all(values, ('parts', 'fft'), split_axis=0, concat_axis=0, axi...]
  transfers between devices with their start and end apart: 23 -> 25, of which waited for: 18 -> 20; matrix products, arithmetic and copies ran while one was open for 3% -> 3% of each run, Pallas kernels for 21% -> 28%
where the time goes in v10:
time: 977 us; the launch traced here: 967 us
  waiting for transfers between devices  471 us (48%)
  Pallas kernels  314 us (32%)
  starting transfers between devices  105 us (11%)
  blocking collectives  30.1 us (3%)
  other arithmetic  23.3 us (2%)
  local copies, waits for them, and re-layouts  23.1 us (2%)
    pallas_call x16, Pallas kernels, call(): pl.pallas_call(kernel, out_shape=[jax.ShapeDtypeStruct(o, jnp.float32) fo...  314 us
    ppermute x12, waiting for transfers between devices, permute(): return lax.ppermute(values, ('parts', 'fft'), pairs)  312 us
    all_to_all x13, waiting for transfers between devices, exchange(): lax.all_to_all(values, ('parts', 'fft'), split_axis=0, concat_axis=0, axi...  159 us
    all_to_all x13, starting transfers between devices, exchange(): lax.all_to_all(values, ('parts', 'fft'), split_axis=0, concat_axis=0, axi...  87.3 us
    all_to_all x1, blocking collectives, exchange(): lax.all_to_all(values, ('parts', 'fft'), split_axis=0, concat_axis=0, axi...  30.1 us
  transfers between devices with their start and end apart: 25, of which 20 were waited for; matrix products, arithmetic and copies ran while one was open for 3% of the time, Pallas kernels for 28%

profile of v10, /device:TPU:3, one launch (start us, length us, event | category | flops | bytes accessed | tf_op | source)
XLA Modules:
  0.0 967.2 jit_solution(14532762323621795034)
XLA Ops:
  10.3 16.9 %collective-permute-done = f32[4,16,4096]{2,1,0:T(8,128)S(1)} collective-permute-done((f32[4,16,4096]{2,1,0:T(8,128)S(1)}, f32[4,16,4096]{2,1,0:T(8,128)S(1)}, u32[]{:S(2)}, u32[]{:S(2)}) %collective-permute-start) | collective-permute-done | bytes 1048608 | tf_op jit(solution)/shard_map/ppermute | solution.py:613
  45.0 51.6 %collective-permute-done.1 = f32[12,16,4096]{2,1,0:T(8,128)} collective-permute-done((f32[12,16,4096]{2,1,0:T(8,128)}, f32[12,16,4096]{2,1,0:T(8,128)}, u32[]{:S(2)}, u32[]{:S(2)}) %collective-permute-start.1) | collective-permute-done | bytes 3145760 | tf_op jit(solution)/shard_map/ppermute | solution.py:613
  96.5 28.8 %shard_map.82 = (f32[16,16,32,128]{3,2,1,0:T(8,128)}, f32[16,2,32,128]{3,2,1,0:T(8,128)}, f32[16,2,32,128]{3,2,1,0:T(8,128)}) custom-call(s32[2]{0:T(128)} %pad_add_fusion.place, s32[32,2]{1,0:T(8,128)} %copy.9.refs_0_.index, s32[32,2]{1,0:T(8,128)} %copy.18.refs_1_.refs_0_.index, f32[4,16,4096]{2,1,0:T(8,128)} %get-tuple-element.64.refs_2_, ...), custom_call_target="tpu_custom_call" | custom-call | flops 2415919104 | bytes 19923464 | tf_op jit(solution)/shard_map/pallas_call | solution.py:479
  138.1 69.8 %collective-permute-done.3.refs_3_ = f32[4,16,4096]{2,1,0:T(8,128)} collective-permute-done((f32[4,16,4096]{2,1,0:T(8,128)S(1)}, f32[4,16,4096]{2,1,0:T(8,128)}, u32[]{:S(2)}, u32[]{:S(2)}) %collective-permute-start.3) | collective-permute-done | bytes 1048608 | tf_op jit(solution)/shard_map/ppermute | solution.py:613
  207.9 28.9 %shard_map.83 = (f32[16,16,32,128]{3,2,1,0:T(8,128)}, f32[16,2,32,128]{3,2,1,0:T(8,128)}, f32[16,2,32,128]{3,2,1,0:T(8,128)}) custom-call(s32[2]{0:T(128)} %pad_add_fusion.place, s32[32,2]{1,0:T(8,128)} %copy.9.refs_0_.index, s32[32,2]{1,0:T(8,128)} %copy.18.refs_1_.refs_0_.index, f32[4,16,4096]{2,1,0:T(8,128)} %get-tuple-element.66.refs_2_, ...), custom_call_target="tpu_custom_call" | custom-call | flops 2415919104 | bytes 19923464 | tf_op jit(solution)/shard_map/pallas_call | solution.py:479
  250.7 69.7 %collective-permute-done.4.refs_3_ = f32[4,16,4096]{2,1,0:T(8,128)S(1)} collective-permute-done((f32[4,16,4096]{2,1,0:T(8,128)S(1)}, f32[4,16,4096]{2,1,0:T(8,128)S(1)}, u32[]{:S(2)}, u32[]{:S(2)}) %collective-permute-start.4) | collective-permute-done | bytes 1048608 | tf_op jit(solution)/shard_map/ppermute | solution.py:613
  321.4 28.8 %shard_map.84 = (f32[16,16,32,128]{3,2,1,0:T(8,128)}, f32[16,2,32,128]{3,2,1,0:T(8,128)}, f32[16,2,32,128]{3,2,1,0:T(8,128)}) custom-call(s32[2]{0:T(128)} %pad_add_fusion.place, s32[32,2]{1,0:T(8,128)} %copy.9.refs_0_.index, s32[32,2]{1,0:T(8,128)} %copy.18.refs_1_.refs_0_.index, f32[4,16,4096]{2,1,0:T(8,128)} %get-tuple-element.69.refs_2_, ...), custom_call_target="tpu_custom_call" | custom-call | flops 2415919104 | bytes 19923464 | tf_op jit(solution)/shard_map/pallas_call | solution.py:479
  353.4 45.7 %collective-permute-done.5.refs_2_ = f32[4,16,4096]{2,1,0:T(8,128)S(1)} collective-permute-done((f32[4,16,4096]{2,1,0:T(8,128)S(1)}, f32[4,16,4096]{2,1,0:T(8,128)S(1)}, u32[]{:S(2)}, u32[]{:S(2)}) %collective-permute-start.5) | collective-permute-done | bytes 1048608 | tf_op jit(solution)/shard_map/ppermute | solution.py:613
  400.0 16.4 %shard_map.89 = (f32[16,8,32,128]{3,2,1,0:T(8,128)}, f32[16,2,32,128]{3,2,1,0:T(8,128)}) custom-call(s32[2]{0:T(128)} %pad_add_fusion.place, s32[32,2]{1,0:T(8,128)} %copy.9.refs_0_.index, f32[4,16,4096]{2,1,0:T(8,128)} %get-tuple-element.72.refs_1_, f32[4,16,4096]{2,1,0:T(8,128)} %copy-done.18, ...), custom_call_target="tpu_custom_call" | custom-call | flops 1207959552 | bytes 13107464 | tf_op jit(solution)/shard_map/pallas_call | solution.py:479
  416.4 30.1 %all_to_all.70.refs_3_ = f32[16,8,32,128]{3,2,1,0:T(8,128)} all-to-all(f32[16,8,32,128]{3,2,1,0:T(8,128)} %get-tuple-element.80), channel_id=1, replica_groups={{0,1,2,3,4,5,6,7,16,17,18,19,20,21,22,23},{8,9,10,11,12,13,14,15,24,25,..., dimensions={0} | all-to-all | bytes 4194304 | tf_op jit(solution)/shard_map/all_to_all | solution.py:599
  453.5 16.4 %shard_map.85 = (f32[16,8,32,128]{3,2,1,0:T(8,128)}, f32[16,2,32,128]{3,2,1,0:T(8,128)}) custom-call(s32[2]{0:T(128)} %pad_add_fusion.place, s32[32,2]{1,0:T(8,128)} %copy.18.refs_1_.refs_0_.index, f32[4,16,4096]{2,1,0:T(8,128)} %get-tuple-element.72.refs_1_, f32[4,16,4096]{2,1,0:T(8,128)} %copy-done.18, ...), custom_call_target="tpu_custom_call" | custom-call | flops 1207959552 | bytes 13107464 | tf_op jit(solution)/shard_map/pallas_call | solution.py:479
  469.9 37.9 %all-to-all-done.2.refs_2_ = f32[16,16,32,128]{3,2,1,0:T(8,128)} async-done(((f32[16,16,32,128]{3,2,1,0:T(8,128)}), f32[16,16,32,128]{3,2,1,0:T(8,128)}, u32[]{:S(2)}, u32[]{:S(2)}) %all-to-all-start.2) | async-done | bytes 4194336 | tf_op jit(solution)/shard_map/all_to_all | solution.py:599
  514.2 22.9 %shard_map.90 = (f32[16,4,128,128]{3,2,1,0:T(8,128)}, f32[16,4,128,128]{3,2,1,0:T(8,128)}) custom-call(f32[16,16,32,128]{3,2,1,0:T(8,128)} %all-to-all-done.refs_0_, f32[16,16,32,128]{3,2,1,0:T(8,128)} %all-to-all-done.1.refs_1_, f32[16,16,32,128]{3,2,1,0:T(8,128)} %all-to-all-done.2.refs_2_, f32[16,8,32,128]{3,2,1,0:T(8,128)} %all_to_all.70.refs_3_, ...), custom_call_target="tpu_custom_call" | custom-call | flops 3221225472 | bytes 27262976 | tf_op jit(solution)/shard_map/pallas_call | solution.py:479
  549.3 22.9 %shard_map.86 = (f32[16,4,128,128]{3,2,1,0:T(8,128)}, f32[16,4,128,128]{3,2,1,0:T(8,128)}) custom-call(f32[16,16,32,128]{3,2,1,0:T(8,128)} %all-to-all-done.refs_0_, f32[16,16,32,128]{3,2,1,0:T(8,128)} %all-to-all-done.1.refs_1_, f32[16,16,32,128]{3,2,1,0:T(8,128)} %all-to-all-done.2.refs_2_, f32[16,8,32,128]{3,2,1,0:T(8,128)} %copy-done.1, ...), custom_call_target="tpu_custom_call" | custom-call | flops 3221225472 | bytes 27262976 | tf_op jit(solution)/shard_map/pallas_call | solution.py:479
  572.2 31.5 %all-to-all-done.8.fields = f32[16,4,128,128]{3,2,1,0:T(8,128)} async-done(((f32[16,4,128,128]{3,2,1,0:T(8,128)}), f32[16,4,128,128]{3,2,1,0:T(8,128)}, u32[]{:S(2)}, u32[]{:S(2)}) %all-to-all-start.8) | async-done | bytes 4194336 | tf_op jit(solution)/shard_map/all_to_all | solution.py:599
  610.7 16.4 %shard_map.91 = f32[16,2,128,128]{3,2,1,0:T(8,128)} custom-call(f32[16,4,128,128]{3,2,1,0:T(8,128)} %all-to-all-done.8.fields, bf16[16,256,256]{2,1,0:T(8,128)(2,1)} %constant.36.clone.refs_8_.refs_5_.mhi, bf16[16,256,256]{2,1,0:T(8,128)(2,1)} %constant.37.clone.refs_9_.refs_6_.mlo), custom_call_target="tpu_custom_call" | custom-call | flops 2415919104 | bytes 10485760 | tf_op jit(solution)/shard_map/pallas_call | solution.py:479
  627.1 38.1 %all-to-all-done.4.fields = f32[16,4,128,128]{3,2,1,0:T(8,128)} async-done(((f32[16,4,128,128]{3,2,1,0:T(8,128)}), f32[16,4,128,128]{3,2,1,0:T(8,128)}, u32[]{:S(2)}, u32[]{:S(2)}) %all-to-all-start.4) | async-done | bytes 4194336 | tf_op jit(solution)/shard_map/all_to_all | solution.py:599
  671.5 16.4 %shard_map.87 = f32[16,2,128,128]{3,2,1,0:T(8,128)} custom-call(f32[16,4,128,128]{3,2,1,0:T(8,128)} %all-to-all-done.4.fields, bf16[16,256,256]{2,1,0:T(8,128)(2,1)} %constant.36.clone.refs_8_.refs_5_.mhi, bf16[16,256,256]{2,1,0:T(8,128)(2,1)} %constant.37.clone.refs_9_.refs_6_.mlo), custom_call_target="tpu_custom_call" | custom-call | flops 2415919104 | bytes 10485760 | tf_op jit(solution)/shard_map/pallas_call | solution.py:479
  688.0 10.0 %all-to-all-done.9.back = f32[16,2,128,128]{3,2,1,0:T(8,128)S(1)} async-done(((f32[16,2,128,128]{3,2,1,0:T(8,128)}), f32[16,2,128,128]{3,2,1,0:T(8,128)S(1)}, u32[]{:S(2)}, u32[]{:S(2)}) %all-to-all-start.9) | async-done | bytes 2097184 | tf_op jit(solution)/shard_map/all_to_all | solution.py:599
  705.6 16.7 %shard_map.92 = (f32[16,4,64,128]{3,2,1,0:T(8,128)}, f32[16,4,64,128]{3,2,1,0:T(8,128)}) custom-call(f32[16,2,128,128]{3,2,1,0:T(8,128)} %copy-done.2, f32[16,4,128,128]{3,2,1,0:T(8,128)} %get-tuple-element.82.kept, bf16[16,256,256]{2,1,0:T(8,128)(2,1)} %constant.34.clone.refs_4_.mhi, bf16[16,256,256]{2,1,0:T(8,128)(2,1)} %constant.35.clone.refs_5_.mlo), custom_call_target="tpu_custom_call" | custom-call | flops 1610612736 | bytes 14680064 | tf_op jit(solution)/shard_map/pallas_call | solution.py:479
  722.3 9.8 %all-to-all-done.5.back = f32[16,2,128,128]{3,2,1,0:T(8,128)S(1)} async-done(((f32[16,2,128,128]{3,2,1,0:T(8,128)}), f32[16,2,128,128]{3,2,1,0:T(8,128)S(1)}, u32[]{:S(2)}, u32[]{:S(2)}) %all-to-all-start.5) | async-done | bytes 2097184 | tf_op jit(solution)/shard_map/all_to_all | solution.py:599
  739.3 16.5 %shard_map.88 = (f32[16,4,64,128]{3,2,1,0:T(8,128)}, f32[16,4,32,128]{3,2,1,0:T(8,128)}, f32[16,4,32,128]{3,2,1,0:T(8,128)}) custom-call(f32[16,2,128,128]{3,2,1,0:T(8,128)} %copy-done, f32[16,4,128,128]{3,2,1,0:T(8,128)} %get-tuple-element.76.kept, bf16[16,256,256]{2,1,0:T(8,128)(2,1)} %constant.34.clone.refs_4_.mhi, ...), custom_call_target="tpu_custom_call" | custom-call | flops 1610612736 | bytes 14680064 | tf_op jit(solution)/shard_map/pallas_call | solution.py:479
  755.8 9.9 %all-to-all-done.10.back = f32[16,4,64,128]{3,2,1,0:T(8,128)} async-done(((f32[16,4,64,128]{3,2,1,0:T(8,128)}), f32[16,4,64,128]{3,2,1,0:T(8,128)}, u32[]{:S(2)}, u32[]{:S(2)}) %all-to-all-start.10) | async-done | bytes 2097184 | tf_op jit(solution)/shard_map/all_to_all | solution.py:599
  771.9 17.3 %shard_map.93 = (f32[2,32,4096]{2,1,0:T(8,128)}, f32[2,32,4096]{2,1,0:T(8,128)}) custom-call(s32[2]{0:T(128)} %pad_add_fusion.place, s32[32,2]{1,0:T(8,128)} %copy.9.refs_0_.index, f32[16,4,64,128]{3,2,1,0:T(8,128)} %all-to-all-done.10.back, bf16[32,256,128]{2,1,0:T(8,128)(2,1)} %get-tuple-element.153.refs_4_.refs_3_.whi, ...), custom_call_target="tpu_custom_call" | custom-call | flops 1207959552 | bytes 13631752 | tf_op jit(solution)/shard_map/pallas_call | solution.py:479
  789.2 9.2 all-to-all-done.6.back
  805.9 17.7 %shard_map.94 = (f32[2,32,4096]{2,1,0:T(8,128)}, f32[2,32,4096]{2,1,0:T(8,128)}) custom-call(s32[2]{0:T(128)} %pad_add_fusion.place, s32[32,2]{1,0:T(8,128)} %copy.18.refs_1_.refs_0_.index, f32[16,4,64,128]{3,2,1,0:T(8,128)} %copy-done.4, bf16[32,256,128]{2,1,0:T(8,128)(2,1)} %get-tuple-element.154.refs_6_.refs_3_.whi, ...), custom_call_target="tpu_custom_call" | custom-call | flops 1207959552 | bytes 15728904 | tf_op jit(solution)/shard_map/pallas_call | solution.py:479
  823.6 8.8 all-to-all-done.12.back
  841.0 17.0 %shard_map.95 = (f32[2,16,4096]{2,1,0:T(8,128)}, f32[2,16,4096]{2,1,0:T(8,128)}, f32[2,16,4096]{2,1,0:T(8,128)}, f32[2,16,4096]{2,1,0:T(8,128)}) custom-call(s32[2]{0:T(128)} %pad_add_fusion.place, s32[32,2]{1,0:T(8,128)} %copy.9.refs_0_.index, f32[16,4,64,128]{3,2,1,0:T(8,128)} %copy-done.3, bf16[32,256,128]{2,1,0:T(8,128)(2,1)} %get-tuple-element.153.refs_4_.refs_3_.whi, ...), custom_call_target="tpu_custom_call" | custom-call | flops 1207959552 | bytes 13631752 | tf_op jit(solution)/shard_map/pallas_call | solution.py:479
  858.0 28.6 %collective-permute-done.6 = f32[2,32,4096]{2,1,0:T(8,128)} collective-permute-done((f32[2,32,4096]{2,1,0:T(8,128)}, f32[2,32,4096]{2,1,0:T(8,128)}, u32[]{:S(2)}, u32[]{:S(2)}) %collective-permute-start.6) | collective-permute-done | bytes 1048608 | tf_op jit(solution)/shard_map/ppermute | solution.py:613
  894.7 15.4 %shard_map.96 = (f32[2,16,4096]{2,1,0:T(8,128)}, f32[2,16,4096]{2,1,0:T(8,128)}) custom-call(s32[2]{0:T(128)} %pad_add_fusion.place, s32[32,2]{1,0:T(8,128)} %copy.18.refs_1_.refs_0_.index, f32[16,4,32,128]{3,2,1,0:T(8,128)} %copy-done.16, bf16[32,256,128]{2,1,0:T(8,128)(2,1)} %get-tuple-element.154.refs_6_.refs_3_.whi, ...), custom_call_target="tpu_custom_call" | custom-call | flops 603979776 | bytes 12058888 | tf_op jit(solution)/shard_map/pallas_call | solution.py:479
  914.6 15.5 %shard_map.97 = (f32[2,16,4096]{2,1,0:T(8,128)}, f32[2,16,4096]{2,1,0:T(8,128)}) custom-call(s32[2]{0:T(128)} %pad_add_fusion.place, s32[32,2]{1,0:T(8,128)} %copy.18.refs_1_.refs_0_.index, f32[16,4,32,128]{3,2,1,0:T(8,128)} %copy-done.17, bf16[32,256,128]{2,1,0:T(8,128)(2,1)} %get-tuple-element.154.refs_6_.refs_3_.whi, ...), custom_call_target="tpu_custom_call" | custom-call | flops 603979776 | bytes 12058888 | tf_op jit(solution)/shard_map/pallas_call | solution.py:479
  933.8 13.0 %collective-permute-done.8 = f32[2,16,4096]{2,1,0:T(8,128)S(1)} collective-permute-done((f32[2,16,4096]{2,1,0:T(8,128)}, f32[2,16,4096]{2,1,0:T(8,128)S(1)}, u32[]{:S(2)}, u32[]{:S(2)}) %collective-permute-start.8) | collective-permute-done | bytes 524320 | tf_op jit(solution)/shard_map/ppermute | solution.py:613
  (116 shorter events, 172.0 us)
Async XLA Ops:
  3.1 24.1 %collective-permute-start = (f32[4,16,4096]{2,1,0:T(8,128)S(1)}, f32[4,16,4096]{2,1,0:T(8,128)S(1)}, u32[]{:S(2)}, u32[]{:S(2)}) collective-permute-start(f32[4,16,4096]{2,1,0:T(8,128)S(1)} %fusion.7), channel_id=1, source_target_pairs={{0,16},{1,17},{2,18},{3,19},{4,20},{5,21},{6,22},{7,23},{8,24},{9,... | collective-permute-start | bytes 3145736 | tf_op jit(solution)/shard_map/ppermute | solution.py:613
  8.3 20.2 %copy-start.26 = (s32[2,32,2]{1,2,0:T(2,128)S(1)}, s32[2,32,2]{1,2,0:T(2,128)}, u32[]{:S(2)}) copy-start(s32[2,32,2]{1,2,0:T(2,128)} %param.10) | copy-start | bytes 1540
  28.2 68.4 %collective-permute-start.1 = (f32[12,16,4096]{2,1,0:T(8,128)}, f32[12,16,4096]{2,1,0:T(8,128)}, u32[]{:S(2)}, u32[]{:S(2)}) collective-permute-start(f32[12,16,4096]{2,1,0:T(8,128)} %pad_maximum_fusion), channel_id=1, source_target_pairs={{0,16},{1,17},{2,18},{3,19},{4,20},{5,21},{6,22},{7,23},{8,24},{9,... | collective-permute-start | bytes 9437192 | tf_op jit(solution)/shard_map/ppermute | solution.py:613
  33.6 63.0 %collective-permute-start.2 = (f32[4,16,4096]{2,1,0:T(8,128)S(1)}, f32[4,16,4096]{2,1,0:T(8,128)}, u32[]{:S(2)}, u32[]{:S(2)}) collective-permute-start(f32[4,16,4096]{2,1,0:T(8,128)S(1)} %get-tuple-element.147), channel_id=1, source_target_pairs={{0,8},{1,9},{2,10},{3,11},{4,12},{5,13},{6,14},{7,15},{8,0},{9,1},... | collective-permute-start | bytes 3145736 | tf_op jit(solution)/shard_map/ppermute | solution.py:613
  125.4 111.4 %all-to-all-start = ((f32[16,16,32,128]{3,2,1,0:T(8,128)}), f32[16,16,32,128]{3,2,1,0:T(8,128)}, u32[]{:S(2)}, u32[]{:S(2)}) async-start(f32[16,16,32,128]{3,2,1,0:T(8,128)} %get-tuple-element.65), calls=%async_computation | async-start | bytes 8388608 | tf_op jit(solution)/shard_map/all_to_all | solution.py:599
  135.8 72.1 %collective-permute-start.3 = (f32[4,16,4096]{2,1,0:T(8,128)S(1)}, f32[4,16,4096]{2,1,0:T(8,128)}, u32[]{:S(2)}, u32[]{:S(2)}) collective-permute-start(f32[4,16,4096]{2,1,0:T(8,128)S(1)} %get-tuple-element.67), channel_id=1, source_target_pairs={{0,8},{1,9},{2,10},{3,11},{4,12},{5,13},{6,14},{7,15},{8,0},{9,1},... | collective-permute-start | bytes 3145736 | tf_op jit(solution)/shard_map/ppermute | solution.py:613
  236.8 113.4 %all-to-all-start.1 = ((f32[16,16,32,128]{3,2,1,0:T(8,128)}), f32[16,16,32,128]{3,2,1,0:T(8,128)}, u32[]{:S(2)}, u32[]{:S(2)}) async-start(f32[16,16,32,128]{3,2,1,0:T(8,128)} %get-tuple-element.68), calls=%async_computation.1 | async-start | bytes 8388608 | tf_op jit(solution)/shard_map/all_to_all | solution.py:599
  248.0 72.4 %collective-permute-start.4 = (f32[4,16,4096]{2,1,0:T(8,128)S(1)}, f32[4,16,4096]{2,1,0:T(8,128)S(1)}, u32[]{:S(2)}, u32[]{:S(2)}) collective-permute-start(f32[4,16,4096]{2,1,0:T(8,128)S(1)} %get-tuple-element.70), channel_id=1, source_target_pairs={{0,8},{1,9},{2,10},{3,11},{4,12},{5,13},{6,14},{7,15},{8,0},{9,1},... | collective-permute-start | bytes 3145736 | tf_op jit(solution)/shard_map/ppermute | solution.py:613
  250.7 99.5 %copy-start.24 = (f32[4,16,4096]{2,1,0:T(8,128)S(1)}, f32[4,16,4096]{2,1,0:T(8,128)}, u32[]{:S(2)}) copy-start(f32[4,16,4096]{2,1,0:T(8,128)} %get-tuple-element.73) | copy-start | bytes 3145732
  350.2 48.8 %collective-permute-start.5 = (f32[4,16,4096]{2,1,0:T(8,128)S(1)}, f32[4,16,4096]{2,1,0:T(8,128)S(1)}, u32[]{:S(2)}, u32[]{:S(2)}) collective-permute-start(f32[4,16,4096]{2,1,0:T(8,128)S(1)} %copy-done.24), channel_id=1, source_target_pairs={{0,8},{1,9},{2,10},{3,11},{4,12},{5,13},{6,14},{7,15},{8,0},{9,1},... | collective-permute-start | bytes 3145736 | tf_op jit(solution)/shard_map/ppermute | solution.py:613
  446.5 61.3 %all-to-all-start.2 = ((f32[16,16,32,128]{3,2,1,0:T(8,128)}), f32[16,16,32,128]{3,2,1,0:T(8,128)}, u32[]{:S(2)}, u32[]{:S(2)}) async-start(f32[16,16,32,128]{3,2,1,0:T(8,128)} %get-tuple-element.71), calls=%async_computation.2 | async-start | bytes 8388608 | tf_op jit(solution)/shard_map/all_to_all | solution.py:599
  507.9 32.8 %all-to-all-start.3 = ((f32[16,8,32,128]{3,2,1,0:T(8,128)}), f32[16,8,32,128]{3,2,1,0:T(8,128)S(1)}, u32[]{:S(2)}, u32[]{:S(2)}) async-start(f32[16,8,32,128]{3,2,1,0:T(8,128)} %get-tuple-element.74), calls=%async_computation.3 | async-start | bytes 4194304 | tf_op jit(solution)/shard_map/all_to_all | solution.py:599
  541.9 61.7 %all-to-all-start.8 = ((f32[16,4,128,128]{3,2,1,0:T(8,128)}), f32[16,4,128,128]{3,2,1,0:T(8,128)}, u32[]{:S(2)}, u32[]{:S(2)}) async-start(f32[16,4,128,128]{3,2,1,0:T(8,128)} %get-tuple-element.81), calls=%async_computation.8 | async-start | bytes 8388608 | tf_op jit(solution)/shard_map/all_to_all | solution.py:599
  603.6 61.6 %all-to-all-start.4 = ((f32[16,4,128,128]{3,2,1,0:T(8,128)}), f32[16,4,128,128]{3,2,1,0:T(8,128)}, u32[]{:S(2)}, u32[]{:S(2)}) async-start(f32[16,4,128,128]{3,2,1,0:T(8,128)} %get-tuple-element.75), calls=%async_computation.4 | async-start | bytes 8388608 | tf_op jit(solution)/shard_map/all_to_all | solution.py:599
  665.2 32.8 %all-to-all-start.9 = ((f32[16,2,128,128]{3,2,1,0:T(8,128)}), f32[16,2,128,128]{3,2,1,0:T(8,128)S(1)}, u32[]{:S(2)}, u32[]{:S(2)}) async-start(f32[16,2,128,128]{3,2,1,0:T(8,128)} %shard_map.91), calls=%async_computation.9 | async-start | bytes 4194304 | tf_op jit(solution)/shard_map/all_to_all | solution.py:599
  699.4 32.7 %all-to-all-start.5 = ((f32[16,2,128,128]{3,2,1,0:T(8,128)}), f32[16,2,128,128]{3,2,1,0:T(8,128)S(1)}, u32[]{:S(2)}, u32[]{:S(2)}) async-start(f32[16,2,128,128]{3,2,1,0:T(8,128)} %shard_map.87), calls=%async_computation.5 | async-start | bytes 4194304 | tf_op jit(solution)/shard_map/all_to_all | solution.py:599
  732.0 7.3 copy-start
  732.0 33.7 %all-to-all-start.10 = ((f32[16,4,64,128]{3,2,1,0:T(8,128)}), f32[16,4,64,128]{3,2,1,0:T(8,128)}, u32[]{:S(2)}, u32[]{:S(2)}) async-start(f32[16,4,64,128]{3,2,1,0:T(8,128)} %get-tuple-element.83), calls=%async_computation.10 | async-start | bytes 4194304 | tf_op jit(solution)/shard_map/all_to_all | solution.py:599
  765.7 32.7 %all-to-all-start.6 = ((f32[16,4,64,128]{3,2,1,0:T(8,128)}), f32[16,4,64,128]{3,2,1,0:T(8,128)S(1)}, u32[]{:S(2)}, u32[]{:S(2)}) async-start(f32[16,4,64,128]{3,2,1,0:T(8,128)} %get-tuple-element.77), calls=%async_computation.6 | async-start | bytes 4194304 | tf_op jit(solution)/shard_map/all_to_all | solution.py:599
  799.7 32.7 %all-to-all-start.12 = ((f32[16,4,64,128]{3,2,1,0:T(8,128)}), f32[16,4,64,128]{3,2,1,0:T(8,128)S(1)}, u32[]{:S(2)}, u32[]{:S(2)}) async-start(f32[16,4,64,128]{3,2,1,0:T(8,128)} %get-tuple-element.94), calls=%async_computation.12 | async-start | bytes 4194304 | tf_op jit(solution)/shard_map/all_to_all | solution.py:599
  832.4 8.7 copy-start.3
  832.4 56.9 %all-to-all-start.11 = ((f32[16,4,32,128]{3,2,1,0:T(8,128)}), f32[16,4,32,128]{3,2,1,0:T(8,128)S(1)}, u32[]{:S(2)}, u32[]{:S(2)}) async-start(f32[16,4,32,128]{3,2,1,0:T(8,128)} %get-tuple-element.91), calls=%async_computation.11 | async-start | bytes 2097152 | tf_op jit(solution)/shard_map/all_to_all | solution.py:599
  838.5 48.1 %collective-permute-start.6 = (f32[2,32,4096]{2,1,0:T(8,128)}, f32[2,32,4096]{2,1,0:T(8,128)}, u32[]{:S(2)}, u32[]{:S(2)}) collective-permute-start(f32[2,32,4096]{2,1,0:T(8,128)} %get-tuple-element.88), channel_id=1, source_target_pairs={{0,8},{1,9},{2,10},{3,11},{4,12},{5,13},{6,14},{7,15},{16,0},{17,1... | collective-permute-start | bytes 3145736 | tf_op jit(solution)/shard_map/ppermute | solution.py:613
  838.5 50.7 %collective-permute-start.7 = (f32[2,32,4096]{2,1,0:T(8,128)}, f32[2,32,4096]{2,1,0:T(8,128)}, u32[]{:S(2)}, u32[]{:S(2)}) collective-permute-start(f32[2,32,4096]{2,1,0:T(8,128)} %get-tuple-element.108), channel_id=1, source_target_pairs={{8,16},{9,17},{10,18},{11,19},{12,20},{13,21},{14,22},{15,23},{16,... | collective-permute-start | bytes 3145736 | tf_op jit(solution)/shard_map/ppermute | solution.py:613
  889.2 5.4 copy-start.16
  889.2 24.4 %all-to-all-start.13 = ((f32[16,4,32,128]{3,2,1,0:T(8,128)}), f32[16,4,32,128]{3,2,1,0:T(8,128)S(1)}, u32[]{:S(2)}, u32[]{:S(2)}) async-start(f32[16,4,32,128]{3,2,1,0:T(8,128)} %get-tuple-element.104), calls=%async_computation.13 | async-start | bytes 2097152 | tf_op jit(solution)/shard_map/all_to_all | solution.py:599
  910.1 36.7 %collective-permute-start.8 = (f32[2,16,4096]{2,1,0:T(8,128)}, f32[2,16,4096]{2,1,0:T(8,128)S(1)}, u32[]{:S(2)}, u32[]{:S(2)}) collective-permute-start(f32[2,16,4096]{2,1,0:T(8,128)} %get-tuple-element.99), channel_id=1, source_target_pairs={{0,8},{1,9},{2,10},{3,11},{4,12},{5,13},{6,14},{7,15},{16,0},{17,1... | collective-permute-start | bytes 1572872 | tf_op jit(solution)/shard_map/ppermute | solution.py:613
  910.2 39.5 %collective-permute-start.9 = (f32[2,16,4096]{2,1,0:T(8,128)}, f32[2,16,4096]{2,1,0:T(8,128)S(1)}, u32[]{:S(2)}, u32[]{:S(2)}) collective-permute-start(f32[2,16,4096]{2,1,0:T(8,128)} %get-tuple-element.111), channel_id=1, source_target_pairs={{8,16},{9,17},{10,18},{11,19},{12,20},{13,21},{14,22},{15,23},{16,... | collective-permute-start | bytes 1572872 | tf_op jit(solution)/shard_map/ppermute | solution.py:613
  914.6 46.3 %copy-start.22 = (f32[2,32,4096]{2,1,0:T(8,128)S(1)}, f32[2,32,4096]{2,1,0:T(8,128)}, u32[]{:S(2)}) copy-start(f32[2,32,4096]{2,1,0:T(8,128)} %get-tuple-element.108) | copy-start | bytes 3145732
  930.0 28.0 %collective-permute-start.10 = (f32[2,16,4096]{2,1,0:T(8,128)}, f32[2,16,4096]{2,1,0:T(8,128)S(1)}, u32[]{:S(2)}, u32[]{:S(2)}) collective-permute-start(f32[2,16,4096]{2,1,0:T(8,128)} %get-tuple-element.106), channel_id=1, source_target_pairs={{0,8},{1,9},{2,10},{3,11},{4,12},{5,13},{6,14},{7,15},{16,0},{17,1... | collective-permute-start | bytes 1572872 | tf_op jit(solution)/shard_map/ppermute | solution.py:613
  930.1 32.8 %copy-start.19 = (f32[2,16,4096]{2,1,0:T(8,128)S(1)}, f32[2,16,4096]{2,1,0:T(8,128)}, u32[]{:S(2)}) copy-start(f32[2,16,4096]{2,1,0:T(8,128)} %get-tuple-element.111) | copy-start | bytes 1572868
  930.1 30.9 %collective-permute-start.11 = (f32[2,16,4096]{2,1,0:T(8,128)}, f32[2,16,4096]{2,1,0:T(8,128)S(1)}, u32[]{:S(2)}, u32[]{:S(2)}) collective-permute-start(f32[2,16,4096]{2,1,0:T(8,128)} %get-tuple-element.114), channel_id=1, source_target_pairs={{8,16},{9,17},{10,18},{11,19},{12,20},{13,21},{14,22},{15,23},{16,... | collective-permute-start | bytes 1572872 | tf_op jit(solution)/shard_map/ppermute | solution.py:613
  (20 other events, 26.3 us)

commit v11 on v8

--- a/solution.py
+++ b/solution.py
@@ -649,7 +649,7 @@
         give = jnp.where(q == b, beside, keep)
         along = permute(after(give, along), ALONG)
         chunks.append((own, along))
-    return chunks, rest
+    return chunks
 
 
 def depart(near, far):
@@ -666,7 +666,7 @@
     q = lax.axis_index("parts")
     b = lax.axis_index("fft") // HALF
     place = jnp.stack([b, q]).astype(jnp.int32)
-    chunks, beside = arrive(potential, direction, q, b)
+    chunks = arrive(potential, direction, q, b)
     whi, wlo = split_weights(block_weights)
     by_column = column_constants()
     column = tuple(jnp.asarray(v) for v in split_constant(by_column))
@@ -676,17 +676,15 @@
     arrived = [[] for _ in angles]
     bases = [[] for _ in angles]
     ahead = [[] for _ in angles]
+    fields = ()
     for c, (own, along) in enumerate(chunks):
-        own = after(own, beside)
-        for part in (angles,) if c + 1 < CHUNKS else [[a] for a in angles]:
-            fields, fronts = enter(
-                place, [block_index[a] for a in part], own, along, [weights[a] for a in part], row
-            )
-            fields = exchange(fields)
-            for i, a in enumerate(part):
-                arrived[a].append(fields)
-                bases[a].append(8 * i)
-                ahead[a].append(fronts[i])
+        further = chunks[c + 1][1] if c + 1 < CHUNKS else ()
+        own = after(own, fields)
+        for a in angles:
+            fields, (front,) = enter(place, [block_index[a]], own, along, [weights[a]], row)
+            arrived[a].append(exchange(after(fields, further) if a else fields))
+            bases[a].append(0)
+            ahead[a].append(front)
     carried = []
     for a in angles:
         out, kept = middle(arrived[a], tuple(bases[a]), column)

time: 946 us -> 868 us (0.918)
  waiting for transfers between devices: 469 us -> 343 us
  starting transfers between devices: 106 us -> 143 us
    ppermute x12, waiting for transfers between devices: 258 us -> 174 us  [permute(): return lax.ppermute(values, ('parts', 'fft'), pairs)]
    all_to_all x14 -> x17, waiting for transfers between devices: 211 us -> 169 us  [exchange(): lax.all_to_all(values, ('parts', 'fft'), split_axis=0, concat_axis=0, axi...]
    all_to_all x14 -> x17, starting transfers between devices: 89.8 us -> 119 us  [exchange(): lax.all_to_all(values, ('parts', 'fft'), split_axis=0, concat_axis=0, axi...]
    select_n x0 -> x3, other arithmetic: none -> 9.78 us  [arrive(): own = jnp.where(q == b, keep, beside)]
    pallas_call x16 -> x19, Pallas kernels: 313 us -> 321 us  [call(): pl.pallas_call(kernel, out_shape=[jax.ShapeDtypeStruct(o, jnp.float32) fo...]
  transfers between devices with their start and end apart: 26 -> 29, of which waited for: 21 -> 23; matrix products, arithmetic and copies ran while one was open for 3% -> 4% of each run, Pallas kernels for 32% -> 37%
where the time goes in v11:
time: 868 us; the launch traced here: 859 us
  waiting for transfers between devices  343 us (40%)
  Pallas kernels  321 us (37%)
  starting transfers between devices  143 us (16%)
  other arithmetic  29.2 us (3%)
  local copies, waits for them, and re-layouts  23.1 us (3%)
    pallas_call x19, Pallas kernels, call(): pl.pallas_call(kernel, out_shape=[jax.ShapeDtypeStruct(o, jnp.float32) fo...  321 us
    ppermute x12, waiting for transfers between devices, permute(): return lax.ppermute(values, ('parts', 'fft'), pairs)  174 us
    all_to_all x17, waiting for transfers between devices, exchange(): lax.all_to_all(values, ('parts', 'fft'), split_axis=0, concat_axis=0, axi...  169 us
    all_to_all x17, starting transfers between devices, exchange(): lax.all_to_all(values, ('parts', 'fft'), split_axis=0, concat_axis=0, axi...  119 us
    ppermute x12, starting transfers between devices, permute(): return lax.ppermute(values, ('parts', 'fft'), pairs)  23.7 us
  transfers between devices with their start and end apart: 29, of which 23 were waited for; matrix products, arithmetic and copies ran while one was open for 4% of the time, Pallas kernels for 37%

profile of v11, /device:TPU:3, one launch (start us, length us, event | category | flops | bytes accessed | tf_op | source)
XLA Modules:
  0.0 859.0 jit_solution(4515237980039541381)
XLA Ops:
  17.1 11.5 %collective-permute-done = f32[4,16,4096]{2,1,0:T(8,128)} collective-permute-done((f32[4,16,4096]{2,1,0:T(8,128)}, f32[4,16,4096]{2,1,0:T(8,128)}, u32[]{:S(2)}, u32[]{:S(2)}) %collective-permute-start) | collective-permute-done | bytes 1048608 | tf_op jit(solution)/shard_map/ppermute | solution.py:613
  42.7 35.6 %collective-permute-done.1.refs_2_ = f32[4,16,4096]{2,1,0:T(8,128)S(1)} collective-permute-done((f32[4,16,4096]{2,1,0:T(8,128)S(1)}, f32[4,16,4096]{2,1,0:T(8,128)S(1)}, u32[]{:S(2)}, u32[]{:S(2)}) %collective-permute-start.1) | collective-permute-done | bytes 1048608 | tf_op jit(solution)/shard_map/ppermute | solution.py:613
  79.4 16.3 %shard_map.89 = (f32[16,8,32,128]{3,2,1,0:T(8,128)}, f32[16,2,32,128]{3,2,1,0:T(8,128)}) custom-call(s32[2]{0:T(128)} %pad_add_fusion.place, s32[32,2]{1,0:T(8,128)} %copy.17.refs_0_.index, f32[4,16,4096]{2,1,0:T(8,128)} %get-tuple-element.158.refs_1_, f32[4,16,4096]{2,1,0:T(8,128)} %copy-done.25, bf16[32,256,128]{2,1,0:T(8,128)(2,1)} %get-tuple-element.164.refs_3_.whi, ...), custom_call_target="tpu_custom_call" | custom-call | flops 1207959552 | bytes 13107464 | tf_op jit(solution)/shard_map/pallas_call | solution.py:479
  108.5 16.3 %shard_map.82 = (f32[16,8,32,128]{3,2,1,0:T(8,128)}, f32[16,2,32,128]{3,2,1,0:T(8,128)}) custom-call(s32[2]{0:T(128)} %pad_add_fusion.place, s32[32,2]{1,0:T(8,128)} %copy.18.refs_0_.index, f32[4,16,4096]{2,1,0:T(8,128)} %get-tuple-element.158.refs_1_, f32[4,16,4096]{2,1,0:T(8,128)} %copy-done.25, bf16[32,256,128]{2,1,0:T(8,128)(2,1)} %get-tuple-element.163.refs_3_.whi, ...), custom_call_target="tpu_custom_call" | custom-call | flops 1207959552 | bytes 13107464 | tf_op jit(solution)/shard_map/pallas_call | solution.py:479
  124.8 23.3 %collective-permute-done.3.refs_2_ = f32[4,16,4096]{2,1,0:T(8,128)} collective-permute-done((f32[4,16,4096]{2,1,0:T(8,128)}, f32[4,16,4096]{2,1,0:T(8,128)}, u32[]{:S(2)}, u32[]{:S(2)}) %collective-permute-start.3) | collective-permute-done | bytes 1048608 | tf_op jit(solution)/shard_map/ppermute | solution.py:613
  148.4 10.7 %all-to-all-start = ((f32[16,8,32,128]{3,2,1,0:T(8,128)}), f32[16,8,32,128]{3,2,1,0:T(8,128)}, u32[]{:S(2)}, u32[]{:S(2)}) async-start(f32[16,8,32,128]{3,2,1,0:T(8,128)} %get-tuple-element.71), calls=%async_computation | async-start | bytes 4194304 | tf_op jit(solution)/shard_map/all_to_all | solution.py:599
  159.0 16.3 %shard_map.90 = (f32[16,8,32,128]{3,2,1,0:T(8,128)}, f32[16,2,32,128]{3,2,1,0:T(8,128)}) custom-call(s32[2]{0:T(128)} %pad_add_fusion.place, s32[32,2]{1,0:T(8,128)} %copy.17.refs_0_.index, f32[4,16,4096]{2,1,0:T(8,128)} %get-tuple-element.72.refs_1_, f32[4,16,4096]{2,1,0:T(8,128)} %collective-permute-done.3.refs_2_, ...), custom_call_target="tpu_custom_call" | custom-call | flops 1207959552 | bytes 13107464 | tf_op jit(solution)/shard_map/pallas_call | solution.py:479
  175.4 10.2 %all-to-all-done.refs_0_ = f32[16,8,32,128]{3,2,1,0:T(8,128)} async-done(((f32[16,8,32,128]{3,2,1,0:T(8,128)}), f32[16,8,32,128]{3,2,1,0:T(8,128)}, u32[]{:S(2)}, u32[]{:S(2)}) %all-to-all-start) | async-done | bytes 2097184 | tf_op jit(solution)/shard_map/all_to_all | solution.py:599
  198.0 16.3 %shard_map.83 = (f32[16,8,32,128]{3,2,1,0:T(8,128)}, f32[16,2,32,128]{3,2,1,0:T(8,128)}) custom-call(s32[2]{0:T(128)} %pad_add_fusion.place, s32[32,2]{1,0:T(8,128)} %copy.18.refs_0_.index, f32[4,16,4096]{2,1,0:T(8,128)} %get-tuple-element.72.refs_1_, f32[4,16,4096]{2,1,0:T(8,128)} %collective-permute-done.3.refs_2_, ...), custom_call_target="tpu_custom_call" | custom-call | flops 1207959552 | bytes 13107464 | tf_op jit(solution)/shard_map/pallas_call | solution.py:479
  214.3 24.7 %collective-permute-done.4.refs_2_ = f32[4,16,4096]{2,1,0:T(8,128)} collective-permute-done((f32[4,16,4096]{2,1,0:T(8,128)}, f32[4,16,4096]{2,1,0:T(8,128)}, u32[]{:S(2)}, u32[]{:S(2)}) %collective-permute-start.4) | collective-permute-done | bytes 1048608 | tf_op jit(solution)/shard_map/ppermute | solution.py:613
  249.2 16.3 %shard_map.91 = (f32[16,8,32,128]{3,2,1,0:T(8,128)}, f32[16,2,32,128]{3,2,1,0:T(8,128)}) custom-call(s32[2]{0:T(128)} %pad_add_fusion.place, s32[32,2]{1,0:T(8,128)} %copy.17.refs_0_.index, f32[4,16,4096]{2,1,0:T(8,128)} %get-tuple-element.76.refs_1_, f32[4,16,4096]{2,1,0:T(8,128)} %collective-permute-done.4.refs_2_, ...), custom_call_target="tpu_custom_call" | custom-call | flops 1207959552 | bytes 13107464 | tf_op jit(solution)/shard_map/pallas_call | solution.py:479
  265.4 10.3 %all-to-all-done.1.refs_1_ = f32[16,8,32,128]{3,2,1,0:T(8,128)} async-done(((f32[16,8,32,128]{3,2,1,0:T(8,128)}), f32[16,8,32,128]{3,2,1,0:T(8,128)}, u32[]{:S(2)}, u32[]{:S(2)}) %all-to-all-start.1) | async-done | bytes 2097184 | tf_op jit(solution)/shard_map/all_to_all | solution.py:599
  288.1 16.3 %shard_map.84 = (f32[16,8,32,128]{3,2,1,0:T(8,128)}, f32[16,2,32,128]{3,2,1,0:T(8,128)}) custom-call(s32[2]{0:T(128)} %pad_add_fusion.place, s32[32,2]{1,0:T(8,128)} %copy.18.refs_0_.index, f32[4,16,4096]{2,1,0:T(8,128)} %get-tuple-element.76.refs_1_, f32[4,16,4096]{2,1,0:T(8,128)} %collective-permute-done.4.refs_2_, ...), custom_call_target="tpu_custom_call" | custom-call | flops 1207959552 | bytes 13107464 | tf_op jit(solution)/shard_map/pallas_call | solution.py:479
  304.4 24.9 %collective-permute-done.5.refs_2_ = f32[4,16,4096]{2,1,0:T(8,128)S(1)} collective-permute-done((f32[4,16,4096]{2,1,0:T(8,128)}, f32[4,16,4096]{2,1,0:T(8,128)S(1)}, u32[]{:S(2)}, u32[]{:S(2)}) %collective-permute-start.5) | collective-permute-done | bytes 1048608 | tf_op jit(solution)/shard_map/ppermute | solution.py:613
  339.2 16.3 %shard_map.92 = (f32[16,8,32,128]{3,2,1,0:T(8,128)}, f32[16,2,32,128]{3,2,1,0:T(8,128)}) custom-call(s32[2]{0:T(128)} %pad_add_fusion.place, s32[32,2]{1,0:T(8,128)} %copy.17.refs_0_.index, f32[4,16,4096]{2,1,0:T(8,128)} %get-tuple-element.80.refs_1_, f32[4,16,4096]{2,1,0:T(8,128)} %copy-done.26, bf16[32,256,128]{2,1,0:T(8,128)(2,1)} %get-tuple-element.164.refs_3_.whi, ...), custom_call_target="tpu_custom_call" | custom-call | flops 1207959552 | bytes 13107464 | tf_op jit(solution)/shard_map/pallas_call | solution.py:479
  355.5 10.3 %all-to-all-done.2.refs_2_ = f32[16,8,32,128]{3,2,1,0:T(8,128)} async-done(((f32[16,8,32,128]{3,2,1,0:T(8,128)}), f32[16,8,32,128]{3,2,1,0:T(8,128)}, u32[]{:S(2)}, u32[]{:S(2)}) %all-to-all-start.2) | async-done | bytes 2097184 | tf_op jit(solution)/shard_map/all_to_all | solution.py:599
  372.0 16.3 %shard_map.85 = (f32[16,8,32,128]{3,2,1,0:T(8,128)}, f32[16,2,32,128]{3,2,1,0:T(8,128)}) custom-call(s32[2]{0:T(128)} %pad_add_fusion.place, s32[32,2]{1,0:T(8,128)} %copy.18.refs_0_.index, f32[4,16,4096]{2,1,0:T(8,128)} %get-tuple-element.80.refs_1_, f32[4,16,4096]{2,1,0:T(8,128)} %copy-done.26, bf16[32,256,128]{2,1,0:T(8,128)(2,1)} %get-tuple-element.163.refs_3_.whi, ...), custom_call_target="tpu_custom_call" | custom-call | flops 1207959552 | bytes 13107464 | tf_op jit(solution)/shard_map/pallas_call | solution.py:479
  406.0 20.8 %shard_map.93 = (f32[16,4,128,128]{3,2,1,0:T(8,128)}, f32[16,4,128,128]{3,2,1,0:T(8,128)}) custom-call(f32[16,8,32,128]{3,2,1,0:T(8,128)} %copy-done.2, f32[16,8,32,128]{3,2,1,0:T(8,128)} %copy-done.3, f32[16,8,32,128]{3,2,1,0:T(8,128)} %copy-done.4, f32[16,8,32,128]{3,2,1,0:T(8,128)} %copy-done.8, bf16[16,256,256]{2,1,0:T(8,128)(2,1)} %constant.34.clone.refs_4_.mhi, ...), custom_call_target="tpu_custom_call" | custom-call | flops 3221225472 | bytes 20971520 | tf_op jit(solution)/shard_map/pallas_call | solution.py:479
  441.0 20.9 %shard_map.86 = (f32[16,4,128,128]{3,2,1,0:T(8,128)}, f32[16,4,128,128]{3,2,1,0:T(8,128)}) custom-call(f32[16,8,32,128]{3,2,1,0:T(8,128)} %all-to-all-done.refs_0_, f32[16,8,32,128]{3,2,1,0:T(8,128)} %all-to-all-done.1.refs_1_, f32[16,8,32,128]{3,2,1,0:T(8,128)} %all-to-all-done.2.refs_2_, f32[16,8,32,128]{3,2,1,0:T(8,128)} %copy-done.7, ...), custom_call_target="tpu_custom_call" | custom-call | flops 3221225472 | bytes 20971520 | tf_op jit(solution)/shard_map/pallas_call | solution.py:479
  462.0 33.4 %all-to-all-done.11.fields = f32[16,4,128,128]{3,2,1,0:T(8,128)} async-done(((f32[16,4,128,128]{3,2,1,0:T(8,128)}), f32[16,4,128,128]{3,2,1,0:T(8,128)}, u32[]{:S(2)}, u32[]{:S(2)}) %all-to-all-start.11) | async-done | bytes 4194336 | tf_op jit(solution)/shard_map/all_to_all | solution.py:599
  502.5 16.4 %shard_map.94 = f32[16,2,128,128]{3,2,1,0:T(8,128)} custom-call(f32[16,4,128,128]{3,2,1,0:T(8,128)} %all-to-all-done.11.fields, bf16[16,256,256]{2,1,0:T(8,128)(2,1)} %constant.36.clone.refs_5_.mhi, bf16[16,256,256]{2,1,0:T(8,128)(2,1)} %constant.37.clone.refs_6_.mlo), custom_call_target="tpu_custom_call" | custom-call | flops 2415919104 | bytes 10485760 | tf_op jit(solution)/shard_map/pallas_call | solution.py:479
  518.9 38.1 %all-to-all-done.4.fields = f32[16,4,128,128]{3,2,1,0:T(8,128)} async-done(((f32[16,4,128,128]{3,2,1,0:T(8,128)}), f32[16,4,128,128]{3,2,1,0:T(8,128)}, u32[]{:S(2)}, u32[]{:S(2)}) %all-to-all-start.4) | async-done | bytes 4194336 | tf_op jit(solution)/shard_map/all_to_all | solution.py:599
  563.3 16.4 %shard_map.87 = f32[16,2,128,128]{3,2,1,0:T(8,128)} custom-call(f32[16,4,128,128]{3,2,1,0:T(8,128)} %all-to-all-done.4.fields, bf16[16,256,256]{2,1,0:T(8,128)(2,1)} %constant.36.clone.refs_5_.mhi, bf16[16,256,256]{2,1,0:T(8,128)(2,1)} %constant.37.clone.refs_6_.mlo), custom_call_target="tpu_custom_call" | custom-call | flops 2415919104 | bytes 10485760 | tf_op jit(solution)/shard_map/pallas_call | solution.py:479
  597.3 16.6 %shard_map.95 = (f32[16,4,64,128]{3,2,1,0:T(8,128)}, f32[16,4,64,128]{3,2,1,0:T(8,128)}) custom-call(f32[16,2,128,128]{3,2,1,0:T(8,128)} %copy-done.1, f32[16,4,128,128]{3,2,1,0:T(8,128)} %get-tuple-element.92.kept, bf16[16,256,256]{2,1,0:T(8,128)(2,1)} %constant.34.clone.refs_4_.mhi, bf16[16,256,256]{2,1,0:T(8,128)(2,1)} %constant.35.clone.refs_5_.mlo), custom_call_target="tpu_custom_call" | custom-call | flops 1610612736 | bytes 14680064 | tf_op jit(solution)/shard_map/pallas_call | solution.py:479
  631.1 16.5 %shard_map.88 = (f32[16,4,64,128]{3,2,1,0:T(8,128)}, f32[16,4,32,128]{3,2,1,0:T(8,128)}, f32[16,4,32,128]{3,2,1,0:T(8,128)}) custom-call(f32[16,2,128,128]{3,2,1,0:T(8,128)} %copy-done, f32[16,4,128,128]{3,2,1,0:T(8,128)} %get-tuple-element.83.kept, bf16[16,256,256]{2,1,0:T(8,128)(2,1)} %constant.34.clone.refs_4_.mhi, ...), custom_call_target="tpu_custom_call" | custom-call | flops 1610612736 | bytes 14680064 | tf_op jit(solution)/shard_map/pallas_call | solution.py:479
  663.7 17.0 %shard_map.96 = (f32[2,32,4096]{2,1,0:T(8,128)}, f32[2,32,4096]{2,1,0:T(8,128)}) custom-call(s32[2]{0:T(128)} %pad_add_fusion.place, s32[32,2]{1,0:T(8,128)} %copy.17.refs_0_.index, f32[16,4,64,128]{3,2,1,0:T(8,128)} %all-to-all-done.13.back, bf16[32,256,128]{2,1,0:T(8,128)(2,1)} %get-tuple-element.164.refs_3_.whi, ...), custom_call_target="tpu_custom_call" | custom-call | flops 1207959552 | bytes 13631752 | tf_op jit(solution)/shard_map/pallas_call | solution.py:479
  697.6 17.6 %shard_map.97 = (f32[2,32,4096]{2,1,0:T(8,128)}, f32[2,32,4096]{2,1,0:T(8,128)}) custom-call(s32[2]{0:T(128)} %pad_add_fusion.place, s32[32,2]{1,0:T(8,128)} %copy.18.refs_0_.index, f32[16,4,64,128]{3,2,1,0:T(8,128)} %copy-done.6, bf16[32,256,128]{2,1,0:T(8,128)(2,1)} %get-tuple-element.163.refs_3_.whi, ...), custom_call_target="tpu_custom_call" | custom-call | flops 1207959552 | bytes 15728904 | tf_op jit(solution)/shard_map/pallas_call | solution.py:479
  730.3 17.0 %shard_map.98 = (f32[2,16,4096]{2,1,0:T(8,128)}, f32[2,16,4096]{2,1,0:T(8,128)}, f32[2,16,4096]{2,1,0:T(8,128)}, f32[2,16,4096]{2,1,0:T(8,128)}) custom-call(s32[2]{0:T(128)} %pad_add_fusion.place, s32[32,2]{1,0:T(8,128)} %copy.17.refs_0_.index, f32[16,4,64,128]{3,2,1,0:T(8,128)} %copy-done.5, bf16[32,256,128]{2,1,0:T(8,128)(2,1)} %get-tuple-element.164.refs_3_.whi, ...), custom_call_target="tpu_custom_call" | custom-call | flops 1207959552 | bytes 13631752 | tf_op jit(solution)/shard_map/pallas_call | solution.py:479
  758.5 15.4 %shard_map.99 = (f32[2,16,4096]{2,1,0:T(8,128)}, f32[2,16,4096]{2,1,0:T(8,128)}) custom-call(s32[2]{0:T(128)} %pad_add_fusion.place, s32[32,2]{1,0:T(8,128)} %copy.18.refs_0_.index, f32[16,4,32,128]{3,2,1,0:T(8,128)} %copy-done.24, bf16[32,256,128]{2,1,0:T(8,128)(2,1)} %get-tuple-element.163.refs_3_.whi, ...), custom_call_target="tpu_custom_call" | custom-call | flops 603979776 | bytes 12058888 | tf_op jit(solution)/shard_map/pallas_call | solution.py:479
  778.8 15.5 %shard_map.100 = (f32[2,16,4096]{2,1,0:T(8,128)}, f32[2,16,4096]{2,1,0:T(8,128)}) custom-call(s32[2]{0:T(128)} %pad_add_fusion.place, s32[32,2]{1,0:T(8,128)} %copy.18.refs_0_.index, f32[16,4,32,128]{3,2,1,0:T(8,128)} %copy-done.23, bf16[32,256,128]{2,1,0:T(8,128)(2,1)} %get-tuple-element.163.refs_3_.whi, ...), custom_call_target="tpu_custom_call" | custom-call | flops 603979776 | bytes 12058888 | tf_op jit(solution)/shard_map/pallas_call | solution.py:479
  796.6 27.3 %collective-permute-done.6 = f32[2,32,4096]{2,1,0:T(8,128)} collective-permute-done((f32[2,32,4096]{2,1,0:T(8,128)}, f32[2,32,4096]{2,1,0:T(8,128)}, u32[]{:S(2)}, u32[]{:S(2)}) %collective-permute-start.6) | collective-permute-done | bytes 1048608 | tf_op jit(solution)/shard_map/ppermute | solution.py:613
  835.1 11.2 %collective-permute-done.10 = f32[2,16,4096]{2,1,0:T(8,128)S(1)} collective-permute-done((f32[2,16,4096]{2,1,0:T(8,128)}, f32[2,16,4096]{2,1,0:T(8,128)S(1)}, u32[]{:S(2)}, u32[]{:S(2)}) %collective-permute-start.10) | collective-permute-done | bytes 524320 | tf_op jit(solution)/shard_map/ppermute | solution.py:613
  (136 shorter events, 266.1 us)
Async XLA Ops:
  4.2 24.3 %collective-permute-start = (f32[4,16,4096]{2,1,0:T(8,128)}, f32[4,16,4096]{2,1,0:T(8,128)}, u32[]{:S(2)}, u32[]{:S(2)}) collective-permute-start(f32[4,16,4096]{2,1,0:T(8,128)} %fusion.7), channel_id=1, source_target_pairs={{0,16},{1,17},{2,18},{3,19},{4,20},{5,21},{6,22},{7,23},{8,24},{9,... | collective-permute-start | bytes 3145736 | tf_op jit(solution)/shard_map/ppermute | solution.py:613
  31.0 47.4 %collective-permute-start.1 = (f32[4,16,4096]{2,1,0:T(8,128)S(1)}, f32[4,16,4096]{2,1,0:T(8,128)S(1)}, u32[]{:S(2)}, u32[]{:S(2)}) collective-permute-start(f32[4,16,4096]{2,1,0:T(8,128)S(1)} %get-tuple-element.157), channel_id=1, source_target_pairs={{0,8},{1,9},{2,10},{3,11},{4,12},{5,13},{6,14},{7,15},{8,0},{9,1},... | collective-permute-start | bytes 3145736 | tf_op jit(solution)/shard_map/ppermute | solution.py:613
  33.3 68.1 %collective-permute-start.2 = (f32[12,16,4096]{2,1,0:T(8,128)}, f32[12,16,4096]{2,1,0:T(8,128)}, u32[]{:S(2)}, u32[]{:S(2)}) collective-permute-start(f32[12,16,4096]{2,1,0:T(8,128)} %pad_maximum_fusion), channel_id=1, source_target_pairs={{0,16},{1,17},{2,18},{3,19},{4,20},{5,21},{6,22},{7,23},{8,24},{9,... | collective-permute-start | bytes 9437192 | tf_op jit(solution)/shard_map/ppermute | solution.py:613
  95.7 52.6 %all-to-all-start.7 = ((f32[16,8,32,128]{3,2,1,0:T(8,128)}), f32[16,8,32,128]{3,2,1,0:T(8,128)S(1)}, u32[]{:S(2)}, u32[]{:S(2)}) async-start(f32[16,8,32,128]{3,2,1,0:T(8,128)} %get-tuple-element.87), calls=%async_computation.7 | async-start | bytes 4194304 | tf_op jit(solution)/shard_map/all_to_all | solution.py:599
  104.8 43.3 %collective-permute-start.3 = (f32[4,16,4096]{2,1,0:T(8,128)}, f32[4,16,4096]{2,1,0:T(8,128)}, u32[]{:S(2)}, u32[]{:S(2)}) collective-permute-start(f32[4,16,4096]{2,1,0:T(8,128)} %get-tuple-element.70), channel_id=1, source_target_pairs={{0,8},{1,9},{2,10},{3,11},{4,12},{5,13},{6,14},{7,15},{8,0},{9,1},... | collective-permute-start | bytes 3145736 | tf_op jit(solution)/shard_map/ppermute | solution.py:613
  148.4 27.0 %copy-start.2 = (f32[16,8,32,128]{3,2,1,0:T(8,128)}, f32[16,8,32,128]{3,2,1,0:T(8,128)S(1)}, u32[]{:S(2)}) copy-start(f32[16,8,32,128]{3,2,1,0:T(8,128)S(1)} %all-to-all-done.7.refs_0_) | copy-start | bytes 6291460
  148.4 37.2 %all-to-all-start = ((f32[16,8,32,128]{3,2,1,0:T(8,128)}), f32[16,8,32,128]{3,2,1,0:T(8,128)}, u32[]{:S(2)}, u32[]{:S(2)}) async-start(f32[16,8,32,128]{3,2,1,0:T(8,128)} %get-tuple-element.71), calls=%async_computation | async-start | bytes 4194304 | tf_op jit(solution)/shard_map/all_to_all | solution.py:599
  185.6 53.5 %all-to-all-start.8 = ((f32[16,8,32,128]{3,2,1,0:T(8,128)}), f32[16,8,32,128]{3,2,1,0:T(8,128)S(1)}, u32[]{:S(2)}, u32[]{:S(2)}) async-start(f32[16,8,32,128]{3,2,1,0:T(8,128)} %get-tuple-element.88), calls=%async_computation.8 | async-start | bytes 4194304 | tf_op jit(solution)/shard_map/all_to_all | solution.py:599
  195.1 43.9 %collective-permute-start.4 = (f32[4,16,4096]{2,1,0:T(8,128)}, f32[4,16,4096]{2,1,0:T(8,128)}, u32[]{:S(2)}, u32[]{:S(2)}) collective-permute-start(f32[4,16,4096]{2,1,0:T(8,128)} %get-tuple-element.74), channel_id=1, source_target_pairs={{0,8},{1,9},{2,10},{3,11},{4,12},{5,13},{6,14},{7,15},{8,0},{9,1},... | collective-permute-start | bytes 3145736 | tf_op jit(solution)/shard_map/ppermute | solution.py:613
  239.0 26.4 %copy-start.3 = (f32[16,8,32,128]{3,2,1,0:T(8,128)}, f32[16,8,32,128]{3,2,1,0:T(8,128)S(1)}, u32[]{:S(2)}) copy-start(f32[16,8,32,128]{3,2,1,0:T(8,128)S(1)} %all-to-all-done.8.refs_1_) | copy-start | bytes 6291460
  239.0 36.7 %all-to-all-start.1 = ((f32[16,8,32,128]{3,2,1,0:T(8,128)}), f32[16,8,32,128]{3,2,1,0:T(8,128)}, u32[]{:S(2)}, u32[]{:S(2)}) async-start(f32[16,8,32,128]{3,2,1,0:T(8,128)} %get-tuple-element.75), calls=%async_computation.1 | async-start | bytes 4194304 | tf_op jit(solution)/shard_map/all_to_all | solution.py:599
  275.7 53.6 %all-to-all-start.9 = ((f32[16,8,32,128]{3,2,1,0:T(8,128)}), f32[16,8,32,128]{3,2,1,0:T(8,128)S(1)}, u32[]{:S(2)}, u32[]{:S(2)}) async-start(f32[16,8,32,128]{3,2,1,0:T(8,128)} %get-tuple-element.89), calls=%async_computation.9 | async-start | bytes 4194304 | tf_op jit(solution)/shard_map/all_to_all | solution.py:599
  285.2 44.1 %collective-permute-start.5 = (f32[4,16,4096]{2,1,0:T(8,128)}, f32[4,16,4096]{2,1,0:T(8,128)S(1)}, u32[]{:S(2)}, u32[]{:S(2)}) collective-permute-start(f32[4,16,4096]{2,1,0:T(8,128)} %get-tuple-element.78), channel_id=1, source_target_pairs={{0,8},{1,9},{2,10},{3,11},{4,12},{5,13},{6,14},{7,15},{8,0},{9,1},... | collective-permute-start | bytes 3145736 | tf_op jit(solution)/shard_map/ppermute | solution.py:613
  329.3 36.4 %all-to-all-start.2 = ((f32[16,8,32,128]{3,2,1,0:T(8,128)}), f32[16,8,32,128]{3,2,1,0:T(8,128)}, u32[]{:S(2)}, u32[]{:S(2)}) async-start(f32[16,8,32,128]{3,2,1,0:T(8,128)} %get-tuple-element.79), calls=%async_computation.2 | async-start | bytes 4194304 | tf_op jit(solution)/shard_map/all_to_all | solution.py:599
  365.7 32.7 %all-to-all-start.10 = ((f32[16,8,32,128]{3,2,1,0:T(8,128)}), f32[16,8,32,128]{3,2,1,0:T(8,128)S(1)}, u32[]{:S(2)}, u32[]{:S(2)}) async-start(f32[16,8,32,128]{3,2,1,0:T(8,128)} %get-tuple-element.90), calls=%async_computation.10 | async-start | bytes 4194304 | tf_op jit(solution)/shard_map/all_to_all | solution.py:599
  399.8 32.7 %all-to-all-start.3 = ((f32[16,8,32,128]{3,2,1,0:T(8,128)}), f32[16,8,32,128]{3,2,1,0:T(8,128)S(1)}, u32[]{:S(2)}, u32[]{:S(2)}) async-start(f32[16,8,32,128]{3,2,1,0:T(8,128)} %get-tuple-element.81), calls=%async_computation.3 | async-start | bytes 4194304 | tf_op jit(solution)/shard_map/all_to_all | solution.py:599
  433.7 61.7 %all-to-all-start.11 = ((f32[16,4,128,128]{3,2,1,0:T(8,128)}), f32[16,4,128,128]{3,2,1,0:T(8,128)}, u32[]{:S(2)}, u32[]{:S(2)}) async-start(f32[16,4,128,128]{3,2,1,0:T(8,128)} %get-tuple-element.91), calls=%async_computation.11 | async-start | bytes 8388608 | tf_op jit(solution)/shard_map/all_to_all | solution.py:599
  495.4 61.6 %all-to-all-start.4 = ((f32[16,4,128,128]{3,2,1,0:T(8,128)}), f32[16,4,128,128]{3,2,1,0:T(8,128)}, u32[]{:S(2)}, u32[]{:S(2)}) async-start(f32[16,4,128,128]{3,2,1,0:T(8,128)} %get-tuple-element.82), calls=%async_computation.4 | async-start | bytes 8388608 | tf_op jit(solution)/shard_map/all_to_all | solution.py:599
  557.0 32.8 %all-to-all-start.12 = ((f32[16,2,128,128]{3,2,1,0:T(8,128)}), f32[16,2,128,128]{3,2,1,0:T(8,128)S(1)}, u32[]{:S(2)}, u32[]{:S(2)}) async-start(f32[16,2,128,128]{3,2,1,0:T(8,128)} %shard_map.94), calls=%async_computation.12 | async-start | bytes 4194304 | tf_op jit(solution)/shard_map/all_to_all | solution.py:599
  591.1 32.7 %all-to-all-start.5 = ((f32[16,2,128,128]{3,2,1,0:T(8,128)}), f32[16,2,128,128]{3,2,1,0:T(8,128)S(1)}, u32[]{:S(2)}, u32[]{:S(2)}) async-start(f32[16,2,128,128]{3,2,1,0:T(8,128)} %shard_map.87), calls=%async_computation.5 | async-start | bytes 4194304 | tf_op jit(solution)/shard_map/all_to_all | solution.py:599
  623.8 33.7 %all-to-all-start.13 = ((f32[16,4,64,128]{3,2,1,0:T(8,128)}), f32[16,4,64,128]{3,2,1,0:T(8,128)}, u32[]{:S(2)}, u32[]{:S(2)}) async-start(f32[16,4,64,128]{3,2,1,0:T(8,128)} %get-tuple-element.93), calls=%async_computation.13 | async-start | bytes 4194304 | tf_op jit(solution)/shard_map/all_to_all | solution.py:599
  657.5 32.7 %all-to-all-start.6 = ((f32[16,4,64,128]{3,2,1,0:T(8,128)}), f32[16,4,64,128]{3,2,1,0:T(8,128)S(1)}, u32[]{:S(2)}, u32[]{:S(2)}) async-start(f32[16,4,64,128]{3,2,1,0:T(8,128)} %get-tuple-element.84), calls=%async_computation.6 | async-start | bytes 4194304 | tf_op jit(solution)/shard_map/all_to_all | solution.py:599
  691.5 32.7 %all-to-all-start.15 = ((f32[16,4,64,128]{3,2,1,0:T(8,128)}), f32[16,4,64,128]{3,2,1,0:T(8,128)S(1)}, u32[]{:S(2)}, u32[]{:S(2)}) async-start(f32[16,4,64,128]{3,2,1,0:T(8,128)} %get-tuple-element.104), calls=%async_computation.15 | async-start | bytes 4194304 | tf_op jit(solution)/shard_map/all_to_all | solution.py:599
  724.1 23.2 %all-to-all-start.14 = ((f32[16,4,32,128]{3,2,1,0:T(8,128)}), f32[16,4,32,128]{3,2,1,0:T(8,128)S(1)}, u32[]{:S(2)}, u32[]{:S(2)}) async-start(f32[16,4,32,128]{3,2,1,0:T(8,128)} %get-tuple-element.101), calls=%async_computation.14 | async-start | bytes 2097152 | tf_op jit(solution)/shard_map/all_to_all | solution.py:599
  747.3 30.6 %all-to-all-start.16 = ((f32[16,4,32,128]{3,2,1,0:T(8,128)}), f32[16,4,32,128]{3,2,1,0:T(8,128)S(1)}, u32[]{:S(2)}, u32[]{:S(2)}) async-start(f32[16,4,32,128]{3,2,1,0:T(8,128)} %get-tuple-element.114), calls=%async_computation.16 | async-start | bytes 2097152 | tf_op jit(solution)/shard_map/all_to_all | solution.py:599
  752.5 71.5 %collective-permute-start.6 = (f32[2,32,4096]{2,1,0:T(8,128)}, f32[2,32,4096]{2,1,0:T(8,128)}, u32[]{:S(2)}, u32[]{:S(2)}) collective-permute-start(f32[2,32,4096]{2,1,0:T(8,128)} %get-tuple-element.98), channel_id=1, source_target_pairs={{0,8},{1,9},{2,10},{3,11},{4,12},{5,13},{6,14},{7,15},{16,0},{17,1... | collective-permute-start | bytes 3145736 | tf_op jit(solution)/shard_map/ppermute | solution.py:613
  752.5 73.3 %collective-permute-start.7 = (f32[2,32,4096]{2,1,0:T(8,128)}, f32[2,32,4096]{2,1,0:T(8,128)}, u32[]{:S(2)}, u32[]{:S(2)}) collective-permute-start(f32[2,32,4096]{2,1,0:T(8,128)} %get-tuple-element.118), channel_id=1, source_target_pairs={{8,16},{9,17},{10,18},{11,19},{12,20},{13,21},{14,22},{15,23},{16,... | collective-permute-start | bytes 3145736 | tf_op jit(solution)/shard_map/ppermute | solution.py:613
  773.9 61.2 %collective-permute-start.8 = (f32[2,16,4096]{2,1,0:T(8,128)}, f32[2,16,4096]{2,1,0:T(8,128)S(1)}, u32[]{:S(2)}, u32[]{:S(2)}) collective-permute-start(f32[2,16,4096]{2,1,0:T(8,128)} %get-tuple-element.109), channel_id=1, source_target_pairs={{0,8},{1,9},{2,10},{3,11},{4,12},{5,13},{6,14},{7,15},{16,0},{17,1... | collective-permute-start | bytes 1572872 | tf_op jit(solution)/shard_map/ppermute | solution.py:613
  773.9 61.2 %collective-permute-start.9 = (f32[2,16,4096]{2,1,0:T(8,128)}, f32[2,16,4096]{2,1,0:T(8,128)S(1)}, u32[]{:S(2)}, u32[]{:S(2)}) collective-permute-start(f32[2,16,4096]{2,1,0:T(8,128)} %get-tuple-element.121), channel_id=1, source_target_pairs={{8,16},{9,17},{10,18},{11,19},{12,20},{13,21},{14,22},{15,23},{16,... | collective-permute-start | bytes 1572872 | tf_op jit(solution)/shard_map/ppermute | solution.py:613
  778.8 73.8 %copy-start.29 = (f32[2,32,4096]{2,1,0:T(8,128)S(1)}, f32[2,32,4096]{2,1,0:T(8,128)}, u32[]{:S(2)}) copy-start(f32[2,32,4096]{2,1,0:T(8,128)} %get-tuple-element.118) | copy-start | bytes 3145732
  794.3 52.0 %collective-permute-start.10 = (f32[2,16,4096]{2,1,0:T(8,128)}, f32[2,16,4096]{2,1,0:T(8,128)S(1)}, u32[]{:S(2)}, u32[]{:S(2)}) collective-permute-start(f32[2,16,4096]{2,1,0:T(8,128)} %get-tuple-element.116), channel_id=1, source_target_pairs={{0,8},{1,9},{2,10},{3,11},{4,12},{5,13},{6,14},{7,15},{16,0},{17,1... | collective-permute-start | bytes 1572872 | tf_op jit(solution)/shard_map/ppermute | solution.py:613
  823.9 28.7 %collective-permute-start.11 = (f32[2,16,4096]{2,1,0:T(8,128)}, f32[2,16,4096]{2,1,0:T(8,128)S(1)}, u32[]{:S(2)}, u32[]{:S(2)}) collective-permute-start(f32[2,16,4096]{2,1,0:T(8,128)} %get-tuple-element.124), channel_id=1, source_target_pairs={{8,16},{9,17},{10,18},{11,19},{12,20},{13,21},{14,22},{15,23},{16,... | collective-permute-start | bytes 1572872 | tf_op jit(solution)/shard_map/ppermute | solution.py:613
  (29 other events, 165.9 us)

commit v12 on v11

--- a/solution.py
+++ b/solution.py
@@ -94,6 +94,12 @@
     return jnp.dot(a, b, preferred_element_type=jnp.float32)
 
 
+def split_dot(high, low, whi, wlo):
+    count = high.shape[0]
+    both = dot32(jnp.concatenate([high, low], axis=0), whi)
+    return both[:count] + (both[count:] + dot32(high, wlo))
+
+
 def times(a, b):
     return (a[0] * b[0] - a[1] * b[1], a[0] * b[1] + a[1] * b[0])
 
@@ -144,8 +150,7 @@
 
 def rows_mix(xhi, xlo, mhi, mlo, y):
     def step(k, carry):
-        high, low = xhi[k], xlo[k]
-        y[k] = dot32(high, mhi[k]) + (dot32(low, mhi[k]) + dot32(high, mlo[k]))
+        y[k] = split_dot(xhi[k], xlo[k], mhi[k], mlo[k])
         return carry
 
     lax.fori_loop(0, XA, step, 0)
@@ -172,8 +177,8 @@
 
 def columns_mix(xhi, xlo, mhi, mlo, y):
     def step(k, carry):
-        high, low = xhi[k], xlo[k]
-        y[k] = dot32(mhi[k], high) + (dot32(mhi[k], low) + dot32(mlo[k], high))
+        both = dot32(jnp.concatenate([mhi[k], mlo[k]], axis=0), xhi[k])
+        y[k] = both[: 2 * XB] + (both[2 * XB :] + dot32(mhi[k], xlo[k]))
         return carry
 
     lax.fori_loop(0, XA, step, 0)
@@ -212,7 +217,7 @@
         at = [pl.ds(pl.multiple_of(index[b, s] * BLK, BLK), BLK) for s in range(SLOTS)]
         high = jnp.concatenate([shi[:, a] for a in at], axis=1)
         low = jnp.concatenate([slo[:, a] for a in at], axis=1)
-        values = dot32(high, whi[b]) + (dot32(low, whi[b]) + dot32(high, wlo[b]))
+        values = split_dot(high, low, whi[b], wlo[b])
         angle, loss, d_re, d_im = (values[i * rows : (i + 1) * rows] for i in range(4))
         sine, cosine = sincos(angle)
         damping = jnp.exp(-loss)
@@ -351,8 +356,7 @@
     strips(rows, turn)
 
     def step(k, carry):
-        high, low = xhi[k, :rows, :], xlo[k, :rows, :]
-        y[k, :rows, :] = dot32(high, mhi[k]) + (dot32(low, mhi[k]) + dot32(high, mlo[k]))
+        y[k, :rows, :] = split_dot(xhi[k, :rows, :], xlo[k, :rows, :], mhi[k], mlo[k])
         return carry
 
     lax.fori_loop(0, XA, step, 0)
@@ -458,7 +462,8 @@
 
     def step(b, carry):
         high, low = shi[b], slo[b]
-        values = across(high, whi[b]) + (across(low, whi[b]) + across(high, wlo[b]))
+        both = across(jnp.concatenate([high, low], axis=0), whi[b])
+        values = both[: 2 * rows] + (both[2 * rows :] + across(high, wlo[b]))
         for s in range(SLOTS):
             at = pl.ds(pl.multiple_of(index[b, s] * BLK, BLK), BLK)
             for i in range(2):
@@ -691,25 +696,20 @@
         carried.append((exchange(out), kept))
     backs = [exchange(detector(out, row)) for out, _ in carried]
     most, half = CHUNKS // 2, XB // CHUNKS // 2
-    rest = (CHUNKS // 4, CHUNKS // 4)
-    spans = (most,) + rest
+    spans = (most, CHUNKS - most)
 
     def home(a, back, first, before, spans):
         t0 = ahead[a][first : first + sum(spans)]
         return leave(place, block_index[a], back, t0, weights[a], row, before, spans)
 
-    early = pull(backs[0], carried[0][1], column, (most, sum(rest)))
+    early = pull(backs[0], carried[0][1], column, (CHUNKS,))
     late = pull(backs[1], carried[1][1], column, spans)
     back = exchange(early[0])
     next_back = exchange(late[0])
-    (start,) = home(0, back, 0, (), (most,))
-    back = exchange(after(early[1], start))
-    totals = home(1, next_back, 0, start, (most,))
-    next_back = exchange(after(late[1], totals))
-    starts = home(0, back, most, (), rest)
-    back = exchange(after(late[2], starts))
-    totals += home(1, next_back, most, starts[0], rest[:1])
-    totals += home(1, back, most + rest[0], starts[1], rest[1:])
+    starts = home(0, back, 0, (), spans)
+    back = exchange(after(late[1], starts))
+    totals = home(1, next_back, 0, starts[0], spans[:1])
+    totals += home(1, back, most, starts[1], spans[1:])
     pieces = []
     leaving = [depart(*total) for total in totals]
     total = totals[-1]

time: 868 us -> 858 us (0.988)
  Pallas kernels: 321 us -> 300 us
  waiting for transfers between devices: 343 us -> 362 us
  starting transfers between devices: 143 us -> 132 us
    pallas_call x19 -> x17, Pallas kernels: 321 us -> 300 us  [call(): pl.pallas_call(kernel, out_shape=[jax.ShapeDtypeStruct(o, jnp.float32) fo...]
    all_to_all x17 -> x15, waiting for transfers between devices: 169 us -> 185 us  [exchange(): lax.all_to_all(values, ('parts', 'fft'), split_axis=0, concat_axis=0, axi...]
    all_to_all x17 -> x15, starting transfers between devices: 119 us -> 108 us  [exchange(): lax.all_to_all(values, ('parts', 'fft'), split_axis=0, concat_axis=0, axi...]
    ppermute x12 -> x10, waiting for transfers between devices: 174 us -> 177 us  [permute(): return lax.ppermute(values, ('parts', 'fft'), pairs)]
    ppermute x12 -> x10, starting transfers between devices: 23.7 us -> 23.5 us  [permute(): return lax.ppermute(values, ('parts', 'fft'), pairs)]
  transfers between devices with their start and end apart: 29 -> 25, of which waited for: 23 -> 22; matrix products, arithmetic and copies ran while one was open for 4% -> 4% of each run, Pallas kernels for 37% -> 35%
where the time goes in v12:
time: 858 us; the launch traced here: 848 us
  waiting for transfers between devices  362 us (42%)
  Pallas kernels  300 us (35%)
  starting transfers between devices  132 us (15%)
  other arithmetic  28.5 us (3%)
  local copies, waits for them, and re-layouts  24.7 us (3%)
    pallas_call x17, Pallas kernels, call(): pl.pallas_call(kernel, out_shape=[jax.ShapeDtypeStruct(o, jnp.float32) fo...  300 us
    all_to_all x15, waiting for transfers between devices, exchange(): lax.all_to_all(values, ('parts', 'fft'), split_axis=0, concat_axis=0, axi...  185 us
    ppermute x10, waiting for transfers between devices, permute(): return lax.ppermute(values, ('parts', 'fft'), pairs)  177 us
    all_to_all x15, starting transfers between devices, exchange(): lax.all_to_all(values, ('parts', 'fft'), split_axis=0, concat_axis=0, axi...  108 us
    ppermute x10, starting transfers between devices, permute(): return lax.ppermute(values, ('parts', 'fft'), pairs)  23.5 us
  transfers between devices with their start and end apart: 25, of which 22 were waited for; matrix products, arithmetic and copies ran while one was open for 4% of the time, Pallas kernels for 35%

profile of v12, /device:TPU:3, one launch (start us, length us, event | category | flops | bytes accessed | tf_op | source)
XLA Modules:
  0.0 847.7 jit_solution(14126777414163325468)
XLA Ops:
  16.9 11.6 %collective-permute-done = f32[4,16,4096]{2,1,0:T(8,128)} collective-permute-done((f32[4,16,4096]{2,1,0:T(8,128)}, f32[4,16,4096]{2,1,0:T(8,128)}, u32[]{:S(2)}, u32[]{:S(2)}) %collective-permute-start) | collective-permute-done | bytes 1048608 | tf_op jit(solution)/shard_map/ppermute | solution.py:618
  42.8 35.6 %collective-permute-done.1.refs_2_ = f32[4,16,4096]{2,1,0:T(8,128)S(1)} collective-permute-done((f32[4,16,4096]{2,1,0:T(8,128)S(1)}, f32[4,16,4096]{2,1,0:T(8,128)S(1)}, u32[]{:S(2)}, u32[]{:S(2)}) %collective-permute-start.1) | collective-permute-done | bytes 1048608 | tf_op jit(solution)/shard_map/ppermute | solution.py:618
  79.4 16.6 %shard_map.89 = (f32[16,8,32,128]{3,2,1,0:T(8,128)}, f32[16,2,32,128]{3,2,1,0:T(8,128)}) custom-call(s32[2]{0:T(128)} %pad_add_fusion.place, s32[32,2]{1,0:T(8,128)} %copy.17.refs_0_.index, f32[4,16,4096]{2,1,0:T(8,128)} %get-tuple-element.136.refs_1_, f32[4,16,4096]{2,1,0:T(8,128)} %copy-done.23, bf16[32,256,128]{2,1,0:T(8,128)(2,1)} %get-tuple-element.142.refs_3_.whi, ...), custom_call_target="tpu_custom_call" | custom-call | flops 1207959552 | bytes 13107464 | tf_op jit(solution)/shard_map/pallas_call | solution.py:484
  108.8 16.5 %shard_map.82 = (f32[16,8,32,128]{3,2,1,0:T(8,128)}, f32[16,2,32,128]{3,2,1,0:T(8,128)}) custom-call(s32[2]{0:T(128)} %pad_add_fusion.place, s32[32,2]{1,0:T(8,128)} %copy.18.refs_0_.index, f32[4,16,4096]{2,1,0:T(8,128)} %get-tuple-element.136.refs_1_, f32[4,16,4096]{2,1,0:T(8,128)} %copy-done.23, bf16[32,256,128]{2,1,0:T(8,128)(2,1)} %get-tuple-element.141.refs_3_.whi, ...), custom_call_target="tpu_custom_call" | custom-call | flops 1207959552 | bytes 13107464 | tf_op jit(solution)/shard_map/pallas_call | solution.py:484
  125.3 23.2 %collective-permute-done.3.refs_2_ = f32[4,16,4096]{2,1,0:T(8,128)} collective-permute-done((f32[4,16,4096]{2,1,0:T(8,128)}, f32[4,16,4096]{2,1,0:T(8,128)}, u32[]{:S(2)}, u32[]{:S(2)}) %collective-permute-start.3) | collective-permute-done | bytes 1048608 | tf_op jit(solution)/shard_map/ppermute | solution.py:618
  148.6 10.7 %all-to-all-start = ((f32[16,8,32,128]{3,2,1,0:T(8,128)}), f32[16,8,32,128]{3,2,1,0:T(8,128)}, u32[]{:S(2)}, u32[]{:S(2)}) async-start(f32[16,8,32,128]{3,2,1,0:T(8,128)} %get-tuple-element.59), calls=%async_computation | async-start | bytes 4194304 | tf_op jit(solution)/shard_map/all_to_all | solution.py:604
  159.3 16.5 %shard_map.90 = (f32[16,8,32,128]{3,2,1,0:T(8,128)}, f32[16,2,32,128]{3,2,1,0:T(8,128)}) custom-call(s32[2]{0:T(128)} %pad_add_fusion.place, s32[32,2]{1,0:T(8,128)} %copy.17.refs_0_.index, f32[4,16,4096]{2,1,0:T(8,128)} %get-tuple-element.60.refs_1_, f32[4,16,4096]{2,1,0:T(8,128)} %collective-permute-done.3.refs_2_, ...), custom_call_target="tpu_custom_call" | custom-call | flops 1207959552 | bytes 13107464 | tf_op jit(solution)/shard_map/pallas_call | solution.py:484
  175.8 10.0 %all-to-all-done.refs_0_ = f32[16,8,32,128]{3,2,1,0:T(8,128)} async-done(((f32[16,8,32,128]{3,2,1,0:T(8,128)}), f32[16,8,32,128]{3,2,1,0:T(8,128)}, u32[]{:S(2)}, u32[]{:S(2)}) %all-to-all-start) | async-done | bytes 2097184 | tf_op jit(solution)/shard_map/all_to_all | solution.py:604
  198.4 16.5 %shard_map.83 = (f32[16,8,32,128]{3,2,1,0:T(8,128)}, f32[16,2,32,128]{3,2,1,0:T(8,128)}) custom-call(s32[2]{0:T(128)} %pad_add_fusion.place, s32[32,2]{1,0:T(8,128)} %copy.18.refs_0_.index, f32[4,16,4096]{2,1,0:T(8,128)} %get-tuple-element.60.refs_1_, f32[4,16,4096]{2,1,0:T(8,128)} %collective-permute-done.3.refs_2_, ...), custom_call_target="tpu_custom_call" | custom-call | flops 1207959552 | bytes 13107464 | tf_op jit(solution)/shard_map/pallas_call | solution.py:484
  215.0 24.3 %collective-permute-done.4.refs_2_ = f32[4,16,4096]{2,1,0:T(8,128)} collective-permute-done((f32[4,16,4096]{2,1,0:T(8,128)}, f32[4,16,4096]{2,1,0:T(8,128)}, u32[]{:S(2)}, u32[]{:S(2)}) %collective-permute-start.4) | collective-permute-done | bytes 1048608 | tf_op jit(solution)/shard_map/ppermute | solution.py:618
  239.3 10.3 %all-to-all-start.1 = ((f32[16,8,32,128]{3,2,1,0:T(8,128)}), f32[16,8,32,128]{3,2,1,0:T(8,128)}, u32[]{:S(2)}, u32[]{:S(2)}) async-start(f32[16,8,32,128]{3,2,1,0:T(8,128)} %get-tuple-element.63), calls=%async_computation.1 | async-start | bytes 4194304 | tf_op jit(solution)/shard_map/all_to_all | solution.py:604
  249.6 16.6 %shard_map.91 = (f32[16,8,32,128]{3,2,1,0:T(8,128)}, f32[16,2,32,128]{3,2,1,0:T(8,128)}) custom-call(s32[2]{0:T(128)} %pad_add_fusion.place, s32[32,2]{1,0:T(8,128)} %copy.17.refs_0_.index, f32[4,16,4096]{2,1,0:T(8,128)} %get-tuple-element.64.refs_1_, f32[4,16,4096]{2,1,0:T(8,128)} %collective-permute-done.4.refs_2_, ...), custom_call_target="tpu_custom_call" | custom-call | flops 1207959552 | bytes 13107464 | tf_op jit(solution)/shard_map/pallas_call | solution.py:484
  266.1 10.0 %all-to-all-done.1.refs_1_ = f32[16,8,32,128]{3,2,1,0:T(8,128)} async-done(((f32[16,8,32,128]{3,2,1,0:T(8,128)}), f32[16,8,32,128]{3,2,1,0:T(8,128)}, u32[]{:S(2)}, u32[]{:S(2)}) %all-to-all-start.1) | async-done | bytes 2097184 | tf_op jit(solution)/shard_map/all_to_all | solution.py:604
  288.6 16.5 %shard_map.84 = (f32[16,8,32,128]{3,2,1,0:T(8,128)}, f32[16,2,32,128]{3,2,1,0:T(8,128)}) custom-call(s32[2]{0:T(128)} %pad_add_fusion.place, s32[32,2]{1,0:T(8,128)} %copy.18.refs_0_.index, f32[4,16,4096]{2,1,0:T(8,128)} %get-tuple-element.64.refs_1_, f32[4,16,4096]{2,1,0:T(8,128)} %collective-permute-done.4.refs_2_, ...), custom_call_target="tpu_custom_call" | custom-call | flops 1207959552 | bytes 13107464 | tf_op jit(solution)/shard_map/pallas_call | solution.py:484
  305.1 24.6 %collective-permute-done.5.refs_2_ = f32[4,16,4096]{2,1,0:T(8,128)S(1)} collective-permute-done((f32[4,16,4096]{2,1,0:T(8,128)}, f32[4,16,4096]{2,1,0:T(8,128)S(1)}, u32[]{:S(2)}, u32[]{:S(2)}) %collective-permute-start.5) | collective-permute-done | bytes 1048608 | tf_op jit(solution)/shard_map/ppermute | solution.py:618
  339.6 16.6 %shard_map.92 = (f32[16,8,32,128]{3,2,1,0:T(8,128)}, f32[16,2,32,128]{3,2,1,0:T(8,128)}) custom-call(s32[2]{0:T(128)} %pad_add_fusion.place, s32[32,2]{1,0:T(8,128)} %copy.17.refs_0_.index, f32[4,16,4096]{2,1,0:T(8,128)} %get-tuple-element.68.refs_1_, f32[4,16,4096]{2,1,0:T(8,128)} %copy-done.24, bf16[32,256,128]{2,1,0:T(8,128)(2,1)} %get-tuple-element.142.refs_3_.whi, ...), custom_call_target="tpu_custom_call" | custom-call | flops 1207959552 | bytes 13107464 | tf_op jit(solution)/shard_map/pallas_call | solution.py:484
  356.2 10.0 %all-to-all-done.2.refs_2_ = f32[16,8,32,128]{3,2,1,0:T(8,128)} async-done(((f32[16,8,32,128]{3,2,1,0:T(8,128)}), f32[16,8,32,128]{3,2,1,0:T(8,128)}, u32[]{:S(2)}, u32[]{:S(2)}) %all-to-all-start.2) | async-done | bytes 2097184 | tf_op jit(solution)/shard_map/all_to_all | solution.py:604
  372.4 16.5 %shard_map.85 = (f32[16,8,32,128]{3,2,1,0:T(8,128)}, f32[16,2,32,128]{3,2,1,0:T(8,128)}) custom-call(s32[2]{0:T(128)} %pad_add_fusion.place, s32[32,2]{1,0:T(8,128)} %copy.18.refs_0_.index, f32[4,16,4096]{2,1,0:T(8,128)} %get-tuple-element.68.refs_1_, f32[4,16,4096]{2,1,0:T(8,128)} %copy-done.24, bf16[32,256,128]{2,1,0:T(8,128)(2,1)} %get-tuple-element.141.refs_3_.whi, ...), custom_call_target="tpu_custom_call" | custom-call | flops 1207959552 | bytes 13107464 | tf_op jit(solution)/shard_map/pallas_call | solution.py:484
  406.4 20.9 %shard_map.93 = (f32[16,4,128,128]{3,2,1,0:T(8,128)}, f32[16,4,128,128]{3,2,1,0:T(8,128)}) custom-call(f32[16,8,32,128]{3,2,1,0:T(8,128)} %copy-done.2, f32[16,8,32,128]{3,2,1,0:T(8,128)} %copy-done.3, f32[16,8,32,128]{3,2,1,0:T(8,128)} %copy-done.4, f32[16,8,32,128]{3,2,1,0:T(8,128)} %copy-done.8, bf16[16,256,256]{2,1,0:T(8,128)(2,1)} %constant.34.clone.refs_4_.mhi, ...), custom_call_target="tpu_custom_call" | custom-call | flops 3221225472 | bytes 20971520 | tf_op jit(solution)/shard_map/pallas_call | solution.py:484
  441.5 21.0 %shard_map.86 = (f32[16,4,128,128]{3,2,1,0:T(8,128)}, f32[16,4,128,128]{3,2,1,0:T(8,128)}) custom-call(f32[16,8,32,128]{3,2,1,0:T(8,128)} %all-to-all-done.refs_0_, f32[16,8,32,128]{3,2,1,0:T(8,128)} %all-to-all-done.1.refs_1_, f32[16,8,32,128]{3,2,1,0:T(8,128)} %all-to-all-done.2.refs_2_, f32[16,8,32,128]{3,2,1,0:T(8,128)} %copy-done.7, ...), custom_call_target="tpu_custom_call" | custom-call | flops 3221225472 | bytes 20971520 | tf_op jit(solution)/shard_map/pallas_call | solution.py:484
  462.5 33.4 %all-to-all-done.11.fields = f32[16,4,128,128]{3,2,1,0:T(8,128)} async-done(((f32[16,4,128,128]{3,2,1,0:T(8,128)}), f32[16,4,128,128]{3,2,1,0:T(8,128)}, u32[]{:S(2)}, u32[]{:S(2)}) %all-to-all-start.11) | async-done | bytes 4194336 | tf_op jit(solution)/shard_map/all_to_all | solution.py:604
  503.0 16.6 %shard_map.94 = f32[16,2,128,128]{3,2,1,0:T(8,128)} custom-call(f32[16,4,128,128]{3,2,1,0:T(8,128)} %all-to-all-done.11.fields, bf16[16,256,256]{2,1,0:T(8,128)(2,1)} %constant.36.clone.refs_5_.mhi, bf16[16,256,256]{2,1,0:T(8,128)(2,1)} %constant.37.clone.refs_6_.mlo), custom_call_target="tpu_custom_call" | custom-call | flops 2415919104 | bytes 10485760 | tf_op jit(solution)/shard_map/pallas_call | solution.py:484
  519.6 38.0 %all-to-all-done.4.fields = f32[16,4,128,128]{3,2,1,0:T(8,128)} async-done(((f32[16,4,128,128]{3,2,1,0:T(8,128)}), f32[16,4,128,128]{3,2,1,0:T(8,128)}, u32[]{:S(2)}, u32[]{:S(2)}) %all-to-all-start.4) | async-done | bytes 4194336 | tf_op jit(solution)/shard_map/all_to_all | solution.py:604
  563.8 16.6 %shard_map.87 = f32[16,2,128,128]{3,2,1,0:T(8,128)} custom-call(f32[16,4,128,128]{3,2,1,0:T(8,128)} %all-to-all-done.4.fields, bf16[16,256,256]{2,1,0:T(8,128)(2,1)} %constant.36.clone.refs_5_.mhi, bf16[16,256,256]{2,1,0:T(8,128)(2,1)} %constant.37.clone.refs_6_.mlo), custom_call_target="tpu_custom_call" | custom-call | flops 2415919104 | bytes 10485760 | tf_op jit(solution)/shard_map/pallas_call | solution.py:484
  597.8 17.5 %shard_map.95 = f32[16,4,128,128]{3,2,1,0:T(8,128)} custom-call(f32[16,2,128,128]{3,2,1,0:T(8,128)} %copy-done.1, f32[16,4,128,128]{3,2,1,0:T(8,128)} %get-tuple-element.80.kept, bf16[16,256,256]{2,1,0:T(8,128)(2,1)} %constant.34.clone.refs_4_.mhi, bf16[16,256,256]{2,1,0:T(8,128)(2,1)} %constant.35.clone.refs_5_.mlo), custom_call_target="tpu_custom_call" | custom-call | flops 1610612736 | bytes 14680064 | tf_op jit(solution)/shard_map/pallas_call | solution.py:484
  633.0 17.2 %shard_map.88 = (f32[16,4,64,128]{3,2,1,0:T(8,128)}, f32[16,4,64,128]{3,2,1,0:T(8,128)}) custom-call(f32[16,2,128,128]{3,2,1,0:T(8,128)} %copy-done, f32[16,4,128,128]{3,2,1,0:T(8,128)} %get-tuple-element.71.kept, bf16[16,256,256]{2,1,0:T(8,128)(2,1)} %constant.34.clone.refs_4_.mhi, bf16[16,256,256]{2,1,0:T(8,128)(2,1)} %constant.35.clone.refs_5_.mlo), custom_call_target="tpu_custom_call" | custom-call | flops 1610612736 | bytes 14680064 | tf_op jit(solution)/shard_map/pallas_call | solution.py:484
  650.2 37.1 %all-to-all-done.13.back = f32[16,4,128,128]{3,2,1,0:T(8,128)} async-done(((f32[16,4,128,128]{3,2,1,0:T(8,128)}), f32[16,4,128,128]{3,2,1,0:T(8,128)}, u32[]{:S(2)}, u32[]{:S(2)}) %all-to-all-start.13) | async-done | bytes 4194336 | tf_op jit(solution)/shard_map/all_to_all | solution.py:604
  693.7 22.1 %shard_map.96 = (f32[2,32,4096]{2,1,0:T(8,128)}, f32[2,32,4096]{2,1,0:T(8,128)}, f32[2,32,4096]{2,1,0:T(8,128)}, f32[2,32,4096]{2,1,0:T(8,128)}) custom-call(s32[2]{0:T(128)} %pad_add_fusion.place, s32[32,2]{1,0:T(8,128)} %copy.17.refs_0_.index, f32[16,4,128,128]{3,2,1,0:T(8,128)} %all-to-all-done.13.back, ...), custom_call_target="tpu_custom_call" | custom-call | flops 2415919104 | bytes 18874632 | tf_op jit(solution)/shard_map/pallas_call | solution.py:484
  727.6 17.9 %shard_map.97 = (f32[2,32,4096]{2,1,0:T(8,128)}, f32[2,32,4096]{2,1,0:T(8,128)}) custom-call(s32[2]{0:T(128)} %pad_add_fusion.place, s32[32,2]{1,0:T(8,128)} %copy.18.refs_0_.index, f32[16,4,64,128]{3,2,1,0:T(8,128)} %copy-done.6, bf16[32,256,128]{2,1,0:T(8,128)(2,1)} %get-tuple-element.141.refs_3_.whi, ...), custom_call_target="tpu_custom_call" | custom-call | flops 1207959552 | bytes 15728904 | tf_op jit(solution)/shard_map/pallas_call | solution.py:484
  760.9 18.1 %shard_map.98 = (f32[2,32,4096]{2,1,0:T(8,128)}, f32[2,32,4096]{2,1,0:T(8,128)}) custom-call(s32[2]{0:T(128)} %pad_add_fusion.place, s32[32,2]{1,0:T(8,128)} %copy.18.refs_0_.index, f32[16,4,64,128]{3,2,1,0:T(8,128)} %copy-done.5, bf16[32,256,128]{2,1,0:T(8,128)(2,1)} %get-tuple-element.141.refs_3_.whi, ...), custom_call_target="tpu_custom_call" | custom-call | flops 1207959552 | bytes 15728904 | tf_op jit(solution)/shard_map/pallas_call | solution.py:484
  784.9 32.1 %collective-permute-done.6 = f32[2,32,4096]{2,1,0:T(8,128)} collective-permute-done((f32[2,32,4096]{2,1,0:T(8,128)}, f32[2,32,4096]{2,1,0:T(8,128)}, u32[]{:S(2)}, u32[]{:S(2)}) %collective-permute-start.6) | collective-permute-done | bytes 1048608 | tf_op jit(solution)/shard_map/ppermute | solution.py:618
  819.8 19.6 %collective-permute-done.8 = f32[2,32,4096]{2,1,0:T(8,128)S(1)} collective-permute-done((f32[2,32,4096]{2,1,0:T(8,128)}, f32[2,32,4096]{2,1,0:T(8,128)S(1)}, u32[]{:S(2)}, u32[]{:S(2)}) %collective-permute-start.8) | collective-permute-done | bytes 1048608 | tf_op jit(solution)/shard_map/ppermute | solution.py:618
  (121 shorter events, 216.4 us)
Async XLA Ops:
  4.2 24.3 %collective-permute-start = (f32[4,16,4096]{2,1,0:T(8,128)}, f32[4,16,4096]{2,1,0:T(8,128)}, u32[]{:S(2)}, u32[]{:S(2)}) collective-permute-start(f32[4,16,4096]{2,1,0:T(8,128)} %fusion.7), channel_id=1, source_target_pairs={{0,16},{1,17},{2,18},{3,19},{4,20},{5,21},{6,22},{7,23},{8,24},{9,... | collective-permute-start | bytes 3145736 | tf_op jit(solution)/shard_map/ppermute | solution.py:618
  14.9 13.6 %copy-start.14 = (f32[2,16,4096]{2,1,0:T(8,128)S(1)}, f32[2,16,4096]{2,1,0:T(8,128)}, u32[]{:S(2)}) copy-start(f32[2,16,4096]{2,1,0:T(8,128)} %copy-done.13) | copy-start | bytes 1572868
  14.9 13.6 %copy-start.16 = (f32[2,16,4096]{2,1,0:T(8,128)S(1)}, f32[2,16,4096]{2,1,0:T(8,128)}, u32[]{:S(2)}) copy-start(f32[2,16,4096]{2,1,0:T(8,128)} %copy-done.15) | copy-start | bytes 1572868
  31.0 47.4 %collective-permute-start.1 = (f32[4,16,4096]{2,1,0:T(8,128)S(1)}, f32[4,16,4096]{2,1,0:T(8,128)S(1)}, u32[]{:S(2)}, u32[]{:S(2)}) collective-permute-start(f32[4,16,4096]{2,1,0:T(8,128)S(1)} %get-tuple-element.135), channel_id=1, source_target_pairs={{0,8},{1,9},{2,10},{3,11},{4,12},{5,13},{6,14},{7,15},{8,0},{9,1},... | collective-permute-start | bytes 3145736 | tf_op jit(solution)/shard_map/ppermute | solution.py:618
  33.4 68.2 %collective-permute-start.2 = (f32[12,16,4096]{2,1,0:T(8,128)}, f32[12,16,4096]{2,1,0:T(8,128)}, u32[]{:S(2)}, u32[]{:S(2)}) collective-permute-start(f32[12,16,4096]{2,1,0:T(8,128)} %pad_maximum_fusion), channel_id=1, source_target_pairs={{0,16},{1,17},{2,18},{3,19},{4,20},{5,21},{6,22},{7,23},{8,24},{9,... | collective-permute-start | bytes 9437192 | tf_op jit(solution)/shard_map/ppermute | solution.py:618
  96.0 52.6 %all-to-all-start.7 = ((f32[16,8,32,128]{3,2,1,0:T(8,128)}), f32[16,8,32,128]{3,2,1,0:T(8,128)S(1)}, u32[]{:S(2)}, u32[]{:S(2)}) async-start(f32[16,8,32,128]{3,2,1,0:T(8,128)} %get-tuple-element.75), calls=%async_computation.7 | async-start | bytes 4194304 | tf_op jit(solution)/shard_map/all_to_all | solution.py:604
  105.0 43.5 %collective-permute-start.3 = (f32[4,16,4096]{2,1,0:T(8,128)}, f32[4,16,4096]{2,1,0:T(8,128)}, u32[]{:S(2)}, u32[]{:S(2)}) collective-permute-start(f32[4,16,4096]{2,1,0:T(8,128)} %get-tuple-element.58), channel_id=1, source_target_pairs={{0,8},{1,9},{2,10},{3,11},{4,12},{5,13},{6,14},{7,15},{8,0},{9,1},... | collective-permute-start | bytes 3145736 | tf_op jit(solution)/shard_map/ppermute | solution.py:618
  148.6 27.2 %copy-start.2 = (f32[16,8,32,128]{3,2,1,0:T(8,128)}, f32[16,8,32,128]{3,2,1,0:T(8,128)S(1)}, u32[]{:S(2)}) copy-start(f32[16,8,32,128]{3,2,1,0:T(8,128)S(1)} %all-to-all-done.7.refs_0_) | copy-start | bytes 6291460
  148.6 37.2 %all-to-all-start = ((f32[16,8,32,128]{3,2,1,0:T(8,128)}), f32[16,8,32,128]{3,2,1,0:T(8,128)}, u32[]{:S(2)}, u32[]{:S(2)}) async-start(f32[16,8,32,128]{3,2,1,0:T(8,128)} %get-tuple-element.59), calls=%async_computation | async-start | bytes 4194304 | tf_op jit(solution)/shard_map/all_to_all | solution.py:604
  185.8 53.4 %all-to-all-start.8 = ((f32[16,8,32,128]{3,2,1,0:T(8,128)}), f32[16,8,32,128]{3,2,1,0:T(8,128)S(1)}, u32[]{:S(2)}, u32[]{:S(2)}) async-start(f32[16,8,32,128]{3,2,1,0:T(8,128)} %get-tuple-element.76), calls=%async_computation.8 | async-start | bytes 4194304 | tf_op jit(solution)/shard_map/all_to_all | solution.py:604
  195.6 43.7 %collective-permute-start.4 = (f32[4,16,4096]{2,1,0:T(8,128)}, f32[4,16,4096]{2,1,0:T(8,128)}, u32[]{:S(2)}, u32[]{:S(2)}) collective-permute-start(f32[4,16,4096]{2,1,0:T(8,128)} %get-tuple-element.62), channel_id=1, source_target_pairs={{0,8},{1,9},{2,10},{3,11},{4,12},{5,13},{6,14},{7,15},{8,0},{9,1},... | collective-permute-start | bytes 3145736 | tf_op jit(solution)/shard_map/ppermute | solution.py:618
  239.3 26.8 %copy-start.3 = (f32[16,8,32,128]{3,2,1,0:T(8,128)}, f32[16,8,32,128]{3,2,1,0:T(8,128)S(1)}, u32[]{:S(2)}) copy-start(f32[16,8,32,128]{3,2,1,0:T(8,128)S(1)} %all-to-all-done.8.refs_1_) | copy-start | bytes 6291460
  239.3 36.8 %all-to-all-start.1 = ((f32[16,8,32,128]{3,2,1,0:T(8,128)}), f32[16,8,32,128]{3,2,1,0:T(8,128)}, u32[]{:S(2)}, u32[]{:S(2)}) async-start(f32[16,8,32,128]{3,2,1,0:T(8,128)} %get-tuple-element.63), calls=%async_computation.1 | async-start | bytes 4194304 | tf_op jit(solution)/shard_map/all_to_all | solution.py:604
  276.1 53.6 %all-to-all-start.9 = ((f32[16,8,32,128]{3,2,1,0:T(8,128)}), f32[16,8,32,128]{3,2,1,0:T(8,128)S(1)}, u32[]{:S(2)}, u32[]{:S(2)}) async-start(f32[16,8,32,128]{3,2,1,0:T(8,128)} %get-tuple-element.77), calls=%async_computation.9 | async-start | bytes 4194304 | tf_op jit(solution)/shard_map/all_to_all | solution.py:604
  285.6 44.1 %collective-permute-start.5 = (f32[4,16,4096]{2,1,0:T(8,128)}, f32[4,16,4096]{2,1,0:T(8,128)S(1)}, u32[]{:S(2)}, u32[]{:S(2)}) collective-permute-start(f32[4,16,4096]{2,1,0:T(8,128)} %get-tuple-element.66), channel_id=1, source_target_pairs={{0,8},{1,9},{2,10},{3,11},{4,12},{5,13},{6,14},{7,15},{8,0},{9,1},... | collective-permute-start | bytes 3145736 | tf_op jit(solution)/shard_map/ppermute | solution.py:618
  329.7 26.5 %copy-start.4 = (f32[16,8,32,128]{3,2,1,0:T(8,128)}, f32[16,8,32,128]{3,2,1,0:T(8,128)S(1)}, u32[]{:S(2)}) copy-start(f32[16,8,32,128]{3,2,1,0:T(8,128)S(1)} %all-to-all-done.9.refs_2_) | copy-start | bytes 6291460
  329.7 36.5 %all-to-all-start.2 = ((f32[16,8,32,128]{3,2,1,0:T(8,128)}), f32[16,8,32,128]{3,2,1,0:T(8,128)}, u32[]{:S(2)}, u32[]{:S(2)}) async-start(f32[16,8,32,128]{3,2,1,0:T(8,128)} %get-tuple-element.67), calls=%async_computation.2 | async-start | bytes 4194304 | tf_op jit(solution)/shard_map/all_to_all | solution.py:604
  366.2 32.7 %all-to-all-start.10 = ((f32[16,8,32,128]{3,2,1,0:T(8,128)}), f32[16,8,32,128]{3,2,1,0:T(8,128)S(1)}, u32[]{:S(2)}, u32[]{:S(2)}) async-start(f32[16,8,32,128]{3,2,1,0:T(8,128)} %get-tuple-element.78), calls=%async_computation.10 | async-start | bytes 4194304 | tf_op jit(solution)/shard_map/all_to_all | solution.py:604
  400.2 32.7 %all-to-all-start.3 = ((f32[16,8,32,128]{3,2,1,0:T(8,128)}), f32[16,8,32,128]{3,2,1,0:T(8,128)S(1)}, u32[]{:S(2)}, u32[]{:S(2)}) async-start(f32[16,8,32,128]{3,2,1,0:T(8,128)} %get-tuple-element.69), calls=%async_computation.3 | async-start | bytes 4194304 | tf_op jit(solution)/shard_map/all_to_all | solution.py:604
  434.2 61.7 %all-to-all-start.11 = ((f32[16,4,128,128]{3,2,1,0:T(8,128)}), f32[16,4,128,128]{3,2,1,0:T(8,128)}, u32[]{:S(2)}, u32[]{:S(2)}) async-start(f32[16,4,128,128]{3,2,1,0:T(8,128)} %get-tuple-element.79), calls=%async_computation.11 | async-start | bytes 8388608 | tf_op jit(solution)/shard_map/all_to_all | solution.py:604
  495.9 61.6 %all-to-all-start.4 = ((f32[16,4,128,128]{3,2,1,0:T(8,128)}), f32[16,4,128,128]{3,2,1,0:T(8,128)}, u32[]{:S(2)}, u32[]{:S(2)}) async-start(f32[16,4,128,128]{3,2,1,0:T(8,128)} %get-tuple-element.70), calls=%async_computation.4 | async-start | bytes 8388608 | tf_op jit(solution)/shard_map/all_to_all | solution.py:604
  557.5 32.8 %all-to-all-start.12 = ((f32[16,2,128,128]{3,2,1,0:T(8,128)}), f32[16,2,128,128]{3,2,1,0:T(8,128)S(1)}, u32[]{:S(2)}, u32[]{:S(2)}) async-start(f32[16,2,128,128]{3,2,1,0:T(8,128)} %shard_map.94), calls=%async_computation.12 | async-start | bytes 4194304 | tf_op jit(solution)/shard_map/all_to_all | solution.py:604
  591.6 32.7 %all-to-all-start.5 = ((f32[16,2,128,128]{3,2,1,0:T(8,128)}), f32[16,2,128,128]{3,2,1,0:T(8,128)S(1)}, u32[]{:S(2)}, u32[]{:S(2)}) async-start(f32[16,2,128,128]{3,2,1,0:T(8,128)} %shard_map.87), calls=%async_computation.5 | async-start | bytes 4194304 | tf_op jit(solution)/shard_map/all_to_all | solution.py:604
  625.6 61.8 %all-to-all-start.13 = ((f32[16,4,128,128]{3,2,1,0:T(8,128)}), f32[16,4,128,128]{3,2,1,0:T(8,128)}, u32[]{:S(2)}, u32[]{:S(2)}) async-start(f32[16,4,128,128]{3,2,1,0:T(8,128)} %shard_map.95), calls=%async_computation.13 | async-start | bytes 8388608 | tf_op jit(solution)/shard_map/all_to_all | solution.py:604
  687.3 32.8 %all-to-all-start.6 = ((f32[16,4,64,128]{3,2,1,0:T(8,128)}), f32[16,4,64,128]{3,2,1,0:T(8,128)S(1)}, u32[]{:S(2)}, u32[]{:S(2)}) async-start(f32[16,4,64,128]{3,2,1,0:T(8,128)} %get-tuple-element.72), calls=%async_computation.6 | async-start | bytes 4194304 | tf_op jit(solution)/shard_map/all_to_all | solution.py:604
  721.4 38.1 %all-to-all-start.14 = ((f32[16,4,64,128]{3,2,1,0:T(8,128)}), f32[16,4,64,128]{3,2,1,0:T(8,128)S(1)}, u32[]{:S(2)}, u32[]{:S(2)}) async-start(f32[16,4,64,128]{3,2,1,0:T(8,128)} %get-tuple-element.92), calls=%async_computation.14 | async-start | bytes 4194304 | tf_op jit(solution)/shard_map/all_to_all | solution.py:604
  745.6 71.5 %collective-permute-start.6 = (f32[2,32,4096]{2,1,0:T(8,128)}, f32[2,32,4096]{2,1,0:T(8,128)}, u32[]{:S(2)}, u32[]{:S(2)}) collective-permute-start(f32[2,32,4096]{2,1,0:T(8,128)} %get-tuple-element.87), channel_id=1, source_target_pairs={{0,8},{1,9},{2,10},{3,11},{4,12},{5,13},{6,14},{7,15},{16,0},{17,1... | collective-permute-start | bytes 3145736 | tf_op jit(solution)/shard_map/ppermute | solution.py:618
  745.6 74.2 %collective-permute-start.7 = (f32[2,32,4096]{2,1,0:T(8,128)}, f32[2,32,4096]{2,1,0:T(8,128)}, u32[]{:S(2)}, u32[]{:S(2)}) collective-permute-start(f32[2,32,4096]{2,1,0:T(8,128)} %get-tuple-element.97), channel_id=1, source_target_pairs={{8,16},{9,17},{10,18},{11,19},{12,20},{13,21},{14,22},{15,23},{16,... | collective-permute-start | bytes 3145736 | tf_op jit(solution)/shard_map/ppermute | solution.py:618
  760.9 81.2 %copy-start.25 = (f32[2,32,4096]{2,1,0:T(8,128)S(1)}, f32[2,32,4096]{2,1,0:T(8,128)}, u32[]{:S(2)}) copy-start(f32[2,32,4096]{2,1,0:T(8,128)} %get-tuple-element.97) | copy-start | bytes 3145732
  779.0 60.4 %collective-permute-start.8 = (f32[2,32,4096]{2,1,0:T(8,128)}, f32[2,32,4096]{2,1,0:T(8,128)S(1)}, u32[]{:S(2)}, u32[]{:S(2)}) collective-permute-start(f32[2,32,4096]{2,1,0:T(8,128)} %get-tuple-element.95), channel_id=1, source_target_pairs={{0,8},{1,9},{2,10},{3,11},{4,12},{5,13},{6,14},{7,15},{16,0},{17,1... | collective-permute-start | bytes 3145736 | tf_op jit(solution)/shard_map/ppermute | solution.py:618
  782.9 61.2 %copy-start.26 = (f32[2,32,4096]{2,1,0:T(8,128)S(1)}, f32[2,32,4096]{2,1,0:T(8,128)}, u32[]{:S(2)}) copy-start(f32[2,32,4096]{2,1,0:T(8,128)} %get-tuple-element.100) | copy-start | bytes 3145732
  782.9 59.3 %collective-permute-start.9 = (f32[2,32,4096]{2,1,0:T(8,128)}, f32[2,32,4096]{2,1,0:T(8,128)S(1)}, u32[]{:S(2)}, u32[]{:S(2)}) collective-permute-start(f32[2,32,4096]{2,1,0:T(8,128)} %get-tuple-element.100), channel_id=1, source_target_pairs={{8,16},{9,17},{10,18},{11,19},{12,20},{13,21},{14,22},{15,23},{16,... | collective-permute-start | bytes 3145736 | tf_op jit(solution)/shard_map/ppermute | solution.py:618
  (22 other events, 89.2 us)

commit v13 on v12

--- a/solution.py
+++ b/solution.py
@@ -702,14 +702,16 @@
         t0 = ahead[a][first : first + sum(spans)]
         return leave(place, block_index[a], back, t0, weights[a], row, before, spans)
 
-    early = pull(backs[0], carried[0][1], column, (CHUNKS,))
+    early = pull(backs[0], carried[0][1], column, spans)
     late = pull(backs[1], carried[1][1], column, spans)
     back = exchange(early[0])
     next_back = exchange(late[0])
-    starts = home(0, back, 0, (), spans)
-    back = exchange(after(late[1], starts))
-    totals = home(1, next_back, 0, starts[0], spans[:1])
-    totals += home(1, back, most, starts[1], spans[1:])
+    (start,) = home(0, back, 0, (), spans[:1])
+    back = exchange(after(early[1], start))
+    totals = home(1, next_back, 0, start, spans[:1])
+    next_back = exchange(after(late[1], totals))
+    (start,) = home(0, back, most, (), spans[1:])
+    totals += home(1, next_back, most, start, spans[1:])
     pieces = []
     leaving = [depart(*total) for total in totals]
     total = totals[-1]

time: 858 us -> 864 us (level)
  Pallas kernels: 300 us -> 312 us
    pallas_call x17 -> x18, Pallas kernels: 300 us -> 312 us  [call(): pl.pallas_call(kernel, out_shape=[jax.ShapeDtypeStruct(o, jnp.float32) fo...]
    ppermute x10, waiting for transfers between devices: 177 us -> 167 us  [permute(): return lax.ppermute(values, ('parts', 'fft'), pairs)]
    all_to_all x15 -> x16, starting transfers between devices: 108 us -> 115 us  [exchange(): lax.all_to_all(values, ('parts', 'fft'), split_axis=0, concat_axis=0, axi...]
    all_to_all x15 -> x16, waiting for transfers between devices: 185 us -> 187 us  [exchange(): lax.all_to_all(values, ('parts', 'fft'), split_axis=0, concat_axis=0, axi...]
  transfers between devices with their start and end apart: 25 -> 26, of which waited for: 22 -> 20; matrix products, arithmetic and copies ran while one was open for 4% -> 4% of each run, Pallas kernels for 35% -> 37%
where the time goes in v13:
time: 864 us; the launch traced here: 855 us
  waiting for transfers between devices  354 us (41%)
  Pallas kernels  312 us (36%)
  starting transfers between devices  137 us (16%)
  other arithmetic  28.2 us (3%)
  local copies, waits for them, and re-layouts  23.3 us (3%)
    pallas_call x18, Pallas kernels, call(): pl.pallas_call(kernel, out_shape=[jax.ShapeDtypeStruct(o, jnp.float32) fo...  312 us
    all_to_all x16, waiting for transfers between devices, exchange(): lax.all_to_all(values, ('parts', 'fft'), split_axis=0, concat_axis=0, axi...  187 us
    ppermute x10, waiting for transfers between devices, permute(): return lax.ppermute(values, ('parts', 'fft'), pairs)  167 us
    all_to_all x16, starting transfers between devices, exchange(): lax.all_to_all(values, ('parts', 'fft'), split_axis=0, concat_axis=0, axi...  115 us
    ppermute x10, starting transfers between devices, permute(): return lax.ppermute(values, ('parts', 'fft'), pairs)  21.9 us
  transfers between devices with their start and end apart: 26, of which 20 were waited for; matrix products, arithmetic and copies ran while one was open for 4% of the time, Pallas kernels for 37%

profile of v13, /device:TPU:3, one launch (start us, length us, event | category | flops | bytes accessed | tf_op | source)
XLA Modules:
  0.0 855.3 jit_solution(2470233873444831505)
XLA Ops:
  16.9 11.7 %collective-permute-done = f32[4,16,4096]{2,1,0:T(8,128)} collective-permute-done((f32[4,16,4096]{2,1,0:T(8,128)}, f32[4,16,4096]{2,1,0:T(8,128)}, u32[]{:S(2)}, u32[]{:S(2)}) %collective-permute-start) | collective-permute-done | bytes 1048608 | tf_op jit(solution)/shard_map/ppermute | solution.py:618
  42.8 35.6 %collective-permute-done.1.refs_2_ = f32[4,16,4096]{2,1,0:T(8,128)S(1)} collective-permute-done((f32[4,16,4096]{2,1,0:T(8,128)S(1)}, f32[4,16,4096]{2,1,0:T(8,128)S(1)}, u32[]{:S(2)}, u32[]{:S(2)}) %collective-permute-start.1) | collective-permute-done | bytes 1048608 | tf_op jit(solution)/shard_map/ppermute | solution.py:618
  79.4 16.6 %shard_map.89 = (f32[16,8,32,128]{3,2,1,0:T(8,128)}, f32[16,2,32,128]{3,2,1,0:T(8,128)}) custom-call(s32[2]{0:T(128)} %pad_add_fusion.place, s32[32,2]{1,0:T(8,128)} %copy.17.refs_0_.index, f32[4,16,4096]{2,1,0:T(8,128)} %get-tuple-element.142.refs_1_, f32[4,16,4096]{2,1,0:T(8,128)} %copy-done.23, bf16[32,256,128]{2,1,0:T(8,128)(2,1)} %get-tuple-element.148.refs_3_.whi, ...), custom_call_target="tpu_custom_call" | custom-call | flops 1207959552 | bytes 13107464 | tf_op jit(solution)/shard_map/pallas_call | solution.py:484
  108.9 16.5 %shard_map.82 = (f32[16,8,32,128]{3,2,1,0:T(8,128)}, f32[16,2,32,128]{3,2,1,0:T(8,128)}) custom-call(s32[2]{0:T(128)} %pad_add_fusion.place, s32[32,2]{1,0:T(8,128)} %copy.18.refs_0_.index, f32[4,16,4096]{2,1,0:T(8,128)} %get-tuple-element.142.refs_1_, f32[4,16,4096]{2,1,0:T(8,128)} %copy-done.23, bf16[32,256,128]{2,1,0:T(8,128)(2,1)} %get-tuple-element.147.refs_3_.whi, ...), custom_call_target="tpu_custom_call" | custom-call | flops 1207959552 | bytes 13107464 | tf_op jit(solution)/shard_map/pallas_call | solution.py:484
  125.4 23.3 %collective-permute-done.3.refs_2_ = f32[4,16,4096]{2,1,0:T(8,128)} collective-permute-done((f32[4,16,4096]{2,1,0:T(8,128)}, f32[4,16,4096]{2,1,0:T(8,128)}, u32[]{:S(2)}, u32[]{:S(2)}) %collective-permute-start.3) | collective-permute-done | bytes 1048608 | tf_op jit(solution)/shard_map/ppermute | solution.py:618
  148.7 10.7 %all-to-all-start = ((f32[16,8,32,128]{3,2,1,0:T(8,128)}), f32[16,8,32,128]{3,2,1,0:T(8,128)}, u32[]{:S(2)}, u32[]{:S(2)}) async-start(f32[16,8,32,128]{3,2,1,0:T(8,128)} %get-tuple-element.62), calls=%async_computation | async-start | bytes 4194304 | tf_op jit(solution)/shard_map/all_to_all | solution.py:604
  159.4 16.6 %shard_map.90 = (f32[16,8,32,128]{3,2,1,0:T(8,128)}, f32[16,2,32,128]{3,2,1,0:T(8,128)}) custom-call(s32[2]{0:T(128)} %pad_add_fusion.place, s32[32,2]{1,0:T(8,128)} %copy.17.refs_0_.index, f32[4,16,4096]{2,1,0:T(8,128)} %get-tuple-element.63.refs_1_, f32[4,16,4096]{2,1,0:T(8,128)} %collective-permute-done.3.refs_2_, ...), custom_call_target="tpu_custom_call" | custom-call | flops 1207959552 | bytes 13107464 | tf_op jit(solution)/shard_map/pallas_call | solution.py:484
  198.4 16.5 %shard_map.83 = (f32[16,8,32,128]{3,2,1,0:T(8,128)}, f32[16,2,32,128]{3,2,1,0:T(8,128)}) custom-call(s32[2]{0:T(128)} %pad_add_fusion.place, s32[32,2]{1,0:T(8,128)} %copy.18.refs_0_.index, f32[4,16,4096]{2,1,0:T(8,128)} %get-tuple-element.63.refs_1_, f32[4,16,4096]{2,1,0:T(8,128)} %collective-permute-done.3.refs_2_, ...), custom_call_target="tpu_custom_call" | custom-call | flops 1207959552 | bytes 13107464 | tf_op jit(solution)/shard_map/pallas_call | solution.py:484
  214.9 24.5 %collective-permute-done.4.refs_2_ = f32[4,16,4096]{2,1,0:T(8,128)} collective-permute-done((f32[4,16,4096]{2,1,0:T(8,128)}, f32[4,16,4096]{2,1,0:T(8,128)}, u32[]{:S(2)}, u32[]{:S(2)}) %collective-permute-start.4) | collective-permute-done | bytes 1048608 | tf_op jit(solution)/shard_map/ppermute | solution.py:618
  239.4 10.1 %all-to-all-start.1 = ((f32[16,8,32,128]{3,2,1,0:T(8,128)}), f32[16,8,32,128]{3,2,1,0:T(8,128)}, u32[]{:S(2)}, u32[]{:S(2)}) async-start(f32[16,8,32,128]{3,2,1,0:T(8,128)} %get-tuple-element.66), calls=%async_computation.1 | async-start | bytes 4194304 | tf_op jit(solution)/shard_map/all_to_all | solution.py:604
  249.5 16.5 %shard_map.91 = (f32[16,8,32,128]{3,2,1,0:T(8,128)}, f32[16,2,32,128]{3,2,1,0:T(8,128)}) custom-call(s32[2]{0:T(128)} %pad_add_fusion.place, s32[32,2]{1,0:T(8,128)} %copy.17.refs_0_.index, f32[4,16,4096]{2,1,0:T(8,128)} %get-tuple-element.67.refs_1_, f32[4,16,4096]{2,1,0:T(8,128)} %collective-permute-done.4.refs_2_, ...), custom_call_target="tpu_custom_call" | custom-call | flops 1207959552 | bytes 13107464 | tf_op jit(solution)/shard_map/pallas_call | solution.py:484
  266.0 10.0 %all-to-all-done.1.refs_1_ = f32[16,8,32,128]{3,2,1,0:T(8,128)} async-done(((f32[16,8,32,128]{3,2,1,0:T(8,128)}), f32[16,8,32,128]{3,2,1,0:T(8,128)}, u32[]{:S(2)}, u32[]{:S(2)}) %all-to-all-start.1) | async-done | bytes 2097184 | tf_op jit(solution)/shard_map/all_to_all | solution.py:604
  288.5 16.5 %shard_map.84 = (f32[16,8,32,128]{3,2,1,0:T(8,128)}, f32[16,2,32,128]{3,2,1,0:T(8,128)}) custom-call(s32[2]{0:T(128)} %pad_add_fusion.place, s32[32,2]{1,0:T(8,128)} %copy.18.refs_0_.index, f32[4,16,4096]{2,1,0:T(8,128)} %get-tuple-element.67.refs_1_, f32[4,16,4096]{2,1,0:T(8,128)} %collective-permute-done.4.refs_2_, ...), custom_call_target="tpu_custom_call" | custom-call | flops 1207959552 | bytes 13107464 | tf_op jit(solution)/shard_map/pallas_call | solution.py:484
  305.0 24.7 %collective-permute-done.5.refs_2_ = f32[4,16,4096]{2,1,0:T(8,128)S(1)} collective-permute-done((f32[4,16,4096]{2,1,0:T(8,128)}, f32[4,16,4096]{2,1,0:T(8,128)S(1)}, u32[]{:S(2)}, u32[]{:S(2)}) %collective-permute-start.5) | collective-permute-done | bytes 1048608 | tf_op jit(solution)/shard_map/ppermute | solution.py:618
  339.5 16.6 %shard_map.92 = (f32[16,8,32,128]{3,2,1,0:T(8,128)}, f32[16,2,32,128]{3,2,1,0:T(8,128)}) custom-call(s32[2]{0:T(128)} %pad_add_fusion.place, s32[32,2]{1,0:T(8,128)} %copy.17.refs_0_.index, f32[4,16,4096]{2,1,0:T(8,128)} %get-tuple-element.71.refs_1_, f32[4,16,4096]{2,1,0:T(8,128)} %copy-done.24, bf16[32,256,128]{2,1,0:T(8,128)(2,1)} %get-tuple-element.148.refs_3_.whi, ...), custom_call_target="tpu_custom_call" | custom-call | flops 1207959552 | bytes 13107464 | tf_op jit(solution)/shard_map/pallas_call | solution.py:484
  356.1 10.0 %all-to-all-done.2.refs_2_ = f32[16,8,32,128]{3,2,1,0:T(8,128)} async-done(((f32[16,8,32,128]{3,2,1,0:T(8,128)}), f32[16,8,32,128]{3,2,1,0:T(8,128)}, u32[]{:S(2)}, u32[]{:S(2)}) %all-to-all-start.2) | async-done | bytes 2097184 | tf_op jit(solution)/shard_map/all_to_all | solution.py:604
  372.3 16.5 %shard_map.85 = (f32[16,8,32,128]{3,2,1,0:T(8,128)}, f32[16,2,32,128]{3,2,1,0:T(8,128)}) custom-call(s32[2]{0:T(128)} %pad_add_fusion.place, s32[32,2]{1,0:T(8,128)} %copy.18.refs_0_.index, f32[4,16,4096]{2,1,0:T(8,128)} %get-tuple-element.71.refs_1_, f32[4,16,4096]{2,1,0:T(8,128)} %copy-done.24, bf16[32,256,128]{2,1,0:T(8,128)(2,1)} %get-tuple-element.147.refs_3_.whi, ...), custom_call_target="tpu_custom_call" | custom-call | flops 1207959552 | bytes 13107464 | tf_op jit(solution)/shard_map/pallas_call | solution.py:484
  388.8 9.9 %all-to-all-done.10.refs_3_ = f32[16,8,32,128]{3,2,1,0:T(8,128)S(1)} async-done(((f32[16,8,32,128]{3,2,1,0:T(8,128)}), f32[16,8,32,128]{3,2,1,0:T(8,128)S(1)}, u32[]{:S(2)}, u32[]{:S(2)}) %all-to-all-start.10) | async-done | bytes 2097184 | tf_op jit(solution)/shard_map/all_to_all | solution.py:604
  406.3 20.9 %shard_map.93 = (f32[16,4,128,128]{3,2,1,0:T(8,128)}, f32[16,4,128,128]{3,2,1,0:T(8,128)}) custom-call(f32[16,8,32,128]{3,2,1,0:T(8,128)} %copy-done.2, f32[16,8,32,128]{3,2,1,0:T(8,128)} %copy-done.3, f32[16,8,32,128]{3,2,1,0:T(8,128)} %copy-done.4, f32[16,8,32,128]{3,2,1,0:T(8,128)} %copy-done.8, bf16[16,256,256]{2,1,0:T(8,128)(2,1)} %constant.34.clone.refs_4_.mhi, ...), custom_call_target="tpu_custom_call" | custom-call | flops 3221225472 | bytes 20971520 | tf_op jit(solution)/shard_map/pallas_call | solution.py:484
  441.4 20.9 %shard_map.86 = (f32[16,4,128,128]{3,2,1,0:T(8,128)}, f32[16,4,128,128]{3,2,1,0:T(8,128)}) custom-call(f32[16,8,32,128]{3,2,1,0:T(8,128)} %all-to-all-done.refs_0_, f32[16,8,32,128]{3,2,1,0:T(8,128)} %all-to-all-done.1.refs_1_, f32[16,8,32,128]{3,2,1,0:T(8,128)} %all-to-all-done.2.refs_2_, f32[16,8,32,128]{3,2,1,0:T(8,128)} %copy-done.7, ...), custom_call_target="tpu_custom_call" | custom-call | flops 3221225472 | bytes 20971520 | tf_op jit(solution)/shard_map/pallas_call | solution.py:484
  462.3 33.4 %all-to-all-done.11.fields = f32[16,4,128,128]{3,2,1,0:T(8,128)} async-done(((f32[16,4,128,128]{3,2,1,0:T(8,128)}), f32[16,4,128,128]{3,2,1,0:T(8,128)}, u32[]{:S(2)}, u32[]{:S(2)}) %all-to-all-start.11) | async-done | bytes 4194336 | tf_op jit(solution)/shard_map/all_to_all | solution.py:604
  502.9 16.6 %shard_map.94 = f32[16,2,128,128]{3,2,1,0:T(8,128)} custom-call(f32[16,4,128,128]{3,2,1,0:T(8,128)} %all-to-all-done.11.fields, bf16[16,256,256]{2,1,0:T(8,128)(2,1)} %constant.36.clone.refs_5_.mhi, bf16[16,256,256]{2,1,0:T(8,128)(2,1)} %constant.37.clone.refs_6_.mlo), custom_call_target="tpu_custom_call" | custom-call | flops 2415919104 | bytes 10485760 | tf_op jit(solution)/shard_map/pallas_call | solution.py:484
  519.4 38.0 %all-to-all-done.4.fields = f32[16,4,128,128]{3,2,1,0:T(8,128)} async-done(((f32[16,4,128,128]{3,2,1,0:T(8,128)}), f32[16,4,128,128]{3,2,1,0:T(8,128)}, u32[]{:S(2)}, u32[]{:S(2)}) %all-to-all-start.4) | async-done | bytes 4194336 | tf_op jit(solution)/shard_map/all_to_all | solution.py:604
  563.7 16.6 %shard_map.87 = f32[16,2,128,128]{3,2,1,0:T(8,128)} custom-call(f32[16,4,128,128]{3,2,1,0:T(8,128)} %all-to-all-done.4.fields, bf16[16,256,256]{2,1,0:T(8,128)(2,1)} %constant.36.clone.refs_5_.mhi, bf16[16,256,256]{2,1,0:T(8,128)(2,1)} %constant.37.clone.refs_6_.mlo), custom_call_target="tpu_custom_call" | custom-call | flops 2415919104 | bytes 10485760 | tf_op jit(solution)/shard_map/pallas_call | solution.py:484
  597.7 17.2 %shard_map.95 = (f32[16,4,64,128]{3,2,1,0:T(8,128)}, f32[16,4,64,128]{3,2,1,0:T(8,128)}) custom-call(f32[16,2,128,128]{3,2,1,0:T(8,128)} %copy-done.1, f32[16,4,128,128]{3,2,1,0:T(8,128)} %get-tuple-element.83.kept, bf16[16,256,256]{2,1,0:T(8,128)(2,1)} %constant.34.clone.refs_4_.mhi, bf16[16,256,256]{2,1,0:T(8,128)(2,1)} %constant.35.clone.refs_5_.mlo), custom_call_target="tpu_custom_call" | custom-call | flops 1610612736 | bytes 14680064 | tf_op jit(solution)/shard_map/pallas_call | solution.py:484
  631.5 17.2 %shard_map.88 = (f32[16,4,64,128]{3,2,1,0:T(8,128)}, f32[16,4,64,128]{3,2,1,0:T(8,128)}) custom-call(f32[16,2,128,128]{3,2,1,0:T(8,128)} %copy-done, f32[16,4,128,128]{3,2,1,0:T(8,128)} %get-tuple-element.74.kept, bf16[16,256,256]{2,1,0:T(8,128)(2,1)} %constant.34.clone.refs_4_.mhi, bf16[16,256,256]{2,1,0:T(8,128)(2,1)} %constant.35.clone.refs_5_.mlo), custom_call_target="tpu_custom_call" | custom-call | flops 1610612736 | bytes 14680064 | tf_op jit(solution)/shard_map/pallas_call | solution.py:484
  664.1 17.4 %shard_map.96 = (f32[2,32,4096]{2,1,0:T(8,128)}, f32[2,32,4096]{2,1,0:T(8,128)}) custom-call(s32[2]{0:T(128)} %pad_add_fusion.place, s32[32,2]{1,0:T(8,128)} %copy.17.refs_0_.index, f32[16,4,64,128]{3,2,1,0:T(8,128)} %all-to-all-done.13.back, bf16[32,256,128]{2,1,0:T(8,128)(2,1)} %get-tuple-element.148.refs_3_.whi, ...), custom_call_target="tpu_custom_call" | custom-call | flops 1207959552 | bytes 13631752 | tf_op jit(solution)/shard_map/pallas_call | solution.py:484
  698.1 17.9 %shard_map.97 = (f32[2,32,4096]{2,1,0:T(8,128)}, f32[2,32,4096]{2,1,0:T(8,128)}) custom-call(s32[2]{0:T(128)} %pad_add_fusion.place, s32[32,2]{1,0:T(8,128)} %copy.18.refs_0_.index, f32[16,4,64,128]{3,2,1,0:T(8,128)} %copy-done.6, bf16[32,256,128]{2,1,0:T(8,128)(2,1)} %get-tuple-element.147.refs_3_.whi, ...), custom_call_target="tpu_custom_call" | custom-call | flops 1207959552 | bytes 15728904 | tf_op jit(solution)/shard_map/pallas_call | solution.py:484
  737.4 17.3 %shard_map.98 = (f32[2,32,4096]{2,1,0:T(8,128)}, f32[2,32,4096]{2,1,0:T(8,128)}) custom-call(s32[2]{0:T(128)} %pad_add_fusion.place, s32[32,2]{1,0:T(8,128)} %copy.17.refs_0_.index, f32[16,4,64,128]{3,2,1,0:T(8,128)} %copy-done.5, bf16[32,256,128]{2,1,0:T(8,128)(2,1)} %get-tuple-element.148.refs_3_.whi, ...), custom_call_target="tpu_custom_call" | custom-call | flops 1207959552 | bytes 13631752 | tf_op jit(solution)/shard_map/pallas_call | solution.py:484
  754.8 24.2 %all-to-all-done.14.back = f32[16,4,64,128]{3,2,1,0:T(8,128)} async-done(((f32[16,4,64,128]{3,2,1,0:T(8,128)}), f32[16,4,64,128]{3,2,1,0:T(8,128)}, u32[]{:S(2)}, u32[]{:S(2)}) %all-to-all-start.14) | async-done | bytes 2097184 | tf_op jit(solution)/shard_map/all_to_all | solution.py:604
  778.9 17.9 %shard_map.99 = (f32[2,32,4096]{2,1,0:T(8,128)}, f32[2,32,4096]{2,1,0:T(8,128)}) custom-call(s32[2]{0:T(128)} %pad_add_fusion.place, s32[32,2]{1,0:T(8,128)} %copy.18.refs_0_.index, f32[16,4,64,128]{3,2,1,0:T(8,128)} %all-to-all-done.14.back, bf16[32,256,128]{2,1,0:T(8,128)(2,1)} %get-tuple-element.147.refs_3_.whi, ...), custom_call_target="tpu_custom_call" | custom-call | flops 1207959552 | bytes 15728904 | tf_op jit(solution)/shard_map/pallas_call | solution.py:484
  801.3 43.9 %collective-permute-done.8 = f32[2,32,4096]{2,1,0:T(8,128)S(1)} collective-permute-done((f32[2,32,4096]{2,1,0:T(8,128)}, f32[2,32,4096]{2,1,0:T(8,128)S(1)}, u32[]{:S(2)}, u32[]{:S(2)}) %collective-permute-start.8) | collective-permute-done | bytes 1048608 | tf_op jit(solution)/shard_map/ppermute | solution.py:618
  (124 shorter events, 232.4 us)
Async XLA Ops:
  4.2 24.3 %collective-permute-start = (f32[4,16,4096]{2,1,0:T(8,128)}, f32[4,16,4096]{2,1,0:T(8,128)}, u32[]{:S(2)}, u32[]{:S(2)}) collective-permute-start(f32[4,16,4096]{2,1,0:T(8,128)} %fusion.7), channel_id=1, source_target_pairs={{0,16},{1,17},{2,18},{3,19},{4,20},{5,21},{6,22},{7,23},{8,24},{9,... | collective-permute-start | bytes 3145736 | tf_op jit(solution)/shard_map/ppermute | solution.py:618
  14.9 13.7 %copy-start.14 = (f32[2,16,4096]{2,1,0:T(8,128)S(1)}, f32[2,16,4096]{2,1,0:T(8,128)}, u32[]{:S(2)}) copy-start(f32[2,16,4096]{2,1,0:T(8,128)} %copy-done.13) | copy-start | bytes 1572868
  14.9 13.7 %copy-start.16 = (f32[2,16,4096]{2,1,0:T(8,128)S(1)}, f32[2,16,4096]{2,1,0:T(8,128)}, u32[]{:S(2)}) copy-start(f32[2,16,4096]{2,1,0:T(8,128)} %copy-done.15) | copy-start | bytes 1572868
  31.0 47.4 %collective-permute-start.1 = (f32[4,16,4096]{2,1,0:T(8,128)S(1)}, f32[4,16,4096]{2,1,0:T(8,128)S(1)}, u32[]{:S(2)}, u32[]{:S(2)}) collective-permute-start(f32[4,16,4096]{2,1,0:T(8,128)S(1)} %get-tuple-element.141), channel_id=1, source_target_pairs={{0,8},{1,9},{2,10},{3,11},{4,12},{5,13},{6,14},{7,15},{8,0},{9,1},... | collective-permute-start | bytes 3145736 | tf_op jit(solution)/shard_map/ppermute | solution.py:618
  33.3 68.3 %collective-permute-start.2 = (f32[12,16,4096]{2,1,0:T(8,128)}, f32[12,16,4096]{2,1,0:T(8,128)}, u32[]{:S(2)}, u32[]{:S(2)}) collective-permute-start(f32[12,16,4096]{2,1,0:T(8,128)} %pad_maximum_fusion), channel_id=1, source_target_pairs={{0,16},{1,17},{2,18},{3,19},{4,20},{5,21},{6,22},{7,23},{8,24},{9,... | collective-permute-start | bytes 9437192 | tf_op jit(solution)/shard_map/ppermute | solution.py:618
  96.0 52.6 %all-to-all-start.7 = ((f32[16,8,32,128]{3,2,1,0:T(8,128)}), f32[16,8,32,128]{3,2,1,0:T(8,128)S(1)}, u32[]{:S(2)}, u32[]{:S(2)}) async-start(f32[16,8,32,128]{3,2,1,0:T(8,128)} %get-tuple-element.78), calls=%async_computation.7 | async-start | bytes 4194304 | tf_op jit(solution)/shard_map/all_to_all | solution.py:604
  105.1 43.6 %collective-permute-start.3 = (f32[4,16,4096]{2,1,0:T(8,128)}, f32[4,16,4096]{2,1,0:T(8,128)}, u32[]{:S(2)}, u32[]{:S(2)}) collective-permute-start(f32[4,16,4096]{2,1,0:T(8,128)} %get-tuple-element.61), channel_id=1, source_target_pairs={{0,8},{1,9},{2,10},{3,11},{4,12},{5,13},{6,14},{7,15},{8,0},{9,1},... | collective-permute-start | bytes 3145736 | tf_op jit(solution)/shard_map/ppermute | solution.py:618
  148.7 27.3 %copy-start.2 = (f32[16,8,32,128]{3,2,1,0:T(8,128)}, f32[16,8,32,128]{3,2,1,0:T(8,128)S(1)}, u32[]{:S(2)}) copy-start(f32[16,8,32,128]{3,2,1,0:T(8,128)S(1)} %all-to-all-done.7.refs_0_) | copy-start | bytes 6291460
  148.7 37.3 %all-to-all-start = ((f32[16,8,32,128]{3,2,1,0:T(8,128)}), f32[16,8,32,128]{3,2,1,0:T(8,128)}, u32[]{:S(2)}, u32[]{:S(2)}) async-start(f32[16,8,32,128]{3,2,1,0:T(8,128)} %get-tuple-element.62), calls=%async_computation | async-start | bytes 4194304 | tf_op jit(solution)/shard_map/all_to_all | solution.py:604
  185.9 53.4 %all-to-all-start.8 = ((f32[16,8,32,128]{3,2,1,0:T(8,128)}), f32[16,8,32,128]{3,2,1,0:T(8,128)S(1)}, u32[]{:S(2)}, u32[]{:S(2)}) async-start(f32[16,8,32,128]{3,2,1,0:T(8,128)} %get-tuple-element.79), calls=%async_computation.8 | async-start | bytes 4194304 | tf_op jit(solution)/shard_map/all_to_all | solution.py:604
  195.5 43.9 %collective-permute-start.4 = (f32[4,16,4096]{2,1,0:T(8,128)}, f32[4,16,4096]{2,1,0:T(8,128)}, u32[]{:S(2)}, u32[]{:S(2)}) collective-permute-start(f32[4,16,4096]{2,1,0:T(8,128)} %get-tuple-element.65), channel_id=1, source_target_pairs={{0,8},{1,9},{2,10},{3,11},{4,12},{5,13},{6,14},{7,15},{8,0},{9,1},... | collective-permute-start | bytes 3145736 | tf_op jit(solution)/shard_map/ppermute | solution.py:618
  239.4 26.7 %copy-start.3 = (f32[16,8,32,128]{3,2,1,0:T(8,128)}, f32[16,8,32,128]{3,2,1,0:T(8,128)S(1)}, u32[]{:S(2)}) copy-start(f32[16,8,32,128]{3,2,1,0:T(8,128)S(1)} %all-to-all-done.8.refs_1_) | copy-start | bytes 6291460
  239.4 36.7 %all-to-all-start.1 = ((f32[16,8,32,128]{3,2,1,0:T(8,128)}), f32[16,8,32,128]{3,2,1,0:T(8,128)}, u32[]{:S(2)}, u32[]{:S(2)}) async-start(f32[16,8,32,128]{3,2,1,0:T(8,128)} %get-tuple-element.66), calls=%async_computation.1 | async-start | bytes 4194304 | tf_op jit(solution)/shard_map/all_to_all | solution.py:604
  276.1 53.6 %all-to-all-start.9 = ((f32[16,8,32,128]{3,2,1,0:T(8,128)}), f32[16,8,32,128]{3,2,1,0:T(8,128)S(1)}, u32[]{:S(2)}, u32[]{:S(2)}) async-start(f32[16,8,32,128]{3,2,1,0:T(8,128)} %get-tuple-element.80), calls=%async_computation.9 | async-start | bytes 4194304 | tf_op jit(solution)/shard_map/all_to_all | solution.py:604
  285.6 44.1 %collective-permute-start.5 = (f32[4,16,4096]{2,1,0:T(8,128)}, f32[4,16,4096]{2,1,0:T(8,128)S(1)}, u32[]{:S(2)}, u32[]{:S(2)}) collective-permute-start(f32[4,16,4096]{2,1,0:T(8,128)} %get-tuple-element.69), channel_id=1, source_target_pairs={{0,8},{1,9},{2,10},{3,11},{4,12},{5,13},{6,14},{7,15},{8,0},{9,1},... | collective-permute-start | bytes 3145736 | tf_op jit(solution)/shard_map/ppermute | solution.py:618
  329.7 26.4 %copy-start.4 = (f32[16,8,32,128]{3,2,1,0:T(8,128)}, f32[16,8,32,128]{3,2,1,0:T(8,128)S(1)}, u32[]{:S(2)}) copy-start(f32[16,8,32,128]{3,2,1,0:T(8,128)S(1)} %all-to-all-done.9.refs_2_) | copy-start | bytes 6291460
  329.7 36.5 %all-to-all-start.2 = ((f32[16,8,32,128]{3,2,1,0:T(8,128)}), f32[16,8,32,128]{3,2,1,0:T(8,128)}, u32[]{:S(2)}, u32[]{:S(2)}) async-start(f32[16,8,32,128]{3,2,1,0:T(8,128)} %get-tuple-element.70), calls=%async_computation.2 | async-start | bytes 4194304 | tf_op jit(solution)/shard_map/all_to_all | solution.py:604
  366.1 32.6 %all-to-all-start.10 = ((f32[16,8,32,128]{3,2,1,0:T(8,128)}), f32[16,8,32,128]{3,2,1,0:T(8,128)S(1)}, u32[]{:S(2)}, u32[]{:S(2)}) async-start(f32[16,8,32,128]{3,2,1,0:T(8,128)} %get-tuple-element.81), calls=%async_computation.10 | async-start | bytes 4194304 | tf_op jit(solution)/shard_map/all_to_all | solution.py:604
  400.1 32.7 %all-to-all-start.3 = ((f32[16,8,32,128]{3,2,1,0:T(8,128)}), f32[16,8,32,128]{3,2,1,0:T(8,128)S(1)}, u32[]{:S(2)}, u32[]{:S(2)}) async-start(f32[16,8,32,128]{3,2,1,0:T(8,128)} %get-tuple-element.72), calls=%async_computation.3 | async-start | bytes 4194304 | tf_op jit(solution)/shard_map/all_to_all | solution.py:604
  434.1 61.7 %all-to-all-start.11 = ((f32[16,4,128,128]{3,2,1,0:T(8,128)}), f32[16,4,128,128]{3,2,1,0:T(8,128)}, u32[]{:S(2)}, u32[]{:S(2)}) async-start(f32[16,4,128,128]{3,2,1,0:T(8,128)} %get-tuple-element.82), calls=%async_computation.11 | async-start | bytes 8388608 | tf_op jit(solution)/shard_map/all_to_all | solution.py:604
  495.8 61.6 %all-to-all-start.4 = ((f32[16,4,128,128]{3,2,1,0:T(8,128)}), f32[16,4,128,128]{3,2,1,0:T(8,128)}, u32[]{:S(2)}, u32[]{:S(2)}) async-start(f32[16,4,128,128]{3,2,1,0:T(8,128)} %get-tuple-element.73), calls=%async_computation.4 | async-start | bytes 8388608 | tf_op jit(solution)/shard_map/all_to_all | solution.py:604
  557.4 32.8 %all-to-all-start.12 = ((f32[16,2,128,128]{3,2,1,0:T(8,128)}), f32[16,2,128,128]{3,2,1,0:T(8,128)S(1)}, u32[]{:S(2)}, u32[]{:S(2)}) async-start(f32[16,2,128,128]{3,2,1,0:T(8,128)} %shard_map.94), calls=%async_computation.12 | async-start | bytes 4194304 | tf_op jit(solution)/shard_map/all_to_all | solution.py:604
  591.5 32.7 %all-to-all-start.5 = ((f32[16,2,128,128]{3,2,1,0:T(8,128)}), f32[16,2,128,128]{3,2,1,0:T(8,128)S(1)}, u32[]{:S(2)}, u32[]{:S(2)}) async-start(f32[16,2,128,128]{3,2,1,0:T(8,128)} %shard_map.87), calls=%async_computation.5 | async-start | bytes 4194304 | tf_op jit(solution)/shard_map/all_to_all | solution.py:604
  624.2 33.7 %all-to-all-start.13 = ((f32[16,4,64,128]{3,2,1,0:T(8,128)}), f32[16,4,64,128]{3,2,1,0:T(8,128)}, u32[]{:S(2)}, u32[]{:S(2)}) async-start(f32[16,4,64,128]{3,2,1,0:T(8,128)} %get-tuple-element.84), calls=%async_computation.13 | async-start | bytes 4194304 | tf_op jit(solution)/shard_map/all_to_all | solution.py:604
  657.9 32.7 %all-to-all-start.6 = ((f32[16,4,64,128]{3,2,1,0:T(8,128)}), f32[16,4,64,128]{3,2,1,0:T(8,128)S(1)}, u32[]{:S(2)}, u32[]{:S(2)}) async-start(f32[16,4,64,128]{3,2,1,0:T(8,128)} %get-tuple-element.75), calls=%async_computation.6 | async-start | bytes 4194304 | tf_op jit(solution)/shard_map/all_to_all | solution.py:604
  691.9 32.7 %all-to-all-start.15 = ((f32[16,4,64,128]{3,2,1,0:T(8,128)}), f32[16,4,64,128]{3,2,1,0:T(8,128)S(1)}, u32[]{:S(2)}, u32[]{:S(2)}) async-start(f32[16,4,64,128]{3,2,1,0:T(8,128)} %get-tuple-element.96), calls=%async_computation.15 | async-start | bytes 4194304 | tf_op jit(solution)/shard_map/all_to_all | solution.py:604
  716.0 15.4 %copy-start.25 = (f32[2,32,4096]{2,1,0:T(8,128)S(1)}, f32[2,32,4096]{2,1,0:T(8,128)}, u32[]{:S(2)}) copy-start(f32[2,32,4096]{2,1,0:T(8,128)} %get-tuple-element.103) | copy-start | bytes 3145732
  724.5 54.4 %all-to-all-start.14 = ((f32[16,4,64,128]{3,2,1,0:T(8,128)}), f32[16,4,64,128]{3,2,1,0:T(8,128)}, u32[]{:S(2)}, u32[]{:S(2)}) async-start(f32[16,4,64,128]{3,2,1,0:T(8,128)} %get-tuple-element.92), calls=%async_computation.14 | async-start | bytes 4194304 | tf_op jit(solution)/shard_map/all_to_all | solution.py:604
  731.4 69.9 %collective-permute-start.6 = (f32[2,32,4096]{2,1,0:T(8,128)}, f32[2,32,4096]{2,1,0:T(8,128)}, u32[]{:S(2)}, u32[]{:S(2)}) collective-permute-start(f32[2,32,4096]{2,1,0:T(8,128)} %get-tuple-element.89), channel_id=1, source_target_pairs={{0,8},{1,9},{2,10},{3,11},{4,12},{5,13},{6,14},{7,15},{16,0},{17,1... | collective-permute-start | bytes 3145736 | tf_op jit(solution)/shard_map/ppermute | solution.py:618
  731.4 69.9 %collective-permute-start.7 = (f32[2,32,4096]{2,1,0:T(8,128)S(1)}, f32[2,32,4096]{2,1,0:T(8,128)}, u32[]{:S(2)}, u32[]{:S(2)}) collective-permute-start(f32[2,32,4096]{2,1,0:T(8,128)S(1)} %copy-done.25), channel_id=1, source_target_pairs={{8,16},{9,17},{10,18},{11,19},{12,20},{13,21},{14,22},{15,23},{16,... | collective-permute-start | bytes 3145736 | tf_op jit(solution)/shard_map/ppermute | solution.py:618
  796.9 48.3 %collective-permute-start.8 = (f32[2,32,4096]{2,1,0:T(8,128)}, f32[2,32,4096]{2,1,0:T(8,128)S(1)}, u32[]{:S(2)}, u32[]{:S(2)}) collective-permute-start(f32[2,32,4096]{2,1,0:T(8,128)} %get-tuple-element.101), channel_id=1, source_target_pairs={{0,8},{1,9},{2,10},{3,11},{4,12},{5,13},{6,14},{7,15},{16,0},{17,1... | collective-permute-start | bytes 3145736 | tf_op jit(solution)/shard_map/ppermute | solution.py:618
  799.4 49.3 %collective-permute-start.9 = (f32[2,32,4096]{2,1,0:T(8,128)}, f32[2,32,4096]{2,1,0:T(8,128)S(1)}, u32[]{:S(2)}, u32[]{:S(2)}) collective-permute-start(f32[2,32,4096]{2,1,0:T(8,128)} %get-tuple-element.106), channel_id=1, source_target_pairs={{8,16},{9,17},{10,18},{11,19},{12,20},{13,21},{14,22},{15,23},{16,... | collective-permute-start | bytes 3145736 | tf_op jit(solution)/shard_map/ppermute | solution.py:618
  (23 other events, 106.3 us)
